TPU v7x, 256 devices: a whole 4x4x8 slice. The times are simulated.
256 devices in a mesh: row: 32 (over z, y_lo, core), col: 8 (over y_hi, x).
Axes of the slice: x: 4, y: 4 (y_hi: 2, y_lo: 2; y = y_hi * 2 + y_lo), z: 8, core: 2. Of those that a mesh axis runs over, the one named last changes fastest.
Arguments:
- matrix: bfloat16 [6144, 6144], P('row', 'col'), may hold values from -1 to 1, as said below
- pattern: int32 [48, 48], replicated, may hold values 0 or 1
- keep: int32 [48, 48], replicated, may hold values 0 or 1
Outputs:
- updated: bfloat16 [6144, 6144], P('row', 'col')
Inputs may be any that keep to these rules, and one draw needn't show every extreme that they name: matrix is symmetric, its diagonal entries of either sign and magnitude well above the off-diagonal ones.
All inputs are finite; a program needn't handle non-finite values.
Results may differ from a plain program's by a relative error of at most 0.0052.
Values may be sent and summed in bfloat16 or wider, within the bound.
No kernel may reach another device: no remote copies, remote signals or barrier semaphores. Data moves between devices by JAX's collectives and lax.ppermute only.
A program may use at most 64 MiB of HBM per device.

v0:
```python
import jax
import jax.numpy as jnp
from jax import lax
from jax.sharding import PartitionSpec as P


def block_table(table, with_diagonal):
    upper = jnp.triu(table)
    sym = upper + jnp.triu(table, 1).T
    if with_diagonal:
        sym = jnp.maximum(sym, jnp.eye(table.shape[0], dtype=jnp.int32))
    return (sym > 0).astype(jnp.float32)


def local_mask(table, row_pick, col_pick):
    picked = jnp.dot(jnp.dot(row_pick, table), col_pick.T)
    return (picked > 0.5).astype(jnp.float32)


def shards(matrix, pattern, keep):
    rows = matrix.shape[0]
    cols = matrix.shape[1]
    nblocks = pattern.shape[0]
    total = cols * lax.axis_size("col")
    bsize = total // nblocks
    row_ids = lax.axis_index("row") * rows + jnp.arange(rows, dtype=jnp.int32)
    col_ids = lax.axis_index("col") * cols + jnp.arange(cols, dtype=jnp.int32)
    block_ids = jnp.arange(nblocks, dtype=jnp.int32)
    row_pick = (row_ids[:, None] // bsize == block_ids[None, :]).astype(jnp.float32)
    col_pick = (col_ids[:, None] // bsize == block_ids[None, :]).astype(jnp.float32)
    smask = local_mask(block_table(pattern, True), row_pick, col_pick)
    kmask = local_mask(block_table(keep, False), row_pick, col_pick)
    xlocal = (matrix.astype(jnp.float32) * smask).astype(jnp.bfloat16)
    panel = lax.all_gather(xlocal, "col", axis=1, tiled=True)

    def add_rows(piece):
        return jnp.dot(panel, piece, preferred_element_type=jnp.float32)

    square = add_rows(lax.all_gather(xlocal, "row", axis=0, tiled=True))
    eye_local = (row_ids[:, None] == col_ids[None, :]).astype(jnp.float32)
    weight = (1.5 * eye_local - 0.5 * (square * kmask)).astype(jnp.bfloat16)
    result = add_rows(lax.all_gather(weight, "row", axis=0, tiled=True))
    return (result * smask).astype(jnp.bfloat16)


def solution(mesh):
    return jax.shard_map(
        shards,
        mesh=mesh,
        in_specs=(P("row", "col"), P(), P()),
        out_specs=P("row", "col"),
        check_vma=False,
    )
```

profile of v0, /device:TPU:1, one launch (start us, length us, event | category | flops | bytes accessed | tf_op | source)
XLA Modules:
  0.0 243.2 jit_solution(5747714793660551674)
XLA Ops:
  6.5 0.0 all-gather.4.cloned.1.call-start
  6.6 0.8 copy.4
  7.4 2.1 select_convert_fusion
  9.5 0.0 all-gather.4.cloned.1.call-update
  9.6 0.0 all-gather.6.cloned.1.call-start
  9.6 0.7 all-gather.6.cloned.1.call-update
  10.3 0.0 all-gather.8.cloned.1.call-start
  10.3 0.8 copy.6
  11.2 1.1 convolution_compare_fusion
  12.3 62.3 %all-gather.4.cloned.1.call-done = bf16[192,6144]{1,0:T(8,128)(2,1)} async-done(((bf16[192,768]{1,0:T(8,128)(2,1)}), bf16[192,6144]{1,0:T(8,128)(2,1)}) %all-gather.4.cloned.1.call-update) | async-done | bytes 2359312 | tf_op jit(solution)/shard_map/all_gather | solution.py:34
  74.6 0.0 copy-start
  74.6 75.3 %all-gather.6.cloned.1.call-done = bf16[6144,768]{1,0:T(8,128)(2,1)} async-done(((bf16[192,768]{1,0:T(8,128)(2,1)}), bf16[6144,768]{1,0:T(8,128)(2,1)}) %all-gather.6.cloned.1.call-update) | async-done | bytes 9437200 | tf_op jit(solution)/shard_map/all_gather | solution.py:39
  149.9 7.1 %fusion.2 = bf16[192,768]{1,0:T(8,128)(2,1)} fusion(pred[192,768]{1,0:T(32,128)(4,1)S(1)} %convolution_compare_fusion, bf16[192,6144]{1,0:T(8,128)(2,1)} %all-gather.4.cloned.1.call-done, bf16[6144,768]{1,0:T(8,128)(2,1)} %all-gather.6.cloned.1.call-done, s32[768]{0:T(1024)S(1)} %iota_add_fusion, s32[192]{0:T(256)S(1)} %iota_add_fusion.1), kind=kOutput, calls=%fused_computation.4 | convolution fusion | flops 1812824064 | bytes 12242688 | tf_op jit(solution)/shard_map/dot_general | solution.py:37
  157.0 0.0 all-gather.8.cloned.1.call-update
  157.0 73.2 %all-gather.8.cloned.1.call-done = bf16[6144,768]{1,0:T(8,128)(2,1)} async-done(((bf16[192,768]{1,0:T(8,128)(2,1)}), bf16[6144,768]{1,0:T(8,128)(2,1)}) %all-gather.8.cloned.1.call-update) | async-done | bytes 9437200 | tf_op jit(solution)/shard_map/all_gather | solution.py:42
  230.2 0.0 copy-done
  230.2 6.4 %fusion.3 = bf16[192,768]{1,0:T(8,128)(2,1)} fusion(pred[192,768]{1,0:T(32,128)(4,1)S(1)} %get-tuple-element.6, bf16[192,6144]{1,0:T(8,128)(2,1)S(1)} %copy-done, bf16[6144,768]{1,0:T(8,128)(2,1)} %all-gather.8.cloned.1.call-done), kind=kOutput, calls=%fused_computation.5 | convolution fusion | flops 1812234240 | bytes 12238848 | tf_op jit(solution)/shard_map/dot_general | solution.py:37
  (5 shorter events, 0.0 us)
Async XLA Ops:
  6.5 68.1 %all-gather.4.cloned.1.call-start = ((), (), s32[]{:S(2)}) async-start(), calls=%async_computation | async-start | bytes 2654208 | tf_op jit(solution)/shard_map/all_gather | solution.py:34
  9.6 140.3 %all-gather.6.cloned.1.call-start = ((), (), s32[]{:S(2)}) async-start(), calls=%async_computation.1 | async-start | bytes 9732096 | tf_op jit(solution)/shard_map/all_gather | solution.py:39
  10.3 219.9 %all-gather.8.cloned.1.call-start = ((), (), s32[]{:S(2)}) async-start(), calls=%async_computation.2 | async-start | bytes 9732096 | tf_op jit(solution)/shard_map/all_gather | solution.py:42
  74.6 155.6 %copy-start = (bf16[192,6144]{1,0:T(8,128)(2,1)S(1)}, bf16[192,6144]{1,0:T(8,128)(2,1)}, u32[]{:S(2)}) copy-start(bf16[192,6144]{1,0:T(8,128)(2,1)} %all-gather.4.cloned.1.call-done) | copy-start | bytes 7077892
Sparse Core Ops, SparseCore 0:
  10.0 64.5 all-gather.3
  76.4 73.3 all-gather.5
  157.2 72.9 all-gather.7
where the time goes:
time: 243 us
  waiting for transfers between devices  211 us (87%)
  matrix products  16.9 us (7%)
  between operations  13.1 us (5%)
    all_gather x1, waiting for transfers between devices, shards(): square = add_rows(lax.all_gather(xlocal, 'row', axis=0, tiled=True))  75.3 us
    all_gather x1, waiting for transfers between devices, shards(): result = add_rows(lax.all_gather(weight, 'row', axis=0, tiled=True))  73.2 us
    all_gather x1, waiting for transfers between devices, shards(): panel = lax.all_gather(xlocal, 'col', axis=1, tiled=True)  62.3 us
    dot_general x2, matrix products, add_rows(): return jnp.dot(panel, piece, preferred_element_type=jnp.float32)  13.6 us
  transfers between devices with their start and end apart: 3, of which 3 were waited for; matrix products, arithmetic and copies ran while one was open for 1% of the time, Pallas kernels for 0%

commit v1 on v0

v1 whole, which is shorter than its diff:
```python
import jax
import jax.numpy as jnp
import numpy as np
from jax import lax
from jax.experimental import pallas as pl
from jax.experimental.pallas import tpu as pltpu
from jax.sharding import PartitionSpec as P

SIZES = (8, 2, 2, 2, 4)
AXES = ("row", "col")
ROWS, COLS = 192, 768
HALF = COLS // 2
SLAB, BLOCK = 64, 128
VMEM_LIMIT = 48 * 1024 * 1024
F32, BF16 = jnp.float32, jnp.bfloat16


def moves(step):
    pairs = []
    for index, place in enumerate(np.ndindex(*SIZES)):
        target = np.mod(step(*place), SIZES)
        pairs.append((index, int(np.ravel_multi_index(target, SIZES))))
    return pairs


def along_y(shift):
    def step(z, yl, core, yh, x):
        y = (2 * yh + yl + shift) % 4
        return z, y % 2, core, y // 2, x

    return moves(step)


EAST = moves(lambda z, yl, core, yh, x: (z, yl, core, yh, x + 1))
WEST = moves(lambda z, yl, core, yh, x: (z, yl, core, yh, x - 1))
NORTH, SOUTH = along_y(1), along_y(-1)
ACROSS = moves(lambda z, yl, core, yh, x: (z, yl, core, yh + 1, x + 2))
TWIN = moves(lambda z, yl, core, yh, x: (z, 1 - yl, core, yh, x))
CORE = moves(lambda z, yl, core, yh, x: (z, yl, 1 - core, yh, x))
RING = moves(lambda z, yl, core, yh, x: (z + 1 - 2 * core, yl, core, yh, x))


def send(value, pairs):
    return lax.ppermute(value, AXES, pairs)


def cat(*parts):
    return jnp.concatenate(parts, axis=0)


def place():
    row, col = lax.axis_index("row"), lax.axis_index("col")
    return row // 4, (row // 2) % 2, row % 2, col


def listed(table, a, b):
    return table[jnp.minimum(a, b), jnp.maximum(a, b)] > 0


def mask_kernel(pattern, matrix, masked, keep, away):
    _, yl, _, col = place()
    row = lax.axis_index("row")
    for i in range(ROWS // SLAB):
        a = (row * 3 + i) // 2
        rows = slice(SLAB * i, SLAB * (i + 1))
        parts = []
        for j in range(COLS // BLOCK):
            b = col * 6 + j
            factor = jnp.where(listed(pattern, a, b) | (a == b), 1.0, 0.0).astype(F32)
            part = matrix[rows, BLOCK * j : BLOCK * (j + 1)].astype(F32) * factor
            parts.append(part.astype(BF16))
        line = jnp.concatenate(parts, axis=1)
        masked[rows, :] = line

    @pl.when(yl == 0)
    def _():
        keep[...] = masked[:, :HALF]
        away[...] = masked[:, HALF:]

    @pl.when(yl == 1)
    def _():
        keep[...] = masked[:, HALF:]
        away[...] = masked[:, :HALF]


OFFSETS = (
    (0, 0), (-1, 0), (1, 0), (0, -1), (0, 1),
    (-1, -1), (1, 1), (1, -1), (-1, 1),
    (2, 0), (0, 2), (-1, 2), (1, 2), (2, -1), (2, 1), (2, 2),
)


def fill_columns(column, pieces):
    own, other, low, low_other, high, far = pieces
    z, yl, core, _ = place()
    sign = 2 * core - 1

    def put(ref, start, k, which):
        k = lax.rem(k + 16, 8)
        column[k, yl * 2 + which] = ref[start : start + ROWS, :]
        column[k, (1 - yl) * 2 + which] = ref[start + ROWS : start + 2 * ROWS, :]

    put(own, 0, z, core)
    put(other, 0, z, 1 - core)
    for s in range(3):
        put(low[s], 0, z + sign * (s + 1), core)
        put(low_other[s], 0, z + sign * (s + 1), 1 - core)
        put(high[s], 0, z - sign * (s + 1), 1 - core)
        put(high[s], 2 * ROWS, z - sign * (s + 1), core)
    put(far[0], 0, z + 4, core)
    put(far[1], 0, z + 4, 1 - core)


def products(panel, column, total):
    total[...] = jnp.zeros_like(total)

    def step(k, carry):
        right = column[k].reshape(COLS, HALF)
        total[...] += jnp.dot(panel[k], right, preferred_element_type=F32)
        return carry

    lax.fori_loop(0, 8, step, 0)


def tiles(body):
    z, yl, core, col = place()
    for h in range(2):
        which = yl if h == 0 else 1 - yl
        slabs = (z * 4 + which * 2 + core) * 3
        for i in range(3):
            for j in range(3):
                a, b = (slabs + i) // 2, col * 6 + yl * 3 + j
                rows = slice(ROWS * h + SLAB * i, ROWS * h + SLAB * (i + 1))
                cols = slice(BLOCK * j, BLOCK * (j + 1))
                body(rows, cols, a, b, (slabs + i) * SLAB, b * BLOCK)


def split_pieces(refs):
    own, other, a1, b1, a2, b2, a3, b3, a4, s1, s2, s3, s4 = refs
    return own, other, (a1, a2, a3), (b1, b2, b3), (s1, s2, s3), (a4, s4)


def square_kernel(*refs):
    keep, blocks, pieces = refs[0], refs[1:17], refs[17:30]
    weight, panel, column, total = refs[30:]
    _, yl, _, col = place()
    yh, x = col // 4, col % 4
    for (dx, dy), ref in zip(OFFSETS, blocks, strict=True):
        x_from = lax.rem(x + dx + 4, 4)
        y_from = lax.rem(2 * yh + yl + dy + 4, 4)
        part = dy % 2
        panel[(y_from // 2) * 4 + x_from, ROWS * part : ROWS * (part + 1), :] = ref[...]
    fill_columns(column, split_pieces(pieces))
    products(panel, column, total)

    def body(rows, cols, a, b, row0, col0):
        factor = jnp.where(listed(keep, a, b), 0.5, 0.0).astype(F32)
        shape = (SLAB, BLOCK)
        down = lax.broadcasted_iota(jnp.int32, shape, 0) + row0
        over = lax.broadcasted_iota(jnp.int32, shape, 1) + col0
        eye = jnp.where(down == over, 1.5, 0.0).astype(F32)
        weight[rows, cols] = (eye - total[rows, cols] * factor).astype(BF16)

    tiles(body)


def update_kernel(*refs):
    pattern, panel, pieces = refs[0], refs[1], refs[2:15]
    mine, away, column, total = refs[15:]
    fill_columns(column, split_pieces(pieces))
    products(panel, column, total)

    def body(rows, cols, a, b, row0, col0):
        del row0, col0
        factor = jnp.where(listed(pattern, a, b) | (a == b), 1.0, 0.0).astype(F32)
        value = (total[rows, cols] * factor).astype(BF16)
        if rows.start < ROWS:
            mine[rows, cols] = value
        else:
            away[rows.start - ROWS : rows.stop - ROWS, cols] = value

    tiles(body)


SMEM, VMEM = (pl.BlockSpec(memory_space=space) for space in (pltpu.SMEM, pltpu.VMEM))


def struct(*shape, dtype=BF16):
    return jax.ShapeDtypeStruct(shape, dtype)


def call(kernel, args, outs, scratch, flops):
    return pl.pallas_call(
        kernel,
        in_specs=[SMEM] + [VMEM] * (len(args) - 1),
        out_specs=[VMEM] * len(outs),
        out_shape=outs,
        scratch_shapes=scratch,
        cost_estimate=pl.CostEstimate(flops=flops, bytes_accessed=0, transcendentals=0),
        compiler_params=pltpu.CompilerParams(vmem_limit_bytes=VMEM_LIMIT),
    )(*args)


def ring(piece):
    other = send(piece, CORE)
    a, b, got, swapped = piece, other, [], []
    for _ in range(3):
        a, b = send(a, RING), send(b, RING)
        got += [a, b]
        swapped.append(send(cat(a, b), CORE))
    a = send(a, RING)
    return [piece, other, *got, a, *swapped, send(a, CORE)]


def plane(x):
    half = ROWS // 2
    d = send(x, ACROSS)
    w, e, s, n = send(x, EAST), send(x, WEST), send(x, NORTH), send(x, SOUTH)
    sw = send(cat(s, w[:half]), EAST)
    ne = send(cat(n, e[half:]), WEST)
    se = send(cat(e, s[:half]), NORTH)
    nw = send(cat(w, n[half:]), SOUTH)
    x2 = cat(sw[ROWS:], ne[ROWS:])
    y2 = cat(se[ROWS:], nw[ROWS:])
    c1, c2, c3, c4 = send(y2, EAST), send(y2, WEST), send(x2, NORTH), send(x2, SOUTH)
    return [x, w, e, s, n, sw[:ROWS], ne[:ROWS], se[:ROWS], nw[:ROWS], x2, y2, c1, c2, c3, c4, d]


SCRATCH = [pltpu.VMEM((8, 4, ROWS, HALF), BF16), pltpu.VMEM((2 * ROWS, HALF), F32)]
FLOPS = 2 * 2 * ROWS * HALF * 6144


def shards(matrix, pattern, keep):
    _, yl, _, _ = place()
    x, kept, away = call(
        mask_kernel,
        [pattern, matrix],
        [struct(ROWS, COLS), struct(ROWS, HALF), struct(ROWS, HALF)],
        [],
        0,
    )
    pieces = ring(cat(kept, send(away, TWIN)))
    weight, panel = call(
        square_kernel,
        [keep, *plane(x), *pieces],
        [struct(2 * ROWS, HALF), struct(8, 2 * ROWS, COLS)],
        SCRATCH,
        FLOPS,
    )
    mine, away = call(
        update_kernel,
        [pattern, panel, *ring(weight)],
        [struct(ROWS, HALF), struct(ROWS, HALF)],
        SCRATCH,
        FLOPS,
    )
    theirs = send(away, TWIN)
    left, right = jnp.where(yl == 0, mine, theirs), jnp.where(yl == 0, theirs, mine)
    return jnp.concatenate([left, right], axis=1)


def solution(mesh):
    return jax.shard_map(
        shards,
        mesh=mesh,
        in_specs=(P("row", "col"), P(), P()),
        out_specs=P("row", "col"),
        check_vma=False,
    )
```

time: 243 us -> 127 us (0.52)
  waiting for transfers between devices: 211 us -> 33 us
  starting transfers between devices: 0.08 us -> 72 us
  matrix products: 16.9 us -> 0 us
  Pallas kernels: 0 us -> 16.7 us
  between operations: 13.1 us -> 0.42 us
    all_gather x3 -> x0, waiting for transfers between devices: 211 us -> none  [the longest x1 75.3 us: shards(): square = add_rows(lax.all_gather(xlocal, 'row', axis=0, tiled=True))]
    ppermute x0 -> x39, starting transfers between devices: none -> 72 us  [send(): return lax.ppermute(value, AXES, pairs)]
    ppermute x0 -> x39, waiting for transfers between devices: none -> 33 us  [send(): return lax.ppermute(value, AXES, pairs)]
    dot_general x4 -> x0, matrix products: 16.9 us -> none  [the longest x2 13.6 us: add_rows(): return jnp.dot(panel, piece, preferred_element_type=jnp.float32)]
    pallas_call x0 -> x3, Pallas kernels: none -> 16.7 us  [call(): pl.pallas_call(kernel, in_specs=[SMEM] + [VMEM] * (len(args) - 1), out_sp...]
  transfers between devices with their start and end apart: 3 -> 39, of which waited for: 3 -> 13; matrix products, arithmetic and copies ran while one was open for 1% -> 1% of each run, Pallas kernels for 0% -> 0%
where the time goes in v1:
time: 127 us
  starting transfers between devices  72 us (57%)
  waiting for transfers between devices  33 us (26%)
  Pallas kernels  16.7 us (13%)
  local copies, waits for them, and re-layouts  3.9 us (3%)
  other arithmetic  1.3 us (1%)
    ppermute x39, starting transfers between devices, send(): return lax.ppermute(value, AXES, pairs)  72 us
    ppermute x39, waiting for transfers between devices, send(): return lax.ppermute(value, AXES, pairs)  33 us
    pallas_call x3, Pallas kernels, call(): pl.pallas_call(kernel, in_specs=[SMEM] + [VMEM] * (len(args) - 1), out_sp...  16.7 us
    unnamed x27, local copies, waits for them, and re-layouts  3.7 us
  transfers between devices with their start and end apart: 39, of which 13 were waited for; matrix products, arithmetic and copies ran while one was open for 1% of the time, Pallas kernels for 0%

profile of v1, /device:TPU:1, one launch (start us, length us, event | category | flops | bytes accessed | tf_op | source)
XLA Modules:
  0.0 127.2 jit_solution(10937611997357591642)
XLA Ops:
  0.0 1.0 copy-done
  1.0 0.7 copy-done.1
  1.7 1.1 shard_map.37
  2.8 2.2 %collective-permute-start.13 = (bf16[192,384]{1,0:T(8,128)(2,1)S(1)}, bf16[192,384]{1,0:T(8,128)(2,1)S(1)}, u32[]{:S(2)}, u32[]{:S(2)}) collective-permute-start(bf16[192,384]{1,0:T(8,128)(2,1)S(1)} %get-tuple-element.14), channel_id=1, source_target_pairs={{0,16},{1,17},{2,18},{3,19},{4,20},{5,21},{6,22},{7,23},{8,24},{9,... | collective-permute-start | bytes 442376 | tf_op jit(solution)/shard_map/ppermute | solution.py:44
  5.0 1.2 collective-permute-start
  6.2 0.2 collective-permute-start.2
  6.4 1.4 %collective-permute-start.1 = (bf16[192,768]{1,0:T(8,128)(2,1)S(1)}, bf16[192,768]{1,0:T(8,128)(2,1)S(1)}, u32[]{:S(2)}, u32[]{:S(2)}) collective-permute-start(bf16[192,768]{1,0:T(8,128)(2,1)S(1)} %get-tuple-element.12.refs_1_), channel_id=1, source_target_pairs={{0,3},{1,0},{2,1},{3,2},{4,7},{5,4},{6,5},{7,6},{8,11},{9,8},{10,9... | collective-permute-start | bytes 884744 | tf_op jit(solution)/shard_map/ppermute | solution.py:44
  7.8 3.7 %collective-permute-start.14 = (bf16[384,384]{1,0:T(8,128)(2,1)S(1)}, bf16[384,384]{1,0:T(8,128)(2,1)S(1)}, u32[]{:S(2)}, u32[]{:S(2)}) collective-permute-start(bf16[384,384]{1,0:T(8,128)(2,1)S(1)} %constant_dynamic-update-slice_fusion.refs_17_), channel_id=1, source_target_pairs={{0,8},{1,9},{2,10},{3,11},{4,12},{5,13},{6,14},{7,15},{8,0},{9,1},... | collective-permute-start | bytes 884744 | tf_op jit(solution)/shard_map/ppermute | solution.py:44
  11.5 2.5 %collective-permute-start.3 = (bf16[192,768]{1,0:T(8,128)(2,1)S(1)}, bf16[192,768]{1,0:T(8,128)(2,1)S(1)}, u32[]{:S(2)}, u32[]{:S(2)}) collective-permute-start(bf16[192,768]{1,0:T(8,128)(2,1)S(1)} %get-tuple-element.12.refs_1_), channel_id=1, source_target_pairs={{0,20},{1,21},{2,22},{3,23},{4,16},{5,17},{6,18},{7,19},{8,28},{9,... | collective-permute-start | bytes 884744 | tf_op jit(solution)/shard_map/ppermute | solution.py:44
  14.0 0.7 collective-permute-done.2.refs_4_
  14.7 1.3 %collective-permute-start.4 = (bf16[288,768]{1,0:T(8,128)(2,1)S(1)}, bf16[288,768]{1,0:T(8,128)(2,1)S(1)}, u32[]{:S(2)}, u32[]{:S(2)}) collective-permute-start(bf16[288,768]{1,0:T(8,128)(2,1)S(1)} %pad_maximum_fusion.6), channel_id=1, source_target_pairs={{0,1},{1,2},{2,3},{3,0},{4,5},{5,6},{6,7},{7,4},{8,9},{9,10},{10,1... | collective-permute-start | bytes 1327112 | tf_op jit(solution)/shard_map/ppermute | solution.py:44
  16.0 5.6 %collective-permute-start.15 = (bf16[384,384]{1,0:T(8,128)(2,1)S(1)}, bf16[384,384]{1,0:T(8,128)(2,1)S(1)}, u32[]{:S(2)}, u32[]{:S(2)}) collective-permute-start(bf16[384,384]{1,0:T(8,128)(2,1)S(1)} %constant_dynamic-update-slice_fusion.refs_17_), channel_id=1, source_target_pairs={{0,32},{1,33},{2,34},{3,35},{4,36},{5,37},{6,38},{7,39},{8,232},{9... | collective-permute-start | bytes 884744 | tf_op jit(solution)/shard_map/ppermute | solution.py:44
  21.6 0.8 collective-permute-start.16
  22.5 1.5 %collective-permute-start.5 = (bf16[288,768]{1,0:T(8,128)(2,1)S(1)}, bf16[288,768]{1,0:T(8,128)(2,1)S(1)}, u32[]{:S(2)}, u32[]{:S(2)}) collective-permute-start(bf16[288,768]{1,0:T(8,128)(2,1)S(1)} %pad_maximum_fusion.7), channel_id=1, source_target_pairs={{0,3},{1,0},{2,1},{3,2},{4,7},{5,4},{6,5},{7,6},{8,11},{9,8},{10,9... | collective-permute-start | bytes 1327112 | tf_op jit(solution)/shard_map/ppermute | solution.py:44
  24.1 1.4 %collective-permute-start.6 = (bf16[288,768]{1,0:T(8,128)(2,1)S(1)}, bf16[288,768]{1,0:T(8,128)(2,1)S(1)}, u32[]{:S(2)}, u32[]{:S(2)}) collective-permute-start(bf16[288,768]{1,0:T(8,128)(2,1)S(1)} %pad_maximum_fusion.8), channel_id=1, source_target_pairs={{0,16},{1,17},{2,18},{3,19},{4,20},{5,21},{6,22},{7,23},{8,24},{9,... | collective-permute-start | bytes 1327112 | tf_op jit(solution)/shard_map/ppermute | solution.py:44
  25.5 4.0 %collective-permute-start.17 = (bf16[384,384]{1,0:T(8,128)(2,1)S(1)}, bf16[384,384]{1,0:T(8,128)(2,1)S(1)}, u32[]{:S(2)}, u32[]{:S(2)}) collective-permute-start(bf16[384,384]{1,0:T(8,128)(2,1)S(1)} %collective-permute-done.15.refs_19_), channel_id=1, source_target_pairs={{0,32},{1,33},{2,34},{3,35},{4,36},{5,37},{6,38},{7,39},{8,232},{9... | collective-permute-start | bytes 884744 | tf_op jit(solution)/shard_map/ppermute | solution.py:44
  29.5 2.7 %collective-permute-start.7 = (bf16[288,768]{1,0:T(8,128)(2,1)S(1)}, bf16[288,768]{1,0:T(8,128)(2,1)S(1)}, u32[]{:S(2)}, u32[]{:S(2)}) collective-permute-start(bf16[288,768]{1,0:T(8,128)(2,1)S(1)} %pad_maximum_fusion.9), channel_id=1, source_target_pairs={{0,20},{1,21},{2,22},{3,23},{4,16},{5,17},{6,18},{7,19},{8,28},{9,... | collective-permute-start | bytes 1327112 | tf_op jit(solution)/shard_map/ppermute | solution.py:44
  32.3 2.2 %collective-permute-start.18 = (bf16[384,384]{1,0:T(8,128)(2,1)S(1)}, bf16[384,384]{1,0:T(8,128)(2,1)S(1)}, u32[]{:S(2)}, u32[]{:S(2)}) collective-permute-start(bf16[384,384]{1,0:T(8,128)(2,1)S(1)} %collective-permute-done.16.refs_20_), channel_id=1, source_target_pairs={{0,32},{1,33},{2,34},{3,35},{4,36},{5,37},{6,38},{7,39},{8,232},{9... | collective-permute-start | bytes 884744 | tf_op jit(solution)/shard_map/ppermute | solution.py:44
  34.5 4.0 %collective-permute-start.12 = (bf16[192,768]{1,0:T(8,128)(2,1)S(1)}, bf16[192,768]{1,0:T(8,128)(2,1)S(1)}, u32[]{:S(2)}, u32[]{:S(2)}) collective-permute-start(bf16[192,768]{1,0:T(8,128)(2,1)S(1)} %get-tuple-element.12.refs_1_), channel_id=1, source_target_pairs={{0,6},{1,7},{2,4},{3,5},{4,2},{5,3},{6,0},{7,1},{8,14},{9,15},{10,... | collective-permute-start | bytes 884744 | tf_op jit(solution)/shard_map/ppermute | solution.py:44
  38.5 3.2 %collective-permute-start.19 = (bf16[384,384]{1,0:T(8,128)(2,1)S(1)}, bf16[384,384]{1,0:T(8,128)(2,1)S(1)}, u32[]{:S(2)}, u32[]{:S(2)}) collective-permute-start(bf16[384,384]{1,0:T(8,128)(2,1)S(1)} %collective-permute-done.17.refs_21_), channel_id=1, source_target_pairs={{0,32},{1,33},{2,34},{3,35},{4,36},{5,37},{6,38},{7,39},{8,232},{9... | collective-permute-start | bytes 884744 | tf_op jit(solution)/shard_map/ppermute | solution.py:44
  41.7 0.1 pad_maximum_fusion
  41.8 1.0 collective-permute-start.20
  42.8 1.7 %collective-permute-start.10 = (bf16[192,768]{1,0:T(8,128)(2,1)S(1)}, bf16[192,768]{1,0:T(8,128)(2,1)S(1)}, u32[]{:S(2)}, u32[]{:S(2)}) collective-permute-start(bf16[192,768]{1,0:T(8,128)(2,1)S(1)} %pad_maximum_fusion.10.refs_10_), channel_id=1, source_target_pairs={{0,16},{1,17},{2,18},{3,19},{4,20},{5,21},{6,22},{7,23},{8,24},{9,... | collective-permute-start | bytes 884744 | tf_op jit(solution)/shard_map/ppermute | solution.py:44
  44.6 3.6 %collective-permute-done.7 = bf16[288,768]{1,0:T(8,128)(2,1)S(1)} collective-permute-done((bf16[288,768]{1,0:T(8,128)(2,1)S(1)}, bf16[288,768]{1,0:T(8,128)(2,1)S(1)}, u32[]{:S(2)}, u32[]{:S(2)}) %collective-permute-start.7) | collective-permute-done | bytes 442400 | tf_op jit(solution)/shard_map/ppermute | solution.py:44
  48.2 3.4 %collective-permute-start.11 = (bf16[192,768]{1,0:T(8,128)(2,1)S(1)}, bf16[192,768]{1,0:T(8,128)(2,1)S(1)}, u32[]{:S(2)}, u32[]{:S(2)}) collective-permute-start(bf16[192,768]{1,0:T(8,128)(2,1)S(1)} %pad_maximum_fusion.10.refs_10_), channel_id=1, source_target_pairs={{0,20},{1,21},{2,22},{3,23},{4,16},{5,17},{6,18},{7,19},{8,28},{9,... | collective-permute-start | bytes 884744 | tf_op jit(solution)/shard_map/ppermute | solution.py:44
  51.6 0.1 pad_maximum_fusion.1
  51.7 0.3 collective-permute-start.8
  52.0 1.4 %collective-permute-start.22 = (bf16[768,384]{1,0:T(8,128)(2,1)S(1)}, bf16[768,384]{1,0:T(8,128)(2,1)S(1)}, u32[]{:S(2)}, u32[]{:S(2)}) collective-permute-start(bf16[768,384]{1,0:T(8,128)(2,1)S(1)} %pad_maximum_fusion), channel_id=1, source_target_pairs={{0,8},{1,9},{2,10},{3,11},{4,12},{5,13},{6,14},{7,15},{8,0},{9,1},... | collective-permute-start | bytes 1769480 | tf_op jit(solution)/shard_map/ppermute | solution.py:44
  53.4 0.1 pad_maximum_fusion.2
  53.5 0.1 collective-permute-start.23
  53.6 0.2 collective-permute-done.10.refs_14_
  53.8 2.3 %collective-permute-start.21 = (bf16[384,384]{1,0:T(8,128)(2,1)S(1)}, bf16[384,384]{1,0:T(8,128)(2,1)S(1)}, u32[]{:S(2)}, u32[]{:S(2)}) collective-permute-start(bf16[384,384]{1,0:T(8,128)(2,1)S(1)} %collective-permute-done.19.refs_23_), channel_id=1, source_target_pairs={{0,32},{1,33},{2,34},{3,35},{4,36},{5,37},{6,38},{7,39},{8,232},{9... | collective-permute-start | bytes 884744 | tf_op jit(solution)/shard_map/ppermute | solution.py:44
  56.1 1.9 %collective-permute-done.11.refs_15_ = bf16[192,768]{1,0:T(8,128)(2,1)S(1)} collective-permute-done((bf16[192,768]{1,0:T(8,128)(2,1)S(1)}, bf16[192,768]{1,0:T(8,128)(2,1)S(1)}, u32[]{:S(2)}, u32[]{:S(2)}) %collective-permute-start.11) | collective-permute-done | bytes 294944 | tf_op jit(solution)/shard_map/ppermute | solution.py:44
  58.0 0.8 collective-permute-start.24
  58.8 2.5 %collective-permute-done.8.refs_12_ = bf16[192,768]{1,0:T(8,128)(2,1)S(1)} collective-permute-done((bf16[192,768]{1,0:T(8,128)(2,1)S(1)}, bf16[192,768]{1,0:T(8,128)(2,1)S(1)}, u32[]{:S(2)}, u32[]{:S(2)}) %collective-permute-start.8) | collective-permute-done | bytes 294944 | tf_op jit(solution)/shard_map/ppermute | solution.py:44
  61.3 1.2 collective-permute-start.25
  62.7 6.0 %collective-permute-done.9.refs_13_ = bf16[192,768]{1,0:T(8,128)(2,1)S(1)} collective-permute-done((bf16[192,768]{1,0:T(8,128)(2,1)S(1)}, bf16[192,768]{1,0:T(8,128)(2,1)S(1)}, u32[]{:S(2)}, u32[]{:S(2)}) %collective-permute-start.9) | collective-permute-done | bytes 294944 | tf_op jit(solution)/shard_map/ppermute | solution.py:44
  68.7 0.8 copy-done.8
  69.5 0.2 copy-done.9
  69.7 0.1 copy-done.12
  69.8 0.8 copy-done.10
  70.7 8.8 %shard_map.38 = (bf16[384,384]{1,0:T(8,128)(2,1)S(1)}, bf16[8,384,768]{2,1,0:T(8,128)(2,1)}) custom-call(s32[48,48]{1,0:T(8,128)S(1)} %copy-done.3, bf16[192,768]{1,0:T(8,128)(2,1)S(1)} %get-tuple-element.12.refs_1_, bf16[192,768]{1,0:T(8,128)(2,1)S(1)} %collective-permute-done.refs_2_, bf16[192,768]{1,0:T(8,128)(2,1)S(1)} %collective-permute-done.1.refs_3_, ...), custom_call_target="tpu_custom_call" | custom-call | flops 1811939328 | tf_op jit(solution)/shard_map/pallas_call | solution.py:193
  79.5 2.1 %collective-permute-start.26 = (bf16[384,384]{1,0:T(8,128)(2,1)S(1)}, bf16[384,384]{1,0:T(8,128)(2,1)S(1)}, u32[]{:S(2)}, u32[]{:S(2)}) collective-permute-start(bf16[384,384]{1,0:T(8,128)(2,1)S(1)} %get-tuple-element.16.refs_2_), channel_id=1, source_target_pairs={{0,8},{1,9},{2,10},{3,11},{4,12},{5,13},{6,14},{7,15},{8,0},{9,1},... | collective-permute-start | bytes 884744 | tf_op jit(solution)/shard_map/ppermute | solution.py:44
  81.6 1.2 collective-permute-done.26.refs_3_
  82.8 4.7 %collective-permute-done.27.refs_4_ = bf16[384,384]{1,0:T(8,128)(2,1)S(1)} collective-permute-done((bf16[384,384]{1,0:T(8,128)(2,1)S(1)}, bf16[384,384]{1,0:T(8,128)(2,1)S(1)}, u32[]{:S(2)}, u32[]{:S(2)}) %collective-permute-start.27) | collective-permute-done | bytes 294944 | tf_op jit(solution)/shard_map/ppermute | solution.py:44
  87.4 0.9 collective-permute-start.29
  88.3 2.2 %collective-permute-done.28.refs_5_ = bf16[384,384]{1,0:T(8,128)(2,1)S(1)} collective-permute-done((bf16[384,384]{1,0:T(8,128)(2,1)S(1)}, bf16[384,384]{1,0:T(8,128)(2,1)S(1)}, u32[]{:S(2)}, u32[]{:S(2)}) %collective-permute-start.28) | collective-permute-done | bytes 294944 | tf_op jit(solution)/shard_map/ppermute | solution.py:44
  90.6 0.9 collective-permute-start.30
  91.5 1.9 %collective-permute-done.29.refs_6_ = bf16[384,384]{1,0:T(8,128)(2,1)S(1)} collective-permute-done((bf16[384,384]{1,0:T(8,128)(2,1)S(1)}, bf16[384,384]{1,0:T(8,128)(2,1)S(1)}, u32[]{:S(2)}, u32[]{:S(2)}) %collective-permute-start.29) | collective-permute-done | bytes 294944 | tf_op jit(solution)/shard_map/ppermute | solution.py:44
  93.5 1.7 %collective-permute-start.31 = (bf16[384,384]{1,0:T(8,128)(2,1)S(1)}, bf16[384,384]{1,0:T(8,128)(2,1)S(1)}, u32[]{:S(2)}, u32[]{:S(2)}) collective-permute-start(bf16[384,384]{1,0:T(8,128)(2,1)S(1)} %collective-permute-done.29.refs_6_), channel_id=1, source_target_pairs={{0,32},{1,33},{2,34},{3,35},{4,36},{5,37},{6,38},{7,39},{8,232},{9... | collective-permute-start | bytes 884744 | tf_op jit(solution)/shard_map/ppermute | solution.py:44
  95.1 1.8 %collective-permute-done.30.refs_7_ = bf16[384,384]{1,0:T(8,128)(2,1)S(1)} collective-permute-done((bf16[384,384]{1,0:T(8,128)(2,1)S(1)}, bf16[384,384]{1,0:T(8,128)(2,1)S(1)}, u32[]{:S(2)}, u32[]{:S(2)}) %collective-permute-start.30) | collective-permute-done | bytes 294944 | tf_op jit(solution)/shard_map/ppermute | solution.py:44
  96.9 1.4 %collective-permute-start.32 = (bf16[384,384]{1,0:T(8,128)(2,1)S(1)}, bf16[384,384]{1,0:T(8,128)(2,1)S(1)}, u32[]{:S(2)}, u32[]{:S(2)}) collective-permute-start(bf16[384,384]{1,0:T(8,128)(2,1)S(1)} %collective-permute-done.30.refs_7_), channel_id=1, source_target_pairs={{0,32},{1,33},{2,34},{3,35},{4,36},{5,37},{6,38},{7,39},{8,232},{9... | collective-permute-start | bytes 884744 | tf_op jit(solution)/shard_map/ppermute | solution.py:44
  98.3 0.1 pad_maximum_fusion.3
  98.4 2.4 %collective-permute-start.34 = (bf16[768,384]{1,0:T(8,128)(2,1)S(1)}, bf16[768,384]{1,0:T(8,128)(2,1)S(1)}, u32[]{:S(2)}, u32[]{:S(2)}) collective-permute-start(bf16[768,384]{1,0:T(8,128)(2,1)S(1)} %pad_maximum_fusion.3), channel_id=1, source_target_pairs={{0,8},{1,9},{2,10},{3,11},{4,12},{5,13},{6,14},{7,15},{8,0},{9,1},... | collective-permute-start | bytes 1769480 | tf_op jit(solution)/shard_map/ppermute | solution.py:44
  100.8 0.1 pad_maximum_fusion.4
  100.8 0.1 collective-permute-start.35
  100.9 3.0 %collective-permute-start.33 = (bf16[384,384]{1,0:T(8,128)(2,1)S(1)}, bf16[384,384]{1,0:T(8,128)(2,1)S(1)}, u32[]{:S(2)}, u32[]{:S(2)}) collective-permute-start(bf16[384,384]{1,0:T(8,128)(2,1)S(1)} %collective-permute-done.31.refs_8_), channel_id=1, source_target_pairs={{0,32},{1,33},{2,34},{3,35},{4,36},{5,37},{6,38},{7,39},{8,232},{9... | collective-permute-start | bytes 884744 | tf_op jit(solution)/shard_map/ppermute | solution.py:44
  104.0 4.6 %collective-permute-start.36 = (bf16[768,384]{1,0:T(8,128)(2,1)S(1)}, bf16[768,384]{1,0:T(8,128)(2,1)S(1)}, u32[]{:S(2)}, u32[]{:S(2)}) collective-permute-start(bf16[768,384]{1,0:T(8,128)(2,1)S(1)} %pad_maximum_fusion.5), channel_id=1, source_target_pairs={{0,8},{1,9},{2,10},{3,11},{4,12},{5,13},{6,14},{7,15},{8,0},{9,1},... | collective-permute-start | bytes 1769480 | tf_op jit(solution)/shard_map/ppermute | solution.py:44
  108.7 4.6 %collective-permute-start.37 = (bf16[384,384]{1,0:T(8,128)(2,1)S(1)}, bf16[384,384]{1,0:T(8,128)(2,1)S(1)}, u32[]{:S(2)}, u32[]{:S(2)}) collective-permute-start(bf16[384,384]{1,0:T(8,128)(2,1)S(1)} %collective-permute-done.33.refs_10_), channel_id=1, source_target_pairs={{0,8},{1,9},{2,10},{3,11},{4,12},{5,13},{6,14},{7,15},{8,0},{9,1},... | collective-permute-start | bytes 884744 | tf_op jit(solution)/shard_map/ppermute | solution.py:44
  113.3 1.2 collective-permute-done.37.refs_14_
  114.5 6.7 %shard_map.39 = (bf16[192,384]{1,0:T(8,128)(2,1)S(1)}, bf16[192,384]{1,0:T(8,128)(2,1)S(1)}) custom-call(s32[48,48]{1,0:T(8,128)S(1)} %copy-done.2, bf16[8,384,768]{2,1,0:T(8,128)(2,1)} %get-tuple-element.15.refs_1_, bf16[384,384]{1,0:T(8,128)(2,1)S(1)} %get-tuple-element.16.refs_2_, bf16[384,384]{1,0:T(8,128)(2,1)S(1)} %collective-permute-done.26.refs_3_, ...), custom_call_target="tpu_custom_call" | custom-call | flops 1811939328 | tf_op jit(solution)/shard_map/pallas_call | solution.py:193
  121.3 0.1 collective-permute-start.38
  121.4 5.0 %collective-permute-done.38 = bf16[192,384]{1,0:T(8,128)(2,1)S(1)} collective-permute-done((bf16[192,384]{1,0:T(8,128)(2,1)S(1)}, bf16[192,384]{1,0:T(8,128)(2,1)S(1)}, u32[]{:S(2)}, u32[]{:S(2)}) %collective-permute-start.38) | collective-permute-done | bytes 147488 | tf_op jit(solution)/shard_map/ppermute | solution.py:44
  126.5 0.7 pad_maximum_fusion.12
  (71 shorter events, 0.6 us)
Async XLA Ops:
  0.0 1.0 copy-start
  1.0 0.7 copy-start.1
  2.8 5.0 %collective-permute-start.13 = (bf16[192,384]{1,0:T(8,128)(2,1)S(1)}, bf16[192,384]{1,0:T(8,128)(2,1)S(1)}, u32[]{:S(2)}, u32[]{:S(2)}) collective-permute-start(bf16[192,384]{1,0:T(8,128)(2,1)S(1)} %get-tuple-element.14), channel_id=1, source_target_pairs={{0,16},{1,17},{2,18},{3,19},{4,20},{5,21},{6,22},{7,23},{8,24},{9,... | collective-permute-start | bytes 442376 | tf_op jit(solution)/shard_map/ppermute | solution.py:44
  5.0 9.0 %collective-permute-start = (bf16[192,768]{1,0:T(8,128)(2,1)S(1)}, bf16[192,768]{1,0:T(8,128)(2,1)S(1)}, u32[]{:S(2)}, u32[]{:S(2)}) collective-permute-start(bf16[192,768]{1,0:T(8,128)(2,1)S(1)} %get-tuple-element.12.refs_1_), channel_id=1, source_target_pairs={{0,1},{1,2},{2,3},{3,0},{4,5},{5,6},{6,7},{7,4},{8,9},{9,10},{10,1... | collective-permute-start | bytes 884744 | tf_op jit(solution)/shard_map/ppermute | solution.py:44
  6.2 8.5 %collective-permute-start.2 = (bf16[192,768]{1,0:T(8,128)(2,1)S(1)}, bf16[192,768]{1,0:T(8,128)(2,1)S(1)}, u32[]{:S(2)}, u32[]{:S(2)}) collective-permute-start(bf16[192,768]{1,0:T(8,128)(2,1)S(1)} %get-tuple-element.12.refs_1_), channel_id=1, source_target_pairs={{0,16},{1,17},{2,18},{3,19},{4,20},{5,21},{6,22},{7,23},{8,24},{9,... | collective-permute-start | bytes 884744 | tf_op jit(solution)/shard_map/ppermute | solution.py:44
  6.4 15.2 %collective-permute-start.1 = (bf16[192,768]{1,0:T(8,128)(2,1)S(1)}, bf16[192,768]{1,0:T(8,128)(2,1)S(1)}, u32[]{:S(2)}, u32[]{:S(2)}) collective-permute-start(bf16[192,768]{1,0:T(8,128)(2,1)S(1)} %get-tuple-element.12.refs_1_), channel_id=1, source_target_pairs={{0,3},{1,0},{2,1},{3,2},{4,7},{5,4},{6,5},{7,6},{8,11},{9,8},{10,9... | collective-permute-start | bytes 884744 | tf_op jit(solution)/shard_map/ppermute | solution.py:44
  7.8 13.8 %collective-permute-start.14 = (bf16[384,384]{1,0:T(8,128)(2,1)S(1)}, bf16[384,384]{1,0:T(8,128)(2,1)S(1)}, u32[]{:S(2)}, u32[]{:S(2)}) collective-permute-start(bf16[384,384]{1,0:T(8,128)(2,1)S(1)} %constant_dynamic-update-slice_fusion.refs_17_), channel_id=1, source_target_pairs={{0,8},{1,9},{2,10},{3,11},{4,12},{5,13},{6,14},{7,15},{8,0},{9,1},... | collective-permute-start | bytes 884744 | tf_op jit(solution)/shard_map/ppermute | solution.py:44
  11.5 10.9 %collective-permute-start.3 = (bf16[192,768]{1,0:T(8,128)(2,1)S(1)}, bf16[192,768]{1,0:T(8,128)(2,1)S(1)}, u32[]{:S(2)}, u32[]{:S(2)}) collective-permute-start(bf16[192,768]{1,0:T(8,128)(2,1)S(1)} %get-tuple-element.12.refs_1_), channel_id=1, source_target_pairs={{0,20},{1,21},{2,22},{3,23},{4,16},{5,17},{6,18},{7,19},{8,28},{9,... | collective-permute-start | bytes 884744 | tf_op jit(solution)/shard_map/ppermute | solution.py:44
  14.7 14.8 %collective-permute-start.4 = (bf16[288,768]{1,0:T(8,128)(2,1)S(1)}, bf16[288,768]{1,0:T(8,128)(2,1)S(1)}, u32[]{:S(2)}, u32[]{:S(2)}) collective-permute-start(bf16[288,768]{1,0:T(8,128)(2,1)S(1)} %pad_maximum_fusion.6), channel_id=1, source_target_pairs={{0,1},{1,2},{2,3},{3,0},{4,5},{5,6},{6,7},{7,4},{8,9},{9,10},{10,1... | collective-permute-start | bytes 1327112 | tf_op jit(solution)/shard_map/ppermute | solution.py:44
  16.0 9.5 %collective-permute-start.15 = (bf16[384,384]{1,0:T(8,128)(2,1)S(1)}, bf16[384,384]{1,0:T(8,128)(2,1)S(1)}, u32[]{:S(2)}, u32[]{:S(2)}) collective-permute-start(bf16[384,384]{1,0:T(8,128)(2,1)S(1)} %constant_dynamic-update-slice_fusion.refs_17_), channel_id=1, source_target_pairs={{0,32},{1,33},{2,34},{3,35},{4,36},{5,37},{6,38},{7,39},{8,232},{9... | collective-permute-start | bytes 884744 | tf_op jit(solution)/shard_map/ppermute | solution.py:44
  21.6 10.7 %collective-permute-start.16 = (bf16[384,384]{1,0:T(8,128)(2,1)S(1)}, bf16[384,384]{1,0:T(8,128)(2,1)S(1)}, u32[]{:S(2)}, u32[]{:S(2)}) collective-permute-start(bf16[384,384]{1,0:T(8,128)(2,1)S(1)} %collective-permute-done.14.refs_18_), channel_id=1, source_target_pairs={{0,32},{1,33},{2,34},{3,35},{4,36},{5,37},{6,38},{7,39},{8,232},{9... | collective-permute-start | bytes 884744 | tf_op jit(solution)/shard_map/ppermute | solution.py:44
  22.5 12.1 %collective-permute-start.5 = (bf16[288,768]{1,0:T(8,128)(2,1)S(1)}, bf16[288,768]{1,0:T(8,128)(2,1)S(1)}, u32[]{:S(2)}, u32[]{:S(2)}) collective-permute-start(bf16[288,768]{1,0:T(8,128)(2,1)S(1)} %pad_maximum_fusion.7), channel_id=1, source_target_pairs={{0,3},{1,0},{2,1},{3,2},{4,7},{5,4},{6,5},{7,6},{8,11},{9,8},{10,9... | collective-permute-start | bytes 1327112 | tf_op jit(solution)/shard_map/ppermute | solution.py:44
  24.1 18.8 %collective-permute-start.6 = (bf16[288,768]{1,0:T(8,128)(2,1)S(1)}, bf16[288,768]{1,0:T(8,128)(2,1)S(1)}, u32[]{:S(2)}, u32[]{:S(2)}) collective-permute-start(bf16[288,768]{1,0:T(8,128)(2,1)S(1)} %pad_maximum_fusion.8), channel_id=1, source_target_pairs={{0,16},{1,17},{2,18},{3,19},{4,20},{5,21},{6,22},{7,23},{8,24},{9,... | collective-permute-start | bytes 1327112 | tf_op jit(solution)/shard_map/ppermute | solution.py:44
  25.5 13.0 %collective-permute-start.17 = (bf16[384,384]{1,0:T(8,128)(2,1)S(1)}, bf16[384,384]{1,0:T(8,128)(2,1)S(1)}, u32[]{:S(2)}, u32[]{:S(2)}) collective-permute-start(bf16[384,384]{1,0:T(8,128)(2,1)S(1)} %collective-permute-done.15.refs_19_), channel_id=1, source_target_pairs={{0,32},{1,33},{2,34},{3,35},{4,36},{5,37},{6,38},{7,39},{8,232},{9... | collective-permute-start | bytes 884744 | tf_op jit(solution)/shard_map/ppermute | solution.py:44
  29.5 18.6 %collective-permute-start.7 = (bf16[288,768]{1,0:T(8,128)(2,1)S(1)}, bf16[288,768]{1,0:T(8,128)(2,1)S(1)}, u32[]{:S(2)}, u32[]{:S(2)}) collective-permute-start(bf16[288,768]{1,0:T(8,128)(2,1)S(1)} %pad_maximum_fusion.9), channel_id=1, source_target_pairs={{0,20},{1,21},{2,22},{3,23},{4,16},{5,17},{6,18},{7,19},{8,28},{9,... | collective-permute-start | bytes 1327112 | tf_op jit(solution)/shard_map/ppermute | solution.py:44
  32.3 9.5 %collective-permute-start.18 = (bf16[384,384]{1,0:T(8,128)(2,1)S(1)}, bf16[384,384]{1,0:T(8,128)(2,1)S(1)}, u32[]{:S(2)}, u32[]{:S(2)}) collective-permute-start(bf16[384,384]{1,0:T(8,128)(2,1)S(1)} %collective-permute-done.16.refs_20_), channel_id=1, source_target_pairs={{0,32},{1,33},{2,34},{3,35},{4,36},{5,37},{6,38},{7,39},{8,232},{9... | collective-permute-start | bytes 884744 | tf_op jit(solution)/shard_map/ppermute | solution.py:44
  34.5 19.0 %collective-permute-start.12 = (bf16[192,768]{1,0:T(8,128)(2,1)S(1)}, bf16[192,768]{1,0:T(8,128)(2,1)S(1)}, u32[]{:S(2)}, u32[]{:S(2)}) collective-permute-start(bf16[192,768]{1,0:T(8,128)(2,1)S(1)} %get-tuple-element.12.refs_1_), channel_id=1, source_target_pairs={{0,6},{1,7},{2,4},{3,5},{4,2},{5,3},{6,0},{7,1},{8,14},{9,15},{10,... | collective-permute-start | bytes 884744 | tf_op jit(solution)/shard_map/ppermute | solution.py:44
  38.5 13.1 %copy-start.4 = (bf16[384,384]{1,0:T(8,128)(2,1)}, bf16[384,384]{1,0:T(8,128)(2,1)S(1)}, u32[]{:S(2)}) copy-start(bf16[384,384]{1,0:T(8,128)(2,1)S(1)} %collective-permute-done.17.refs_21_) | copy-start | bytes 884740
  38.5 13.2 %collective-permute-start.19 = (bf16[384,384]{1,0:T(8,128)(2,1)S(1)}, bf16[384,384]{1,0:T(8,128)(2,1)S(1)}, u32[]{:S(2)}, u32[]{:S(2)}) collective-permute-start(bf16[384,384]{1,0:T(8,128)(2,1)S(1)} %collective-permute-done.17.refs_21_), channel_id=1, source_target_pairs={{0,32},{1,33},{2,34},{3,35},{4,36},{5,37},{6,38},{7,39},{8,232},{9... | collective-permute-start | bytes 884744 | tf_op jit(solution)/shard_map/ppermute | solution.py:44
  41.8 9.9 %copy-start.5 = (bf16[384,384]{1,0:T(8,128)(2,1)}, bf16[384,384]{1,0:T(8,128)(2,1)S(1)}, u32[]{:S(2)}) copy-start(bf16[384,384]{1,0:T(8,128)(2,1)S(1)} %collective-permute-done.18.refs_22_) | copy-start | bytes 884740
  41.8 10.2 %collective-permute-start.20 = (bf16[384,384]{1,0:T(8,128)(2,1)S(1)}, bf16[384,384]{1,0:T(8,128)(2,1)S(1)}, u32[]{:S(2)}, u32[]{:S(2)}) collective-permute-start(bf16[384,384]{1,0:T(8,128)(2,1)S(1)} %collective-permute-done.18.refs_22_), channel_id=1, source_target_pairs={{0,32},{1,33},{2,34},{3,35},{4,36},{5,37},{6,38},{7,39},{8,232},{9... | collective-permute-start | bytes 884744 | tf_op jit(solution)/shard_map/ppermute | solution.py:44
  42.8 11.0 %collective-permute-start.10 = (bf16[192,768]{1,0:T(8,128)(2,1)S(1)}, bf16[192,768]{1,0:T(8,128)(2,1)S(1)}, u32[]{:S(2)}, u32[]{:S(2)}) collective-permute-start(bf16[192,768]{1,0:T(8,128)(2,1)S(1)} %pad_maximum_fusion.10.refs_10_), channel_id=1, source_target_pairs={{0,16},{1,17},{2,18},{3,19},{4,20},{5,21},{6,22},{7,23},{8,24},{9,... | collective-permute-start | bytes 884744 | tf_op jit(solution)/shard_map/ppermute | solution.py:44
  48.2 9.8 %collective-permute-start.11 = (bf16[192,768]{1,0:T(8,128)(2,1)S(1)}, bf16[192,768]{1,0:T(8,128)(2,1)S(1)}, u32[]{:S(2)}, u32[]{:S(2)}) collective-permute-start(bf16[192,768]{1,0:T(8,128)(2,1)S(1)} %pad_maximum_fusion.10.refs_10_), channel_id=1, source_target_pairs={{0,20},{1,21},{2,22},{3,23},{4,16},{5,17},{6,18},{7,19},{8,28},{9,... | collective-permute-start | bytes 884744 | tf_op jit(solution)/shard_map/ppermute | solution.py:44
  51.7 10.9 %copy-start.6 = (bf16[384,384]{1,0:T(8,128)(2,1)}, bf16[384,384]{1,0:T(8,128)(2,1)S(1)}, u32[]{:S(2)}) copy-start(bf16[384,384]{1,0:T(8,128)(2,1)S(1)} %collective-permute-done.19.refs_23_) | copy-start | bytes 884740
  51.7 9.6 %collective-permute-start.8 = (bf16[192,768]{1,0:T(8,128)(2,1)S(1)}, bf16[192,768]{1,0:T(8,128)(2,1)S(1)}, u32[]{:S(2)}, u32[]{:S(2)}) collective-permute-start(bf16[192,768]{1,0:T(8,128)(2,1)S(1)} %pad_maximum_fusion.11.refs_11_), channel_id=1, source_target_pairs={{0,1},{1,2},{2,3},{3,0},{4,5},{5,6},{6,7},{7,4},{8,9},{9,10},{10,1... | collective-permute-start | bytes 884744 | tf_op jit(solution)/shard_map/ppermute | solution.py:44
  52.0 10.6 %copy-start.7 = (bf16[384,384]{1,0:T(8,128)(2,1)}, bf16[384,384]{1,0:T(8,128)(2,1)S(1)}, u32[]{:S(2)}) copy-start(bf16[384,384]{1,0:T(8,128)(2,1)S(1)} %collective-permute-done.20.refs_24_) | copy-start | bytes 884740
  52.0 16.6 %collective-permute-start.22 = (bf16[768,384]{1,0:T(8,128)(2,1)S(1)}, bf16[768,384]{1,0:T(8,128)(2,1)S(1)}, u32[]{:S(2)}, u32[]{:S(2)}) collective-permute-start(bf16[768,384]{1,0:T(8,128)(2,1)S(1)} %pad_maximum_fusion), channel_id=1, source_target_pairs={{0,8},{1,9},{2,10},{3,11},{4,12},{5,13},{6,14},{7,15},{8,0},{9,1},... | collective-permute-start | bytes 1769480 | tf_op jit(solution)/shard_map/ppermute | solution.py:44
  53.5 17.2 %copy-start.3 = (s32[48,48]{1,0:T(8,128)S(1)}, s32[48,48]{1,0:T(8,128)}, u32[]{:S(2)}) copy-start(s32[48,48]{1,0:T(8,128)} %refs_0_.2) | copy-start | bytes 27652
  53.5 15.2 %collective-permute-start.23 = (bf16[768,384]{1,0:T(8,128)(2,1)S(1)}, bf16[768,384]{1,0:T(8,128)(2,1)S(1)}, u32[]{:S(2)}, u32[]{:S(2)}) collective-permute-start(bf16[768,384]{1,0:T(8,128)(2,1)S(1)} %pad_maximum_fusion.1), channel_id=1, source_target_pairs={{0,8},{1,9},{2,10},{3,11},{4,12},{5,13},{6,14},{7,15},{8,0},{9,1},... | collective-permute-start | bytes 1769480 | tf_op jit(solution)/shard_map/ppermute | solution.py:44
  53.8 7.5 %collective-permute-start.21 = (bf16[384,384]{1,0:T(8,128)(2,1)S(1)}, bf16[384,384]{1,0:T(8,128)(2,1)S(1)}, u32[]{:S(2)}, u32[]{:S(2)}) collective-permute-start(bf16[384,384]{1,0:T(8,128)(2,1)S(1)} %collective-permute-done.19.refs_23_), channel_id=1, source_target_pairs={{0,32},{1,33},{2,34},{3,35},{4,36},{5,37},{6,38},{7,39},{8,232},{9... | collective-permute-start | bytes 884744 | tf_op jit(solution)/shard_map/ppermute | solution.py:44
  58.0 10.7 %collective-permute-start.24 = (bf16[768,384]{1,0:T(8,128)(2,1)S(1)}, bf16[768,384]{1,0:T(8,128)(2,1)S(1)}, u32[]{:S(2)}, u32[]{:S(2)}) collective-permute-start(bf16[768,384]{1,0:T(8,128)(2,1)S(1)} %pad_maximum_fusion.2), channel_id=1, source_target_pairs={{0,8},{1,9},{2,10},{3,11},{4,12},{5,13},{6,14},{7,15},{8,0},{9,1},... | collective-permute-start | bytes 1769480 | tf_op jit(solution)/shard_map/ppermute | solution.py:44
  61.3 7.4 %collective-permute-start.9 = (bf16[192,768]{1,0:T(8,128)(2,1)S(1)}, bf16[192,768]{1,0:T(8,128)(2,1)S(1)}, u32[]{:S(2)}, u32[]{:S(2)}) collective-permute-start(bf16[192,768]{1,0:T(8,128)(2,1)S(1)} %pad_maximum_fusion.11.refs_11_), channel_id=1, source_target_pairs={{0,3},{1,0},{2,1},{3,2},{4,7},{5,4},{6,5},{7,6},{8,11},{9,8},{10,9... | collective-permute-start | bytes 884744 | tf_op jit(solution)/shard_map/ppermute | solution.py:44
  61.3 1.4 %copy-start.11 = (bf16[384,384]{1,0:T(8,128)(2,1)}, bf16[384,384]{1,0:T(8,128)(2,1)S(1)}, u32[]{:S(2)}) copy-start(bf16[384,384]{1,0:T(8,128)(2,1)S(1)} %collective-permute-done.21.refs_25_) | copy-start | bytes 884740
  61.3 7.4 %collective-permute-start.25 = (bf16[384,384]{1,0:T(8,128)(2,1)S(1)}, bf16[384,384]{1,0:T(8,128)(2,1)S(1)}, u32[]{:S(2)}, u32[]{:S(2)}) collective-permute-start(bf16[384,384]{1,0:T(8,128)(2,1)S(1)} %collective-permute-done.21.refs_25_), channel_id=1, source_target_pairs={{0,8},{1,9},{2,10},{3,11},{4,12},{5,13},{6,14},{7,15},{8,0},{9,1},... | collective-permute-start | bytes 884744 | tf_op jit(solution)/shard_map/ppermute | solution.py:44
  68.7 0.8 copy-start.8
  68.7 1.0 copy-start.9
  68.7 1.1 copy-start.12
  69.8 0.8 copy-start.10
  79.5 3.3 %collective-permute-start.26 = (bf16[384,384]{1,0:T(8,128)(2,1)S(1)}, bf16[384,384]{1,0:T(8,128)(2,1)S(1)}, u32[]{:S(2)}, u32[]{:S(2)}) collective-permute-start(bf16[384,384]{1,0:T(8,128)(2,1)S(1)} %get-tuple-element.16.refs_2_), channel_id=1, source_target_pairs={{0,8},{1,9},{2,10},{3,11},{4,12},{5,13},{6,14},{7,15},{8,0},{9,1},... | collective-permute-start | bytes 884744 | tf_op jit(solution)/shard_map/ppermute | solution.py:44
  81.6 5.9 %collective-permute-start.27 = (bf16[384,384]{1,0:T(8,128)(2,1)S(1)}, bf16[384,384]{1,0:T(8,128)(2,1)S(1)}, u32[]{:S(2)}, u32[]{:S(2)}) collective-permute-start(bf16[384,384]{1,0:T(8,128)(2,1)S(1)} %get-tuple-element.16.refs_2_), channel_id=1, source_target_pairs={{0,32},{1,33},{2,34},{3,35},{4,36},{5,37},{6,38},{7,39},{8,232},{9... | collective-permute-start | bytes 884744 | tf_op jit(solution)/shard_map/ppermute | solution.py:44
  82.8 7.8 %collective-permute-start.28 = (bf16[384,384]{1,0:T(8,128)(2,1)S(1)}, bf16[384,384]{1,0:T(8,128)(2,1)S(1)}, u32[]{:S(2)}, u32[]{:S(2)}) collective-permute-start(bf16[384,384]{1,0:T(8,128)(2,1)S(1)} %collective-permute-done.26.refs_3_), channel_id=1, source_target_pairs={{0,32},{1,33},{2,34},{3,35},{4,36},{5,37},{6,38},{7,39},{8,232},{9... | collective-permute-start | bytes 884744 | tf_op jit(solution)/shard_map/ppermute | solution.py:44
  87.4 6.0 %collective-permute-start.29 = (bf16[384,384]{1,0:T(8,128)(2,1)S(1)}, bf16[384,384]{1,0:T(8,128)(2,1)S(1)}, u32[]{:S(2)}, u32[]{:S(2)}) collective-permute-start(bf16[384,384]{1,0:T(8,128)(2,1)S(1)} %collective-permute-done.27.refs_4_), channel_id=1, source_target_pairs={{0,32},{1,33},{2,34},{3,35},{4,36},{5,37},{6,38},{7,39},{8,232},{9... | collective-permute-start | bytes 884744 | tf_op jit(solution)/shard_map/ppermute | solution.py:44
  90.6 6.3 %collective-permute-start.30 = (bf16[384,384]{1,0:T(8,128)(2,1)S(1)}, bf16[384,384]{1,0:T(8,128)(2,1)S(1)}, u32[]{:S(2)}, u32[]{:S(2)}) collective-permute-start(bf16[384,384]{1,0:T(8,128)(2,1)S(1)} %collective-permute-done.28.refs_5_), channel_id=1, source_target_pairs={{0,32},{1,33},{2,34},{3,35},{4,36},{5,37},{6,38},{7,39},{8,232},{9... | collective-permute-start | bytes 884744 | tf_op jit(solution)/shard_map/ppermute | solution.py:44
  93.5 7.5 %collective-permute-start.31 = (bf16[384,384]{1,0:T(8,128)(2,1)S(1)}, bf16[384,384]{1,0:T(8,128)(2,1)S(1)}, u32[]{:S(2)}, u32[]{:S(2)}) collective-permute-start(bf16[384,384]{1,0:T(8,128)(2,1)S(1)} %collective-permute-done.29.refs_6_), channel_id=1, source_target_pairs={{0,32},{1,33},{2,34},{3,35},{4,36},{5,37},{6,38},{7,39},{8,232},{9... | collective-permute-start | bytes 884744 | tf_op jit(solution)/shard_map/ppermute | solution.py:44
  96.9 7.1 %collective-permute-start.32 = (bf16[384,384]{1,0:T(8,128)(2,1)S(1)}, bf16[384,384]{1,0:T(8,128)(2,1)S(1)}, u32[]{:S(2)}, u32[]{:S(2)}) collective-permute-start(bf16[384,384]{1,0:T(8,128)(2,1)S(1)} %collective-permute-done.30.refs_7_), channel_id=1, source_target_pairs={{0,32},{1,33},{2,34},{3,35},{4,36},{5,37},{6,38},{7,39},{8,232},{9... | collective-permute-start | bytes 884744 | tf_op jit(solution)/shard_map/ppermute | solution.py:44
  98.4 16.2 %copy-start.2 = (s32[48,48]{1,0:T(8,128)S(1)}, s32[48,48]{1,0:T(8,128)}, u32[]{:S(2)}) copy-start(s32[48,48]{1,0:T(8,128)} %refs_0_.3) | copy-start | bytes 27652
  98.4 14.9 %collective-permute-start.34 = (bf16[768,384]{1,0:T(8,128)(2,1)S(1)}, bf16[768,384]{1,0:T(8,128)(2,1)S(1)}, u32[]{:S(2)}, u32[]{:S(2)}) collective-permute-start(bf16[768,384]{1,0:T(8,128)(2,1)S(1)} %pad_maximum_fusion.3), channel_id=1, source_target_pairs={{0,8},{1,9},{2,10},{3,11},{4,12},{5,13},{6,14},{7,15},{8,0},{9,1},... | collective-permute-start | bytes 1769480 | tf_op jit(solution)/shard_map/ppermute | solution.py:44
  100.8 12.5 %collective-permute-start.35 = (bf16[768,384]{1,0:T(8,128)(2,1)S(1)}, bf16[768,384]{1,0:T(8,128)(2,1)S(1)}, u32[]{:S(2)}, u32[]{:S(2)}) collective-permute-start(bf16[768,384]{1,0:T(8,128)(2,1)S(1)} %pad_maximum_fusion.4), channel_id=1, source_target_pairs={{0,8},{1,9},{2,10},{3,11},{4,12},{5,13},{6,14},{7,15},{8,0},{9,1},... | collective-permute-start | bytes 1769480 | tf_op jit(solution)/shard_map/ppermute | solution.py:44
  100.9 7.7 %collective-permute-start.33 = (bf16[384,384]{1,0:T(8,128)(2,1)S(1)}, bf16[384,384]{1,0:T(8,128)(2,1)S(1)}, u32[]{:S(2)}, u32[]{:S(2)}) collective-permute-start(bf16[384,384]{1,0:T(8,128)(2,1)S(1)} %collective-permute-done.31.refs_8_), channel_id=1, source_target_pairs={{0,32},{1,33},{2,34},{3,35},{4,36},{5,37},{6,38},{7,39},{8,232},{9... | collective-permute-start | bytes 884744 | tf_op jit(solution)/shard_map/ppermute | solution.py:44
  104.0 10.5 %collective-permute-start.36 = (bf16[768,384]{1,0:T(8,128)(2,1)S(1)}, bf16[768,384]{1,0:T(8,128)(2,1)S(1)}, u32[]{:S(2)}, u32[]{:S(2)}) collective-permute-start(bf16[768,384]{1,0:T(8,128)(2,1)S(1)} %pad_maximum_fusion.5), channel_id=1, source_target_pairs={{0,8},{1,9},{2,10},{3,11},{4,12},{5,13},{6,14},{7,15},{8,0},{9,1},... | collective-permute-start | bytes 1769480 | tf_op jit(solution)/shard_map/ppermute | solution.py:44
  108.7 5.8 %collective-permute-start.37 = (bf16[384,384]{1,0:T(8,128)(2,1)S(1)}, bf16[384,384]{1,0:T(8,128)(2,1)S(1)}, u32[]{:S(2)}, u32[]{:S(2)}) collective-permute-start(bf16[384,384]{1,0:T(8,128)(2,1)S(1)} %collective-permute-done.33.refs_10_), channel_id=1, source_target_pairs={{0,8},{1,9},{2,10},{3,11},{4,12},{5,13},{6,14},{7,15},{8,0},{9,1},... | collective-permute-start | bytes 884744 | tf_op jit(solution)/shard_map/ppermute | solution.py:44
  121.3 5.1 %collective-permute-start.38 = (bf16[192,384]{1,0:T(8,128)(2,1)S(1)}, bf16[192,384]{1,0:T(8,128)(2,1)S(1)}, u32[]{:S(2)}, u32[]{:S(2)}) collective-permute-start(bf16[192,384]{1,0:T(8,128)(2,1)S(1)} %get-tuple-element.18), channel_id=1, source_target_pairs={{0,16},{1,17},{2,18},{3,19},{4,20},{5,21},{6,22},{7,23},{8,24},{9,... | collective-permute-start | bytes 442376 | tf_op jit(solution)/shard_map/ppermute | solution.py:44

commit v2 on v0

v2 whole, which is shorter than its diff:
```python
import jax
import jax.numpy as jnp
import numpy as np
from jax import lax
from jax.experimental import pallas as pl
from jax.experimental.pallas import tpu as pltpu
from jax.sharding import PartitionSpec as P

SIZES = (8, 2, 2, 2, 4)
AXES = ("row", "col")
ROWS, COLS = 192, 768
HALF = COLS // 2
SLAB, BLOCK = 64, 128
VMEM_LIMIT = 18 * 1024 * 1024
F32, BF16 = jnp.float32, jnp.bfloat16


def moves(step):
    pairs = []
    for index, place in enumerate(np.ndindex(*SIZES)):
        target = np.mod(step(*place), SIZES)
        pairs.append((index, int(np.ravel_multi_index(target, SIZES))))
    return pairs


def along_y(sign):
    def step(z, yl, core, yh, x):
        y = (2 * yh + yl + sign) % 4
        return z, y % 2, core, y // 2, x

    return moves(step)


EAST = moves(lambda z, yl, core, yh, x: (z, yl, core, yh, x + 1))
WEST = moves(lambda z, yl, core, yh, x: (z, yl, core, yh, x - 1))
NORTH, SOUTH = along_y(1), along_y(-1)
ACROSS = moves(lambda z, yl, core, yh, x: (z, yl, core, 1 - yh, x))
TWIN = moves(lambda z, yl, core, yh, x: (z, 1 - yl, core, yh, x))
CORE = moves(lambda z, yl, core, yh, x: (z, yl, 1 - core, yh, x))
RING = moves(lambda z, yl, core, yh, x: (z + 1 - 2 * core, yl, core, yh, x))


def send(value, pairs):
    return lax.ppermute(value, AXES, pairs)


def cat(*parts):
    return jnp.concatenate(parts, axis=0)


def place():
    row, col = lax.axis_index("row"), lax.axis_index("col")
    return row // 4, (row // 2) % 2, row % 2, col


def listed(table, a, b):
    return table[jnp.minimum(a, b), jnp.maximum(a, b)] > 0


def mask_kernel(pattern, matrix, masked, keep, away):
    _, yl, _, col = place()
    row = lax.axis_index("row")
    for i in range(ROWS // SLAB):
        a = (row * 3 + i) // 2
        rows = slice(SLAB * i, SLAB * (i + 1))
        parts = []
        for j in range(COLS // BLOCK):
            b = col * 6 + j
            factor = jnp.where(listed(pattern, a, b) | (a == b), 1.0, 0.0).astype(F32)
            part = matrix[rows, BLOCK * j : BLOCK * (j + 1)].astype(F32) * factor
            parts.append(part.astype(BF16))
        line = jnp.concatenate(parts, axis=1)
        masked[rows, :] = line

    @pl.when(yl == 0)
    def _():
        keep[...] = masked[:, :HALF]
        away[...] = masked[:, HALF:]

    @pl.when(yl == 1)
    def _():
        keep[...] = masked[:, HALF:]
        away[...] = masked[:, :HALF]


def tiles(body):
    row, col = lax.axis_index("row"), lax.axis_index("col")
    for i in range(ROWS // SLAB):
        for j in range(COLS // BLOCK):
            rows, cols = slice(SLAB * i, SLAB * (i + 1)), slice(BLOCK * j, BLOCK * (j + 1))
            body(rows, cols, (row * 3 + i) // 2, col * 6 + j)


def fill_ring(put, pieces):
    own, other, a1, b1, a2, b2, a3, b3, a4, *far = pieces
    z, _, core, _ = place()
    sign, rows = 2 * core - 1, own.shape[0]

    def place_piece(ref, start, k, which):
        put(ref, start * rows, lax.rem(k + 16, 8), which)

    place_piece(own, 0, z, core)
    place_piece(other, 0, z, 1 - core)
    for s, (a, b) in enumerate(((a1, b1), (a2, b2), (a3, b3))):
        place_piece(a, 0, z + sign * (s + 1), core)
        place_piece(b, 0, z + sign * (s + 1), 1 - core)
        place_piece(far[s], 0, z - sign * (s + 1), 1 - core)
        place_piece(far[s], 1, z - sign * (s + 1), core)
    place_piece(a4, 0, z + 4, core)
    place_piece(far[3], 0, z + 4, 1 - core)


def fill_left(left, pieces):
    own, w, e, y, x2, x2_too, yw, ye, y2 = pieces
    _, _, _, col = place()
    yh, x = col // 4, col % 4

    def at(dx, dy):
        return lax.rem(yh + dy, 2) * 4 + lax.rem(x + dx + 4, 4)

    left[at(0, 0)] = own[...]
    left[at(-1, 0)] = w[...]
    left[at(1, 0)] = e[...]
    left[at(0, 1)] = y[...]
    left[at(2, 0), :ROWS, :] = x2[...]
    left[at(2, 0), ROWS:, :] = x2_too[...]
    left[at(-1, 1)] = yw[...]
    left[at(1, 1)] = ye[...]
    left[at(2, 1)] = y2[...]


def multiply(left, column, kept, away):
    def part(k):
        return jnp.dot(left[k], column[k].reshape(HALF, COLS), preferred_element_type=F32)

    total = sum((part(k) for k in range(1, 8)), part(0))
    kept[...] = total[:ROWS]
    away[...] = total[ROWS:].astype(BF16)


def fill_column(column, pieces):
    def put(ref, start, k, which):
        column[k, which] = ref[start : start + ROWS, :]

    fill_ring(put, pieces)


def square_kernel(*refs):
    kept, away, left, column = refs[22:]
    fill_left(left, refs[:9])
    fill_column(column, refs[9:22])
    multiply(left, column, kept, away)


def update_kernel(*refs):
    kept, away, column = refs[14:]
    fill_column(column, refs[1:14])
    multiply(refs[0], column, kept, away)


def weight_kernel(keep, kept, theirs, weight):
    row, col = lax.axis_index("row"), lax.axis_index("col")

    def body(rows, cols, a, b):
        factor = jnp.where(listed(keep, a, b), 0.5, 0.0).astype(F32)
        down = lax.broadcasted_iota(jnp.int32, (SLAB, BLOCK), 0) + (row * ROWS + rows.start)
        over = lax.broadcasted_iota(jnp.int32, (SLAB, BLOCK), 1) + (col * COLS + cols.start)
        eye = jnp.where(down == over, 1.5, 0.0).astype(F32)
        square = kept[rows, cols] + theirs[rows, cols].astype(F32)
        weight[rows, cols] = (eye - square * factor).astype(BF16)

    tiles(body)


def result_kernel(pattern, kept, theirs, result):
    def body(rows, cols, a, b):
        factor = jnp.where(listed(pattern, a, b) | (a == b), 1.0, 0.0).astype(F32)
        total = kept[rows, cols] + theirs[rows, cols].astype(F32)
        result[rows, cols] = (total * factor).astype(BF16)

    tiles(body)


SMEM, VMEM = (pl.BlockSpec(memory_space=space) for space in (pltpu.SMEM, pltpu.VMEM))


def struct(*shape, dtype=BF16):
    return jax.ShapeDtypeStruct(shape, dtype)


def call(kernel, args, outs, scratch, flops):
    return pl.pallas_call(
        kernel,
        in_specs=[SMEM if arg.dtype == jnp.int32 else VMEM for arg in args],
        out_specs=[VMEM] * len(outs),
        out_shape=outs,
        scratch_shapes=scratch,
        cost_estimate=pl.CostEstimate(flops=flops, bytes_accessed=0, transcendentals=0),
        compiler_params=pltpu.CompilerParams(vmem_limit_bytes=VMEM_LIMIT),
    )(*args)


def after(value, *others):
    return lax.optimization_barrier((value, *others))[0]


def ring(piece, first=(), second=(), third=(), fourth=(), last=()):
    other = send(piece, CORE)
    a1, b1 = send(piece, RING), send(other, RING)
    a2, b2 = send(after(a1, *first), RING), send(b1, RING)
    a3, b3 = send(after(a2, *second), RING), send(after(b2, *third), RING)
    a4 = send(after(a3, *fourth), RING)
    far = [send(cat(a, b), CORE) for a, b in ((a1, b1), (a2, b2), (a3, b3))]
    return [piece, other, a1, b1, a2, b2, a3, b3, a4, *far, send(after(a4, *last), CORE)]


def row(piece):
    w, e, y = send(piece, EAST), send(piece, WEST), send(piece, ACROSS)
    x2, x2_too = send(w[:ROWS], EAST), send(e[ROWS:], WEST)
    yw, ye = send(y, EAST), send(y, WEST)
    y2 = send(cat(x2, x2_too), ACROSS)
    return [piece, w, e, y, x2, x2_too, yw, ye, y2]


FLOPS = 2 * ROWS * COLS * 6144
SUMS = [struct(ROWS, COLS, dtype=F32), struct(ROWS, COLS)]
COLUMN = pltpu.VMEM((8, 2, ROWS, COLS), BF16)


def shards(matrix, pattern, keep):
    x, kept, away = call(
        mask_kernel,
        [pattern, matrix],
        [struct(ROWS, COLS), struct(ROWS, HALF), struct(ROWS, HALF)],
        [],
        0,
    )
    pieces = row(cat(kept, send(away, TWIN)))
    kept, away, left = call(
        square_kernel,
        [*pieces, *ring(x, pieces[:1], pieces[1:4], pieces[4:6], pieces[6:8], pieces[8:])],
        [*SUMS, struct(8, HALF, HALF)],
        [COLUMN],
        FLOPS,
    )
    (weight,) = call(weight_kernel, [keep, kept, send(away, TWIN)], [struct(ROWS, COLS)], [], 0)
    kept, away = call(update_kernel, [left, *ring(weight)], SUMS, [COLUMN], FLOPS)
    (result,) = call(result_kernel, [pattern, kept, send(away, TWIN)], [struct(ROWS, COLS)], [], 0)
    return result


def solution(mesh):
    return jax.shard_map(
        shards,
        mesh=mesh,
        in_specs=(P("row", "col"), P(), P()),
        out_specs=P("row", "col"),
        check_vma=False,
    )
```

time: 243 us -> 108 us (0.44)
  waiting for transfers between devices: 211 us -> 25.3 us
  starting transfers between devices: 0.08 us -> 70.3 us
  matrix products: 16.9 us -> 0 us
  between operations: 13.1 us -> 0.16 us
  Pallas kernels: 0 us -> 9.98 us
    all_gather x3 -> x0, waiting for transfers between devices: 211 us -> none  [the longest x1 75.3 us: shards(): square = add_rows(lax.all_gather(xlocal, 'row', axis=0, tiled=True))]
    ppermute x0 -> x35, starting transfers between devices: none -> 70.3 us  [send(): return lax.ppermute(value, AXES, pairs)]
    ppermute x0 -> x35, waiting for transfers between devices: none -> 25.3 us  [send(): return lax.ppermute(value, AXES, pairs)]
    dot_general x4 -> x0, matrix products: 16.9 us -> none  [the longest x2 13.6 us: add_rows(): return jnp.dot(panel, piece, preferred_element_type=jnp.float32)]
    pallas_call x0 -> x5, Pallas kernels: none -> 9.98 us  [call(): pl.pallas_call(kernel, in_specs=[SMEM if arg.dtype == jnp.int32 else VMEM...]
  transfers between devices with their start and end apart: 3 -> 35, of which waited for: 3 -> 11; matrix products, arithmetic and copies ran while one was open for 1% -> 0% of each run, Pallas kernels for 0% -> 0%
where the time goes in v2:
time: 108 us
  starting transfers between devices  70.3 us (65%)
  waiting for transfers between devices  25.3 us (23%)
  Pallas kernels  9.98 us (9%)
  local copies, waits for them, and re-layouts  1.78 us (2%)
    ppermute x35, starting transfers between devices, send(): return lax.ppermute(value, AXES, pairs)  70.3 us
    ppermute x35, waiting for transfers between devices, send(): return lax.ppermute(value, AXES, pairs)  25.3 us
    pallas_call x5, Pallas kernels, call(): pl.pallas_call(kernel, in_specs=[SMEM if arg.dtype == jnp.int32 else VMEM...  9.98 us
  transfers between devices with their start and end apart: 35, of which 11 were waited for; matrix products, arithmetic and copies ran while one was open for 0% of the time, Pallas kernels for 0%

profile of v2, /device:TPU:1, one launch (start us, length us, event | category | flops | bytes accessed | tf_op | source)
XLA Modules:
  0.0 107.8 jit_solution(8707791206034021737)
XLA Ops:
  0.0 1.0 copy-done
  1.0 0.7 copy-done.1
  1.7 1.1 %shard_map.37 = (bf16[192,768]{1,0:T(8,128)(2,1)S(1)}, bf16[192,384]{1,0:T(8,128)(2,1)S(1)}, bf16[192,384]{1,0:T(8,128)(2,1)S(1)}) custom-call(s32[48,48]{1,0:T(8,128)S(1)} %copy-done.1, bf16[192,768]{1,0:T(8,128)(2,1)S(1)} %copy-done), custom_call_target="tpu_custom_call" | custom-call | tf_op jit(solution)/shard_map/pallas_call | solution.py:192
  2.8 3.3 %collective-permute-start.9 = (bf16[192,768]{1,0:T(8,128)(2,1)S(1)}, bf16[192,768]{1,0:T(8,128)(2,1)S(1)}, u32[]{:S(2)}, u32[]{:S(2)}) collective-permute-start(bf16[192,768]{1,0:T(8,128)(2,1)S(1)} %get-tuple-element.20.refs_9_), channel_id=1, source_target_pairs={{0,8},{1,9},{2,10},{3,11},{4,12},{5,13},{6,14},{7,15},{8,0},{9,1},... | collective-permute-start | bytes 884744 | tf_op jit(solution)/shard_map/ppermute | solution.py:44
  6.1 5.2 %collective-permute-start.10 = (bf16[192,768]{1,0:T(8,128)(2,1)S(1)}, bf16[192,768]{1,0:T(8,128)(2,1)S(1)}, u32[]{:S(2)}, u32[]{:S(2)}) collective-permute-start(bf16[192,768]{1,0:T(8,128)(2,1)S(1)} %get-tuple-element.20.refs_9_), channel_id=1, source_target_pairs={{0,32},{1,33},{2,34},{3,35},{4,36},{5,37},{6,38},{7,39},{8,232},{9... | collective-permute-start | bytes 884744 | tf_op jit(solution)/shard_map/ppermute | solution.py:44
  11.3 0.8 collective-permute-start.11
  12.1 0.0 collective-permute-done
  12.1 2.6 %collective-permute-start.2 = (bf16[384,384]{1,0:T(8,128)(2,1)S(1)}, bf16[384,384]{1,0:T(8,128)(2,1)S(1)}, u32[]{:S(2)}, u32[]{:S(2)}) collective-permute-start(bf16[384,384]{1,0:T(8,128)(2,1)S(1)} %constant_dynamic-update-slice_fusion.refs_0_), channel_id=1, source_target_pairs={{0,3},{1,0},{2,1},{3,2},{4,7},{5,4},{6,5},{7,6},{8,11},{9,8},{10,9... | collective-permute-start | bytes 884744 | tf_op jit(solution)/shard_map/ppermute | solution.py:44
  14.7 2.6 %collective-permute-start.3 = (bf16[384,384]{1,0:T(8,128)(2,1)S(1)}, bf16[384,384]{1,0:T(8,128)(2,1)S(1)}, u32[]{:S(2)}, u32[]{:S(2)}) collective-permute-start(bf16[384,384]{1,0:T(8,128)(2,1)S(1)} %constant_dynamic-update-slice_fusion.refs_0_), channel_id=1, source_target_pairs={{0,4},{1,5},{2,6},{3,7},{4,0},{5,1},{6,2},{7,3},{8,12},{9,13},{10,... | collective-permute-start | bytes 884744 | tf_op jit(solution)/shard_map/ppermute | solution.py:44
  17.3 0.0 collective-permute-done.10.refs_11_
  17.3 3.5 %collective-permute-start.12 = (bf16[192,768]{1,0:T(8,128)(2,1)S(1)}, bf16[192,768]{1,0:T(8,128)(2,1)S(1)}, u32[]{:S(2)}, u32[]{:S(2)}) collective-permute-start(bf16[192,768]{1,0:T(8,128)(2,1)S(1)} %collective-permute-done.10.refs_11_), channel_id=1, source_target_pairs={{0,32},{1,33},{2,34},{3,35},{4,36},{5,37},{6,38},{7,39},{8,232},{9... | collective-permute-start | bytes 884744 | tf_op jit(solution)/shard_map/ppermute | solution.py:44
  20.9 0.0 collective-permute-done.11.refs_12_
  20.9 0.7 collective-permute-start.13
  21.6 2.8 %collective-permute-start.5 = (bf16[192,384]{1,0:T(8,128)(2,1)S(1)}, bf16[192,384]{1,0:T(8,128)(2,1)S(1)}, u32[]{:S(2)}, u32[]{:S(2)}) collective-permute-start(bf16[192,384]{1,0:T(8,128)(2,1)S(1)} %slice.9), channel_id=1, source_target_pairs={{0,3},{1,0},{2,1},{3,2},{4,7},{5,4},{6,5},{7,6},{8,11},{9,8},{10,9... | collective-permute-start | bytes 442376 | tf_op jit(solution)/shard_map/ppermute | solution.py:44
  24.4 0.1 collective-permute-start.4
  24.5 0.4 collective-permute-done.3.refs_3_
  24.9 2.2 %collective-permute-start.7 = (bf16[384,384]{1,0:T(8,128)(2,1)S(1)}, bf16[384,384]{1,0:T(8,128)(2,1)S(1)}, u32[]{:S(2)}, u32[]{:S(2)}) collective-permute-start(bf16[384,384]{1,0:T(8,128)(2,1)S(1)} %collective-permute-done.3.refs_3_), channel_id=1, source_target_pairs={{0,3},{1,0},{2,1},{3,2},{4,7},{5,4},{6,5},{7,6},{8,11},{9,8},{10,9... | collective-permute-start | bytes 884744 | tf_op jit(solution)/shard_map/ppermute | solution.py:44
  27.2 0.9 collective-permute-done.5.refs_5_
  28.0 1.7 %collective-permute-start.14 = (bf16[192,768]{1,0:T(8,128)(2,1)S(1)}, bf16[192,768]{1,0:T(8,128)(2,1)S(1)}, u32[]{:S(2)}, u32[]{:S(2)}) collective-permute-start(bf16[192,768]{1,0:T(8,128)(2,1)S(1)} %collective-permute-done.12.refs_13_), channel_id=1, source_target_pairs={{0,32},{1,33},{2,34},{3,35},{4,36},{5,37},{6,38},{7,39},{8,232},{9... | collective-permute-start | bytes 884744 | tf_op jit(solution)/shard_map/ppermute | solution.py:44
  29.8 1.5 %collective-permute-done.4.refs_4_ = bf16[192,384]{1,0:T(8,128)(2,1)S(1)} collective-permute-done((bf16[192,384]{1,0:T(8,128)(2,1)S(1)}, bf16[192,384]{1,0:T(8,128)(2,1)S(1)}, u32[]{:S(2)}, u32[]{:S(2)}) %collective-permute-start.4) | collective-permute-done | bytes 147488 | tf_op jit(solution)/shard_map/ppermute | solution.py:44
  31.3 0.9 collective-permute-start.15
  32.3 3.0 %collective-permute-start.8 = (bf16[384,384]{1,0:T(8,128)(2,1)S(1)}, bf16[384,384]{1,0:T(8,128)(2,1)S(1)}, u32[]{:S(2)}, u32[]{:S(2)}) collective-permute-start(bf16[384,384]{1,0:T(8,128)(2,1)S(1)} %pad_maximum_fusion.6), channel_id=1, source_target_pairs={{0,4},{1,5},{2,6},{3,7},{4,0},{5,1},{6,2},{7,3},{8,12},{9,13},{10,... | collective-permute-start | bytes 884744 | tf_op jit(solution)/shard_map/ppermute | solution.py:44
  35.3 1.9 %collective-permute-start.17 = (bf16[384,768]{1,0:T(8,128)(2,1)S(1)}, bf16[384,768]{1,0:T(8,128)(2,1)S(1)}, u32[]{:S(2)}, u32[]{:S(2)}) collective-permute-start(bf16[384,768]{1,0:T(8,128)(2,1)S(1)} %pad_maximum_fusion), channel_id=1, source_target_pairs={{0,8},{1,9},{2,10},{3,11},{4,12},{5,13},{6,14},{7,15},{8,0},{9,1},... | collective-permute-start | bytes 1769480 | tf_op jit(solution)/shard_map/ppermute | solution.py:44
  37.2 0.0 collective-permute-done.6.refs_6_
  37.2 0.0 collective-permute-done.14.refs_15_
  37.2 3.3 %collective-permute-start.16 = (bf16[192,768]{1,0:T(8,128)(2,1)S(1)}, bf16[192,768]{1,0:T(8,128)(2,1)S(1)}, u32[]{:S(2)}, u32[]{:S(2)}) collective-permute-start(bf16[192,768]{1,0:T(8,128)(2,1)S(1)} %collective-permute-done.14.refs_15_), channel_id=1, source_target_pairs={{0,32},{1,33},{2,34},{3,35},{4,36},{5,37},{6,38},{7,39},{8,232},{9... | collective-permute-start | bytes 884744 | tf_op jit(solution)/shard_map/ppermute | solution.py:44
  40.5 0.1 collective-permute-start.18
  40.6 0.0 collective-permute-done.15.refs_16_
  40.7 0.0 copy-start.3
  40.7 1.3 %collective-permute-start.19 = (bf16[384,768]{1,0:T(8,128)(2,1)S(1)}, bf16[384,768]{1,0:T(8,128)(2,1)S(1)}, u32[]{:S(2)}, u32[]{:S(2)}) collective-permute-start(bf16[384,768]{1,0:T(8,128)(2,1)S(1)} %pad_maximum_fusion.2), channel_id=1, source_target_pairs={{0,8},{1,9},{2,10},{3,11},{4,12},{5,13},{6,14},{7,15},{8,0},{9,1},... | collective-permute-start | bytes 1769480 | tf_op jit(solution)/shard_map/ppermute | solution.py:44
  41.9 0.0 collective-permute-done.8.refs_8_
  42.0 2.2 %collective-permute-done.16.refs_17_ = bf16[192,768]{1,0:T(8,128)(2,1)S(1)} collective-permute-done((bf16[192,768]{1,0:T(8,128)(2,1)S(1)}, bf16[192,768]{1,0:T(8,128)(2,1)S(1)}, u32[]{:S(2)}, u32[]{:S(2)}) %collective-permute-start.16) | collective-permute-done | bytes 294944 | tf_op jit(solution)/shard_map/ppermute | solution.py:44
  44.1 2.6 %collective-permute-start.20 = (bf16[192,768]{1,0:T(8,128)(2,1)S(1)}, bf16[192,768]{1,0:T(8,128)(2,1)S(1)}, u32[]{:S(2)}, u32[]{:S(2)}) collective-permute-start(bf16[192,768]{1,0:T(8,128)(2,1)S(1)} %collective-permute-done.16.refs_17_), channel_id=1, source_target_pairs={{0,8},{1,9},{2,10},{3,11},{4,12},{5,13},{6,14},{7,15},{8,0},{9,1},... | collective-permute-start | bytes 884744 | tf_op jit(solution)/shard_map/ppermute | solution.py:44
  46.7 0.0 collective-permute-done.17.refs_18_
  46.7 1.2 %collective-permute-done.20.refs_21_ = bf16[192,768]{1,0:T(8,128)(2,1)S(1)} collective-permute-done((bf16[192,768]{1,0:T(8,128)(2,1)S(1)}, bf16[192,768]{1,0:T(8,128)(2,1)S(1)}, u32[]{:S(2)}, u32[]{:S(2)}) %collective-permute-start.20) | collective-permute-done | bytes 294944 | tf_op jit(solution)/shard_map/ppermute | solution.py:44
  47.9 0.0 collective-permute-done.18.refs_19_
  47.9 0.0 collective-permute-done.19.refs_20_
  47.9 3.1 %shard_map.38 = (f32[192,768]{1,0:T(8,128)S(1)}, bf16[192,768]{1,0:T(8,128)(2,1)S(1)}, bf16[8,384,384]{2,1,0:T(8,128)(2,1)S(1)}) custom-call(bf16[384,384]{1,0:T(8,128)(2,1)S(1)} %constant_dynamic-update-slice_fusion.refs_0_, bf16[384,384]{1,0:T(8,128)(2,1)S(1)} %collective-permute-done.1.refs_1_, bf16[384,384]{1,0:T(8,128)(2,1)S(1)} %collective-permute-done.2.refs_2_, ...), custom_call_target="tpu_custom_call" | custom-call | flops 1811939328 | tf_op jit(solution)/shard_map/pallas_call | solution.py:192
  51.1 1.4 %collective-permute-start.21 = (bf16[192,768]{1,0:T(8,128)(2,1)S(1)}, bf16[192,768]{1,0:T(8,128)(2,1)S(1)}, u32[]{:S(2)}, u32[]{:S(2)}) collective-permute-start(bf16[192,768]{1,0:T(8,128)(2,1)S(1)} %get-tuple-element.28), channel_id=1, source_target_pairs={{0,16},{1,17},{2,18},{3,19},{4,20},{5,21},{6,22},{7,23},{8,24},{9,... | collective-permute-start | bytes 884744 | tf_op jit(solution)/shard_map/ppermute | solution.py:44
  52.5 6.9 %collective-permute-done.21.theirs = bf16[192,768]{1,0:T(8,128)(2,1)S(1)} collective-permute-done((bf16[192,768]{1,0:T(8,128)(2,1)S(1)}, bf16[192,768]{1,0:T(8,128)(2,1)S(1)}, u32[]{:S(2)}, u32[]{:S(2)}) %collective-permute-start.21) | collective-permute-done | bytes 294944 | tf_op jit(solution)/shard_map/ppermute | solution.py:44
  59.4 1.1 %shard_map.39.refs_1_ = bf16[192,768]{1,0:T(8,128)(2,1)S(1)} custom-call(s32[48,48]{1,0:T(8,128)S(1)} %copy-done.3, f32[192,768]{1,0:T(8,128)S(1)} %get-tuple-element.27.kept, bf16[192,768]{1,0:T(8,128)(2,1)S(1)} %collective-permute-done.21.theirs), custom_call_target="tpu_custom_call" | custom-call | tf_op jit(solution)/shard_map/pallas_call | solution.py:192
  60.5 1.3 %collective-permute-start.22 = (bf16[192,768]{1,0:T(8,128)(2,1)S(1)}, bf16[192,768]{1,0:T(8,128)(2,1)S(1)}, u32[]{:S(2)}, u32[]{:S(2)}) collective-permute-start(bf16[192,768]{1,0:T(8,128)(2,1)S(1)} %shard_map.39.refs_1_), channel_id=1, source_target_pairs={{0,8},{1,9},{2,10},{3,11},{4,12},{5,13},{6,14},{7,15},{8,0},{9,1},... | collective-permute-start | bytes 884744 | tf_op jit(solution)/shard_map/ppermute | solution.py:44
  61.8 1.7 %collective-permute-start.23 = (bf16[192,768]{1,0:T(8,128)(2,1)S(1)}, bf16[192,768]{1,0:T(8,128)(2,1)S(1)}, u32[]{:S(2)}, u32[]{:S(2)}) collective-permute-start(bf16[192,768]{1,0:T(8,128)(2,1)S(1)} %shard_map.39.refs_1_), channel_id=1, source_target_pairs={{0,32},{1,33},{2,34},{3,35},{4,36},{5,37},{6,38},{7,39},{8,232},{9... | collective-permute-start | bytes 884744 | tf_op jit(solution)/shard_map/ppermute | solution.py:44
  63.5 0.0 collective-permute-done.22.refs_2_
  63.5 1.2 %collective-permute-start.24 = (bf16[192,768]{1,0:T(8,128)(2,1)S(1)}, bf16[192,768]{1,0:T(8,128)(2,1)S(1)}, u32[]{:S(2)}, u32[]{:S(2)}) collective-permute-start(bf16[192,768]{1,0:T(8,128)(2,1)S(1)} %collective-permute-done.22.refs_2_), channel_id=1, source_target_pairs={{0,32},{1,33},{2,34},{3,35},{4,36},{5,37},{6,38},{7,39},{8,232},{9... | collective-permute-start | bytes 884744 | tf_op jit(solution)/shard_map/ppermute | solution.py:44
  64.7 2.9 %collective-permute-done.23.refs_3_ = bf16[192,768]{1,0:T(8,128)(2,1)S(1)} collective-permute-done((bf16[192,768]{1,0:T(8,128)(2,1)S(1)}, bf16[192,768]{1,0:T(8,128)(2,1)S(1)}, u32[]{:S(2)}, u32[]{:S(2)}) %collective-permute-start.23) | collective-permute-done | bytes 294944 | tf_op jit(solution)/shard_map/ppermute | solution.py:44
  67.6 2.7 %collective-permute-start.25 = (bf16[192,768]{1,0:T(8,128)(2,1)S(1)}, bf16[192,768]{1,0:T(8,128)(2,1)S(1)}, u32[]{:S(2)}, u32[]{:S(2)}) collective-permute-start(bf16[192,768]{1,0:T(8,128)(2,1)S(1)} %collective-permute-done.23.refs_3_), channel_id=1, source_target_pairs={{0,32},{1,33},{2,34},{3,35},{4,36},{5,37},{6,38},{7,39},{8,232},{9... | collective-permute-start | bytes 884744 | tf_op jit(solution)/shard_map/ppermute | solution.py:44
  70.3 0.5 collective-permute-done.24.refs_4_
  70.8 2.7 %collective-permute-start.26 = (bf16[192,768]{1,0:T(8,128)(2,1)S(1)}, bf16[192,768]{1,0:T(8,128)(2,1)S(1)}, u32[]{:S(2)}, u32[]{:S(2)}) collective-permute-start(bf16[192,768]{1,0:T(8,128)(2,1)S(1)} %collective-permute-done.24.refs_4_), channel_id=1, source_target_pairs={{0,32},{1,33},{2,34},{3,35},{4,36},{5,37},{6,38},{7,39},{8,232},{9... | collective-permute-start | bytes 884744 | tf_op jit(solution)/shard_map/ppermute | solution.py:44
  73.5 0.5 collective-permute-done.25.refs_5_
  74.0 3.1 %collective-permute-start.27 = (bf16[192,768]{1,0:T(8,128)(2,1)S(1)}, bf16[192,768]{1,0:T(8,128)(2,1)S(1)}, u32[]{:S(2)}, u32[]{:S(2)}) collective-permute-start(bf16[192,768]{1,0:T(8,128)(2,1)S(1)} %collective-permute-done.25.refs_5_), channel_id=1, source_target_pairs={{0,32},{1,33},{2,34},{3,35},{4,36},{5,37},{6,38},{7,39},{8,232},{9... | collective-permute-start | bytes 884744 | tf_op jit(solution)/shard_map/ppermute | solution.py:44
  77.1 0.0 collective-permute-done.26.refs_6_
  77.1 3.1 %collective-permute-start.28 = (bf16[192,768]{1,0:T(8,128)(2,1)S(1)}, bf16[192,768]{1,0:T(8,128)(2,1)S(1)}, u32[]{:S(2)}, u32[]{:S(2)}) collective-permute-start(bf16[192,768]{1,0:T(8,128)(2,1)S(1)} %collective-permute-done.26.refs_6_), channel_id=1, source_target_pairs={{0,32},{1,33},{2,34},{3,35},{4,36},{5,37},{6,38},{7,39},{8,232},{9... | collective-permute-start | bytes 884744 | tf_op jit(solution)/shard_map/ppermute | solution.py:44
  80.3 0.7 collective-permute-start.30
  81.0 3.0 %collective-permute-start.29 = (bf16[192,768]{1,0:T(8,128)(2,1)S(1)}, bf16[192,768]{1,0:T(8,128)(2,1)S(1)}, u32[]{:S(2)}, u32[]{:S(2)}) collective-permute-start(bf16[192,768]{1,0:T(8,128)(2,1)S(1)} %collective-permute-done.27.refs_7_), channel_id=1, source_target_pairs={{0,32},{1,33},{2,34},{3,35},{4,36},{5,37},{6,38},{7,39},{8,232},{9... | collective-permute-start | bytes 884744 | tf_op jit(solution)/shard_map/ppermute | solution.py:44
  84.0 2.0 %collective-permute-start.31 = (bf16[384,768]{1,0:T(8,128)(2,1)S(1)}, bf16[384,768]{1,0:T(8,128)(2,1)S(1)}, u32[]{:S(2)}, u32[]{:S(2)}) collective-permute-start(bf16[384,768]{1,0:T(8,128)(2,1)S(1)} %pad_maximum_fusion.4), channel_id=1, source_target_pairs={{0,8},{1,9},{2,10},{3,11},{4,12},{5,13},{6,14},{7,15},{8,0},{9,1},... | collective-permute-start | bytes 1769480 | tf_op jit(solution)/shard_map/ppermute | solution.py:44
  86.0 0.0 collective-permute-done.28.refs_8_
  86.1 2.9 %collective-permute-start.32 = (bf16[384,768]{1,0:T(8,128)(2,1)S(1)}, bf16[384,768]{1,0:T(8,128)(2,1)S(1)}, u32[]{:S(2)}, u32[]{:S(2)}) collective-permute-start(bf16[384,768]{1,0:T(8,128)(2,1)S(1)} %pad_maximum_fusion.5), channel_id=1, source_target_pairs={{0,8},{1,9},{2,10},{3,11},{4,12},{5,13},{6,14},{7,15},{8,0},{9,1},... | collective-permute-start | bytes 1769480 | tf_op jit(solution)/shard_map/ppermute | solution.py:44
  89.0 4.6 %collective-permute-start.33 = (bf16[192,768]{1,0:T(8,128)(2,1)S(1)}, bf16[192,768]{1,0:T(8,128)(2,1)S(1)}, u32[]{:S(2)}, u32[]{:S(2)}) collective-permute-start(bf16[192,768]{1,0:T(8,128)(2,1)S(1)} %collective-permute-done.29.refs_9_), channel_id=1, source_target_pairs={{0,8},{1,9},{2,10},{3,11},{4,12},{5,13},{6,14},{7,15},{8,0},{9,1},... | collective-permute-start | bytes 884744 | tf_op jit(solution)/shard_map/ppermute | solution.py:44
  93.6 1.2 %collective-permute-done.33.refs_13_ = bf16[192,768]{1,0:T(8,128)(2,1)S(1)} collective-permute-done((bf16[192,768]{1,0:T(8,128)(2,1)S(1)}, bf16[192,768]{1,0:T(8,128)(2,1)S(1)}, u32[]{:S(2)}, u32[]{:S(2)}) %collective-permute-start.33) | collective-permute-done | bytes 294944 | tf_op jit(solution)/shard_map/ppermute | solution.py:44
  94.8 2.9 %shard_map.40 = (f32[192,768]{1,0:T(8,128)S(1)}, bf16[192,768]{1,0:T(8,128)(2,1)S(1)}) custom-call(bf16[8,384,384]{2,1,0:T(8,128)(2,1)S(1)} %get-tuple-element.26.refs_0_, bf16[192,768]{1,0:T(8,128)(2,1)S(1)} %shard_map.39.refs_1_, bf16[192,768]{1,0:T(8,128)(2,1)S(1)} %collective-permute-done.22.refs_2_, ...), custom_call_target="tpu_custom_call" | custom-call | flops 1811939328 | tf_op jit(solution)/shard_map/pallas_call | solution.py:192
  97.7 1.4 %collective-permute-start.34 = (bf16[192,768]{1,0:T(8,128)(2,1)S(1)}, bf16[192,768]{1,0:T(8,128)(2,1)S(1)}, u32[]{:S(2)}, u32[]{:S(2)}) collective-permute-start(bf16[192,768]{1,0:T(8,128)(2,1)S(1)} %get-tuple-element.30), channel_id=1, source_target_pairs={{0,16},{1,17},{2,18},{3,19},{4,20},{5,21},{6,22},{7,23},{8,24},{9,... | collective-permute-start | bytes 884744 | tf_op jit(solution)/shard_map/ppermute | solution.py:44
  99.1 6.9 %collective-permute-done.34.theirs = bf16[192,768]{1,0:T(8,128)(2,1)S(1)} collective-permute-done((bf16[192,768]{1,0:T(8,128)(2,1)S(1)}, bf16[192,768]{1,0:T(8,128)(2,1)S(1)}, u32[]{:S(2)}, u32[]{:S(2)}) %collective-permute-start.34) | collective-permute-done | bytes 294944 | tf_op jit(solution)/shard_map/ppermute | solution.py:44
  106.0 1.8 %shard_map.41 = bf16[192,768]{1,0:T(8,128)(2,1)} custom-call(s32[48,48]{1,0:T(8,128)S(1)} %copy-done.2, f32[192,768]{1,0:T(8,128)S(1)} %get-tuple-element.29.kept, bf16[192,768]{1,0:T(8,128)(2,1)S(1)} %collective-permute-done.34.theirs), custom_call_target="tpu_custom_call" | custom-call | tf_op jit(solution)/shard_map/pallas_call | solution.py:192
  (30 shorter events, 0.4 us)
Async XLA Ops:
  0.0 1.0 copy-start
  1.0 0.7 copy-start.1
  2.8 8.5 %collective-permute-start.9 = (bf16[192,768]{1,0:T(8,128)(2,1)S(1)}, bf16[192,768]{1,0:T(8,128)(2,1)S(1)}, u32[]{:S(2)}, u32[]{:S(2)}) collective-permute-start(bf16[192,768]{1,0:T(8,128)(2,1)S(1)} %get-tuple-element.20.refs_9_), channel_id=1, source_target_pairs={{0,8},{1,9},{2,10},{3,11},{4,12},{5,13},{6,14},{7,15},{8,0},{9,1},... | collective-permute-start | bytes 884744 | tf_op jit(solution)/shard_map/ppermute | solution.py:44
  6.1 6.0 %collective-permute-start = (bf16[192,384]{1,0:T(8,128)(2,1)S(1)}, bf16[192,384]{1,0:T(8,128)(2,1)S(1)}, u32[]{:S(2)}, u32[]{:S(2)}) collective-permute-start(bf16[192,384]{1,0:T(8,128)(2,1)S(1)} %get-tuple-element.19), channel_id=1, source_target_pairs={{0,16},{1,17},{2,18},{3,19},{4,20},{5,21},{6,22},{7,23},{8,24},{9,... | collective-permute-start | bytes 442376 | tf_op jit(solution)/shard_map/ppermute | solution.py:44
  6.1 11.2 %collective-permute-start.10 = (bf16[192,768]{1,0:T(8,128)(2,1)S(1)}, bf16[192,768]{1,0:T(8,128)(2,1)S(1)}, u32[]{:S(2)}, u32[]{:S(2)}) collective-permute-start(bf16[192,768]{1,0:T(8,128)(2,1)S(1)} %get-tuple-element.20.refs_9_), channel_id=1, source_target_pairs={{0,32},{1,33},{2,34},{3,35},{4,36},{5,37},{6,38},{7,39},{8,232},{9... | collective-permute-start | bytes 884744 | tf_op jit(solution)/shard_map/ppermute | solution.py:44
  11.3 9.6 %collective-permute-start.11 = (bf16[192,768]{1,0:T(8,128)(2,1)S(1)}, bf16[192,768]{1,0:T(8,128)(2,1)S(1)}, u32[]{:S(2)}, u32[]{:S(2)}) collective-permute-start(bf16[192,768]{1,0:T(8,128)(2,1)S(1)} %collective-permute-done.9.refs_10_), channel_id=1, source_target_pairs={{0,32},{1,33},{2,34},{3,35},{4,36},{5,37},{6,38},{7,39},{8,232},{9... | collective-permute-start | bytes 884744 | tf_op jit(solution)/shard_map/ppermute | solution.py:44
  12.1 9.5 %collective-permute-start.2 = (bf16[384,384]{1,0:T(8,128)(2,1)S(1)}, bf16[384,384]{1,0:T(8,128)(2,1)S(1)}, u32[]{:S(2)}, u32[]{:S(2)}) collective-permute-start(bf16[384,384]{1,0:T(8,128)(2,1)S(1)} %constant_dynamic-update-slice_fusion.refs_0_), channel_id=1, source_target_pairs={{0,3},{1,0},{2,1},{3,2},{4,7},{5,4},{6,5},{7,6},{8,11},{9,8},{10,9... | collective-permute-start | bytes 884744 | tf_op jit(solution)/shard_map/ppermute | solution.py:44
  14.7 9.7 %collective-permute-start.1 = (bf16[384,384]{1,0:T(8,128)(2,1)S(1)}, bf16[384,384]{1,0:T(8,128)(2,1)S(1)}, u32[]{:S(2)}, u32[]{:S(2)}) collective-permute-start(bf16[384,384]{1,0:T(8,128)(2,1)S(1)} %constant_dynamic-update-slice_fusion.refs_0_), channel_id=1, source_target_pairs={{0,1},{1,2},{2,3},{3,0},{4,5},{5,6},{6,7},{7,4},{8,9},{9,10},{10,1... | collective-permute-start | bytes 884744 | tf_op jit(solution)/shard_map/ppermute | solution.py:44
  14.7 10.2 %collective-permute-start.3 = (bf16[384,384]{1,0:T(8,128)(2,1)S(1)}, bf16[384,384]{1,0:T(8,128)(2,1)S(1)}, u32[]{:S(2)}, u32[]{:S(2)}) collective-permute-start(bf16[384,384]{1,0:T(8,128)(2,1)S(1)} %constant_dynamic-update-slice_fusion.refs_0_), channel_id=1, source_target_pairs={{0,4},{1,5},{2,6},{3,7},{4,0},{5,1},{6,2},{7,3},{8,12},{9,13},{10,... | collective-permute-start | bytes 884744 | tf_op jit(solution)/shard_map/ppermute | solution.py:44
  17.3 9.9 %collective-permute-start.12 = (bf16[192,768]{1,0:T(8,128)(2,1)S(1)}, bf16[192,768]{1,0:T(8,128)(2,1)S(1)}, u32[]{:S(2)}, u32[]{:S(2)}) collective-permute-start(bf16[192,768]{1,0:T(8,128)(2,1)S(1)} %collective-permute-done.10.refs_11_), channel_id=1, source_target_pairs={{0,32},{1,33},{2,34},{3,35},{4,36},{5,37},{6,38},{7,39},{8,232},{9... | collective-permute-start | bytes 884744 | tf_op jit(solution)/shard_map/ppermute | solution.py:44
  20.9 10.4 %collective-permute-start.13 = (bf16[192,768]{1,0:T(8,128)(2,1)S(1)}, bf16[192,768]{1,0:T(8,128)(2,1)S(1)}, u32[]{:S(2)}, u32[]{:S(2)}) collective-permute-start(bf16[192,768]{1,0:T(8,128)(2,1)S(1)} %collective-permute-done.11.refs_12_), channel_id=1, source_target_pairs={{0,32},{1,33},{2,34},{3,35},{4,36},{5,37},{6,38},{7,39},{8,232},{9... | collective-permute-start | bytes 884744 | tf_op jit(solution)/shard_map/ppermute | solution.py:44
  21.6 6.4 %collective-permute-start.5 = (bf16[192,384]{1,0:T(8,128)(2,1)S(1)}, bf16[192,384]{1,0:T(8,128)(2,1)S(1)}, u32[]{:S(2)}, u32[]{:S(2)}) collective-permute-start(bf16[192,384]{1,0:T(8,128)(2,1)S(1)} %slice.9), channel_id=1, source_target_pairs={{0,3},{1,0},{2,1},{3,2},{4,7},{5,4},{6,5},{7,6},{8,11},{9,8},{10,9... | collective-permute-start | bytes 442376 | tf_op jit(solution)/shard_map/ppermute | solution.py:44
  24.4 6.9 %collective-permute-start.4 = (bf16[192,384]{1,0:T(8,128)(2,1)S(1)}, bf16[192,384]{1,0:T(8,128)(2,1)S(1)}, u32[]{:S(2)}, u32[]{:S(2)}) collective-permute-start(bf16[192,384]{1,0:T(8,128)(2,1)S(1)} %slice.8), channel_id=1, source_target_pairs={{0,1},{1,2},{2,3},{3,0},{4,5},{5,6},{6,7},{7,4},{8,9},{9,10},{10,1... | collective-permute-start | bytes 442376 | tf_op jit(solution)/shard_map/ppermute | solution.py:44
  24.9 10.4 %collective-permute-start.7 = (bf16[384,384]{1,0:T(8,128)(2,1)S(1)}, bf16[384,384]{1,0:T(8,128)(2,1)S(1)}, u32[]{:S(2)}, u32[]{:S(2)}) collective-permute-start(bf16[384,384]{1,0:T(8,128)(2,1)S(1)} %collective-permute-done.3.refs_3_), channel_id=1, source_target_pairs={{0,3},{1,0},{2,1},{3,2},{4,7},{5,4},{6,5},{7,6},{8,11},{9,8},{10,9... | collective-permute-start | bytes 884744 | tf_op jit(solution)/shard_map/ppermute | solution.py:44
  27.2 10.0 %collective-permute-start.6 = (bf16[384,384]{1,0:T(8,128)(2,1)S(1)}, bf16[384,384]{1,0:T(8,128)(2,1)S(1)}, u32[]{:S(2)}, u32[]{:S(2)}) collective-permute-start(bf16[384,384]{1,0:T(8,128)(2,1)S(1)} %collective-permute-done.3.refs_3_), channel_id=1, source_target_pairs={{0,1},{1,2},{2,3},{3,0},{4,5},{5,6},{6,7},{7,4},{8,9},{9,10},{10,1... | collective-permute-start | bytes 884744 | tf_op jit(solution)/shard_map/ppermute | solution.py:44
  28.0 9.2 %collective-permute-start.14 = (bf16[192,768]{1,0:T(8,128)(2,1)S(1)}, bf16[192,768]{1,0:T(8,128)(2,1)S(1)}, u32[]{:S(2)}, u32[]{:S(2)}) collective-permute-start(bf16[192,768]{1,0:T(8,128)(2,1)S(1)} %collective-permute-done.12.refs_13_), channel_id=1, source_target_pairs={{0,32},{1,33},{2,34},{3,35},{4,36},{5,37},{6,38},{7,39},{8,232},{9... | collective-permute-start | bytes 884744 | tf_op jit(solution)/shard_map/ppermute | solution.py:44
  31.3 9.3 %collective-permute-start.15 = (bf16[192,768]{1,0:T(8,128)(2,1)S(1)}, bf16[192,768]{1,0:T(8,128)(2,1)S(1)}, u32[]{:S(2)}, u32[]{:S(2)}) collective-permute-start(bf16[192,768]{1,0:T(8,128)(2,1)S(1)} %collective-permute-done.13.refs_14_), channel_id=1, source_target_pairs={{0,32},{1,33},{2,34},{3,35},{4,36},{5,37},{6,38},{7,39},{8,232},{9... | collective-permute-start | bytes 884744 | tf_op jit(solution)/shard_map/ppermute | solution.py:44
  32.3 9.7 %collective-permute-start.8 = (bf16[384,384]{1,0:T(8,128)(2,1)S(1)}, bf16[384,384]{1,0:T(8,128)(2,1)S(1)}, u32[]{:S(2)}, u32[]{:S(2)}) collective-permute-start(bf16[384,384]{1,0:T(8,128)(2,1)S(1)} %pad_maximum_fusion.6), channel_id=1, source_target_pairs={{0,4},{1,5},{2,6},{3,7},{4,0},{5,1},{6,2},{7,3},{8,12},{9,13},{10,... | collective-permute-start | bytes 884744 | tf_op jit(solution)/shard_map/ppermute | solution.py:44
  35.3 11.4 %collective-permute-start.17 = (bf16[384,768]{1,0:T(8,128)(2,1)S(1)}, bf16[384,768]{1,0:T(8,128)(2,1)S(1)}, u32[]{:S(2)}, u32[]{:S(2)}) collective-permute-start(bf16[384,768]{1,0:T(8,128)(2,1)S(1)} %pad_maximum_fusion), channel_id=1, source_target_pairs={{0,8},{1,9},{2,10},{3,11},{4,12},{5,13},{6,14},{7,15},{8,0},{9,1},... | collective-permute-start | bytes 1769480 | tf_op jit(solution)/shard_map/ppermute | solution.py:44
  37.2 6.9 %collective-permute-start.16 = (bf16[192,768]{1,0:T(8,128)(2,1)S(1)}, bf16[192,768]{1,0:T(8,128)(2,1)S(1)}, u32[]{:S(2)}, u32[]{:S(2)}) collective-permute-start(bf16[192,768]{1,0:T(8,128)(2,1)S(1)} %collective-permute-done.14.refs_15_), channel_id=1, source_target_pairs={{0,32},{1,33},{2,34},{3,35},{4,36},{5,37},{6,38},{7,39},{8,232},{9... | collective-permute-start | bytes 884744 | tf_op jit(solution)/shard_map/ppermute | solution.py:44
  40.5 7.4 %collective-permute-start.18 = (bf16[384,768]{1,0:T(8,128)(2,1)S(1)}, bf16[384,768]{1,0:T(8,128)(2,1)S(1)}, u32[]{:S(2)}, u32[]{:S(2)}) collective-permute-start(bf16[384,768]{1,0:T(8,128)(2,1)S(1)} %pad_maximum_fusion.1), channel_id=1, source_target_pairs={{0,8},{1,9},{2,10},{3,11},{4,12},{5,13},{6,14},{7,15},{8,0},{9,1},... | collective-permute-start | bytes 1769480 | tf_op jit(solution)/shard_map/ppermute | solution.py:44
  40.7 18.7 %copy-start.3 = (s32[48,48]{1,0:T(8,128)S(1)}, s32[48,48]{1,0:T(8,128)}, u32[]{:S(2)}) copy-start(s32[48,48]{1,0:T(8,128)} %keep.1) | copy-start | bytes 27652
  40.7 7.3 %collective-permute-start.19 = (bf16[384,768]{1,0:T(8,128)(2,1)S(1)}, bf16[384,768]{1,0:T(8,128)(2,1)S(1)}, u32[]{:S(2)}, u32[]{:S(2)}) collective-permute-start(bf16[384,768]{1,0:T(8,128)(2,1)S(1)} %pad_maximum_fusion.2), channel_id=1, source_target_pairs={{0,8},{1,9},{2,10},{3,11},{4,12},{5,13},{6,14},{7,15},{8,0},{9,1},... | collective-permute-start | bytes 1769480 | tf_op jit(solution)/shard_map/ppermute | solution.py:44
  44.1 3.8 %collective-permute-start.20 = (bf16[192,768]{1,0:T(8,128)(2,1)S(1)}, bf16[192,768]{1,0:T(8,128)(2,1)S(1)}, u32[]{:S(2)}, u32[]{:S(2)}) collective-permute-start(bf16[192,768]{1,0:T(8,128)(2,1)S(1)} %collective-permute-done.16.refs_17_), channel_id=1, source_target_pairs={{0,8},{1,9},{2,10},{3,11},{4,12},{5,13},{6,14},{7,15},{8,0},{9,1},... | collective-permute-start | bytes 884744 | tf_op jit(solution)/shard_map/ppermute | solution.py:44
  51.1 8.3 %collective-permute-start.21 = (bf16[192,768]{1,0:T(8,128)(2,1)S(1)}, bf16[192,768]{1,0:T(8,128)(2,1)S(1)}, u32[]{:S(2)}, u32[]{:S(2)}) collective-permute-start(bf16[192,768]{1,0:T(8,128)(2,1)S(1)} %get-tuple-element.28), channel_id=1, source_target_pairs={{0,16},{1,17},{2,18},{3,19},{4,20},{5,21},{6,22},{7,23},{8,24},{9,... | collective-permute-start | bytes 884744 | tf_op jit(solution)/shard_map/ppermute | solution.py:44
  60.5 3.0 %collective-permute-start.22 = (bf16[192,768]{1,0:T(8,128)(2,1)S(1)}, bf16[192,768]{1,0:T(8,128)(2,1)S(1)}, u32[]{:S(2)}, u32[]{:S(2)}) collective-permute-start(bf16[192,768]{1,0:T(8,128)(2,1)S(1)} %shard_map.39.refs_1_), channel_id=1, source_target_pairs={{0,8},{1,9},{2,10},{3,11},{4,12},{5,13},{6,14},{7,15},{8,0},{9,1},... | collective-permute-start | bytes 884744 | tf_op jit(solution)/shard_map/ppermute | solution.py:44
  61.8 5.9 %collective-permute-start.23 = (bf16[192,768]{1,0:T(8,128)(2,1)S(1)}, bf16[192,768]{1,0:T(8,128)(2,1)S(1)}, u32[]{:S(2)}, u32[]{:S(2)}) collective-permute-start(bf16[192,768]{1,0:T(8,128)(2,1)S(1)} %shard_map.39.refs_1_), channel_id=1, source_target_pairs={{0,32},{1,33},{2,34},{3,35},{4,36},{5,37},{6,38},{7,39},{8,232},{9... | collective-permute-start | bytes 884744 | tf_op jit(solution)/shard_map/ppermute | solution.py:44
  63.5 7.3 %collective-permute-start.24 = (bf16[192,768]{1,0:T(8,128)(2,1)S(1)}, bf16[192,768]{1,0:T(8,128)(2,1)S(1)}, u32[]{:S(2)}, u32[]{:S(2)}) collective-permute-start(bf16[192,768]{1,0:T(8,128)(2,1)S(1)} %collective-permute-done.22.refs_2_), channel_id=1, source_target_pairs={{0,32},{1,33},{2,34},{3,35},{4,36},{5,37},{6,38},{7,39},{8,232},{9... | collective-permute-start | bytes 884744 | tf_op jit(solution)/shard_map/ppermute | solution.py:44
  67.6 6.3 %collective-permute-start.25 = (bf16[192,768]{1,0:T(8,128)(2,1)S(1)}, bf16[192,768]{1,0:T(8,128)(2,1)S(1)}, u32[]{:S(2)}, u32[]{:S(2)}) collective-permute-start(bf16[192,768]{1,0:T(8,128)(2,1)S(1)} %collective-permute-done.23.refs_3_), channel_id=1, source_target_pairs={{0,32},{1,33},{2,34},{3,35},{4,36},{5,37},{6,38},{7,39},{8,232},{9... | collective-permute-start | bytes 884744 | tf_op jit(solution)/shard_map/ppermute | solution.py:44
  70.8 6.3 %collective-permute-start.26 = (bf16[192,768]{1,0:T(8,128)(2,1)S(1)}, bf16[192,768]{1,0:T(8,128)(2,1)S(1)}, u32[]{:S(2)}, u32[]{:S(2)}) collective-permute-start(bf16[192,768]{1,0:T(8,128)(2,1)S(1)} %collective-permute-done.24.refs_4_), channel_id=1, source_target_pairs={{0,32},{1,33},{2,34},{3,35},{4,36},{5,37},{6,38},{7,39},{8,232},{9... | collective-permute-start | bytes 884744 | tf_op jit(solution)/shard_map/ppermute | solution.py:44
  74.0 7.1 %collective-permute-start.27 = (bf16[192,768]{1,0:T(8,128)(2,1)S(1)}, bf16[192,768]{1,0:T(8,128)(2,1)S(1)}, u32[]{:S(2)}, u32[]{:S(2)}) collective-permute-start(bf16[192,768]{1,0:T(8,128)(2,1)S(1)} %collective-permute-done.25.refs_5_), channel_id=1, source_target_pairs={{0,32},{1,33},{2,34},{3,35},{4,36},{5,37},{6,38},{7,39},{8,232},{9... | collective-permute-start | bytes 884744 | tf_op jit(solution)/shard_map/ppermute | solution.py:44
  77.1 8.9 %collective-permute-start.28 = (bf16[192,768]{1,0:T(8,128)(2,1)S(1)}, bf16[192,768]{1,0:T(8,128)(2,1)S(1)}, u32[]{:S(2)}, u32[]{:S(2)}) collective-permute-start(bf16[192,768]{1,0:T(8,128)(2,1)S(1)} %collective-permute-done.26.refs_6_), channel_id=1, source_target_pairs={{0,32},{1,33},{2,34},{3,35},{4,36},{5,37},{6,38},{7,39},{8,232},{9... | collective-permute-start | bytes 884744 | tf_op jit(solution)/shard_map/ppermute | solution.py:44
  80.3 13.3 %collective-permute-start.30 = (bf16[384,768]{1,0:T(8,128)(2,1)S(1)}, bf16[384,768]{1,0:T(8,128)(2,1)S(1)}, u32[]{:S(2)}, u32[]{:S(2)}) collective-permute-start(bf16[384,768]{1,0:T(8,128)(2,1)S(1)} %pad_maximum_fusion.3), channel_id=1, source_target_pairs={{0,8},{1,9},{2,10},{3,11},{4,12},{5,13},{6,14},{7,15},{8,0},{9,1},... | collective-permute-start | bytes 1769480 | tf_op jit(solution)/shard_map/ppermute | solution.py:44
  81.0 7.9 %collective-permute-start.29 = (bf16[192,768]{1,0:T(8,128)(2,1)S(1)}, bf16[192,768]{1,0:T(8,128)(2,1)S(1)}, u32[]{:S(2)}, u32[]{:S(2)}) collective-permute-start(bf16[192,768]{1,0:T(8,128)(2,1)S(1)} %collective-permute-done.27.refs_7_), channel_id=1, source_target_pairs={{0,32},{1,33},{2,34},{3,35},{4,36},{5,37},{6,38},{7,39},{8,232},{9... | collective-permute-start | bytes 884744 | tf_op jit(solution)/shard_map/ppermute | solution.py:44
  84.0 9.6 %collective-permute-start.31 = (bf16[384,768]{1,0:T(8,128)(2,1)S(1)}, bf16[384,768]{1,0:T(8,128)(2,1)S(1)}, u32[]{:S(2)}, u32[]{:S(2)}) collective-permute-start(bf16[384,768]{1,0:T(8,128)(2,1)S(1)} %pad_maximum_fusion.4), channel_id=1, source_target_pairs={{0,8},{1,9},{2,10},{3,11},{4,12},{5,13},{6,14},{7,15},{8,0},{9,1},... | collective-permute-start | bytes 1769480 | tf_op jit(solution)/shard_map/ppermute | solution.py:44
  86.1 8.7 %collective-permute-start.32 = (bf16[384,768]{1,0:T(8,128)(2,1)S(1)}, bf16[384,768]{1,0:T(8,128)(2,1)S(1)}, u32[]{:S(2)}, u32[]{:S(2)}) collective-permute-start(bf16[384,768]{1,0:T(8,128)(2,1)S(1)} %pad_maximum_fusion.5), channel_id=1, source_target_pairs={{0,8},{1,9},{2,10},{3,11},{4,12},{5,13},{6,14},{7,15},{8,0},{9,1},... | collective-permute-start | bytes 1769480 | tf_op jit(solution)/shard_map/ppermute | solution.py:44
  89.0 5.9 %collective-permute-start.33 = (bf16[192,768]{1,0:T(8,128)(2,1)S(1)}, bf16[192,768]{1,0:T(8,128)(2,1)S(1)}, u32[]{:S(2)}, u32[]{:S(2)}) collective-permute-start(bf16[192,768]{1,0:T(8,128)(2,1)S(1)} %collective-permute-done.29.refs_9_), channel_id=1, source_target_pairs={{0,8},{1,9},{2,10},{3,11},{4,12},{5,13},{6,14},{7,15},{8,0},{9,1},... | collective-permute-start | bytes 884744 | tf_op jit(solution)/shard_map/ppermute | solution.py:44
  94.8 11.2 %copy-start.2 = (s32[48,48]{1,0:T(8,128)S(1)}, s32[48,48]{1,0:T(8,128)}, u32[]{:S(2)}) copy-start(s32[48,48]{1,0:T(8,128)} %pattern.3) | copy-start | bytes 27652
  97.7 8.3 %collective-permute-start.34 = (bf16[192,768]{1,0:T(8,128)(2,1)S(1)}, bf16[192,768]{1,0:T(8,128)(2,1)S(1)}, u32[]{:S(2)}, u32[]{:S(2)}) collective-permute-start(bf16[192,768]{1,0:T(8,128)(2,1)S(1)} %get-tuple-element.30), channel_id=1, source_target_pairs={{0,16},{1,17},{2,18},{3,19},{4,20},{5,21},{6,22},{7,23},{8,24},{9,... | collective-permute-start | bytes 884744 | tf_op jit(solution)/shard_map/ppermute | solution.py:44

commit v3 on v2

v3 whole, which is shorter than its diff:
```python
import functools

import jax
import jax.numpy as jnp
import numpy as np
from jax import lax
from jax.experimental import pallas as pl
from jax.experimental.pallas import tpu as pltpu
from jax.sharding import PartitionSpec as P

SIZES = (8, 2, 2, 2, 4)
AXES = ("row", "col")
ROWS, COLS = 192, 768
HALF = COLS // 2
SLAB, BLOCK = 64, 128
VMEM_LIMIT = 18 * 1024 * 1024
F32, BF16 = jnp.float32, jnp.bfloat16


def moves(step):
    pairs = []
    for index, place in enumerate(np.ndindex(*SIZES)):
        target = np.mod(step(*place), SIZES)
        pairs.append((index, int(np.ravel_multi_index(target, SIZES))))
    return pairs


def along_y(sign):
    def step(z, yl, core, yh, x):
        y = (2 * yh + yl + sign) % 4
        return z, y % 2, core, y // 2, x

    return moves(step)


EAST = moves(lambda z, yl, core, yh, x: (z, yl, core, yh, x + 1))
WEST = moves(lambda z, yl, core, yh, x: (z, yl, core, yh, x - 1))
NORTH, SOUTH = along_y(1), along_y(-1)
ACROSS = moves(lambda z, yl, core, yh, x: (z, yl, core, 1 - yh, x))
TWIN = moves(lambda z, yl, core, yh, x: (z, 1 - yl, core, yh, x))
CORE = moves(lambda z, yl, core, yh, x: (z, yl, 1 - core, yh, x))
RING = moves(lambda z, yl, core, yh, x: (z + 1 - 2 * core, yl, core, yh, x))


def send(value, pairs):
    return lax.ppermute(value, AXES, pairs)


def cat(*parts):
    return jnp.concatenate(parts, axis=0)


def place():
    row, col = lax.axis_index("row"), lax.axis_index("col")
    return row // 4, (row // 2) % 2, row % 2, col


def listed(table, a, b):
    return table[jnp.minimum(a, b), jnp.maximum(a, b)] > 0


def mask_kernel(pattern, matrix, masked, keep, away, table, block, sems):
    fetches = [
        pltpu.make_async_copy(pattern, table, sems.at[0]),
        pltpu.make_async_copy(matrix, block, sems.at[1]),
    ]
    for fetch in fetches:
        fetch.start()
    for fetch in fetches:
        fetch.wait()
    _, yl, _, _ = place()

    def body(rows, cols, a, b):
        factor = jnp.where(listed(table, a, b) | (a == b), 1.0, 0.0).astype(F32)
        masked[rows, cols] = (block[rows, cols].astype(F32) * factor).astype(BF16)

    tiles(body)

    @pl.when(yl == 0)
    def _():
        keep[...] = masked[:, :HALF]
        away[...] = masked[:, HALF:]

    @pl.when(yl == 1)
    def _():
        keep[...] = masked[:, HALF:]
        away[...] = masked[:, :HALF]


def tiles(body):
    row, col = lax.axis_index("row"), lax.axis_index("col")
    for i in range(ROWS // SLAB):
        for j in range(COLS // BLOCK):
            rows, cols = slice(SLAB * i, SLAB * (i + 1)), slice(BLOCK * j, BLOCK * (j + 1))
            body(rows, cols, (row * 3 + i) // 2, col * 6 + j)


def fill_left(left, pieces):
    own, w, e, y, x2, x2_too, yw, ye, y2 = pieces
    _, _, _, col = place()
    yh, x = col // 4, col % 4

    def at(dx, dy):
        return lax.rem(yh + dy, 2) * 4 + lax.rem(x + dx + 4, 4)

    left[at(0, 0)] = own[...]
    left[at(-1, 0)] = w[...]
    left[at(1, 0)] = e[...]
    left[at(0, 1)] = y[...]
    left[at(2, 0), :ROWS, :] = x2[...]
    left[at(2, 0), ROWS:, :] = x2_too[...]
    left[at(-1, 1)] = yw[...]
    left[at(1, 1)] = ye[...]
    left[at(2, 1)] = y2[...]


def multiply(left, rows, blocks):
    _, _, core, _ = place()

    def part(k, mine, others, pair):
        pair[core] = mine[...]
        pair[1 - core] = others[...]
        right = pair[...].reshape(HALF, COLS)
        return jnp.dot(left[lax.rem(k + 16, 8), rows], right, preferred_element_type=F32)

    return sum((part(*block) for block in blocks[1:]), part(*blocks[0]))


def near_sums(left, pieces, column):
    z, _, core, _ = place()
    sign = 2 * core - 1
    pairs = [(pieces[2 * s], pieces[2 * s + 1], column.at[s]) for s in range(4)]
    return multiply(left, slice(0, HALF), [(z + sign * s, *pair) for s, pair in enumerate(pairs)])


def square_kernel(*refs):
    total, left, column = refs[17:]
    fill_left(left, refs[:9])
    total[...] = near_sums(left, refs[9:17], column)


def update_kernel(*refs):
    total, column = refs[9:]
    total[...] = near_sums(refs[0], refs[1:9], column)


def last_kernel(part, left, total, a4, s1, s2, s3, s4, result, column):
    z, _, core, _ = place()
    sign = 2 * core - 1
    rows = slice(ROWS * part, ROWS * (part + 1))
    blocks = [(z + 4, a4, s4, column.at[3])]
    for s, ref in enumerate((s1, s2, s3)):
        blocks.append((z - sign * (s + 1), ref.at[ROWS:], ref.at[:ROWS], column.at[s]))
    result[...] = (total[rows] + multiply(left, rows, blocks)).astype(result.dtype)


def factor_kernel(pattern, keep, kept_square, eye, kept_result):
    row, col = lax.axis_index("row"), lax.axis_index("col")

    def body(rows, cols, a, b):
        shape = (SLAB, BLOCK)
        down = lax.broadcasted_iota(jnp.int32, shape, 0) + (row * ROWS + rows.start)
        over = lax.broadcasted_iota(jnp.int32, shape, 1) + (col * COLS + cols.start)
        eye[rows, cols] = jnp.where(down == over, 1.5, 0.0).astype(F32)
        square_factor = jnp.where(listed(keep, a, b), 0.5, 0.0).astype(F32)
        kept_square[rows, cols] = jnp.full(shape, square_factor, F32)
        result_factor = jnp.where(listed(pattern, a, b) | (a == b), 1.0, 0.0).astype(F32)
        kept_result[rows, cols] = jnp.full(shape, result_factor, F32)

    tiles(body)


SMEM, VMEM = (pl.BlockSpec(memory_space=space) for space in (pltpu.SMEM, pltpu.VMEM))


def struct(*shape, dtype=BF16):
    return jax.ShapeDtypeStruct(shape, dtype)


def call(kernel, args, outs, scratch, flops, specs=None):
    return pl.pallas_call(
        kernel,
        in_specs=specs or [SMEM if arg.dtype == jnp.int32 else VMEM for arg in args],
        out_specs=[VMEM] * len(outs),
        out_shape=outs,
        scratch_shapes=scratch,
        cost_estimate=pl.CostEstimate(flops=flops, bytes_accessed=0, transcendentals=0),
        compiler_params=pltpu.CompilerParams(vmem_limit_bytes=VMEM_LIMIT),
    )(*args)


def after(value, *others):
    return lax.optimization_barrier((value, *others))[0]


def ring(piece, multiply_by, **awaited):
    def step(value, name):
        return send(after(value, *awaited.get(name, ())), RING)

    other = send(piece, CORE)
    a1, b1 = step(piece, "a1"), step(other, "b1")
    a2, b2 = step(a1, "a2"), step(b1, "b2")
    a3, b3 = step(a2, "a3"), step(b2, "b3")
    a4 = step(a3, "a4")
    sums = multiply_by([piece, other, a1, b1, a2, b2, a3, b3])
    far = [send(cat(a, b), CORE) for a, b in ((a1, b1), (a2, b2), (a3, b3))]
    return sums, [a4, *far, send(after(a4, sums[0]), CORE)]


def row(piece):
    w, e, y = send(piece, EAST), send(piece, WEST), send(piece, ACROSS)
    x2, x2_too = send(w[:ROWS], EAST), send(e[ROWS:], WEST)
    yw, ye = send(y, EAST), send(y, WEST)
    y2 = send(cat(x2, x2_too), ACROSS)
    return [piece, w, e, y, x2, x2_too, yw, ye, y2]


FLOPS = 2 * ROWS * COLS * 6144
SUMS = struct(HALF, COLS, dtype=F32)
COLUMN = pltpu.VMEM((4, 2, ROWS, COLS), BF16)


def sums(left, total, last):
    args = [left, total, *last]
    away_kernel, keep_kernel = functools.partial(last_kernel, 1), functools.partial(last_kernel, 0)
    (away,) = call(away_kernel, args, [struct(ROWS, COLS)], [COLUMN], FLOPS // 4)
    theirs = send(away, TWIN)
    (kept,) = call(keep_kernel, args, [struct(ROWS, COLS, dtype=F32)], [COLUMN], FLOPS // 4)
    return kept + theirs.astype(F32)


def shards(matrix, pattern, keep):
    x, kept, away = call(
        mask_kernel,
        [pattern, matrix],
        [struct(ROWS, COLS), struct(ROWS, HALF), struct(ROWS, HALF)],
        [pltpu.SMEM((48, 48), jnp.int32), pltpu.VMEM((ROWS, COLS), BF16), pltpu.SemaphoreType.DMA((2,))],
        0,
        [pl.BlockSpec(memory_space=pltpu.HBM)] * 2,
    )
    kept_square, eye, kept_result = call(
        factor_kernel, [pattern, keep], [struct(ROWS, COLS, dtype=F32)] * 3, [], ROWS * COLS
    )
    pieces = row(cat(kept, send(away, TWIN)))

    def square(near):
        return call(square_kernel, [*pieces, *near], [SUMS, struct(8, HALF, HALF)], [COLUMN], FLOPS // 2)

    (total, left), last = ring(x, square, a2=pieces[:1], a3=pieces[1:4], b3=pieces[4:6], a4=pieces[6:8])
    weight = (eye - sums(left, total, last) * kept_square).astype(BF16)

    def update(near):
        return call(update_kernel, [left, *near], [SUMS], [COLUMN], FLOPS // 2)

    (total,), last = ring(weight, update)
    return (sums(left, total, last) * kept_result).astype(BF16)


def solution(mesh):
    return jax.shard_map(
        shards,
        mesh=mesh,
        in_specs=(P("row", "col"), P(), P()),
        out_specs=P("row", "col"),
        check_vma=False,
    )
```

time: 108 us -> 102 us (0.944)
  starting transfers between devices: 70.3 us -> 66.8 us
  waiting for transfers between devices: 25.3 us -> 22 us
    ppermute x35, starting transfers between devices: 70.3 us -> 66.8 us  [send(): return lax.ppermute(value, AXES, pairs)]
    ppermute x35, waiting for transfers between devices: 25.3 us -> 22 us  [send(): return lax.ppermute(value, AXES, pairs)]
    pallas_call x5 -> x8, Pallas kernels: 9.98 us -> 9.78 us  [call(): pl.pallas_call(kernel, in_specs=specs or [SMEM if arg.dtype == jnp.int32...]
  transfers between devices with their start and end apart: 35 -> 35, of which waited for: 11 -> 9; matrix products, arithmetic and copies ran while one was open for 0% -> 0% of each run, Pallas kernels for 0% -> 7%
where the time goes in v3:
time: 102 us
  starting transfers between devices  66.8 us (65%)
  waiting for transfers between devices  22 us (22%)
  Pallas kernels  9.78 us (10%)
  local copies, waits for them, and re-layouts  1.78 us (2%)
  other arithmetic  1.18 us (1%)
    ppermute x35, starting transfers between devices, send(): return lax.ppermute(value, AXES, pairs)  66.8 us
    ppermute x35, waiting for transfers between devices, send(): return lax.ppermute(value, AXES, pairs)  22 us
    pallas_call x8, Pallas kernels, call(): pl.pallas_call(kernel, in_specs=specs or [SMEM if arg.dtype == jnp.int32...  9.78 us
  transfers between devices with their start and end apart: 35, of which 9 were waited for; matrix products, arithmetic and copies ran while one was open for 0% of the time, Pallas kernels for 7%

profile of v3, /device:TPU:1, one launch (start us, length us, event | category | flops | bytes accessed | tf_op | source)
XLA Modules:
  0.0 101.7 jit_solution(6656893142612879806)
XLA Ops:
  0.0 1.0 copy-done
  1.0 0.7 copy-done.1
  1.7 1.1 %shard_map.37 = (bf16[192,768]{1,0:T(8,128)(2,1)S(1)}, bf16[192,384]{1,0:T(8,128)(2,1)S(1)}, bf16[192,384]{1,0:T(8,128)(2,1)S(1)}) custom-call(s32[48,48]{1,0:T(8,128)S(1)} %copy-done.1, bf16[192,768]{1,0:T(8,128)(2,1)S(1)} %copy-done), custom_call_target="tpu_custom_call" | custom-call | tf_op jit(solution)/shard_map/pallas_call | solution.py:181
  2.8 3.3 %collective-permute-start.9 = (bf16[192,768]{1,0:T(8,128)(2,1)S(1)}, bf16[192,768]{1,0:T(8,128)(2,1)S(1)}, u32[]{:S(2)}, u32[]{:S(2)}) collective-permute-start(bf16[192,768]{1,0:T(8,128)(2,1)S(1)} %get-tuple-element.21.refs_9_), channel_id=1, source_target_pairs={{0,8},{1,9},{2,10},{3,11},{4,12},{5,13},{6,14},{7,15},{8,0},{9,1},... | collective-permute-start | bytes 884744 | tf_op jit(solution)/shard_map/ppermute | solution.py:46
  6.1 5.2 %collective-permute-start.10 = (bf16[192,768]{1,0:T(8,128)(2,1)S(1)}, bf16[192,768]{1,0:T(8,128)(2,1)S(1)}, u32[]{:S(2)}, u32[]{:S(2)}) collective-permute-start(bf16[192,768]{1,0:T(8,128)(2,1)S(1)} %get-tuple-element.21.refs_9_), channel_id=1, source_target_pairs={{0,32},{1,33},{2,34},{3,35},{4,36},{5,37},{6,38},{7,39},{8,232},{9... | collective-permute-start | bytes 884744 | tf_op jit(solution)/shard_map/ppermute | solution.py:46
  11.3 0.0 collective-permute-done.9.refs_10_
  11.3 0.8 collective-permute-start.11
  12.2 1.3 %collective-permute-start.1 = (bf16[384,384]{1,0:T(8,128)(2,1)S(1)}, bf16[384,384]{1,0:T(8,128)(2,1)S(1)}, u32[]{:S(2)}, u32[]{:S(2)}) collective-permute-start(bf16[384,384]{1,0:T(8,128)(2,1)S(1)} %constant_dynamic-update-slice_fusion.refs_0_), channel_id=1, source_target_pairs={{0,1},{1,2},{2,3},{3,0},{4,5},{5,6},{6,7},{7,4},{8,9},{9,10},{10,1... | collective-permute-start | bytes 884744 | tf_op jit(solution)/shard_map/ppermute | solution.py:46
  13.4 1.5 %collective-permute-start.2 = (bf16[384,384]{1,0:T(8,128)(2,1)S(1)}, bf16[384,384]{1,0:T(8,128)(2,1)S(1)}, u32[]{:S(2)}, u32[]{:S(2)}) collective-permute-start(bf16[384,384]{1,0:T(8,128)(2,1)S(1)} %constant_dynamic-update-slice_fusion.refs_0_), channel_id=1, source_target_pairs={{0,3},{1,0},{2,1},{3,2},{4,7},{5,4},{6,5},{7,6},{8,11},{9,8},{10,9... | collective-permute-start | bytes 884744 | tf_op jit(solution)/shard_map/ppermute | solution.py:46
  14.9 2.6 %collective-permute-start.3 = (bf16[384,384]{1,0:T(8,128)(2,1)S(1)}, bf16[384,384]{1,0:T(8,128)(2,1)S(1)}, u32[]{:S(2)}, u32[]{:S(2)}) collective-permute-start(bf16[384,384]{1,0:T(8,128)(2,1)S(1)} %constant_dynamic-update-slice_fusion.refs_0_), channel_id=1, source_target_pairs={{0,4},{1,5},{2,6},{3,7},{4,0},{5,1},{6,2},{7,3},{8,12},{9,13},{10,... | collective-permute-start | bytes 884744 | tf_op jit(solution)/shard_map/ppermute | solution.py:46
  17.5 0.0 collective-permute-done.10.refs_11_
  17.5 3.5 %collective-permute-start.12 = (bf16[192,768]{1,0:T(8,128)(2,1)S(1)}, bf16[192,768]{1,0:T(8,128)(2,1)S(1)}, u32[]{:S(2)}, u32[]{:S(2)}) collective-permute-start(bf16[192,768]{1,0:T(8,128)(2,1)S(1)} %collective-permute-done.10.refs_11_), channel_id=1, source_target_pairs={{0,32},{1,33},{2,34},{3,35},{4,36},{5,37},{6,38},{7,39},{8,232},{9... | collective-permute-start | bytes 884744 | tf_op jit(solution)/shard_map/ppermute | solution.py:46
  21.1 0.0 collective-permute-done.11.refs_12_
  21.1 0.7 collective-permute-start.13
  21.8 0.0 collective-permute-done.1.refs_1_
  21.8 0.7 collective-permute-start.4
  22.5 0.0 collective-permute-done.2.refs_2_
  22.6 2.1 %collective-permute-start.5 = (bf16[192,384]{1,0:T(8,128)(2,1)S(1)}, bf16[192,384]{1,0:T(8,128)(2,1)S(1)}, u32[]{:S(2)}, u32[]{:S(2)}) collective-permute-start(bf16[192,384]{1,0:T(8,128)(2,1)S(1)} %slice.9), channel_id=1, source_target_pairs={{0,3},{1,0},{2,1},{3,2},{4,7},{5,4},{6,5},{7,6},{8,11},{9,8},{10,9... | collective-permute-start | bytes 442376 | tf_op jit(solution)/shard_map/ppermute | solution.py:46
  24.7 0.0 collective-permute-done.3.refs_3_
  24.7 0.6 collective-permute-start.6
  25.3 0.0 collective-permute-done.12.refs_13_
  25.3 2.1 %collective-permute-start.7 = (bf16[384,384]{1,0:T(8,128)(2,1)S(1)}, bf16[384,384]{1,0:T(8,128)(2,1)S(1)}, u32[]{:S(2)}, u32[]{:S(2)}) collective-permute-start(bf16[384,384]{1,0:T(8,128)(2,1)S(1)} %collective-permute-done.3.refs_3_), channel_id=1, source_target_pairs={{0,3},{1,0},{2,1},{3,2},{4,7},{5,4},{6,5},{7,6},{8,11},{9,8},{10,9... | collective-permute-start | bytes 884744 | tf_op jit(solution)/shard_map/ppermute | solution.py:46
  27.4 0.0 collective-permute-done.4.refs_4_
  27.4 2.5 %collective-permute-start.14 = (bf16[192,768]{1,0:T(8,128)(2,1)S(1)}, bf16[192,768]{1,0:T(8,128)(2,1)S(1)}, u32[]{:S(2)}, u32[]{:S(2)}) collective-permute-start(bf16[192,768]{1,0:T(8,128)(2,1)S(1)} %collective-permute-done.12.refs_13_), channel_id=1, source_target_pairs={{0,32},{1,33},{2,34},{3,35},{4,36},{5,37},{6,38},{7,39},{8,232},{9... | collective-permute-start | bytes 884744 | tf_op jit(solution)/shard_map/ppermute | solution.py:46
  29.9 0.0 collective-permute-done.5.refs_5_
  29.9 1.4 %collective-permute-start.15 = (bf16[192,768]{1,0:T(8,128)(2,1)S(1)}, bf16[192,768]{1,0:T(8,128)(2,1)S(1)}, u32[]{:S(2)}, u32[]{:S(2)}) collective-permute-start(bf16[192,768]{1,0:T(8,128)(2,1)S(1)} %collective-permute-done.13.refs_14_), channel_id=1, source_target_pairs={{0,32},{1,33},{2,34},{3,35},{4,36},{5,37},{6,38},{7,39},{8,232},{9... | collective-permute-start | bytes 884744 | tf_op jit(solution)/shard_map/ppermute | solution.py:46
  31.4 2.3 %collective-permute-start.8 = (bf16[384,384]{1,0:T(8,128)(2,1)S(1)}, bf16[384,384]{1,0:T(8,128)(2,1)S(1)}, u32[]{:S(2)}, u32[]{:S(2)}) collective-permute-start(bf16[384,384]{1,0:T(8,128)(2,1)S(1)} %pad_maximum_fusion.6), channel_id=1, source_target_pairs={{0,4},{1,5},{2,6},{3,7},{4,0},{5,1},{6,2},{7,3},{8,12},{9,13},{10,... | collective-permute-start | bytes 884744 | tf_op jit(solution)/shard_map/ppermute | solution.py:46
  33.7 2.0 %collective-permute-start.17 = (bf16[384,768]{1,0:T(8,128)(2,1)S(1)}, bf16[384,768]{1,0:T(8,128)(2,1)S(1)}, u32[]{:S(2)}, u32[]{:S(2)}) collective-permute-start(bf16[384,768]{1,0:T(8,128)(2,1)S(1)} %pad_maximum_fusion), channel_id=1, source_target_pairs={{0,8},{1,9},{2,10},{3,11},{4,12},{5,13},{6,14},{7,15},{8,0},{9,1},... | collective-permute-start | bytes 1769480 | tf_op jit(solution)/shard_map/ppermute | solution.py:46
  35.8 3.1 %collective-permute-start.16 = (bf16[192,768]{1,0:T(8,128)(2,1)S(1)}, bf16[192,768]{1,0:T(8,128)(2,1)S(1)}, u32[]{:S(2)}, u32[]{:S(2)}) collective-permute-start(bf16[192,768]{1,0:T(8,128)(2,1)S(1)} %collective-permute-done.14.refs_15_), channel_id=1, source_target_pairs={{0,32},{1,33},{2,34},{3,35},{4,36},{5,37},{6,38},{7,39},{8,232},{9... | collective-permute-start | bytes 884744 | tf_op jit(solution)/shard_map/ppermute | solution.py:46
  38.9 0.1 collective-permute-start.18
  39.1 2.8 %collective-permute-start.19 = (bf16[384,768]{1,0:T(8,128)(2,1)S(1)}, bf16[384,768]{1,0:T(8,128)(2,1)S(1)}, u32[]{:S(2)}, u32[]{:S(2)}) collective-permute-start(bf16[384,768]{1,0:T(8,128)(2,1)S(1)} %pad_maximum_fusion.2), channel_id=1, source_target_pairs={{0,8},{1,9},{2,10},{3,11},{4,12},{5,13},{6,14},{7,15},{8,0},{9,1},... | collective-permute-start | bytes 1769480 | tf_op jit(solution)/shard_map/ppermute | solution.py:46
  41.9 1.7 %shard_map.38 = (f32[384,768]{1,0:T(8,128)S(1)}, bf16[8,384,384]{2,1,0:T(8,128)(2,1)S(1)}) custom-call(bf16[384,384]{1,0:T(8,128)(2,1)S(1)} %constant_dynamic-update-slice_fusion.refs_0_, bf16[384,384]{1,0:T(8,128)(2,1)S(1)} %collective-permute-done.1.refs_1_, bf16[384,384]{1,0:T(8,128)(2,1)S(1)} %collective-permute-done.2.refs_2_, ...), custom_call_target="tpu_custom_call" | custom-call | flops 905969664 | tf_op jit(solution)/shard_map/pallas_call | solution.py:181
  43.6 3.0 %collective-permute-start.20 = (bf16[192,768]{1,0:T(8,128)(2,1)S(1)}, bf16[192,768]{1,0:T(8,128)(2,1)S(1)}, u32[]{:S(2)}, u32[]{:S(2)}) collective-permute-start(bf16[192,768]{1,0:T(8,128)(2,1)S(1)} %collective-permute-done.16.a4), channel_id=1, source_target_pairs={{0,8},{1,9},{2,10},{3,11},{4,12},{5,13},{6,14},{7,15},{8,0},{9,1},... | collective-permute-start | bytes 884744 | tf_op jit(solution)/shard_map/ppermute | solution.py:46
  46.6 1.2 %collective-permute-done.20.s4 = bf16[192,768]{1,0:T(8,128)(2,1)S(1)} collective-permute-done((bf16[192,768]{1,0:T(8,128)(2,1)S(1)}, bf16[192,768]{1,0:T(8,128)(2,1)S(1)}, u32[]{:S(2)}, u32[]{:S(2)}) %collective-permute-start.20) | collective-permute-done | bytes 294944 | tf_op jit(solution)/shard_map/ppermute | solution.py:46
  47.8 1.0 shard_map.41
  48.8 1.4 %collective-permute-start.21 = (bf16[192,768]{1,0:T(8,128)(2,1)S(1)}, bf16[192,768]{1,0:T(8,128)(2,1)S(1)}, u32[]{:S(2)}, u32[]{:S(2)}) collective-permute-start(bf16[192,768]{1,0:T(8,128)(2,1)S(1)} %shard_map.41), channel_id=1, source_target_pairs={{0,16},{1,17},{2,18},{3,19},{4,20},{5,21},{6,22},{7,23},{8,24},{9,... | collective-permute-start | bytes 884744 | tf_op jit(solution)/shard_map/ppermute | solution.py:46
  50.2 1.5 %shard_map.39 = (f32[192,768]{1,0:T(8,128)S(1)}, f32[192,768]{1,0:T(8,128)S(1)}, f32[192,768]{1,0:T(8,128)S(1)}) custom-call(s32[48,48]{1,0:T(8,128)S(1)} %copy-done.2, s32[48,48]{1,0:T(8,128)S(1)} %copy-done.3), custom_call_target="tpu_custom_call" | custom-call | flops 147456 | tf_op jit(solution)/shard_map/pallas_call | solution.py:181
  51.7 1.0 shard_map.40
  52.7 4.4 %collective-permute-done.21 = bf16[192,768]{1,0:T(8,128)(2,1)S(1)} collective-permute-done((bf16[192,768]{1,0:T(8,128)(2,1)S(1)}, bf16[192,768]{1,0:T(8,128)(2,1)S(1)}, u32[]{:S(2)}, u32[]{:S(2)}) %collective-permute-start.21) | collective-permute-done | bytes 294944 | tf_op jit(solution)/shard_map/ppermute | solution.py:46
  57.1 0.1 subtract_convert_fusion.refs_1_
  57.3 1.3 %collective-permute-start.22 = (bf16[192,768]{1,0:T(8,128)(2,1)S(1)}, bf16[192,768]{1,0:T(8,128)(2,1)S(1)}, u32[]{:S(2)}, u32[]{:S(2)}) collective-permute-start(bf16[192,768]{1,0:T(8,128)(2,1)S(1)} %subtract_convert_fusion.refs_1_), channel_id=1, source_target_pairs={{0,8},{1,9},{2,10},{3,11},{4,12},{5,13},{6,14},{7,15},{8,0},{9,1},... | collective-permute-start | bytes 884744 | tf_op jit(solution)/shard_map/ppermute | solution.py:46
  58.6 0.5 collective-permute-start.23
  59.1 0.7 collective-permute-done.22.refs_2_
  59.8 0.5 collective-permute-start.24
  60.3 4.1 %collective-permute-done.23.refs_3_ = bf16[192,768]{1,0:T(8,128)(2,1)S(1)} collective-permute-done((bf16[192,768]{1,0:T(8,128)(2,1)S(1)}, bf16[192,768]{1,0:T(8,128)(2,1)S(1)}, u32[]{:S(2)}, u32[]{:S(2)}) %collective-permute-start.23) | collective-permute-done | bytes 294944 | tf_op jit(solution)/shard_map/ppermute | solution.py:46
  64.4 1.4 %collective-permute-start.25 = (bf16[192,768]{1,0:T(8,128)(2,1)S(1)}, bf16[192,768]{1,0:T(8,128)(2,1)S(1)}, u32[]{:S(2)}, u32[]{:S(2)}) collective-permute-start(bf16[192,768]{1,0:T(8,128)(2,1)S(1)} %collective-permute-done.23.refs_3_), channel_id=1, source_target_pairs={{0,32},{1,33},{2,34},{3,35},{4,36},{5,37},{6,38},{7,39},{8,232},{9... | collective-permute-start | bytes 884744 | tf_op jit(solution)/shard_map/ppermute | solution.py:46
  65.9 1.7 %collective-permute-done.24.refs_4_ = bf16[192,768]{1,0:T(8,128)(2,1)S(1)} collective-permute-done((bf16[192,768]{1,0:T(8,128)(2,1)S(1)}, bf16[192,768]{1,0:T(8,128)(2,1)S(1)}, u32[]{:S(2)}, u32[]{:S(2)}) %collective-permute-start.24) | collective-permute-done | bytes 294944 | tf_op jit(solution)/shard_map/ppermute | solution.py:46
  67.6 1.4 %collective-permute-start.26 = (bf16[192,768]{1,0:T(8,128)(2,1)S(1)}, bf16[192,768]{1,0:T(8,128)(2,1)S(1)}, u32[]{:S(2)}, u32[]{:S(2)}) collective-permute-start(bf16[192,768]{1,0:T(8,128)(2,1)S(1)} %collective-permute-done.24.refs_4_), channel_id=1, source_target_pairs={{0,32},{1,33},{2,34},{3,35},{4,36},{5,37},{6,38},{7,39},{8,232},{9... | collective-permute-start | bytes 884744 | tf_op jit(solution)/shard_map/ppermute | solution.py:46
  69.0 1.4 %collective-permute-done.25.refs_5_ = bf16[192,768]{1,0:T(8,128)(2,1)S(1)} collective-permute-done((bf16[192,768]{1,0:T(8,128)(2,1)S(1)}, bf16[192,768]{1,0:T(8,128)(2,1)S(1)}, u32[]{:S(2)}, u32[]{:S(2)}) %collective-permute-start.25) | collective-permute-done | bytes 294944 | tf_op jit(solution)/shard_map/ppermute | solution.py:46
  70.5 2.2 %collective-permute-start.27 = (bf16[192,768]{1,0:T(8,128)(2,1)S(1)}, bf16[192,768]{1,0:T(8,128)(2,1)S(1)}, u32[]{:S(2)}, u32[]{:S(2)}) collective-permute-start(bf16[192,768]{1,0:T(8,128)(2,1)S(1)} %collective-permute-done.25.refs_5_), channel_id=1, source_target_pairs={{0,32},{1,33},{2,34},{3,35},{4,36},{5,37},{6,38},{7,39},{8,232},{9... | collective-permute-start | bytes 884744 | tf_op jit(solution)/shard_map/ppermute | solution.py:46
  72.7 1.2 %collective-permute-done.26.refs_6_ = bf16[192,768]{1,0:T(8,128)(2,1)S(1)} collective-permute-done((bf16[192,768]{1,0:T(8,128)(2,1)S(1)}, bf16[192,768]{1,0:T(8,128)(2,1)S(1)}, u32[]{:S(2)}, u32[]{:S(2)}) %collective-permute-start.26) | collective-permute-done | bytes 294944 | tf_op jit(solution)/shard_map/ppermute | solution.py:46
  73.9 1.9 %collective-permute-start.28 = (bf16[192,768]{1,0:T(8,128)(2,1)S(1)}, bf16[192,768]{1,0:T(8,128)(2,1)S(1)}, u32[]{:S(2)}, u32[]{:S(2)}) collective-permute-start(bf16[192,768]{1,0:T(8,128)(2,1)S(1)} %collective-permute-done.26.refs_6_), channel_id=1, source_target_pairs={{0,32},{1,33},{2,34},{3,35},{4,36},{5,37},{6,38},{7,39},{8,232},{9... | collective-permute-start | bytes 884744 | tf_op jit(solution)/shard_map/ppermute | solution.py:46
  75.9 1.9 %collective-permute-start.30 = (bf16[384,768]{1,0:T(8,128)(2,1)S(1)}, bf16[384,768]{1,0:T(8,128)(2,1)S(1)}, u32[]{:S(2)}, u32[]{:S(2)}) collective-permute-start(bf16[384,768]{1,0:T(8,128)(2,1)S(1)} %pad_maximum_fusion.3), channel_id=1, source_target_pairs={{0,8},{1,9},{2,10},{3,11},{4,12},{5,13},{6,14},{7,15},{8,0},{9,1},... | collective-permute-start | bytes 1769480 | tf_op jit(solution)/shard_map/ppermute | solution.py:46
  77.8 3.0 %collective-permute-start.29 = (bf16[192,768]{1,0:T(8,128)(2,1)S(1)}, bf16[192,768]{1,0:T(8,128)(2,1)S(1)}, u32[]{:S(2)}, u32[]{:S(2)}) collective-permute-start(bf16[192,768]{1,0:T(8,128)(2,1)S(1)} %collective-permute-done.27.refs_7_), channel_id=1, source_target_pairs={{0,32},{1,33},{2,34},{3,35},{4,36},{5,37},{6,38},{7,39},{8,232},{9... | collective-permute-start | bytes 884744 | tf_op jit(solution)/shard_map/ppermute | solution.py:46
  80.8 1.8 %collective-permute-start.31 = (bf16[384,768]{1,0:T(8,128)(2,1)S(1)}, bf16[384,768]{1,0:T(8,128)(2,1)S(1)}, u32[]{:S(2)}, u32[]{:S(2)}) collective-permute-start(bf16[384,768]{1,0:T(8,128)(2,1)S(1)} %pad_maximum_fusion.4), channel_id=1, source_target_pairs={{0,8},{1,9},{2,10},{3,11},{4,12},{5,13},{6,14},{7,15},{8,0},{9,1},... | collective-permute-start | bytes 1769480 | tf_op jit(solution)/shard_map/ppermute | solution.py:46
  82.6 3.1 %collective-permute-start.32 = (bf16[384,768]{1,0:T(8,128)(2,1)S(1)}, bf16[384,768]{1,0:T(8,128)(2,1)S(1)}, u32[]{:S(2)}, u32[]{:S(2)}) collective-permute-start(bf16[384,768]{1,0:T(8,128)(2,1)S(1)} %pad_maximum_fusion.5), channel_id=1, source_target_pairs={{0,8},{1,9},{2,10},{3,11},{4,12},{5,13},{6,14},{7,15},{8,0},{9,1},... | collective-permute-start | bytes 1769480 | tf_op jit(solution)/shard_map/ppermute | solution.py:46
  85.7 1.5 %shard_map.42.total = f32[384,768]{1,0:T(8,128)S(1)} custom-call(bf16[8,384,384]{2,1,0:T(8,128)(2,1)S(1)} %get-tuple-element.25.left.refs_0_, bf16[192,768]{1,0:T(8,128)(2,1)S(1)} %subtract_convert_fusion.refs_1_, bf16[192,768]{1,0:T(8,128)(2,1)S(1)} %collective-permute-done.22.refs_2_, bf16[192,768]{1,0:T(8,128)(2,1)S(1)} %collective-permute-done.23.refs_3_, ...), custom_call_target="tpu_custom_call" | custom-call | flops 905969664 | tf_op jit(solution)/shard_map/pallas_call | solution.py:181
  87.3 3.1 %collective-permute-start.33 = (bf16[192,768]{1,0:T(8,128)(2,1)S(1)}, bf16[192,768]{1,0:T(8,128)(2,1)S(1)}, u32[]{:S(2)}, u32[]{:S(2)}) collective-permute-start(bf16[192,768]{1,0:T(8,128)(2,1)S(1)} %collective-permute-done.29.a4), channel_id=1, source_target_pairs={{0,8},{1,9},{2,10},{3,11},{4,12},{5,13},{6,14},{7,15},{8,0},{9,1},... | collective-permute-start | bytes 884744 | tf_op jit(solution)/shard_map/ppermute | solution.py:46
  90.4 1.2 %collective-permute-done.33.s4 = bf16[192,768]{1,0:T(8,128)(2,1)S(1)} collective-permute-done((bf16[192,768]{1,0:T(8,128)(2,1)S(1)}, bf16[192,768]{1,0:T(8,128)(2,1)S(1)}, u32[]{:S(2)}, u32[]{:S(2)}) %collective-permute-start.33) | collective-permute-done | bytes 294944 | tf_op jit(solution)/shard_map/ppermute | solution.py:46
  91.6 1.0 shard_map.44
  92.6 1.4 %collective-permute-start.34 = (bf16[192,768]{1,0:T(8,128)(2,1)S(1)}, bf16[192,768]{1,0:T(8,128)(2,1)S(1)}, u32[]{:S(2)}, u32[]{:S(2)}) collective-permute-start(bf16[192,768]{1,0:T(8,128)(2,1)S(1)} %shard_map.44), channel_id=1, source_target_pairs={{0,16},{1,17},{2,18},{3,19},{4,20},{5,21},{6,22},{7,23},{8,24},{9,... | collective-permute-start | bytes 884744 | tf_op jit(solution)/shard_map/ppermute | solution.py:46
  94.0 1.0 shard_map.43
  95.0 5.9 %collective-permute-done.34 = bf16[192,768]{1,0:T(8,128)(2,1)S(1)} collective-permute-done((bf16[192,768]{1,0:T(8,128)(2,1)S(1)}, bf16[192,768]{1,0:T(8,128)(2,1)S(1)}, u32[]{:S(2)}, u32[]{:S(2)}) %collective-permute-start.34) | collective-permute-done | bytes 294944 | tf_op jit(solution)/shard_map/ppermute | solution.py:46
  100.9 0.8 multiply_convert_fusion
  (35 shorter events, 0.4 us)
Async XLA Ops:
  0.0 1.0 copy-start
  1.0 0.7 copy-start.1
  2.8 8.5 %collective-permute-start.9 = (bf16[192,768]{1,0:T(8,128)(2,1)S(1)}, bf16[192,768]{1,0:T(8,128)(2,1)S(1)}, u32[]{:S(2)}, u32[]{:S(2)}) collective-permute-start(bf16[192,768]{1,0:T(8,128)(2,1)S(1)} %get-tuple-element.21.refs_9_), channel_id=1, source_target_pairs={{0,8},{1,9},{2,10},{3,11},{4,12},{5,13},{6,14},{7,15},{8,0},{9,1},... | collective-permute-start | bytes 884744 | tf_op jit(solution)/shard_map/ppermute | solution.py:46
  6.1 6.0 %collective-permute-start = (bf16[192,384]{1,0:T(8,128)(2,1)S(1)}, bf16[192,384]{1,0:T(8,128)(2,1)S(1)}, u32[]{:S(2)}, u32[]{:S(2)}) collective-permute-start(bf16[192,384]{1,0:T(8,128)(2,1)S(1)} %get-tuple-element.20), channel_id=1, source_target_pairs={{0,16},{1,17},{2,18},{3,19},{4,20},{5,21},{6,22},{7,23},{8,24},{9,... | collective-permute-start | bytes 442376 | tf_op jit(solution)/shard_map/ppermute | solution.py:46
  6.1 11.4 %collective-permute-start.10 = (bf16[192,768]{1,0:T(8,128)(2,1)S(1)}, bf16[192,768]{1,0:T(8,128)(2,1)S(1)}, u32[]{:S(2)}, u32[]{:S(2)}) collective-permute-start(bf16[192,768]{1,0:T(8,128)(2,1)S(1)} %get-tuple-element.21.refs_9_), channel_id=1, source_target_pairs={{0,32},{1,33},{2,34},{3,35},{4,36},{5,37},{6,38},{7,39},{8,232},{9... | collective-permute-start | bytes 884744 | tf_op jit(solution)/shard_map/ppermute | solution.py:46
  11.3 9.8 %collective-permute-start.11 = (bf16[192,768]{1,0:T(8,128)(2,1)S(1)}, bf16[192,768]{1,0:T(8,128)(2,1)S(1)}, u32[]{:S(2)}, u32[]{:S(2)}) collective-permute-start(bf16[192,768]{1,0:T(8,128)(2,1)S(1)} %collective-permute-done.9.refs_10_), channel_id=1, source_target_pairs={{0,32},{1,33},{2,34},{3,35},{4,36},{5,37},{6,38},{7,39},{8,232},{9... | collective-permute-start | bytes 884744 | tf_op jit(solution)/shard_map/ppermute | solution.py:46
  12.2 9.7 %collective-permute-start.1 = (bf16[384,384]{1,0:T(8,128)(2,1)S(1)}, bf16[384,384]{1,0:T(8,128)(2,1)S(1)}, u32[]{:S(2)}, u32[]{:S(2)}) collective-permute-start(bf16[384,384]{1,0:T(8,128)(2,1)S(1)} %constant_dynamic-update-slice_fusion.refs_0_), channel_id=1, source_target_pairs={{0,1},{1,2},{2,3},{3,0},{4,5},{5,6},{6,7},{7,4},{8,9},{9,10},{10,1... | collective-permute-start | bytes 884744 | tf_op jit(solution)/shard_map/ppermute | solution.py:46
  13.4 9.1 %collective-permute-start.2 = (bf16[384,384]{1,0:T(8,128)(2,1)S(1)}, bf16[384,384]{1,0:T(8,128)(2,1)S(1)}, u32[]{:S(2)}, u32[]{:S(2)}) collective-permute-start(bf16[384,384]{1,0:T(8,128)(2,1)S(1)} %constant_dynamic-update-slice_fusion.refs_0_), channel_id=1, source_target_pairs={{0,3},{1,0},{2,1},{3,2},{4,7},{5,4},{6,5},{7,6},{8,11},{9,8},{10,9... | collective-permute-start | bytes 884744 | tf_op jit(solution)/shard_map/ppermute | solution.py:46
  14.9 9.8 %collective-permute-start.3 = (bf16[384,384]{1,0:T(8,128)(2,1)S(1)}, bf16[384,384]{1,0:T(8,128)(2,1)S(1)}, u32[]{:S(2)}, u32[]{:S(2)}) collective-permute-start(bf16[384,384]{1,0:T(8,128)(2,1)S(1)} %constant_dynamic-update-slice_fusion.refs_0_), channel_id=1, source_target_pairs={{0,4},{1,5},{2,6},{3,7},{4,0},{5,1},{6,2},{7,3},{8,12},{9,13},{10,... | collective-permute-start | bytes 884744 | tf_op jit(solution)/shard_map/ppermute | solution.py:46
  17.5 7.7 %collective-permute-start.12 = (bf16[192,768]{1,0:T(8,128)(2,1)S(1)}, bf16[192,768]{1,0:T(8,128)(2,1)S(1)}, u32[]{:S(2)}, u32[]{:S(2)}) collective-permute-start(bf16[192,768]{1,0:T(8,128)(2,1)S(1)} %collective-permute-done.10.refs_11_), channel_id=1, source_target_pairs={{0,32},{1,33},{2,34},{3,35},{4,36},{5,37},{6,38},{7,39},{8,232},{9... | collective-permute-start | bytes 884744 | tf_op jit(solution)/shard_map/ppermute | solution.py:46
  21.1 8.8 %collective-permute-start.13 = (bf16[192,768]{1,0:T(8,128)(2,1)S(1)}, bf16[192,768]{1,0:T(8,128)(2,1)S(1)}, u32[]{:S(2)}, u32[]{:S(2)}) collective-permute-start(bf16[192,768]{1,0:T(8,128)(2,1)S(1)} %collective-permute-done.11.refs_12_), channel_id=1, source_target_pairs={{0,32},{1,33},{2,34},{3,35},{4,36},{5,37},{6,38},{7,39},{8,232},{9... | collective-permute-start | bytes 884744 | tf_op jit(solution)/shard_map/ppermute | solution.py:46
  21.8 5.6 %collective-permute-start.4 = (bf16[192,384]{1,0:T(8,128)(2,1)S(1)}, bf16[192,384]{1,0:T(8,128)(2,1)S(1)}, u32[]{:S(2)}, u32[]{:S(2)}) collective-permute-start(bf16[192,384]{1,0:T(8,128)(2,1)S(1)} %slice.8), channel_id=1, source_target_pairs={{0,1},{1,2},{2,3},{3,0},{4,5},{5,6},{6,7},{7,4},{8,9},{9,10},{10,1... | collective-permute-start | bytes 442376 | tf_op jit(solution)/shard_map/ppermute | solution.py:46
  22.6 7.3 %collective-permute-start.5 = (bf16[192,384]{1,0:T(8,128)(2,1)S(1)}, bf16[192,384]{1,0:T(8,128)(2,1)S(1)}, u32[]{:S(2)}, u32[]{:S(2)}) collective-permute-start(bf16[192,384]{1,0:T(8,128)(2,1)S(1)} %slice.9), channel_id=1, source_target_pairs={{0,3},{1,0},{2,1},{3,2},{4,7},{5,4},{6,5},{7,6},{8,11},{9,8},{10,9... | collective-permute-start | bytes 442376 | tf_op jit(solution)/shard_map/ppermute | solution.py:46
  24.7 9.0 %collective-permute-start.6 = (bf16[384,384]{1,0:T(8,128)(2,1)S(1)}, bf16[384,384]{1,0:T(8,128)(2,1)S(1)}, u32[]{:S(2)}, u32[]{:S(2)}) collective-permute-start(bf16[384,384]{1,0:T(8,128)(2,1)S(1)} %collective-permute-done.3.refs_3_), channel_id=1, source_target_pairs={{0,1},{1,2},{2,3},{3,0},{4,5},{5,6},{6,7},{7,4},{8,9},{9,10},{10,1... | collective-permute-start | bytes 884744 | tf_op jit(solution)/shard_map/ppermute | solution.py:46
  25.3 10.5 %collective-permute-start.7 = (bf16[384,384]{1,0:T(8,128)(2,1)S(1)}, bf16[384,384]{1,0:T(8,128)(2,1)S(1)}, u32[]{:S(2)}, u32[]{:S(2)}) collective-permute-start(bf16[384,384]{1,0:T(8,128)(2,1)S(1)} %collective-permute-done.3.refs_3_), channel_id=1, source_target_pairs={{0,3},{1,0},{2,1},{3,2},{4,7},{5,4},{6,5},{7,6},{8,11},{9,8},{10,9... | collective-permute-start | bytes 884744 | tf_op jit(solution)/shard_map/ppermute | solution.py:46
  27.4 8.4 %collective-permute-start.14 = (bf16[192,768]{1,0:T(8,128)(2,1)S(1)}, bf16[192,768]{1,0:T(8,128)(2,1)S(1)}, u32[]{:S(2)}, u32[]{:S(2)}) collective-permute-start(bf16[192,768]{1,0:T(8,128)(2,1)S(1)} %collective-permute-done.12.refs_13_), channel_id=1, source_target_pairs={{0,32},{1,33},{2,34},{3,35},{4,36},{5,37},{6,38},{7,39},{8,232},{9... | collective-permute-start | bytes 884744 | tf_op jit(solution)/shard_map/ppermute | solution.py:46
  29.9 9.1 %collective-permute-start.15 = (bf16[192,768]{1,0:T(8,128)(2,1)S(1)}, bf16[192,768]{1,0:T(8,128)(2,1)S(1)}, u32[]{:S(2)}, u32[]{:S(2)}) collective-permute-start(bf16[192,768]{1,0:T(8,128)(2,1)S(1)} %collective-permute-done.13.refs_14_), channel_id=1, source_target_pairs={{0,32},{1,33},{2,34},{3,35},{4,36},{5,37},{6,38},{7,39},{8,232},{9... | collective-permute-start | bytes 884744 | tf_op jit(solution)/shard_map/ppermute | solution.py:46
  31.4 10.6 %collective-permute-start.8 = (bf16[384,384]{1,0:T(8,128)(2,1)S(1)}, bf16[384,384]{1,0:T(8,128)(2,1)S(1)}, u32[]{:S(2)}, u32[]{:S(2)}) collective-permute-start(bf16[384,384]{1,0:T(8,128)(2,1)S(1)} %pad_maximum_fusion.6), channel_id=1, source_target_pairs={{0,4},{1,5},{2,6},{3,7},{4,0},{5,1},{6,2},{7,3},{8,12},{9,13},{10,... | collective-permute-start | bytes 884744 | tf_op jit(solution)/shard_map/ppermute | solution.py:46
  33.7 12.8 %collective-permute-start.17 = (bf16[384,768]{1,0:T(8,128)(2,1)S(1)}, bf16[384,768]{1,0:T(8,128)(2,1)S(1)}, u32[]{:S(2)}, u32[]{:S(2)}) collective-permute-start(bf16[384,768]{1,0:T(8,128)(2,1)S(1)} %pad_maximum_fusion), channel_id=1, source_target_pairs={{0,8},{1,9},{2,10},{3,11},{4,12},{5,13},{6,14},{7,15},{8,0},{9,1},... | collective-permute-start | bytes 1769480 | tf_op jit(solution)/shard_map/ppermute | solution.py:46
  35.8 7.8 %collective-permute-start.16 = (bf16[192,768]{1,0:T(8,128)(2,1)S(1)}, bf16[192,768]{1,0:T(8,128)(2,1)S(1)}, u32[]{:S(2)}, u32[]{:S(2)}) collective-permute-start(bf16[192,768]{1,0:T(8,128)(2,1)S(1)} %collective-permute-done.14.refs_15_), channel_id=1, source_target_pairs={{0,32},{1,33},{2,34},{3,35},{4,36},{5,37},{6,38},{7,39},{8,232},{9... | collective-permute-start | bytes 884744 | tf_op jit(solution)/shard_map/ppermute | solution.py:46
  38.9 8.8 %collective-permute-start.18 = (bf16[384,768]{1,0:T(8,128)(2,1)S(1)}, bf16[384,768]{1,0:T(8,128)(2,1)S(1)}, u32[]{:S(2)}, u32[]{:S(2)}) collective-permute-start(bf16[384,768]{1,0:T(8,128)(2,1)S(1)} %pad_maximum_fusion.1), channel_id=1, source_target_pairs={{0,8},{1,9},{2,10},{3,11},{4,12},{5,13},{6,14},{7,15},{8,0},{9,1},... | collective-permute-start | bytes 1769480 | tf_op jit(solution)/shard_map/ppermute | solution.py:46
  39.1 8.7 %collective-permute-start.19 = (bf16[384,768]{1,0:T(8,128)(2,1)S(1)}, bf16[384,768]{1,0:T(8,128)(2,1)S(1)}, u32[]{:S(2)}, u32[]{:S(2)}) collective-permute-start(bf16[384,768]{1,0:T(8,128)(2,1)S(1)} %pad_maximum_fusion.2), channel_id=1, source_target_pairs={{0,8},{1,9},{2,10},{3,11},{4,12},{5,13},{6,14},{7,15},{8,0},{9,1},... | collective-permute-start | bytes 1769480 | tf_op jit(solution)/shard_map/ppermute | solution.py:46
  43.6 4.2 %collective-permute-start.20 = (bf16[192,768]{1,0:T(8,128)(2,1)S(1)}, bf16[192,768]{1,0:T(8,128)(2,1)S(1)}, u32[]{:S(2)}, u32[]{:S(2)}) collective-permute-start(bf16[192,768]{1,0:T(8,128)(2,1)S(1)} %collective-permute-done.16.a4), channel_id=1, source_target_pairs={{0,8},{1,9},{2,10},{3,11},{4,12},{5,13},{6,14},{7,15},{8,0},{9,1},... | collective-permute-start | bytes 884744 | tf_op jit(solution)/shard_map/ppermute | solution.py:46
  47.8 2.4 %copy-start.2 = (s32[48,48]{1,0:T(8,128)S(1)}, s32[48,48]{1,0:T(8,128)}, u32[]{:S(2)}) copy-start(s32[48,48]{1,0:T(8,128)} %pattern.3) | copy-start | bytes 27652
  47.8 2.4 %copy-start.3 = (s32[48,48]{1,0:T(8,128)S(1)}, s32[48,48]{1,0:T(8,128)}, u32[]{:S(2)}) copy-start(s32[48,48]{1,0:T(8,128)} %keep.1) | copy-start | bytes 27652
  48.8 8.3 %collective-permute-start.21 = (bf16[192,768]{1,0:T(8,128)(2,1)S(1)}, bf16[192,768]{1,0:T(8,128)(2,1)S(1)}, u32[]{:S(2)}, u32[]{:S(2)}) collective-permute-start(bf16[192,768]{1,0:T(8,128)(2,1)S(1)} %shard_map.41), channel_id=1, source_target_pairs={{0,16},{1,17},{2,18},{3,19},{4,20},{5,21},{6,22},{7,23},{8,24},{9,... | collective-permute-start | bytes 884744 | tf_op jit(solution)/shard_map/ppermute | solution.py:46
  57.3 2.5 %collective-permute-start.22 = (bf16[192,768]{1,0:T(8,128)(2,1)S(1)}, bf16[192,768]{1,0:T(8,128)(2,1)S(1)}, u32[]{:S(2)}, u32[]{:S(2)}) collective-permute-start(bf16[192,768]{1,0:T(8,128)(2,1)S(1)} %subtract_convert_fusion.refs_1_), channel_id=1, source_target_pairs={{0,8},{1,9},{2,10},{3,11},{4,12},{5,13},{6,14},{7,15},{8,0},{9,1},... | collective-permute-start | bytes 884744 | tf_op jit(solution)/shard_map/ppermute | solution.py:46
  58.6 5.9 %collective-permute-start.23 = (bf16[192,768]{1,0:T(8,128)(2,1)S(1)}, bf16[192,768]{1,0:T(8,128)(2,1)S(1)}, u32[]{:S(2)}, u32[]{:S(2)}) collective-permute-start(bf16[192,768]{1,0:T(8,128)(2,1)S(1)} %subtract_convert_fusion.refs_1_), channel_id=1, source_target_pairs={{0,32},{1,33},{2,34},{3,35},{4,36},{5,37},{6,38},{7,39},{8,232},{9... | collective-permute-start | bytes 884744 | tf_op jit(solution)/shard_map/ppermute | solution.py:46
  59.8 7.8 %collective-permute-start.24 = (bf16[192,768]{1,0:T(8,128)(2,1)S(1)}, bf16[192,768]{1,0:T(8,128)(2,1)S(1)}, u32[]{:S(2)}, u32[]{:S(2)}) collective-permute-start(bf16[192,768]{1,0:T(8,128)(2,1)S(1)} %collective-permute-done.22.refs_2_), channel_id=1, source_target_pairs={{0,32},{1,33},{2,34},{3,35},{4,36},{5,37},{6,38},{7,39},{8,232},{9... | collective-permute-start | bytes 884744 | tf_op jit(solution)/shard_map/ppermute | solution.py:46
  64.4 6.0 %collective-permute-start.25 = (bf16[192,768]{1,0:T(8,128)(2,1)S(1)}, bf16[192,768]{1,0:T(8,128)(2,1)S(1)}, u32[]{:S(2)}, u32[]{:S(2)}) collective-permute-start(bf16[192,768]{1,0:T(8,128)(2,1)S(1)} %collective-permute-done.23.refs_3_), channel_id=1, source_target_pairs={{0,32},{1,33},{2,34},{3,35},{4,36},{5,37},{6,38},{7,39},{8,232},{9... | collective-permute-start | bytes 884744 | tf_op jit(solution)/shard_map/ppermute | solution.py:46
  67.6 6.3 %collective-permute-start.26 = (bf16[192,768]{1,0:T(8,128)(2,1)S(1)}, bf16[192,768]{1,0:T(8,128)(2,1)S(1)}, u32[]{:S(2)}, u32[]{:S(2)}) collective-permute-start(bf16[192,768]{1,0:T(8,128)(2,1)S(1)} %collective-permute-done.24.refs_4_), channel_id=1, source_target_pairs={{0,32},{1,33},{2,34},{3,35},{4,36},{5,37},{6,38},{7,39},{8,232},{9... | collective-permute-start | bytes 884744 | tf_op jit(solution)/shard_map/ppermute | solution.py:46
  70.5 7.4 %collective-permute-start.27 = (bf16[192,768]{1,0:T(8,128)(2,1)S(1)}, bf16[192,768]{1,0:T(8,128)(2,1)S(1)}, u32[]{:S(2)}, u32[]{:S(2)}) collective-permute-start(bf16[192,768]{1,0:T(8,128)(2,1)S(1)} %collective-permute-done.25.refs_5_), channel_id=1, source_target_pairs={{0,32},{1,33},{2,34},{3,35},{4,36},{5,37},{6,38},{7,39},{8,232},{9... | collective-permute-start | bytes 884744 | tf_op jit(solution)/shard_map/ppermute | solution.py:46
  73.9 8.7 %collective-permute-start.28 = (bf16[192,768]{1,0:T(8,128)(2,1)S(1)}, bf16[192,768]{1,0:T(8,128)(2,1)S(1)}, u32[]{:S(2)}, u32[]{:S(2)}) collective-permute-start(bf16[192,768]{1,0:T(8,128)(2,1)S(1)} %collective-permute-done.26.refs_6_), channel_id=1, source_target_pairs={{0,32},{1,33},{2,34},{3,35},{4,36},{5,37},{6,38},{7,39},{8,232},{9... | collective-permute-start | bytes 884744 | tf_op jit(solution)/shard_map/ppermute | solution.py:46
  75.9 14.5 %collective-permute-start.30 = (bf16[384,768]{1,0:T(8,128)(2,1)S(1)}, bf16[384,768]{1,0:T(8,128)(2,1)S(1)}, u32[]{:S(2)}, u32[]{:S(2)}) collective-permute-start(bf16[384,768]{1,0:T(8,128)(2,1)S(1)} %pad_maximum_fusion.3), channel_id=1, source_target_pairs={{0,8},{1,9},{2,10},{3,11},{4,12},{5,13},{6,14},{7,15},{8,0},{9,1},... | collective-permute-start | bytes 1769480 | tf_op jit(solution)/shard_map/ppermute | solution.py:46
  77.8 9.4 %collective-permute-start.29 = (bf16[192,768]{1,0:T(8,128)(2,1)S(1)}, bf16[192,768]{1,0:T(8,128)(2,1)S(1)}, u32[]{:S(2)}, u32[]{:S(2)}) collective-permute-start(bf16[192,768]{1,0:T(8,128)(2,1)S(1)} %collective-permute-done.27.refs_7_), channel_id=1, source_target_pairs={{0,32},{1,33},{2,34},{3,35},{4,36},{5,37},{6,38},{7,39},{8,232},{9... | collective-permute-start | bytes 884744 | tf_op jit(solution)/shard_map/ppermute | solution.py:46
  80.8 9.6 %collective-permute-start.31 = (bf16[384,768]{1,0:T(8,128)(2,1)S(1)}, bf16[384,768]{1,0:T(8,128)(2,1)S(1)}, u32[]{:S(2)}, u32[]{:S(2)}) collective-permute-start(bf16[384,768]{1,0:T(8,128)(2,1)S(1)} %pad_maximum_fusion.4), channel_id=1, source_target_pairs={{0,8},{1,9},{2,10},{3,11},{4,12},{5,13},{6,14},{7,15},{8,0},{9,1},... | collective-permute-start | bytes 1769480 | tf_op jit(solution)/shard_map/ppermute | solution.py:46
  82.6 9.0 %collective-permute-start.32 = (bf16[384,768]{1,0:T(8,128)(2,1)S(1)}, bf16[384,768]{1,0:T(8,128)(2,1)S(1)}, u32[]{:S(2)}, u32[]{:S(2)}) collective-permute-start(bf16[384,768]{1,0:T(8,128)(2,1)S(1)} %pad_maximum_fusion.5), channel_id=1, source_target_pairs={{0,8},{1,9},{2,10},{3,11},{4,12},{5,13},{6,14},{7,15},{8,0},{9,1},... | collective-permute-start | bytes 1769480 | tf_op jit(solution)/shard_map/ppermute | solution.py:46
  87.3 4.3 %collective-permute-start.33 = (bf16[192,768]{1,0:T(8,128)(2,1)S(1)}, bf16[192,768]{1,0:T(8,128)(2,1)S(1)}, u32[]{:S(2)}, u32[]{:S(2)}) collective-permute-start(bf16[192,768]{1,0:T(8,128)(2,1)S(1)} %collective-permute-done.29.a4), channel_id=1, source_target_pairs={{0,8},{1,9},{2,10},{3,11},{4,12},{5,13},{6,14},{7,15},{8,0},{9,1},... | collective-permute-start | bytes 884744 | tf_op jit(solution)/shard_map/ppermute | solution.py:46
  92.6 8.3 %collective-permute-start.34 = (bf16[192,768]{1,0:T(8,128)(2,1)S(1)}, bf16[192,768]{1,0:T(8,128)(2,1)S(1)}, u32[]{:S(2)}, u32[]{:S(2)}) collective-permute-start(bf16[192,768]{1,0:T(8,128)(2,1)S(1)} %shard_map.44), channel_id=1, source_target_pairs={{0,16},{1,17},{2,18},{3,19},{4,20},{5,21},{6,22},{7,23},{8,24},{9,... | collective-permute-start | bytes 884744 | tf_op jit(solution)/shard_map/ppermute | solution.py:46

commit v4 on v3

--- a/solution.py
+++ b/solution.py
@@ -229,10 +229,14 @@
     return kept + theirs.astype(F32)
 
 
+def in_hbm(value):
+    return pltpu.with_memory_space_constraint(value, pltpu.HBM)
+
+
 def shards(matrix, pattern, keep):
     x, kept, away = call(
         mask_kernel,
-        [pattern, matrix],
+        [in_hbm(pattern), in_hbm(matrix)],
         [struct(ROWS, COLS), struct(ROWS, HALF), struct(ROWS, HALF)],
         [pltpu.SMEM((48, 48), jnp.int32), pltpu.VMEM((ROWS, COLS), BF16), pltpu.SemaphoreType.DMA((2,))],
         0,

time: 102 us -> 100 us (0.980)
  local copies, waits for them, and re-layouts: 1.78 us -> 0.08 us
    unnamed x9 -> x5, local copies, waits for them, and re-layouts: 1.72 us -> 0.02 us
where the time goes in v4:
time: 100 us
  starting transfers between devices  66.8 us (67%)
  waiting for transfers between devices  22 us (22%)
  Pallas kernels  9.91 us (10%)
  other arithmetic  1.18 us (1%)
    ppermute x35, starting transfers between devices, send(): return lax.ppermute(value, AXES, pairs)  66.8 us
    ppermute x35, waiting for transfers between devices, send(): return lax.ppermute(value, AXES, pairs)  22 us
    pallas_call x8, Pallas kernels, call(): pl.pallas_call(kernel, in_specs=specs or [SMEM if arg.dtype == jnp.int32...  9.91 us
  transfers between devices with their start and end apart: 35, of which 9 were waited for; matrix products, arithmetic and copies ran while one was open for 0% of the time, Pallas kernels for 7%

profile of v4, /device:TPU:1, one launch (start us, length us, event | category | flops | bytes accessed | tf_op | source)
XLA Modules:
  0.0 100.1 jit_solution(17616739825659970049)
XLA Ops:
  0.0 1.2 %shard_map.37 = (bf16[192,768]{1,0:T(8,128)(2,1)S(1)}, bf16[192,384]{1,0:T(8,128)(2,1)S(1)}, bf16[192,384]{1,0:T(8,128)(2,1)S(1)}) custom-call(s32[48,48]{1,0:T(8,128)} %pattern.3, bf16[192,768]{1,0:T(8,128)(2,1)} %matrix.1), custom_call_target="tpu_custom_call" | custom-call | tf_op jit(solution)/shard_map/pallas_call | solution.py:181
  1.2 3.3 %collective-permute-start.9 = (bf16[192,768]{1,0:T(8,128)(2,1)S(1)}, bf16[192,768]{1,0:T(8,128)(2,1)S(1)}, u32[]{:S(2)}, u32[]{:S(2)}) collective-permute-start(bf16[192,768]{1,0:T(8,128)(2,1)S(1)} %get-tuple-element.21.refs_9_), channel_id=1, source_target_pairs={{0,8},{1,9},{2,10},{3,11},{4,12},{5,13},{6,14},{7,15},{8,0},{9,1},... | collective-permute-start | bytes 884744 | tf_op jit(solution)/shard_map/ppermute | solution.py:46
  4.6 0.0 collective-permute-start
  4.6 5.2 %collective-permute-start.10 = (bf16[192,768]{1,0:T(8,128)(2,1)S(1)}, bf16[192,768]{1,0:T(8,128)(2,1)S(1)}, u32[]{:S(2)}, u32[]{:S(2)}) collective-permute-start(bf16[192,768]{1,0:T(8,128)(2,1)S(1)} %get-tuple-element.21.refs_9_), channel_id=1, source_target_pairs={{0,32},{1,33},{2,34},{3,35},{4,36},{5,37},{6,38},{7,39},{8,232},{9... | collective-permute-start | bytes 884744 | tf_op jit(solution)/shard_map/ppermute | solution.py:46
  9.7 0.8 collective-permute-start.11
  10.5 0.0 collective-permute-done
  10.6 1.3 %collective-permute-start.1 = (bf16[384,384]{1,0:T(8,128)(2,1)S(1)}, bf16[384,384]{1,0:T(8,128)(2,1)S(1)}, u32[]{:S(2)}, u32[]{:S(2)}) collective-permute-start(bf16[384,384]{1,0:T(8,128)(2,1)S(1)} %constant_dynamic-update-slice_fusion.refs_0_), channel_id=1, source_target_pairs={{0,1},{1,2},{2,3},{3,0},{4,5},{5,6},{6,7},{7,4},{8,9},{9,10},{10,1... | collective-permute-start | bytes 884744 | tf_op jit(solution)/shard_map/ppermute | solution.py:46
  11.9 1.5 %collective-permute-start.2 = (bf16[384,384]{1,0:T(8,128)(2,1)S(1)}, bf16[384,384]{1,0:T(8,128)(2,1)S(1)}, u32[]{:S(2)}, u32[]{:S(2)}) collective-permute-start(bf16[384,384]{1,0:T(8,128)(2,1)S(1)} %constant_dynamic-update-slice_fusion.refs_0_), channel_id=1, source_target_pairs={{0,3},{1,0},{2,1},{3,2},{4,7},{5,4},{6,5},{7,6},{8,11},{9,8},{10,9... | collective-permute-start | bytes 884744 | tf_op jit(solution)/shard_map/ppermute | solution.py:46
  13.3 2.6 %collective-permute-start.3 = (bf16[384,384]{1,0:T(8,128)(2,1)S(1)}, bf16[384,384]{1,0:T(8,128)(2,1)S(1)}, u32[]{:S(2)}, u32[]{:S(2)}) collective-permute-start(bf16[384,384]{1,0:T(8,128)(2,1)S(1)} %constant_dynamic-update-slice_fusion.refs_0_), channel_id=1, source_target_pairs={{0,4},{1,5},{2,6},{3,7},{4,0},{5,1},{6,2},{7,3},{8,12},{9,13},{10,... | collective-permute-start | bytes 884744 | tf_op jit(solution)/shard_map/ppermute | solution.py:46
  16.0 0.0 collective-permute-done.10.refs_11_
  16.0 3.5 %collective-permute-start.12 = (bf16[192,768]{1,0:T(8,128)(2,1)S(1)}, bf16[192,768]{1,0:T(8,128)(2,1)S(1)}, u32[]{:S(2)}, u32[]{:S(2)}) collective-permute-start(bf16[192,768]{1,0:T(8,128)(2,1)S(1)} %collective-permute-done.10.refs_11_), channel_id=1, source_target_pairs={{0,32},{1,33},{2,34},{3,35},{4,36},{5,37},{6,38},{7,39},{8,232},{9... | collective-permute-start | bytes 884744 | tf_op jit(solution)/shard_map/ppermute | solution.py:46
  19.5 0.7 collective-permute-start.13
  20.3 0.7 collective-permute-start.4
  21.0 0.0 collective-permute-done.2.refs_2_
  21.0 2.1 %collective-permute-start.5 = (bf16[192,384]{1,0:T(8,128)(2,1)S(1)}, bf16[192,384]{1,0:T(8,128)(2,1)S(1)}, u32[]{:S(2)}, u32[]{:S(2)}) collective-permute-start(bf16[192,384]{1,0:T(8,128)(2,1)S(1)} %slice.9), channel_id=1, source_target_pairs={{0,3},{1,0},{2,1},{3,2},{4,7},{5,4},{6,5},{7,6},{8,11},{9,8},{10,9... | collective-permute-start | bytes 442376 | tf_op jit(solution)/shard_map/ppermute | solution.py:46
  23.1 0.6 collective-permute-start.6
  23.7 2.1 %collective-permute-start.7 = (bf16[384,384]{1,0:T(8,128)(2,1)S(1)}, bf16[384,384]{1,0:T(8,128)(2,1)S(1)}, u32[]{:S(2)}, u32[]{:S(2)}) collective-permute-start(bf16[384,384]{1,0:T(8,128)(2,1)S(1)} %collective-permute-done.3.refs_3_), channel_id=1, source_target_pairs={{0,3},{1,0},{2,1},{3,2},{4,7},{5,4},{6,5},{7,6},{8,11},{9,8},{10,9... | collective-permute-start | bytes 884744 | tf_op jit(solution)/shard_map/ppermute | solution.py:46
  25.8 0.0 collective-permute-done.4.refs_4_
  25.8 2.5 %collective-permute-start.14 = (bf16[192,768]{1,0:T(8,128)(2,1)S(1)}, bf16[192,768]{1,0:T(8,128)(2,1)S(1)}, u32[]{:S(2)}, u32[]{:S(2)}) collective-permute-start(bf16[192,768]{1,0:T(8,128)(2,1)S(1)} %collective-permute-done.12.refs_13_), channel_id=1, source_target_pairs={{0,32},{1,33},{2,34},{3,35},{4,36},{5,37},{6,38},{7,39},{8,232},{9... | collective-permute-start | bytes 884744 | tf_op jit(solution)/shard_map/ppermute | solution.py:46
  28.3 0.0 collective-permute-done.5.refs_5_
  28.3 0.0 collective-permute-done.13.refs_14_
  28.3 1.4 %collective-permute-start.15 = (bf16[192,768]{1,0:T(8,128)(2,1)S(1)}, bf16[192,768]{1,0:T(8,128)(2,1)S(1)}, u32[]{:S(2)}, u32[]{:S(2)}) collective-permute-start(bf16[192,768]{1,0:T(8,128)(2,1)S(1)} %collective-permute-done.13.refs_14_), channel_id=1, source_target_pairs={{0,32},{1,33},{2,34},{3,35},{4,36},{5,37},{6,38},{7,39},{8,232},{9... | collective-permute-start | bytes 884744 | tf_op jit(solution)/shard_map/ppermute | solution.py:46
  29.8 2.3 %collective-permute-start.8 = (bf16[384,384]{1,0:T(8,128)(2,1)S(1)}, bf16[384,384]{1,0:T(8,128)(2,1)S(1)}, u32[]{:S(2)}, u32[]{:S(2)}) collective-permute-start(bf16[384,384]{1,0:T(8,128)(2,1)S(1)} %pad_maximum_fusion.6), channel_id=1, source_target_pairs={{0,4},{1,5},{2,6},{3,7},{4,0},{5,1},{6,2},{7,3},{8,12},{9,13},{10,... | collective-permute-start | bytes 884744 | tf_op jit(solution)/shard_map/ppermute | solution.py:46
  32.2 2.0 %collective-permute-start.17 = (bf16[384,768]{1,0:T(8,128)(2,1)S(1)}, bf16[384,768]{1,0:T(8,128)(2,1)S(1)}, u32[]{:S(2)}, u32[]{:S(2)}) collective-permute-start(bf16[384,768]{1,0:T(8,128)(2,1)S(1)} %pad_maximum_fusion), channel_id=1, source_target_pairs={{0,8},{1,9},{2,10},{3,11},{4,12},{5,13},{6,14},{7,15},{8,0},{9,1},... | collective-permute-start | bytes 1769480 | tf_op jit(solution)/shard_map/ppermute | solution.py:46
  34.2 0.0 collective-permute-done.7.refs_7_
  34.2 0.0 collective-permute-done.14.refs_15_
  34.2 3.1 %collective-permute-start.16 = (bf16[192,768]{1,0:T(8,128)(2,1)S(1)}, bf16[192,768]{1,0:T(8,128)(2,1)S(1)}, u32[]{:S(2)}, u32[]{:S(2)}) collective-permute-start(bf16[192,768]{1,0:T(8,128)(2,1)S(1)} %collective-permute-done.14.refs_15_), channel_id=1, source_target_pairs={{0,32},{1,33},{2,34},{3,35},{4,36},{5,37},{6,38},{7,39},{8,232},{9... | collective-permute-start | bytes 884744 | tf_op jit(solution)/shard_map/ppermute | solution.py:46
  37.4 0.1 collective-permute-start.18
  37.5 0.0 collective-permute-done.15.refs_16_
  37.5 2.8 %collective-permute-start.19 = (bf16[384,768]{1,0:T(8,128)(2,1)S(1)}, bf16[384,768]{1,0:T(8,128)(2,1)S(1)}, u32[]{:S(2)}, u32[]{:S(2)}) collective-permute-start(bf16[384,768]{1,0:T(8,128)(2,1)S(1)} %pad_maximum_fusion.2), channel_id=1, source_target_pairs={{0,8},{1,9},{2,10},{3,11},{4,12},{5,13},{6,14},{7,15},{8,0},{9,1},... | collective-permute-start | bytes 1769480 | tf_op jit(solution)/shard_map/ppermute | solution.py:46
  40.4 0.0 collective-permute-done.8.refs_8_
  40.4 1.7 %shard_map.38 = (f32[384,768]{1,0:T(8,128)S(1)}, bf16[8,384,384]{2,1,0:T(8,128)(2,1)S(1)}) custom-call(bf16[384,384]{1,0:T(8,128)(2,1)S(1)} %constant_dynamic-update-slice_fusion.refs_0_, bf16[384,384]{1,0:T(8,128)(2,1)S(1)} %collective-permute-done.1.refs_1_, bf16[384,384]{1,0:T(8,128)(2,1)S(1)} %collective-permute-done.2.refs_2_, ...), custom_call_target="tpu_custom_call" | custom-call | flops 905969664 | tf_op jit(solution)/shard_map/pallas_call | solution.py:181
  42.0 3.0 %collective-permute-start.20 = (bf16[192,768]{1,0:T(8,128)(2,1)S(1)}, bf16[192,768]{1,0:T(8,128)(2,1)S(1)}, u32[]{:S(2)}, u32[]{:S(2)}) collective-permute-start(bf16[192,768]{1,0:T(8,128)(2,1)S(1)} %collective-permute-done.16.a4), channel_id=1, source_target_pairs={{0,8},{1,9},{2,10},{3,11},{4,12},{5,13},{6,14},{7,15},{8,0},{9,1},... | collective-permute-start | bytes 884744 | tf_op jit(solution)/shard_map/ppermute | solution.py:46
  45.0 1.2 %collective-permute-done.20.s4 = bf16[192,768]{1,0:T(8,128)(2,1)S(1)} collective-permute-done((bf16[192,768]{1,0:T(8,128)(2,1)S(1)}, bf16[192,768]{1,0:T(8,128)(2,1)S(1)}, u32[]{:S(2)}, u32[]{:S(2)}) %collective-permute-start.20) | collective-permute-done | bytes 294944 | tf_op jit(solution)/shard_map/ppermute | solution.py:46
  46.2 1.0 %shard_map.41 = bf16[192,768]{1,0:T(8,128)(2,1)S(1)} custom-call(bf16[8,384,384]{2,1,0:T(8,128)(2,1)S(1)} %get-tuple-element.25.left.refs_0_, f32[384,768]{1,0:T(8,128)S(1)} %get-tuple-element.27.total, bf16[192,768]{1,0:T(8,128)(2,1)S(1)} %collective-permute-done.16.a4, bf16[384,768]{1,0:T(8,128)(2,1)S(1)} %collective-permute-done.17.s1, ...), custom_call_target="tpu_custom_call" | custom-call | flops 452984832 | tf_op jit(solution)/shard_map/pallas_call | solution.py:181
  47.3 1.4 %collective-permute-start.21 = (bf16[192,768]{1,0:T(8,128)(2,1)S(1)}, bf16[192,768]{1,0:T(8,128)(2,1)S(1)}, u32[]{:S(2)}, u32[]{:S(2)}) collective-permute-start(bf16[192,768]{1,0:T(8,128)(2,1)S(1)} %shard_map.41), channel_id=1, source_target_pairs={{0,16},{1,17},{2,18},{3,19},{4,20},{5,21},{6,22},{7,23},{8,24},{9,... | collective-permute-start | bytes 884744 | tf_op jit(solution)/shard_map/ppermute | solution.py:46
  48.6 1.5 %shard_map.39 = (f32[192,768]{1,0:T(8,128)S(1)}, f32[192,768]{1,0:T(8,128)S(1)}, f32[192,768]{1,0:T(8,128)S(1)}) custom-call(s32[48,48]{1,0:T(8,128)S(1)} %copy-done, s32[48,48]{1,0:T(8,128)S(1)} %copy-done.1), custom_call_target="tpu_custom_call" | custom-call | flops 147456 | tf_op jit(solution)/shard_map/pallas_call | solution.py:181
  50.1 1.0 %shard_map.40 = f32[192,768]{1,0:T(8,128)S(1)} custom-call(bf16[8,384,384]{2,1,0:T(8,128)(2,1)S(1)} %get-tuple-element.25.left.refs_0_, f32[384,768]{1,0:T(8,128)S(1)} %get-tuple-element.27.total, bf16[192,768]{1,0:T(8,128)(2,1)S(1)} %collective-permute-done.16.a4, bf16[384,768]{1,0:T(8,128)(2,1)S(1)} %collective-permute-done.17.s1, ...), custom_call_target="tpu_custom_call" | custom-call | flops 452984832 | tf_op jit(solution)/shard_map/pallas_call | solution.py:181
  51.2 4.4 %collective-permute-done.21 = bf16[192,768]{1,0:T(8,128)(2,1)S(1)} collective-permute-done((bf16[192,768]{1,0:T(8,128)(2,1)S(1)}, bf16[192,768]{1,0:T(8,128)(2,1)S(1)}, u32[]{:S(2)}, u32[]{:S(2)}) %collective-permute-start.21) | collective-permute-done | bytes 294944 | tf_op jit(solution)/shard_map/ppermute | solution.py:46
  55.5 0.1 subtract_convert_fusion.refs_1_
  55.7 1.3 %collective-permute-start.22 = (bf16[192,768]{1,0:T(8,128)(2,1)S(1)}, bf16[192,768]{1,0:T(8,128)(2,1)S(1)}, u32[]{:S(2)}, u32[]{:S(2)}) collective-permute-start(bf16[192,768]{1,0:T(8,128)(2,1)S(1)} %subtract_convert_fusion.refs_1_), channel_id=1, source_target_pairs={{0,8},{1,9},{2,10},{3,11},{4,12},{5,13},{6,14},{7,15},{8,0},{9,1},... | collective-permute-start | bytes 884744 | tf_op jit(solution)/shard_map/ppermute | solution.py:46
  57.0 0.5 collective-permute-start.23
  57.5 0.7 collective-permute-done.22.refs_2_
  58.2 0.5 collective-permute-start.24
  58.7 4.1 %collective-permute-done.23.refs_3_ = bf16[192,768]{1,0:T(8,128)(2,1)S(1)} collective-permute-done((bf16[192,768]{1,0:T(8,128)(2,1)S(1)}, bf16[192,768]{1,0:T(8,128)(2,1)S(1)}, u32[]{:S(2)}, u32[]{:S(2)}) %collective-permute-start.23) | collective-permute-done | bytes 294944 | tf_op jit(solution)/shard_map/ppermute | solution.py:46
  62.9 1.4 %collective-permute-start.25 = (bf16[192,768]{1,0:T(8,128)(2,1)S(1)}, bf16[192,768]{1,0:T(8,128)(2,1)S(1)}, u32[]{:S(2)}, u32[]{:S(2)}) collective-permute-start(bf16[192,768]{1,0:T(8,128)(2,1)S(1)} %collective-permute-done.23.refs_3_), channel_id=1, source_target_pairs={{0,32},{1,33},{2,34},{3,35},{4,36},{5,37},{6,38},{7,39},{8,232},{9... | collective-permute-start | bytes 884744 | tf_op jit(solution)/shard_map/ppermute | solution.py:46
  64.3 1.7 %collective-permute-done.24.refs_4_ = bf16[192,768]{1,0:T(8,128)(2,1)S(1)} collective-permute-done((bf16[192,768]{1,0:T(8,128)(2,1)S(1)}, bf16[192,768]{1,0:T(8,128)(2,1)S(1)}, u32[]{:S(2)}, u32[]{:S(2)}) %collective-permute-start.24) | collective-permute-done | bytes 294944 | tf_op jit(solution)/shard_map/ppermute | solution.py:46
  66.0 1.4 %collective-permute-start.26 = (bf16[192,768]{1,0:T(8,128)(2,1)S(1)}, bf16[192,768]{1,0:T(8,128)(2,1)S(1)}, u32[]{:S(2)}, u32[]{:S(2)}) collective-permute-start(bf16[192,768]{1,0:T(8,128)(2,1)S(1)} %collective-permute-done.24.refs_4_), channel_id=1, source_target_pairs={{0,32},{1,33},{2,34},{3,35},{4,36},{5,37},{6,38},{7,39},{8,232},{9... | collective-permute-start | bytes 884744 | tf_op jit(solution)/shard_map/ppermute | solution.py:46
  67.5 1.4 %collective-permute-done.25.refs_5_ = bf16[192,768]{1,0:T(8,128)(2,1)S(1)} collective-permute-done((bf16[192,768]{1,0:T(8,128)(2,1)S(1)}, bf16[192,768]{1,0:T(8,128)(2,1)S(1)}, u32[]{:S(2)}, u32[]{:S(2)}) %collective-permute-start.25) | collective-permute-done | bytes 294944 | tf_op jit(solution)/shard_map/ppermute | solution.py:46
  68.9 2.2 %collective-permute-start.27 = (bf16[192,768]{1,0:T(8,128)(2,1)S(1)}, bf16[192,768]{1,0:T(8,128)(2,1)S(1)}, u32[]{:S(2)}, u32[]{:S(2)}) collective-permute-start(bf16[192,768]{1,0:T(8,128)(2,1)S(1)} %collective-permute-done.25.refs_5_), channel_id=1, source_target_pairs={{0,32},{1,33},{2,34},{3,35},{4,36},{5,37},{6,38},{7,39},{8,232},{9... | collective-permute-start | bytes 884744 | tf_op jit(solution)/shard_map/ppermute | solution.py:46
  71.1 1.2 %collective-permute-done.26.refs_6_ = bf16[192,768]{1,0:T(8,128)(2,1)S(1)} collective-permute-done((bf16[192,768]{1,0:T(8,128)(2,1)S(1)}, bf16[192,768]{1,0:T(8,128)(2,1)S(1)}, u32[]{:S(2)}, u32[]{:S(2)}) %collective-permute-start.26) | collective-permute-done | bytes 294944 | tf_op jit(solution)/shard_map/ppermute | solution.py:46
  72.3 1.9 %collective-permute-start.28 = (bf16[192,768]{1,0:T(8,128)(2,1)S(1)}, bf16[192,768]{1,0:T(8,128)(2,1)S(1)}, u32[]{:S(2)}, u32[]{:S(2)}) collective-permute-start(bf16[192,768]{1,0:T(8,128)(2,1)S(1)} %collective-permute-done.26.refs_6_), channel_id=1, source_target_pairs={{0,32},{1,33},{2,34},{3,35},{4,36},{5,37},{6,38},{7,39},{8,232},{9... | collective-permute-start | bytes 884744 | tf_op jit(solution)/shard_map/ppermute | solution.py:46
  74.3 2.0 %collective-permute-start.30 = (bf16[384,768]{1,0:T(8,128)(2,1)S(1)}, bf16[384,768]{1,0:T(8,128)(2,1)S(1)}, u32[]{:S(2)}, u32[]{:S(2)}) collective-permute-start(bf16[384,768]{1,0:T(8,128)(2,1)S(1)} %pad_maximum_fusion.3), channel_id=1, source_target_pairs={{0,8},{1,9},{2,10},{3,11},{4,12},{5,13},{6,14},{7,15},{8,0},{9,1},... | collective-permute-start | bytes 1769480 | tf_op jit(solution)/shard_map/ppermute | solution.py:46
  76.2 3.0 %collective-permute-start.29 = (bf16[192,768]{1,0:T(8,128)(2,1)S(1)}, bf16[192,768]{1,0:T(8,128)(2,1)S(1)}, u32[]{:S(2)}, u32[]{:S(2)}) collective-permute-start(bf16[192,768]{1,0:T(8,128)(2,1)S(1)} %collective-permute-done.27.refs_7_), channel_id=1, source_target_pairs={{0,32},{1,33},{2,34},{3,35},{4,36},{5,37},{6,38},{7,39},{8,232},{9... | collective-permute-start | bytes 884744 | tf_op jit(solution)/shard_map/ppermute | solution.py:46
  79.2 1.8 %collective-permute-start.31 = (bf16[384,768]{1,0:T(8,128)(2,1)S(1)}, bf16[384,768]{1,0:T(8,128)(2,1)S(1)}, u32[]{:S(2)}, u32[]{:S(2)}) collective-permute-start(bf16[384,768]{1,0:T(8,128)(2,1)S(1)} %pad_maximum_fusion.4), channel_id=1, source_target_pairs={{0,8},{1,9},{2,10},{3,11},{4,12},{5,13},{6,14},{7,15},{8,0},{9,1},... | collective-permute-start | bytes 1769480 | tf_op jit(solution)/shard_map/ppermute | solution.py:46
  81.1 3.1 %collective-permute-start.32 = (bf16[384,768]{1,0:T(8,128)(2,1)S(1)}, bf16[384,768]{1,0:T(8,128)(2,1)S(1)}, u32[]{:S(2)}, u32[]{:S(2)}) collective-permute-start(bf16[384,768]{1,0:T(8,128)(2,1)S(1)} %pad_maximum_fusion.5), channel_id=1, source_target_pairs={{0,8},{1,9},{2,10},{3,11},{4,12},{5,13},{6,14},{7,15},{8,0},{9,1},... | collective-permute-start | bytes 1769480 | tf_op jit(solution)/shard_map/ppermute | solution.py:46
  84.2 1.5 %shard_map.42.total = f32[384,768]{1,0:T(8,128)S(1)} custom-call(bf16[8,384,384]{2,1,0:T(8,128)(2,1)S(1)} %get-tuple-element.25.left.refs_0_, bf16[192,768]{1,0:T(8,128)(2,1)S(1)} %subtract_convert_fusion.refs_1_, bf16[192,768]{1,0:T(8,128)(2,1)S(1)} %collective-permute-done.22.refs_2_, bf16[192,768]{1,0:T(8,128)(2,1)S(1)} %collective-permute-done.23.refs_3_, ...), custom_call_target="tpu_custom_call" | custom-call | flops 905969664 | tf_op jit(solution)/shard_map/pallas_call | solution.py:181
  85.7 3.1 %collective-permute-start.33 = (bf16[192,768]{1,0:T(8,128)(2,1)S(1)}, bf16[192,768]{1,0:T(8,128)(2,1)S(1)}, u32[]{:S(2)}, u32[]{:S(2)}) collective-permute-start(bf16[192,768]{1,0:T(8,128)(2,1)S(1)} %collective-permute-done.29.a4), channel_id=1, source_target_pairs={{0,8},{1,9},{2,10},{3,11},{4,12},{5,13},{6,14},{7,15},{8,0},{9,1},... | collective-permute-start | bytes 884744 | tf_op jit(solution)/shard_map/ppermute | solution.py:46
  88.8 1.2 %collective-permute-done.33.s4 = bf16[192,768]{1,0:T(8,128)(2,1)S(1)} collective-permute-done((bf16[192,768]{1,0:T(8,128)(2,1)S(1)}, bf16[192,768]{1,0:T(8,128)(2,1)S(1)}, u32[]{:S(2)}, u32[]{:S(2)}) %collective-permute-start.33) | collective-permute-done | bytes 294944 | tf_op jit(solution)/shard_map/ppermute | solution.py:46
  90.0 1.0 %shard_map.44 = bf16[192,768]{1,0:T(8,128)(2,1)S(1)} custom-call(bf16[8,384,384]{2,1,0:T(8,128)(2,1)S(1)} %get-tuple-element.25.left.refs_0_, f32[384,768]{1,0:T(8,128)S(1)} %shard_map.42.total, bf16[192,768]{1,0:T(8,128)(2,1)S(1)} %collective-permute-done.29.a4, bf16[384,768]{1,0:T(8,128)(2,1)S(1)} %collective-permute-done.30.s1, ...), custom_call_target="tpu_custom_call" | custom-call | flops 452984832 | tf_op jit(solution)/shard_map/pallas_call | solution.py:181
  91.0 1.4 %collective-permute-start.34 = (bf16[192,768]{1,0:T(8,128)(2,1)S(1)}, bf16[192,768]{1,0:T(8,128)(2,1)S(1)}, u32[]{:S(2)}, u32[]{:S(2)}) collective-permute-start(bf16[192,768]{1,0:T(8,128)(2,1)S(1)} %shard_map.44), channel_id=1, source_target_pairs={{0,16},{1,17},{2,18},{3,19},{4,20},{5,21},{6,22},{7,23},{8,24},{9,... | collective-permute-start | bytes 884744 | tf_op jit(solution)/shard_map/ppermute | solution.py:46
  92.4 1.0 %shard_map.43 = f32[192,768]{1,0:T(8,128)S(1)} custom-call(bf16[8,384,384]{2,1,0:T(8,128)(2,1)S(1)} %get-tuple-element.25.left.refs_0_, f32[384,768]{1,0:T(8,128)S(1)} %shard_map.42.total, bf16[192,768]{1,0:T(8,128)(2,1)S(1)} %collective-permute-done.29.a4, bf16[384,768]{1,0:T(8,128)(2,1)S(1)} %collective-permute-done.30.s1, ...), custom_call_target="tpu_custom_call" | custom-call | flops 452984832 | tf_op jit(solution)/shard_map/pallas_call | solution.py:181
  93.5 5.9 %collective-permute-done.34 = bf16[192,768]{1,0:T(8,128)(2,1)S(1)} collective-permute-done((bf16[192,768]{1,0:T(8,128)(2,1)S(1)}, bf16[192,768]{1,0:T(8,128)(2,1)S(1)}, u32[]{:S(2)}, u32[]{:S(2)}) %collective-permute-start.34) | collective-permute-done | bytes 294944 | tf_op jit(solution)/shard_map/ppermute | solution.py:46
  99.4 0.8 multiply_convert_fusion
  (31 shorter events, 0.4 us)
Async XLA Ops:
  1.2 8.5 %collective-permute-start.9 = (bf16[192,768]{1,0:T(8,128)(2,1)S(1)}, bf16[192,768]{1,0:T(8,128)(2,1)S(1)}, u32[]{:S(2)}, u32[]{:S(2)}) collective-permute-start(bf16[192,768]{1,0:T(8,128)(2,1)S(1)} %get-tuple-element.21.refs_9_), channel_id=1, source_target_pairs={{0,8},{1,9},{2,10},{3,11},{4,12},{5,13},{6,14},{7,15},{8,0},{9,1},... | collective-permute-start | bytes 884744 | tf_op jit(solution)/shard_map/ppermute | solution.py:46
  4.6 6.0 %collective-permute-start = (bf16[192,384]{1,0:T(8,128)(2,1)S(1)}, bf16[192,384]{1,0:T(8,128)(2,1)S(1)}, u32[]{:S(2)}, u32[]{:S(2)}) collective-permute-start(bf16[192,384]{1,0:T(8,128)(2,1)S(1)} %get-tuple-element.20), channel_id=1, source_target_pairs={{0,16},{1,17},{2,18},{3,19},{4,20},{5,21},{6,22},{7,23},{8,24},{9,... | collective-permute-start | bytes 442376 | tf_op jit(solution)/shard_map/ppermute | solution.py:46
  4.6 11.4 %collective-permute-start.10 = (bf16[192,768]{1,0:T(8,128)(2,1)S(1)}, bf16[192,768]{1,0:T(8,128)(2,1)S(1)}, u32[]{:S(2)}, u32[]{:S(2)}) collective-permute-start(bf16[192,768]{1,0:T(8,128)(2,1)S(1)} %get-tuple-element.21.refs_9_), channel_id=1, source_target_pairs={{0,32},{1,33},{2,34},{3,35},{4,36},{5,37},{6,38},{7,39},{8,232},{9... | collective-permute-start | bytes 884744 | tf_op jit(solution)/shard_map/ppermute | solution.py:46
  9.7 9.8 %collective-permute-start.11 = (bf16[192,768]{1,0:T(8,128)(2,1)S(1)}, bf16[192,768]{1,0:T(8,128)(2,1)S(1)}, u32[]{:S(2)}, u32[]{:S(2)}) collective-permute-start(bf16[192,768]{1,0:T(8,128)(2,1)S(1)} %collective-permute-done.9.refs_10_), channel_id=1, source_target_pairs={{0,32},{1,33},{2,34},{3,35},{4,36},{5,37},{6,38},{7,39},{8,232},{9... | collective-permute-start | bytes 884744 | tf_op jit(solution)/shard_map/ppermute | solution.py:46
  10.6 9.7 %collective-permute-start.1 = (bf16[384,384]{1,0:T(8,128)(2,1)S(1)}, bf16[384,384]{1,0:T(8,128)(2,1)S(1)}, u32[]{:S(2)}, u32[]{:S(2)}) collective-permute-start(bf16[384,384]{1,0:T(8,128)(2,1)S(1)} %constant_dynamic-update-slice_fusion.refs_0_), channel_id=1, source_target_pairs={{0,1},{1,2},{2,3},{3,0},{4,5},{5,6},{6,7},{7,4},{8,9},{9,10},{10,1... | collective-permute-start | bytes 884744 | tf_op jit(solution)/shard_map/ppermute | solution.py:46
  11.9 9.1 %collective-permute-start.2 = (bf16[384,384]{1,0:T(8,128)(2,1)S(1)}, bf16[384,384]{1,0:T(8,128)(2,1)S(1)}, u32[]{:S(2)}, u32[]{:S(2)}) collective-permute-start(bf16[384,384]{1,0:T(8,128)(2,1)S(1)} %constant_dynamic-update-slice_fusion.refs_0_), channel_id=1, source_target_pairs={{0,3},{1,0},{2,1},{3,2},{4,7},{5,4},{6,5},{7,6},{8,11},{9,8},{10,9... | collective-permute-start | bytes 884744 | tf_op jit(solution)/shard_map/ppermute | solution.py:46
  13.3 9.8 %collective-permute-start.3 = (bf16[384,384]{1,0:T(8,128)(2,1)S(1)}, bf16[384,384]{1,0:T(8,128)(2,1)S(1)}, u32[]{:S(2)}, u32[]{:S(2)}) collective-permute-start(bf16[384,384]{1,0:T(8,128)(2,1)S(1)} %constant_dynamic-update-slice_fusion.refs_0_), channel_id=1, source_target_pairs={{0,4},{1,5},{2,6},{3,7},{4,0},{5,1},{6,2},{7,3},{8,12},{9,13},{10,... | collective-permute-start | bytes 884744 | tf_op jit(solution)/shard_map/ppermute | solution.py:46
  16.0 7.7 %collective-permute-start.12 = (bf16[192,768]{1,0:T(8,128)(2,1)S(1)}, bf16[192,768]{1,0:T(8,128)(2,1)S(1)}, u32[]{:S(2)}, u32[]{:S(2)}) collective-permute-start(bf16[192,768]{1,0:T(8,128)(2,1)S(1)} %collective-permute-done.10.refs_11_), channel_id=1, source_target_pairs={{0,32},{1,33},{2,34},{3,35},{4,36},{5,37},{6,38},{7,39},{8,232},{9... | collective-permute-start | bytes 884744 | tf_op jit(solution)/shard_map/ppermute | solution.py:46
  19.5 8.8 %collective-permute-start.13 = (bf16[192,768]{1,0:T(8,128)(2,1)S(1)}, bf16[192,768]{1,0:T(8,128)(2,1)S(1)}, u32[]{:S(2)}, u32[]{:S(2)}) collective-permute-start(bf16[192,768]{1,0:T(8,128)(2,1)S(1)} %collective-permute-done.11.refs_12_), channel_id=1, source_target_pairs={{0,32},{1,33},{2,34},{3,35},{4,36},{5,37},{6,38},{7,39},{8,232},{9... | collective-permute-start | bytes 884744 | tf_op jit(solution)/shard_map/ppermute | solution.py:46
  20.3 5.6 %collective-permute-start.4 = (bf16[192,384]{1,0:T(8,128)(2,1)S(1)}, bf16[192,384]{1,0:T(8,128)(2,1)S(1)}, u32[]{:S(2)}, u32[]{:S(2)}) collective-permute-start(bf16[192,384]{1,0:T(8,128)(2,1)S(1)} %slice.8), channel_id=1, source_target_pairs={{0,1},{1,2},{2,3},{3,0},{4,5},{5,6},{6,7},{7,4},{8,9},{9,10},{10,1... | collective-permute-start | bytes 442376 | tf_op jit(solution)/shard_map/ppermute | solution.py:46
  21.0 7.3 %collective-permute-start.5 = (bf16[192,384]{1,0:T(8,128)(2,1)S(1)}, bf16[192,384]{1,0:T(8,128)(2,1)S(1)}, u32[]{:S(2)}, u32[]{:S(2)}) collective-permute-start(bf16[192,384]{1,0:T(8,128)(2,1)S(1)} %slice.9), channel_id=1, source_target_pairs={{0,3},{1,0},{2,1},{3,2},{4,7},{5,4},{6,5},{7,6},{8,11},{9,8},{10,9... | collective-permute-start | bytes 442376 | tf_op jit(solution)/shard_map/ppermute | solution.py:46
  23.1 9.0 %collective-permute-start.6 = (bf16[384,384]{1,0:T(8,128)(2,1)S(1)}, bf16[384,384]{1,0:T(8,128)(2,1)S(1)}, u32[]{:S(2)}, u32[]{:S(2)}) collective-permute-start(bf16[384,384]{1,0:T(8,128)(2,1)S(1)} %collective-permute-done.3.refs_3_), channel_id=1, source_target_pairs={{0,1},{1,2},{2,3},{3,0},{4,5},{5,6},{6,7},{7,4},{8,9},{9,10},{10,1... | collective-permute-start | bytes 884744 | tf_op jit(solution)/shard_map/ppermute | solution.py:46
  23.7 10.5 %collective-permute-start.7 = (bf16[384,384]{1,0:T(8,128)(2,1)S(1)}, bf16[384,384]{1,0:T(8,128)(2,1)S(1)}, u32[]{:S(2)}, u32[]{:S(2)}) collective-permute-start(bf16[384,384]{1,0:T(8,128)(2,1)S(1)} %collective-permute-done.3.refs_3_), channel_id=1, source_target_pairs={{0,3},{1,0},{2,1},{3,2},{4,7},{5,4},{6,5},{7,6},{8,11},{9,8},{10,9... | collective-permute-start | bytes 884744 | tf_op jit(solution)/shard_map/ppermute | solution.py:46
  25.8 8.4 %collective-permute-start.14 = (bf16[192,768]{1,0:T(8,128)(2,1)S(1)}, bf16[192,768]{1,0:T(8,128)(2,1)S(1)}, u32[]{:S(2)}, u32[]{:S(2)}) collective-permute-start(bf16[192,768]{1,0:T(8,128)(2,1)S(1)} %collective-permute-done.12.refs_13_), channel_id=1, source_target_pairs={{0,32},{1,33},{2,34},{3,35},{4,36},{5,37},{6,38},{7,39},{8,232},{9... | collective-permute-start | bytes 884744 | tf_op jit(solution)/shard_map/ppermute | solution.py:46
  28.3 9.1 %collective-permute-start.15 = (bf16[192,768]{1,0:T(8,128)(2,1)S(1)}, bf16[192,768]{1,0:T(8,128)(2,1)S(1)}, u32[]{:S(2)}, u32[]{:S(2)}) collective-permute-start(bf16[192,768]{1,0:T(8,128)(2,1)S(1)} %collective-permute-done.13.refs_14_), channel_id=1, source_target_pairs={{0,32},{1,33},{2,34},{3,35},{4,36},{5,37},{6,38},{7,39},{8,232},{9... | collective-permute-start | bytes 884744 | tf_op jit(solution)/shard_map/ppermute | solution.py:46
  29.8 10.6 %collective-permute-start.8 = (bf16[384,384]{1,0:T(8,128)(2,1)S(1)}, bf16[384,384]{1,0:T(8,128)(2,1)S(1)}, u32[]{:S(2)}, u32[]{:S(2)}) collective-permute-start(bf16[384,384]{1,0:T(8,128)(2,1)S(1)} %pad_maximum_fusion.6), channel_id=1, source_target_pairs={{0,4},{1,5},{2,6},{3,7},{4,0},{5,1},{6,2},{7,3},{8,12},{9,13},{10,... | collective-permute-start | bytes 884744 | tf_op jit(solution)/shard_map/ppermute | solution.py:46
  32.2 12.8 %collective-permute-start.17 = (bf16[384,768]{1,0:T(8,128)(2,1)S(1)}, bf16[384,768]{1,0:T(8,128)(2,1)S(1)}, u32[]{:S(2)}, u32[]{:S(2)}) collective-permute-start(bf16[384,768]{1,0:T(8,128)(2,1)S(1)} %pad_maximum_fusion), channel_id=1, source_target_pairs={{0,8},{1,9},{2,10},{3,11},{4,12},{5,13},{6,14},{7,15},{8,0},{9,1},... | collective-permute-start | bytes 1769480 | tf_op jit(solution)/shard_map/ppermute | solution.py:46
  34.2 7.8 %collective-permute-start.16 = (bf16[192,768]{1,0:T(8,128)(2,1)S(1)}, bf16[192,768]{1,0:T(8,128)(2,1)S(1)}, u32[]{:S(2)}, u32[]{:S(2)}) collective-permute-start(bf16[192,768]{1,0:T(8,128)(2,1)S(1)} %collective-permute-done.14.refs_15_), channel_id=1, source_target_pairs={{0,32},{1,33},{2,34},{3,35},{4,36},{5,37},{6,38},{7,39},{8,232},{9... | collective-permute-start | bytes 884744 | tf_op jit(solution)/shard_map/ppermute | solution.py:46
  37.4 8.8 %collective-permute-start.18 = (bf16[384,768]{1,0:T(8,128)(2,1)S(1)}, bf16[384,768]{1,0:T(8,128)(2,1)S(1)}, u32[]{:S(2)}, u32[]{:S(2)}) collective-permute-start(bf16[384,768]{1,0:T(8,128)(2,1)S(1)} %pad_maximum_fusion.1), channel_id=1, source_target_pairs={{0,8},{1,9},{2,10},{3,11},{4,12},{5,13},{6,14},{7,15},{8,0},{9,1},... | collective-permute-start | bytes 1769480 | tf_op jit(solution)/shard_map/ppermute | solution.py:46
  37.5 8.7 %collective-permute-start.19 = (bf16[384,768]{1,0:T(8,128)(2,1)S(1)}, bf16[384,768]{1,0:T(8,128)(2,1)S(1)}, u32[]{:S(2)}, u32[]{:S(2)}) collective-permute-start(bf16[384,768]{1,0:T(8,128)(2,1)S(1)} %pad_maximum_fusion.2), channel_id=1, source_target_pairs={{0,8},{1,9},{2,10},{3,11},{4,12},{5,13},{6,14},{7,15},{8,0},{9,1},... | collective-permute-start | bytes 1769480 | tf_op jit(solution)/shard_map/ppermute | solution.py:46
  42.0 4.2 %collective-permute-start.20 = (bf16[192,768]{1,0:T(8,128)(2,1)S(1)}, bf16[192,768]{1,0:T(8,128)(2,1)S(1)}, u32[]{:S(2)}, u32[]{:S(2)}) collective-permute-start(bf16[192,768]{1,0:T(8,128)(2,1)S(1)} %collective-permute-done.16.a4), channel_id=1, source_target_pairs={{0,8},{1,9},{2,10},{3,11},{4,12},{5,13},{6,14},{7,15},{8,0},{9,1},... | collective-permute-start | bytes 884744 | tf_op jit(solution)/shard_map/ppermute | solution.py:46
  46.2 2.4 %copy-start = (s32[48,48]{1,0:T(8,128)S(1)}, s32[48,48]{1,0:T(8,128)}, u32[]{:S(2)}) copy-start(s32[48,48]{1,0:T(8,128)} %pattern.3) | copy-start | bytes 27652
  46.2 2.4 %copy-start.1 = (s32[48,48]{1,0:T(8,128)S(1)}, s32[48,48]{1,0:T(8,128)}, u32[]{:S(2)}) copy-start(s32[48,48]{1,0:T(8,128)} %keep.1) | copy-start | bytes 27652
  47.3 8.3 %collective-permute-start.21 = (bf16[192,768]{1,0:T(8,128)(2,1)S(1)}, bf16[192,768]{1,0:T(8,128)(2,1)S(1)}, u32[]{:S(2)}, u32[]{:S(2)}) collective-permute-start(bf16[192,768]{1,0:T(8,128)(2,1)S(1)} %shard_map.41), channel_id=1, source_target_pairs={{0,16},{1,17},{2,18},{3,19},{4,20},{5,21},{6,22},{7,23},{8,24},{9,... | collective-permute-start | bytes 884744 | tf_op jit(solution)/shard_map/ppermute | solution.py:46
  55.7 2.5 %collective-permute-start.22 = (bf16[192,768]{1,0:T(8,128)(2,1)S(1)}, bf16[192,768]{1,0:T(8,128)(2,1)S(1)}, u32[]{:S(2)}, u32[]{:S(2)}) collective-permute-start(bf16[192,768]{1,0:T(8,128)(2,1)S(1)} %subtract_convert_fusion.refs_1_), channel_id=1, source_target_pairs={{0,8},{1,9},{2,10},{3,11},{4,12},{5,13},{6,14},{7,15},{8,0},{9,1},... | collective-permute-start | bytes 884744 | tf_op jit(solution)/shard_map/ppermute | solution.py:46
  57.0 5.9 %collective-permute-start.23 = (bf16[192,768]{1,0:T(8,128)(2,1)S(1)}, bf16[192,768]{1,0:T(8,128)(2,1)S(1)}, u32[]{:S(2)}, u32[]{:S(2)}) collective-permute-start(bf16[192,768]{1,0:T(8,128)(2,1)S(1)} %subtract_convert_fusion.refs_1_), channel_id=1, source_target_pairs={{0,32},{1,33},{2,34},{3,35},{4,36},{5,37},{6,38},{7,39},{8,232},{9... | collective-permute-start | bytes 884744 | tf_op jit(solution)/shard_map/ppermute | solution.py:46
  58.2 7.8 %collective-permute-start.24 = (bf16[192,768]{1,0:T(8,128)(2,1)S(1)}, bf16[192,768]{1,0:T(8,128)(2,1)S(1)}, u32[]{:S(2)}, u32[]{:S(2)}) collective-permute-start(bf16[192,768]{1,0:T(8,128)(2,1)S(1)} %collective-permute-done.22.refs_2_), channel_id=1, source_target_pairs={{0,32},{1,33},{2,34},{3,35},{4,36},{5,37},{6,38},{7,39},{8,232},{9... | collective-permute-start | bytes 884744 | tf_op jit(solution)/shard_map/ppermute | solution.py:46
  62.9 6.0 %collective-permute-start.25 = (bf16[192,768]{1,0:T(8,128)(2,1)S(1)}, bf16[192,768]{1,0:T(8,128)(2,1)S(1)}, u32[]{:S(2)}, u32[]{:S(2)}) collective-permute-start(bf16[192,768]{1,0:T(8,128)(2,1)S(1)} %collective-permute-done.23.refs_3_), channel_id=1, source_target_pairs={{0,32},{1,33},{2,34},{3,35},{4,36},{5,37},{6,38},{7,39},{8,232},{9... | collective-permute-start | bytes 884744 | tf_op jit(solution)/shard_map/ppermute | solution.py:46
  66.0 6.3 %collective-permute-start.26 = (bf16[192,768]{1,0:T(8,128)(2,1)S(1)}, bf16[192,768]{1,0:T(8,128)(2,1)S(1)}, u32[]{:S(2)}, u32[]{:S(2)}) collective-permute-start(bf16[192,768]{1,0:T(8,128)(2,1)S(1)} %collective-permute-done.24.refs_4_), channel_id=1, source_target_pairs={{0,32},{1,33},{2,34},{3,35},{4,36},{5,37},{6,38},{7,39},{8,232},{9... | collective-permute-start | bytes 884744 | tf_op jit(solution)/shard_map/ppermute | solution.py:46
  68.9 7.4 %collective-permute-start.27 = (bf16[192,768]{1,0:T(8,128)(2,1)S(1)}, bf16[192,768]{1,0:T(8,128)(2,1)S(1)}, u32[]{:S(2)}, u32[]{:S(2)}) collective-permute-start(bf16[192,768]{1,0:T(8,128)(2,1)S(1)} %collective-permute-done.25.refs_5_), channel_id=1, source_target_pairs={{0,32},{1,33},{2,34},{3,35},{4,36},{5,37},{6,38},{7,39},{8,232},{9... | collective-permute-start | bytes 884744 | tf_op jit(solution)/shard_map/ppermute | solution.py:46
  72.3 8.7 %collective-permute-start.28 = (bf16[192,768]{1,0:T(8,128)(2,1)S(1)}, bf16[192,768]{1,0:T(8,128)(2,1)S(1)}, u32[]{:S(2)}, u32[]{:S(2)}) collective-permute-start(bf16[192,768]{1,0:T(8,128)(2,1)S(1)} %collective-permute-done.26.refs_6_), channel_id=1, source_target_pairs={{0,32},{1,33},{2,34},{3,35},{4,36},{5,37},{6,38},{7,39},{8,232},{9... | collective-permute-start | bytes 884744 | tf_op jit(solution)/shard_map/ppermute | solution.py:46
  74.3 14.5 %collective-permute-start.30 = (bf16[384,768]{1,0:T(8,128)(2,1)S(1)}, bf16[384,768]{1,0:T(8,128)(2,1)S(1)}, u32[]{:S(2)}, u32[]{:S(2)}) collective-permute-start(bf16[384,768]{1,0:T(8,128)(2,1)S(1)} %pad_maximum_fusion.3), channel_id=1, source_target_pairs={{0,8},{1,9},{2,10},{3,11},{4,12},{5,13},{6,14},{7,15},{8,0},{9,1},... | collective-permute-start | bytes 1769480 | tf_op jit(solution)/shard_map/ppermute | solution.py:46
  76.2 9.4 %collective-permute-start.29 = (bf16[192,768]{1,0:T(8,128)(2,1)S(1)}, bf16[192,768]{1,0:T(8,128)(2,1)S(1)}, u32[]{:S(2)}, u32[]{:S(2)}) collective-permute-start(bf16[192,768]{1,0:T(8,128)(2,1)S(1)} %collective-permute-done.27.refs_7_), channel_id=1, source_target_pairs={{0,32},{1,33},{2,34},{3,35},{4,36},{5,37},{6,38},{7,39},{8,232},{9... | collective-permute-start | bytes 884744 | tf_op jit(solution)/shard_map/ppermute | solution.py:46
  79.2 9.6 %collective-permute-start.31 = (bf16[384,768]{1,0:T(8,128)(2,1)S(1)}, bf16[384,768]{1,0:T(8,128)(2,1)S(1)}, u32[]{:S(2)}, u32[]{:S(2)}) collective-permute-start(bf16[384,768]{1,0:T(8,128)(2,1)S(1)} %pad_maximum_fusion.4), channel_id=1, source_target_pairs={{0,8},{1,9},{2,10},{3,11},{4,12},{5,13},{6,14},{7,15},{8,0},{9,1},... | collective-permute-start | bytes 1769480 | tf_op jit(solution)/shard_map/ppermute | solution.py:46
  81.1 9.0 %collective-permute-start.32 = (bf16[384,768]{1,0:T(8,128)(2,1)S(1)}, bf16[384,768]{1,0:T(8,128)(2,1)S(1)}, u32[]{:S(2)}, u32[]{:S(2)}) collective-permute-start(bf16[384,768]{1,0:T(8,128)(2,1)S(1)} %pad_maximum_fusion.5), channel_id=1, source_target_pairs={{0,8},{1,9},{2,10},{3,11},{4,12},{5,13},{6,14},{7,15},{8,0},{9,1},... | collective-permute-start | bytes 1769480 | tf_op jit(solution)/shard_map/ppermute | solution.py:46
  85.7 4.3 %collective-permute-start.33 = (bf16[192,768]{1,0:T(8,128)(2,1)S(1)}, bf16[192,768]{1,0:T(8,128)(2,1)S(1)}, u32[]{:S(2)}, u32[]{:S(2)}) collective-permute-start(bf16[192,768]{1,0:T(8,128)(2,1)S(1)} %collective-permute-done.29.a4), channel_id=1, source_target_pairs={{0,8},{1,9},{2,10},{3,11},{4,12},{5,13},{6,14},{7,15},{8,0},{9,1},... | collective-permute-start | bytes 884744 | tf_op jit(solution)/shard_map/ppermute | solution.py:46
  91.0 8.3 %collective-permute-start.34 = (bf16[192,768]{1,0:T(8,128)(2,1)S(1)}, bf16[192,768]{1,0:T(8,128)(2,1)S(1)}, u32[]{:S(2)}, u32[]{:S(2)}) collective-permute-start(bf16[192,768]{1,0:T(8,128)(2,1)S(1)} %shard_map.44), channel_id=1, source_target_pairs={{0,16},{1,17},{2,18},{3,19},{4,20},{5,21},{6,22},{7,23},{8,24},{9,... | collective-permute-start | bytes 884744 | tf_op jit(solution)/shard_map/ppermute | solution.py:46

commit v5 on v4

--- a/solution.py
+++ b/solution.py
@@ -100,58 +100,61 @@
     _, _, _, col = place()
     yh, x = col // 4, col % 4
 
-    def at(dx, dy):
-        return lax.rem(yh + dy, 2) * 4 + lax.rem(x + dx + 4, 4)
-
-    left[at(0, 0)] = own[...]
-    left[at(-1, 0)] = w[...]
-    left[at(1, 0)] = e[...]
-    left[at(0, 1)] = y[...]
-    left[at(2, 0), :ROWS, :] = x2[...]
-    left[at(2, 0), ROWS:, :] = x2_too[...]
-    left[at(-1, 1)] = yw[...]
-    left[at(1, 1)] = ye[...]
-    left[at(2, 1)] = y2[...]
-
-
-def multiply(left, rows, blocks):
-    _, _, core, _ = place()
-
-    def part(k, mine, others, pair):
-        pair[core] = mine[...]
-        pair[1 - core] = others[...]
-        right = pair[...].reshape(HALF, COLS)
-        return jnp.dot(left[lax.rem(k + 16, 8), rows], right, preferred_element_type=F32)
-
-    return sum((part(*block) for block in blocks[1:]), part(*blocks[0]))
-
-
-def near_sums(left, pieces, column):
+    def put(ref, dx, dy, first=0):
+        index = lax.rem(yh + dy, 2) * 4 + lax.rem(x + dx + 4, 4)
+        for core in range(2):
+            columns = slice(ROWS * core, ROWS * (core + 1))
+            left[index, core, first : first + ref.shape[0], :] = ref[:, columns]
+
+    put(own, 0, 0)
+    put(w, -1, 0)
+    put(e, 1, 0)
+    put(y, 0, 1)
+    put(x2, 2, 0)
+    put(x2_too, 2, 0, ROWS)
+    put(yw, -1, 1)
+    put(ye, 1, 1)
+    put(y2, 2, 1)
+
+
+def multiply(left, rows, parts):
+    def part(k, core, ref, first):
+        return jnp.dot(
+            left[lax.rem(k + 16, 8), core, rows], ref[first : first + ROWS, :], preferred_element_type=F32
+        )
+
+    return sum((part(*p) for p in parts[1:]), part(*parts[0]))
+
+
+def near_sums(left, pieces):
     z, _, core, _ = place()
     sign = 2 * core - 1
-    pairs = [(pieces[2 * s], pieces[2 * s + 1], column.at[s]) for s in range(4)]
-    return multiply(left, slice(0, HALF), [(z + sign * s, *pair) for s, pair in enumerate(pairs)])
+    parts = []
+    for s in range(4):
+        parts.append((z + sign * s, core, pieces[2 * s], 0))
+        parts.append((z + sign * s, 1 - core, pieces[2 * s + 1], 0))
+    return multiply(left, slice(0, HALF), parts)
 
 
 def square_kernel(*refs):
-    total, left, column = refs[17:]
+    total, left = refs[17:]
     fill_left(left, refs[:9])
-    total[...] = near_sums(left, refs[9:17], column)
+    total[...] = near_sums(left, refs[9:17])
 
 
 def update_kernel(*refs):
-    total, column = refs[9:]
-    total[...] = near_sums(refs[0], refs[1:9], column)
-
-
-def last_kernel(part, left, total, a4, s1, s2, s3, s4, result, column):
+    refs[9][...] = near_sums(refs[0], refs[1:9])
+
+
+def last_kernel(half, left, total, a4, s1, s2, s3, s4, result):
     z, _, core, _ = place()
     sign = 2 * core - 1
-    rows = slice(ROWS * part, ROWS * (part + 1))
-    blocks = [(z + 4, a4, s4, column.at[3])]
+    rows = slice(ROWS * half, ROWS * (half + 1))
+    parts = [(z + 4, core, a4, 0), (z + 4, 1 - core, s4, 0)]
     for s, ref in enumerate((s1, s2, s3)):
-        blocks.append((z - sign * (s + 1), ref.at[ROWS:], ref.at[:ROWS], column.at[s]))
-    result[...] = (total[rows] + multiply(left, rows, blocks)).astype(result.dtype)
+        parts.append((z - sign * (s + 1), 1 - core, ref, 0))
+        parts.append((z - sign * (s + 1), core, ref, ROWS))
+    result[...] = (total[rows] + multiply(left, rows, parts)).astype(result.dtype)
 
 
 def factor_kernel(pattern, keep, kept_square, eye, kept_result):
@@ -217,15 +220,14 @@
 
 FLOPS = 2 * ROWS * COLS * 6144
 SUMS = struct(HALF, COLS, dtype=F32)
-COLUMN = pltpu.VMEM((4, 2, ROWS, COLS), BF16)
 
 
 def sums(left, total, last):
     args = [left, total, *last]
     away_kernel, keep_kernel = functools.partial(last_kernel, 1), functools.partial(last_kernel, 0)
-    (away,) = call(away_kernel, args, [struct(ROWS, COLS)], [COLUMN], FLOPS // 4)
+    (away,) = call(away_kernel, args, [struct(ROWS, COLS)], [], FLOPS // 4)
     theirs = send(away, TWIN)
-    (kept,) = call(keep_kernel, args, [struct(ROWS, COLS, dtype=F32)], [COLUMN], FLOPS // 4)
+    (kept,) = call(keep_kernel, args, [struct(ROWS, COLS, dtype=F32)], [], FLOPS // 4)
     return kept + theirs.astype(F32)
 
 
@@ -248,13 +250,13 @@
     pieces = row(cat(kept, send(away, TWIN)))
 
     def square(near):
-        return call(square_kernel, [*pieces, *near], [SUMS, struct(8, HALF, HALF)], [COLUMN], FLOPS // 2)
+        return call(square_kernel, [*pieces, *near], [SUMS, struct(8, 2, HALF, ROWS)], [], FLOPS // 2)
 
     (total, left), last = ring(x, square, a2=pieces[:1], a3=pieces[1:4], b3=pieces[4:6], a4=pieces[6:8])
     weight = (eye - sums(left, total, last) * kept_square).astype(BF16)
 
     def update(near):
-        return call(update_kernel, [left, *near], [SUMS], [COLUMN], FLOPS // 2)
+        return call(update_kernel, [left, *near], [SUMS], [], FLOPS // 2)
 
     (total,), last = ring(weight, update)
     return (sums(left, total, last) * kept_result).astype(BF16)

time: 100 us -> 99.8 us (level)
  transfers between devices with their start and end apart: 35 -> 35, of which waited for: 9 -> 9; matrix products, arithmetic and copies ran while one was open for 0% -> 0% of each run, Pallas kernels for 7% -> 6%
where the time goes in v5:
time: 99.8 us; the launch traced here: 99.7 us
  starting transfers between devices  66.7 us (67%)
  waiting for transfers between devices  22.5 us (23%)
  Pallas kernels  8.96 us (9%)
  other arithmetic  1.18 us (1%)
    ppermute x35, starting transfers between devices, send(): return lax.ppermute(value, AXES, pairs)  66.7 us
    ppermute x35, waiting for transfers between devices, send(): return lax.ppermute(value, AXES, pairs)  22.5 us
    pallas_call x8, Pallas kernels, call(): pl.pallas_call(kernel, in_specs=specs or [SMEM if arg.dtype == jnp.int32...  8.96 us
  transfers between devices with their start and end apart: 35, of which 9 were waited for; matrix products, arithmetic and copies ran while one was open for 0% of the time, Pallas kernels for 6%

profile of v5, /device:TPU:1, one launch (start us, length us, event | category | flops | bytes accessed | tf_op | source)
XLA Modules:
  0.0 99.7 jit_solution(14407925412667234542)
XLA Ops:
  0.0 1.2 %shard_map.37 = (bf16[192,768]{1,0:T(8,128)(2,1)S(1)}, bf16[192,384]{1,0:T(8,128)(2,1)S(1)}, bf16[192,384]{1,0:T(8,128)(2,1)S(1)}) custom-call(s32[48,48]{1,0:T(8,128)} %pattern.3, bf16[192,768]{1,0:T(8,128)(2,1)} %matrix.1), custom_call_target="tpu_custom_call" | custom-call | tf_op jit(solution)/shard_map/pallas_call | solution.py:184
  1.2 3.3 %collective-permute-start.9 = (bf16[192,768]{1,0:T(8,128)(2,1)S(1)}, bf16[192,768]{1,0:T(8,128)(2,1)S(1)}, u32[]{:S(2)}, u32[]{:S(2)}) collective-permute-start(bf16[192,768]{1,0:T(8,128)(2,1)S(1)} %get-tuple-element.21.refs_9_), channel_id=1, source_target_pairs={{0,8},{1,9},{2,10},{3,11},{4,12},{5,13},{6,14},{7,15},{8,0},{9,1},... | collective-permute-start | bytes 884744 | tf_op jit(solution)/shard_map/ppermute | solution.py:46
  4.6 5.2 %collective-permute-start.10 = (bf16[192,768]{1,0:T(8,128)(2,1)S(1)}, bf16[192,768]{1,0:T(8,128)(2,1)S(1)}, u32[]{:S(2)}, u32[]{:S(2)}) collective-permute-start(bf16[192,768]{1,0:T(8,128)(2,1)S(1)} %get-tuple-element.21.refs_9_), channel_id=1, source_target_pairs={{0,32},{1,33},{2,34},{3,35},{4,36},{5,37},{6,38},{7,39},{8,232},{9... | collective-permute-start | bytes 884744 | tf_op jit(solution)/shard_map/ppermute | solution.py:46
  9.7 0.0 collective-permute-done.9.refs_10_
  9.7 0.8 collective-permute-start.11
  10.6 1.3 %collective-permute-start.1 = (bf16[384,384]{1,0:T(8,128)(2,1)S(1)}, bf16[384,384]{1,0:T(8,128)(2,1)S(1)}, u32[]{:S(2)}, u32[]{:S(2)}) collective-permute-start(bf16[384,384]{1,0:T(8,128)(2,1)S(1)} %constant_dynamic-update-slice_fusion.refs_0_), channel_id=1, source_target_pairs={{0,1},{1,2},{2,3},{3,0},{4,5},{5,6},{6,7},{7,4},{8,9},{9,10},{10,1... | collective-permute-start | bytes 884744 | tf_op jit(solution)/shard_map/ppermute | solution.py:46
  11.9 1.5 %collective-permute-start.2 = (bf16[384,384]{1,0:T(8,128)(2,1)S(1)}, bf16[384,384]{1,0:T(8,128)(2,1)S(1)}, u32[]{:S(2)}, u32[]{:S(2)}) collective-permute-start(bf16[384,384]{1,0:T(8,128)(2,1)S(1)} %constant_dynamic-update-slice_fusion.refs_0_), channel_id=1, source_target_pairs={{0,3},{1,0},{2,1},{3,2},{4,7},{5,4},{6,5},{7,6},{8,11},{9,8},{10,9... | collective-permute-start | bytes 884744 | tf_op jit(solution)/shard_map/ppermute | solution.py:46
  13.3 2.6 %collective-permute-start.3 = (bf16[384,384]{1,0:T(8,128)(2,1)S(1)}, bf16[384,384]{1,0:T(8,128)(2,1)S(1)}, u32[]{:S(2)}, u32[]{:S(2)}) collective-permute-start(bf16[384,384]{1,0:T(8,128)(2,1)S(1)} %constant_dynamic-update-slice_fusion.refs_0_), channel_id=1, source_target_pairs={{0,4},{1,5},{2,6},{3,7},{4,0},{5,1},{6,2},{7,3},{8,12},{9,13},{10,... | collective-permute-start | bytes 884744 | tf_op jit(solution)/shard_map/ppermute | solution.py:46
  16.0 0.0 collective-permute-done.10.refs_11_
  16.0 3.5 %collective-permute-start.12 = (bf16[192,768]{1,0:T(8,128)(2,1)S(1)}, bf16[192,768]{1,0:T(8,128)(2,1)S(1)}, u32[]{:S(2)}, u32[]{:S(2)}) collective-permute-start(bf16[192,768]{1,0:T(8,128)(2,1)S(1)} %collective-permute-done.10.refs_11_), channel_id=1, source_target_pairs={{0,32},{1,33},{2,34},{3,35},{4,36},{5,37},{6,38},{7,39},{8,232},{9... | collective-permute-start | bytes 884744 | tf_op jit(solution)/shard_map/ppermute | solution.py:46
  19.5 0.7 collective-permute-start.13
  20.2 0.0 collective-permute-done.1.refs_1_
  20.3 0.7 collective-permute-start.4
  21.0 0.0 collective-permute-done.2.refs_2_
  21.0 2.1 %collective-permute-start.5 = (bf16[192,384]{1,0:T(8,128)(2,1)S(1)}, bf16[192,384]{1,0:T(8,128)(2,1)S(1)}, u32[]{:S(2)}, u32[]{:S(2)}) collective-permute-start(bf16[192,384]{1,0:T(8,128)(2,1)S(1)} %slice.9), channel_id=1, source_target_pairs={{0,3},{1,0},{2,1},{3,2},{4,7},{5,4},{6,5},{7,6},{8,11},{9,8},{10,9... | collective-permute-start | bytes 442376 | tf_op jit(solution)/shard_map/ppermute | solution.py:46
  23.1 0.0 collective-permute-done.3.refs_3_
  23.1 0.6 collective-permute-start.6
  23.7 0.0 collective-permute-done.12.refs_13_
  23.7 2.1 %collective-permute-start.7 = (bf16[384,384]{1,0:T(8,128)(2,1)S(1)}, bf16[384,384]{1,0:T(8,128)(2,1)S(1)}, u32[]{:S(2)}, u32[]{:S(2)}) collective-permute-start(bf16[384,384]{1,0:T(8,128)(2,1)S(1)} %collective-permute-done.3.refs_3_), channel_id=1, source_target_pairs={{0,3},{1,0},{2,1},{3,2},{4,7},{5,4},{6,5},{7,6},{8,11},{9,8},{10,9... | collective-permute-start | bytes 884744 | tf_op jit(solution)/shard_map/ppermute | solution.py:46
  25.8 0.0 collective-permute-done.4.refs_4_
  25.8 2.5 %collective-permute-start.14 = (bf16[192,768]{1,0:T(8,128)(2,1)S(1)}, bf16[192,768]{1,0:T(8,128)(2,1)S(1)}, u32[]{:S(2)}, u32[]{:S(2)}) collective-permute-start(bf16[192,768]{1,0:T(8,128)(2,1)S(1)} %collective-permute-done.12.refs_13_), channel_id=1, source_target_pairs={{0,32},{1,33},{2,34},{3,35},{4,36},{5,37},{6,38},{7,39},{8,232},{9... | collective-permute-start | bytes 884744 | tf_op jit(solution)/shard_map/ppermute | solution.py:46
  28.3 0.0 collective-permute-done.5.refs_5_
  28.3 0.0 collective-permute-done.13.refs_14_
  28.3 1.4 %collective-permute-start.15 = (bf16[192,768]{1,0:T(8,128)(2,1)S(1)}, bf16[192,768]{1,0:T(8,128)(2,1)S(1)}, u32[]{:S(2)}, u32[]{:S(2)}) collective-permute-start(bf16[192,768]{1,0:T(8,128)(2,1)S(1)} %collective-permute-done.13.refs_14_), channel_id=1, source_target_pairs={{0,32},{1,33},{2,34},{3,35},{4,36},{5,37},{6,38},{7,39},{8,232},{9... | collective-permute-start | bytes 884744 | tf_op jit(solution)/shard_map/ppermute | solution.py:46
  29.8 2.3 %collective-permute-start.8 = (bf16[384,384]{1,0:T(8,128)(2,1)S(1)}, bf16[384,384]{1,0:T(8,128)(2,1)S(1)}, u32[]{:S(2)}, u32[]{:S(2)}) collective-permute-start(bf16[384,384]{1,0:T(8,128)(2,1)S(1)} %pad_maximum_fusion.6), channel_id=1, source_target_pairs={{0,4},{1,5},{2,6},{3,7},{4,0},{5,1},{6,2},{7,3},{8,12},{9,13},{10,... | collective-permute-start | bytes 884744 | tf_op jit(solution)/shard_map/ppermute | solution.py:46
  32.2 2.0 %collective-permute-start.17 = (bf16[384,768]{1,0:T(8,128)(2,1)S(1)}, bf16[384,768]{1,0:T(8,128)(2,1)S(1)}, u32[]{:S(2)}, u32[]{:S(2)}) collective-permute-start(bf16[384,768]{1,0:T(8,128)(2,1)S(1)} %pad_maximum_fusion), channel_id=1, source_target_pairs={{0,8},{1,9},{2,10},{3,11},{4,12},{5,13},{6,14},{7,15},{8,0},{9,1},... | collective-permute-start | bytes 1769480 | tf_op jit(solution)/shard_map/ppermute | solution.py:46
  34.2 3.1 %collective-permute-start.16 = (bf16[192,768]{1,0:T(8,128)(2,1)S(1)}, bf16[192,768]{1,0:T(8,128)(2,1)S(1)}, u32[]{:S(2)}, u32[]{:S(2)}) collective-permute-start(bf16[192,768]{1,0:T(8,128)(2,1)S(1)} %collective-permute-done.14.refs_15_), channel_id=1, source_target_pairs={{0,32},{1,33},{2,34},{3,35},{4,36},{5,37},{6,38},{7,39},{8,232},{9... | collective-permute-start | bytes 884744 | tf_op jit(solution)/shard_map/ppermute | solution.py:46
  37.4 0.1 collective-permute-start.18
  37.5 0.0 collective-permute-done.15.refs_16_
  37.5 2.8 %collective-permute-start.19 = (bf16[384,768]{1,0:T(8,128)(2,1)S(1)}, bf16[384,768]{1,0:T(8,128)(2,1)S(1)}, u32[]{:S(2)}, u32[]{:S(2)}) collective-permute-start(bf16[384,768]{1,0:T(8,128)(2,1)S(1)} %pad_maximum_fusion.2), channel_id=1, source_target_pairs={{0,8},{1,9},{2,10},{3,11},{4,12},{5,13},{6,14},{7,15},{8,0},{9,1},... | collective-permute-start | bytes 1769480 | tf_op jit(solution)/shard_map/ppermute | solution.py:46
  40.4 1.8 %shard_map.38 = (f32[384,768]{1,0:T(8,128)S(1)}, bf16[8,2,384,192]{3,2,1,0:T(8,128)(2,1)S(1)}) custom-call(bf16[384,384]{1,0:T(8,128)(2,1)S(1)} %constant_dynamic-update-slice_fusion.refs_0_, bf16[384,384]{1,0:T(8,128)(2,1)S(1)} %collective-permute-done.1.refs_1_, bf16[384,384]{1,0:T(8,128)(2,1)S(1)} %collective-permute-done.2.refs_2_, ...), custom_call_target="tpu_custom_call" | custom-call | flops 905969664 | tf_op jit(solution)/shard_map/pallas_call | solution.py:184
  42.2 0.0 collective-permute-done.16.a4
  42.2 2.8 %collective-permute-start.20 = (bf16[192,768]{1,0:T(8,128)(2,1)S(1)}, bf16[192,768]{1,0:T(8,128)(2,1)S(1)}, u32[]{:S(2)}, u32[]{:S(2)}) collective-permute-start(bf16[192,768]{1,0:T(8,128)(2,1)S(1)} %collective-permute-done.16.a4), channel_id=1, source_target_pairs={{0,8},{1,9},{2,10},{3,11},{4,12},{5,13},{6,14},{7,15},{8,0},{9,1},... | collective-permute-start | bytes 884744 | tf_op jit(solution)/shard_map/ppermute | solution.py:46
  45.0 1.2 %collective-permute-done.20.s4 = bf16[192,768]{1,0:T(8,128)(2,1)S(1)} collective-permute-done((bf16[192,768]{1,0:T(8,128)(2,1)S(1)}, bf16[192,768]{1,0:T(8,128)(2,1)S(1)}, u32[]{:S(2)}, u32[]{:S(2)}) %collective-permute-start.20) | collective-permute-done | bytes 294944 | tf_op jit(solution)/shard_map/ppermute | solution.py:46
  46.2 0.8 shard_map.41
  47.0 1.4 %collective-permute-start.21 = (bf16[192,768]{1,0:T(8,128)(2,1)S(1)}, bf16[192,768]{1,0:T(8,128)(2,1)S(1)}, u32[]{:S(2)}, u32[]{:S(2)}) collective-permute-start(bf16[192,768]{1,0:T(8,128)(2,1)S(1)} %shard_map.41), channel_id=1, source_target_pairs={{0,16},{1,17},{2,18},{3,19},{4,20},{5,21},{6,22},{7,23},{8,24},{9,... | collective-permute-start | bytes 884744 | tf_op jit(solution)/shard_map/ppermute | solution.py:46
  48.4 1.5 %shard_map.39 = (f32[192,768]{1,0:T(8,128)S(1)}, f32[192,768]{1,0:T(8,128)S(1)}, f32[192,768]{1,0:T(8,128)S(1)}) custom-call(s32[48,48]{1,0:T(8,128)S(1)} %copy-done, s32[48,48]{1,0:T(8,128)S(1)} %copy-done.1), custom_call_target="tpu_custom_call" | custom-call | flops 147456 | tf_op jit(solution)/shard_map/pallas_call | solution.py:184
  49.9 0.8 shard_map.40
  50.7 4.6 %collective-permute-done.21 = bf16[192,768]{1,0:T(8,128)(2,1)S(1)} collective-permute-done((bf16[192,768]{1,0:T(8,128)(2,1)S(1)}, bf16[192,768]{1,0:T(8,128)(2,1)S(1)}, u32[]{:S(2)}, u32[]{:S(2)}) %collective-permute-start.21) | collective-permute-done | bytes 294944 | tf_op jit(solution)/shard_map/ppermute | solution.py:46
  55.3 0.1 subtract_convert_fusion.refs_1_
  55.4 1.3 %collective-permute-start.22 = (bf16[192,768]{1,0:T(8,128)(2,1)S(1)}, bf16[192,768]{1,0:T(8,128)(2,1)S(1)}, u32[]{:S(2)}, u32[]{:S(2)}) collective-permute-start(bf16[192,768]{1,0:T(8,128)(2,1)S(1)} %subtract_convert_fusion.refs_1_), channel_id=1, source_target_pairs={{0,8},{1,9},{2,10},{3,11},{4,12},{5,13},{6,14},{7,15},{8,0},{9,1},... | collective-permute-start | bytes 884744 | tf_op jit(solution)/shard_map/ppermute | solution.py:46
  56.7 0.5 collective-permute-start.23
  57.3 0.7 collective-permute-done.22.refs_2_
  57.9 0.5 collective-permute-start.24
  58.5 4.1 %collective-permute-done.23.refs_3_ = bf16[192,768]{1,0:T(8,128)(2,1)S(1)} collective-permute-done((bf16[192,768]{1,0:T(8,128)(2,1)S(1)}, bf16[192,768]{1,0:T(8,128)(2,1)S(1)}, u32[]{:S(2)}, u32[]{:S(2)}) %collective-permute-start.23) | collective-permute-done | bytes 294944 | tf_op jit(solution)/shard_map/ppermute | solution.py:46
  62.6 1.4 %collective-permute-start.25 = (bf16[192,768]{1,0:T(8,128)(2,1)S(1)}, bf16[192,768]{1,0:T(8,128)(2,1)S(1)}, u32[]{:S(2)}, u32[]{:S(2)}) collective-permute-start(bf16[192,768]{1,0:T(8,128)(2,1)S(1)} %collective-permute-done.23.refs_3_), channel_id=1, source_target_pairs={{0,32},{1,33},{2,34},{3,35},{4,36},{5,37},{6,38},{7,39},{8,232},{9... | collective-permute-start | bytes 884744 | tf_op jit(solution)/shard_map/ppermute | solution.py:46
  64.1 1.7 %collective-permute-done.24.refs_4_ = bf16[192,768]{1,0:T(8,128)(2,1)S(1)} collective-permute-done((bf16[192,768]{1,0:T(8,128)(2,1)S(1)}, bf16[192,768]{1,0:T(8,128)(2,1)S(1)}, u32[]{:S(2)}, u32[]{:S(2)}) %collective-permute-start.24) | collective-permute-done | bytes 294944 | tf_op jit(solution)/shard_map/ppermute | solution.py:46
  65.8 1.4 %collective-permute-start.26 = (bf16[192,768]{1,0:T(8,128)(2,1)S(1)}, bf16[192,768]{1,0:T(8,128)(2,1)S(1)}, u32[]{:S(2)}, u32[]{:S(2)}) collective-permute-start(bf16[192,768]{1,0:T(8,128)(2,1)S(1)} %collective-permute-done.24.refs_4_), channel_id=1, source_target_pairs={{0,32},{1,33},{2,34},{3,35},{4,36},{5,37},{6,38},{7,39},{8,232},{9... | collective-permute-start | bytes 884744 | tf_op jit(solution)/shard_map/ppermute | solution.py:46
  67.2 1.4 %collective-permute-done.25.refs_5_ = bf16[192,768]{1,0:T(8,128)(2,1)S(1)} collective-permute-done((bf16[192,768]{1,0:T(8,128)(2,1)S(1)}, bf16[192,768]{1,0:T(8,128)(2,1)S(1)}, u32[]{:S(2)}, u32[]{:S(2)}) %collective-permute-start.25) | collective-permute-done | bytes 294944 | tf_op jit(solution)/shard_map/ppermute | solution.py:46
  68.6 2.2 %collective-permute-start.27 = (bf16[192,768]{1,0:T(8,128)(2,1)S(1)}, bf16[192,768]{1,0:T(8,128)(2,1)S(1)}, u32[]{:S(2)}, u32[]{:S(2)}) collective-permute-start(bf16[192,768]{1,0:T(8,128)(2,1)S(1)} %collective-permute-done.25.refs_5_), channel_id=1, source_target_pairs={{0,32},{1,33},{2,34},{3,35},{4,36},{5,37},{6,38},{7,39},{8,232},{9... | collective-permute-start | bytes 884744 | tf_op jit(solution)/shard_map/ppermute | solution.py:46
  70.8 1.2 %collective-permute-done.26.refs_6_ = bf16[192,768]{1,0:T(8,128)(2,1)S(1)} collective-permute-done((bf16[192,768]{1,0:T(8,128)(2,1)S(1)}, bf16[192,768]{1,0:T(8,128)(2,1)S(1)}, u32[]{:S(2)}, u32[]{:S(2)}) %collective-permute-start.26) | collective-permute-done | bytes 294944 | tf_op jit(solution)/shard_map/ppermute | solution.py:46
  72.1 1.9 %collective-permute-start.28 = (bf16[192,768]{1,0:T(8,128)(2,1)S(1)}, bf16[192,768]{1,0:T(8,128)(2,1)S(1)}, u32[]{:S(2)}, u32[]{:S(2)}) collective-permute-start(bf16[192,768]{1,0:T(8,128)(2,1)S(1)} %collective-permute-done.26.refs_6_), channel_id=1, source_target_pairs={{0,32},{1,33},{2,34},{3,35},{4,36},{5,37},{6,38},{7,39},{8,232},{9... | collective-permute-start | bytes 884744 | tf_op jit(solution)/shard_map/ppermute | solution.py:46
  74.0 1.9 %collective-permute-start.30 = (bf16[384,768]{1,0:T(8,128)(2,1)S(1)}, bf16[384,768]{1,0:T(8,128)(2,1)S(1)}, u32[]{:S(2)}, u32[]{:S(2)}) collective-permute-start(bf16[384,768]{1,0:T(8,128)(2,1)S(1)} %pad_maximum_fusion.3), channel_id=1, source_target_pairs={{0,8},{1,9},{2,10},{3,11},{4,12},{5,13},{6,14},{7,15},{8,0},{9,1},... | collective-permute-start | bytes 1769480 | tf_op jit(solution)/shard_map/ppermute | solution.py:46
  76.0 3.0 %collective-permute-start.29 = (bf16[192,768]{1,0:T(8,128)(2,1)S(1)}, bf16[192,768]{1,0:T(8,128)(2,1)S(1)}, u32[]{:S(2)}, u32[]{:S(2)}) collective-permute-start(bf16[192,768]{1,0:T(8,128)(2,1)S(1)} %collective-permute-done.27.refs_7_), channel_id=1, source_target_pairs={{0,32},{1,33},{2,34},{3,35},{4,36},{5,37},{6,38},{7,39},{8,232},{9... | collective-permute-start | bytes 884744 | tf_op jit(solution)/shard_map/ppermute | solution.py:46
  79.0 1.8 %collective-permute-start.31 = (bf16[384,768]{1,0:T(8,128)(2,1)S(1)}, bf16[384,768]{1,0:T(8,128)(2,1)S(1)}, u32[]{:S(2)}, u32[]{:S(2)}) collective-permute-start(bf16[384,768]{1,0:T(8,128)(2,1)S(1)} %pad_maximum_fusion.4), channel_id=1, source_target_pairs={{0,8},{1,9},{2,10},{3,11},{4,12},{5,13},{6,14},{7,15},{8,0},{9,1},... | collective-permute-start | bytes 1769480 | tf_op jit(solution)/shard_map/ppermute | solution.py:46
  80.8 3.1 %collective-permute-start.32 = (bf16[384,768]{1,0:T(8,128)(2,1)S(1)}, bf16[384,768]{1,0:T(8,128)(2,1)S(1)}, u32[]{:S(2)}, u32[]{:S(2)}) collective-permute-start(bf16[384,768]{1,0:T(8,128)(2,1)S(1)} %pad_maximum_fusion.5), channel_id=1, source_target_pairs={{0,8},{1,9},{2,10},{3,11},{4,12},{5,13},{6,14},{7,15},{8,0},{9,1},... | collective-permute-start | bytes 1769480 | tf_op jit(solution)/shard_map/ppermute | solution.py:46
  83.9 1.4 %shard_map.42.total = f32[384,768]{1,0:T(8,128)S(1)} custom-call(bf16[8,2,384,192]{3,2,1,0:T(8,128)(2,1)S(1)} %get-tuple-element.25.left.refs_0_, bf16[192,768]{1,0:T(8,128)(2,1)S(1)} %subtract_convert_fusion.refs_1_, bf16[192,768]{1,0:T(8,128)(2,1)S(1)} %collective-permute-done.22.refs_2_, bf16[192,768]{1,0:T(8,128)(2,1)S(1)} %collective-permute-done.23.refs_3_, ...), custom_call_target="tpu_custom_call" | custom-call | flops 905969664 | tf_op jit(solution)/shard_map/pallas_call | solution.py:184
  85.3 3.3 %collective-permute-start.33 = (bf16[192,768]{1,0:T(8,128)(2,1)S(1)}, bf16[192,768]{1,0:T(8,128)(2,1)S(1)}, u32[]{:S(2)}, u32[]{:S(2)}) collective-permute-start(bf16[192,768]{1,0:T(8,128)(2,1)S(1)} %collective-permute-done.29.a4), channel_id=1, source_target_pairs={{0,8},{1,9},{2,10},{3,11},{4,12},{5,13},{6,14},{7,15},{8,0},{9,1},... | collective-permute-start | bytes 884744 | tf_op jit(solution)/shard_map/ppermute | solution.py:46
  88.6 1.2 %collective-permute-done.33.s4 = bf16[192,768]{1,0:T(8,128)(2,1)S(1)} collective-permute-done((bf16[192,768]{1,0:T(8,128)(2,1)S(1)}, bf16[192,768]{1,0:T(8,128)(2,1)S(1)}, u32[]{:S(2)}, u32[]{:S(2)}) %collective-permute-start.33) | collective-permute-done | bytes 294944 | tf_op jit(solution)/shard_map/ppermute | solution.py:46
  89.8 0.8 shard_map.44
  90.6 1.4 %collective-permute-start.34 = (bf16[192,768]{1,0:T(8,128)(2,1)S(1)}, bf16[192,768]{1,0:T(8,128)(2,1)S(1)}, u32[]{:S(2)}, u32[]{:S(2)}) collective-permute-start(bf16[192,768]{1,0:T(8,128)(2,1)S(1)} %shard_map.44), channel_id=1, source_target_pairs={{0,16},{1,17},{2,18},{3,19},{4,20},{5,21},{6,22},{7,23},{8,24},{9,... | collective-permute-start | bytes 884744 | tf_op jit(solution)/shard_map/ppermute | solution.py:46
  91.9 0.8 shard_map.43
  92.7 6.2 %collective-permute-done.34 = bf16[192,768]{1,0:T(8,128)(2,1)S(1)} collective-permute-done((bf16[192,768]{1,0:T(8,128)(2,1)S(1)}, bf16[192,768]{1,0:T(8,128)(2,1)S(1)}, u32[]{:S(2)}, u32[]{:S(2)}) %collective-permute-start.34) | collective-permute-done | bytes 294944 | tf_op jit(solution)/shard_map/ppermute | solution.py:46
  98.9 0.8 multiply_convert_fusion
  (31 shorter events, 0.4 us)
Async XLA Ops:
  1.2 8.5 %collective-permute-start.9 = (bf16[192,768]{1,0:T(8,128)(2,1)S(1)}, bf16[192,768]{1,0:T(8,128)(2,1)S(1)}, u32[]{:S(2)}, u32[]{:S(2)}) collective-permute-start(bf16[192,768]{1,0:T(8,128)(2,1)S(1)} %get-tuple-element.21.refs_9_), channel_id=1, source_target_pairs={{0,8},{1,9},{2,10},{3,11},{4,12},{5,13},{6,14},{7,15},{8,0},{9,1},... | collective-permute-start | bytes 884744 | tf_op jit(solution)/shard_map/ppermute | solution.py:46
  4.6 6.0 %collective-permute-start = (bf16[192,384]{1,0:T(8,128)(2,1)S(1)}, bf16[192,384]{1,0:T(8,128)(2,1)S(1)}, u32[]{:S(2)}, u32[]{:S(2)}) collective-permute-start(bf16[192,384]{1,0:T(8,128)(2,1)S(1)} %get-tuple-element.20), channel_id=1, source_target_pairs={{0,16},{1,17},{2,18},{3,19},{4,20},{5,21},{6,22},{7,23},{8,24},{9,... | collective-permute-start | bytes 442376 | tf_op jit(solution)/shard_map/ppermute | solution.py:46
  4.6 11.4 %collective-permute-start.10 = (bf16[192,768]{1,0:T(8,128)(2,1)S(1)}, bf16[192,768]{1,0:T(8,128)(2,1)S(1)}, u32[]{:S(2)}, u32[]{:S(2)}) collective-permute-start(bf16[192,768]{1,0:T(8,128)(2,1)S(1)} %get-tuple-element.21.refs_9_), channel_id=1, source_target_pairs={{0,32},{1,33},{2,34},{3,35},{4,36},{5,37},{6,38},{7,39},{8,232},{9... | collective-permute-start | bytes 884744 | tf_op jit(solution)/shard_map/ppermute | solution.py:46
  9.7 9.8 %collective-permute-start.11 = (bf16[192,768]{1,0:T(8,128)(2,1)S(1)}, bf16[192,768]{1,0:T(8,128)(2,1)S(1)}, u32[]{:S(2)}, u32[]{:S(2)}) collective-permute-start(bf16[192,768]{1,0:T(8,128)(2,1)S(1)} %collective-permute-done.9.refs_10_), channel_id=1, source_target_pairs={{0,32},{1,33},{2,34},{3,35},{4,36},{5,37},{6,38},{7,39},{8,232},{9... | collective-permute-start | bytes 884744 | tf_op jit(solution)/shard_map/ppermute | solution.py:46
  10.6 9.7 %collective-permute-start.1 = (bf16[384,384]{1,0:T(8,128)(2,1)S(1)}, bf16[384,384]{1,0:T(8,128)(2,1)S(1)}, u32[]{:S(2)}, u32[]{:S(2)}) collective-permute-start(bf16[384,384]{1,0:T(8,128)(2,1)S(1)} %constant_dynamic-update-slice_fusion.refs_0_), channel_id=1, source_target_pairs={{0,1},{1,2},{2,3},{3,0},{4,5},{5,6},{6,7},{7,4},{8,9},{9,10},{10,1... | collective-permute-start | bytes 884744 | tf_op jit(solution)/shard_map/ppermute | solution.py:46
  11.9 9.1 %collective-permute-start.2 = (bf16[384,384]{1,0:T(8,128)(2,1)S(1)}, bf16[384,384]{1,0:T(8,128)(2,1)S(1)}, u32[]{:S(2)}, u32[]{:S(2)}) collective-permute-start(bf16[384,384]{1,0:T(8,128)(2,1)S(1)} %constant_dynamic-update-slice_fusion.refs_0_), channel_id=1, source_target_pairs={{0,3},{1,0},{2,1},{3,2},{4,7},{5,4},{6,5},{7,6},{8,11},{9,8},{10,9... | collective-permute-start | bytes 884744 | tf_op jit(solution)/shard_map/ppermute | solution.py:46
  13.3 9.8 %collective-permute-start.3 = (bf16[384,384]{1,0:T(8,128)(2,1)S(1)}, bf16[384,384]{1,0:T(8,128)(2,1)S(1)}, u32[]{:S(2)}, u32[]{:S(2)}) collective-permute-start(bf16[384,384]{1,0:T(8,128)(2,1)S(1)} %constant_dynamic-update-slice_fusion.refs_0_), channel_id=1, source_target_pairs={{0,4},{1,5},{2,6},{3,7},{4,0},{5,1},{6,2},{7,3},{8,12},{9,13},{10,... | collective-permute-start | bytes 884744 | tf_op jit(solution)/shard_map/ppermute | solution.py:46
  16.0 7.7 %collective-permute-start.12 = (bf16[192,768]{1,0:T(8,128)(2,1)S(1)}, bf16[192,768]{1,0:T(8,128)(2,1)S(1)}, u32[]{:S(2)}, u32[]{:S(2)}) collective-permute-start(bf16[192,768]{1,0:T(8,128)(2,1)S(1)} %collective-permute-done.10.refs_11_), channel_id=1, source_target_pairs={{0,32},{1,33},{2,34},{3,35},{4,36},{5,37},{6,38},{7,39},{8,232},{9... | collective-permute-start | bytes 884744 | tf_op jit(solution)/shard_map/ppermute | solution.py:46
  19.5 8.8 %collective-permute-start.13 = (bf16[192,768]{1,0:T(8,128)(2,1)S(1)}, bf16[192,768]{1,0:T(8,128)(2,1)S(1)}, u32[]{:S(2)}, u32[]{:S(2)}) collective-permute-start(bf16[192,768]{1,0:T(8,128)(2,1)S(1)} %collective-permute-done.11.refs_12_), channel_id=1, source_target_pairs={{0,32},{1,33},{2,34},{3,35},{4,36},{5,37},{6,38},{7,39},{8,232},{9... | collective-permute-start | bytes 884744 | tf_op jit(solution)/shard_map/ppermute | solution.py:46
  20.3 5.6 %collective-permute-start.4 = (bf16[192,384]{1,0:T(8,128)(2,1)S(1)}, bf16[192,384]{1,0:T(8,128)(2,1)S(1)}, u32[]{:S(2)}, u32[]{:S(2)}) collective-permute-start(bf16[192,384]{1,0:T(8,128)(2,1)S(1)} %slice.8), channel_id=1, source_target_pairs={{0,1},{1,2},{2,3},{3,0},{4,5},{5,6},{6,7},{7,4},{8,9},{9,10},{10,1... | collective-permute-start | bytes 442376 | tf_op jit(solution)/shard_map/ppermute | solution.py:46
  21.0 7.3 %collective-permute-start.5 = (bf16[192,384]{1,0:T(8,128)(2,1)S(1)}, bf16[192,384]{1,0:T(8,128)(2,1)S(1)}, u32[]{:S(2)}, u32[]{:S(2)}) collective-permute-start(bf16[192,384]{1,0:T(8,128)(2,1)S(1)} %slice.9), channel_id=1, source_target_pairs={{0,3},{1,0},{2,1},{3,2},{4,7},{5,4},{6,5},{7,6},{8,11},{9,8},{10,9... | collective-permute-start | bytes 442376 | tf_op jit(solution)/shard_map/ppermute | solution.py:46
  23.1 9.0 %collective-permute-start.6 = (bf16[384,384]{1,0:T(8,128)(2,1)S(1)}, bf16[384,384]{1,0:T(8,128)(2,1)S(1)}, u32[]{:S(2)}, u32[]{:S(2)}) collective-permute-start(bf16[384,384]{1,0:T(8,128)(2,1)S(1)} %collective-permute-done.3.refs_3_), channel_id=1, source_target_pairs={{0,1},{1,2},{2,3},{3,0},{4,5},{5,6},{6,7},{7,4},{8,9},{9,10},{10,1... | collective-permute-start | bytes 884744 | tf_op jit(solution)/shard_map/ppermute | solution.py:46
  23.7 10.5 %collective-permute-start.7 = (bf16[384,384]{1,0:T(8,128)(2,1)S(1)}, bf16[384,384]{1,0:T(8,128)(2,1)S(1)}, u32[]{:S(2)}, u32[]{:S(2)}) collective-permute-start(bf16[384,384]{1,0:T(8,128)(2,1)S(1)} %collective-permute-done.3.refs_3_), channel_id=1, source_target_pairs={{0,3},{1,0},{2,1},{3,2},{4,7},{5,4},{6,5},{7,6},{8,11},{9,8},{10,9... | collective-permute-start | bytes 884744 | tf_op jit(solution)/shard_map/ppermute | solution.py:46
  25.8 8.4 %collective-permute-start.14 = (bf16[192,768]{1,0:T(8,128)(2,1)S(1)}, bf16[192,768]{1,0:T(8,128)(2,1)S(1)}, u32[]{:S(2)}, u32[]{:S(2)}) collective-permute-start(bf16[192,768]{1,0:T(8,128)(2,1)S(1)} %collective-permute-done.12.refs_13_), channel_id=1, source_target_pairs={{0,32},{1,33},{2,34},{3,35},{4,36},{5,37},{6,38},{7,39},{8,232},{9... | collective-permute-start | bytes 884744 | tf_op jit(solution)/shard_map/ppermute | solution.py:46
  28.3 9.1 %collective-permute-start.15 = (bf16[192,768]{1,0:T(8,128)(2,1)S(1)}, bf16[192,768]{1,0:T(8,128)(2,1)S(1)}, u32[]{:S(2)}, u32[]{:S(2)}) collective-permute-start(bf16[192,768]{1,0:T(8,128)(2,1)S(1)} %collective-permute-done.13.refs_14_), channel_id=1, source_target_pairs={{0,32},{1,33},{2,34},{3,35},{4,36},{5,37},{6,38},{7,39},{8,232},{9... | collective-permute-start | bytes 884744 | tf_op jit(solution)/shard_map/ppermute | solution.py:46
  29.8 10.6 %collective-permute-start.8 = (bf16[384,384]{1,0:T(8,128)(2,1)S(1)}, bf16[384,384]{1,0:T(8,128)(2,1)S(1)}, u32[]{:S(2)}, u32[]{:S(2)}) collective-permute-start(bf16[384,384]{1,0:T(8,128)(2,1)S(1)} %pad_maximum_fusion.6), channel_id=1, source_target_pairs={{0,4},{1,5},{2,6},{3,7},{4,0},{5,1},{6,2},{7,3},{8,12},{9,13},{10,... | collective-permute-start | bytes 884744 | tf_op jit(solution)/shard_map/ppermute | solution.py:46
  32.2 12.8 %collective-permute-start.17 = (bf16[384,768]{1,0:T(8,128)(2,1)S(1)}, bf16[384,768]{1,0:T(8,128)(2,1)S(1)}, u32[]{:S(2)}, u32[]{:S(2)}) collective-permute-start(bf16[384,768]{1,0:T(8,128)(2,1)S(1)} %pad_maximum_fusion), channel_id=1, source_target_pairs={{0,8},{1,9},{2,10},{3,11},{4,12},{5,13},{6,14},{7,15},{8,0},{9,1},... | collective-permute-start | bytes 1769480 | tf_op jit(solution)/shard_map/ppermute | solution.py:46
  34.2 8.0 %collective-permute-start.16 = (bf16[192,768]{1,0:T(8,128)(2,1)S(1)}, bf16[192,768]{1,0:T(8,128)(2,1)S(1)}, u32[]{:S(2)}, u32[]{:S(2)}) collective-permute-start(bf16[192,768]{1,0:T(8,128)(2,1)S(1)} %collective-permute-done.14.refs_15_), channel_id=1, source_target_pairs={{0,32},{1,33},{2,34},{3,35},{4,36},{5,37},{6,38},{7,39},{8,232},{9... | collective-permute-start | bytes 884744 | tf_op jit(solution)/shard_map/ppermute | solution.py:46
  37.4 8.8 %collective-permute-start.18 = (bf16[384,768]{1,0:T(8,128)(2,1)S(1)}, bf16[384,768]{1,0:T(8,128)(2,1)S(1)}, u32[]{:S(2)}, u32[]{:S(2)}) collective-permute-start(bf16[384,768]{1,0:T(8,128)(2,1)S(1)} %pad_maximum_fusion.1), channel_id=1, source_target_pairs={{0,8},{1,9},{2,10},{3,11},{4,12},{5,13},{6,14},{7,15},{8,0},{9,1},... | collective-permute-start | bytes 1769480 | tf_op jit(solution)/shard_map/ppermute | solution.py:46
  37.5 8.7 %collective-permute-start.19 = (bf16[384,768]{1,0:T(8,128)(2,1)S(1)}, bf16[384,768]{1,0:T(8,128)(2,1)S(1)}, u32[]{:S(2)}, u32[]{:S(2)}) collective-permute-start(bf16[384,768]{1,0:T(8,128)(2,1)S(1)} %pad_maximum_fusion.2), channel_id=1, source_target_pairs={{0,8},{1,9},{2,10},{3,11},{4,12},{5,13},{6,14},{7,15},{8,0},{9,1},... | collective-permute-start | bytes 1769480 | tf_op jit(solution)/shard_map/ppermute | solution.py:46
  42.2 4.0 %collective-permute-start.20 = (bf16[192,768]{1,0:T(8,128)(2,1)S(1)}, bf16[192,768]{1,0:T(8,128)(2,1)S(1)}, u32[]{:S(2)}, u32[]{:S(2)}) collective-permute-start(bf16[192,768]{1,0:T(8,128)(2,1)S(1)} %collective-permute-done.16.a4), channel_id=1, source_target_pairs={{0,8},{1,9},{2,10},{3,11},{4,12},{5,13},{6,14},{7,15},{8,0},{9,1},... | collective-permute-start | bytes 884744 | tf_op jit(solution)/shard_map/ppermute | solution.py:46
  46.2 2.2 %copy-start = (s32[48,48]{1,0:T(8,128)S(1)}, s32[48,48]{1,0:T(8,128)}, u32[]{:S(2)}) copy-start(s32[48,48]{1,0:T(8,128)} %pattern.3) | copy-start | bytes 27652
  46.2 2.2 %copy-start.1 = (s32[48,48]{1,0:T(8,128)S(1)}, s32[48,48]{1,0:T(8,128)}, u32[]{:S(2)}) copy-start(s32[48,48]{1,0:T(8,128)} %keep.1) | copy-start | bytes 27652
  47.0 8.3 %collective-permute-start.21 = (bf16[192,768]{1,0:T(8,128)(2,1)S(1)}, bf16[192,768]{1,0:T(8,128)(2,1)S(1)}, u32[]{:S(2)}, u32[]{:S(2)}) collective-permute-start(bf16[192,768]{1,0:T(8,128)(2,1)S(1)} %shard_map.41), channel_id=1, source_target_pairs={{0,16},{1,17},{2,18},{3,19},{4,20},{5,21},{6,22},{7,23},{8,24},{9,... | collective-permute-start | bytes 884744 | tf_op jit(solution)/shard_map/ppermute | solution.py:46
  55.4 2.5 %collective-permute-start.22 = (bf16[192,768]{1,0:T(8,128)(2,1)S(1)}, bf16[192,768]{1,0:T(8,128)(2,1)S(1)}, u32[]{:S(2)}, u32[]{:S(2)}) collective-permute-start(bf16[192,768]{1,0:T(8,128)(2,1)S(1)} %subtract_convert_fusion.refs_1_), channel_id=1, source_target_pairs={{0,8},{1,9},{2,10},{3,11},{4,12},{5,13},{6,14},{7,15},{8,0},{9,1},... | collective-permute-start | bytes 884744 | tf_op jit(solution)/shard_map/ppermute | solution.py:46
  56.7 5.9 %collective-permute-start.23 = (bf16[192,768]{1,0:T(8,128)(2,1)S(1)}, bf16[192,768]{1,0:T(8,128)(2,1)S(1)}, u32[]{:S(2)}, u32[]{:S(2)}) collective-permute-start(bf16[192,768]{1,0:T(8,128)(2,1)S(1)} %subtract_convert_fusion.refs_1_), channel_id=1, source_target_pairs={{0,32},{1,33},{2,34},{3,35},{4,36},{5,37},{6,38},{7,39},{8,232},{9... | collective-permute-start | bytes 884744 | tf_op jit(solution)/shard_map/ppermute | solution.py:46
  57.9 7.8 %collective-permute-start.24 = (bf16[192,768]{1,0:T(8,128)(2,1)S(1)}, bf16[192,768]{1,0:T(8,128)(2,1)S(1)}, u32[]{:S(2)}, u32[]{:S(2)}) collective-permute-start(bf16[192,768]{1,0:T(8,128)(2,1)S(1)} %collective-permute-done.22.refs_2_), channel_id=1, source_target_pairs={{0,32},{1,33},{2,34},{3,35},{4,36},{5,37},{6,38},{7,39},{8,232},{9... | collective-permute-start | bytes 884744 | tf_op jit(solution)/shard_map/ppermute | solution.py:46
  62.6 6.0 %collective-permute-start.25 = (bf16[192,768]{1,0:T(8,128)(2,1)S(1)}, bf16[192,768]{1,0:T(8,128)(2,1)S(1)}, u32[]{:S(2)}, u32[]{:S(2)}) collective-permute-start(bf16[192,768]{1,0:T(8,128)(2,1)S(1)} %collective-permute-done.23.refs_3_), channel_id=1, source_target_pairs={{0,32},{1,33},{2,34},{3,35},{4,36},{5,37},{6,38},{7,39},{8,232},{9... | collective-permute-start | bytes 884744 | tf_op jit(solution)/shard_map/ppermute | solution.py:46
  65.8 6.3 %collective-permute-start.26 = (bf16[192,768]{1,0:T(8,128)(2,1)S(1)}, bf16[192,768]{1,0:T(8,128)(2,1)S(1)}, u32[]{:S(2)}, u32[]{:S(2)}) collective-permute-start(bf16[192,768]{1,0:T(8,128)(2,1)S(1)} %collective-permute-done.24.refs_4_), channel_id=1, source_target_pairs={{0,32},{1,33},{2,34},{3,35},{4,36},{5,37},{6,38},{7,39},{8,232},{9... | collective-permute-start | bytes 884744 | tf_op jit(solution)/shard_map/ppermute | solution.py:46
  68.6 7.4 %collective-permute-start.27 = (bf16[192,768]{1,0:T(8,128)(2,1)S(1)}, bf16[192,768]{1,0:T(8,128)(2,1)S(1)}, u32[]{:S(2)}, u32[]{:S(2)}) collective-permute-start(bf16[192,768]{1,0:T(8,128)(2,1)S(1)} %collective-permute-done.25.refs_5_), channel_id=1, source_target_pairs={{0,32},{1,33},{2,34},{3,35},{4,36},{5,37},{6,38},{7,39},{8,232},{9... | collective-permute-start | bytes 884744 | tf_op jit(solution)/shard_map/ppermute | solution.py:46
  72.1 8.7 %collective-permute-start.28 = (bf16[192,768]{1,0:T(8,128)(2,1)S(1)}, bf16[192,768]{1,0:T(8,128)(2,1)S(1)}, u32[]{:S(2)}, u32[]{:S(2)}) collective-permute-start(bf16[192,768]{1,0:T(8,128)(2,1)S(1)} %collective-permute-done.26.refs_6_), channel_id=1, source_target_pairs={{0,32},{1,33},{2,34},{3,35},{4,36},{5,37},{6,38},{7,39},{8,232},{9... | collective-permute-start | bytes 884744 | tf_op jit(solution)/shard_map/ppermute | solution.py:46
  74.0 14.5 %collective-permute-start.30 = (bf16[384,768]{1,0:T(8,128)(2,1)S(1)}, bf16[384,768]{1,0:T(8,128)(2,1)S(1)}, u32[]{:S(2)}, u32[]{:S(2)}) collective-permute-start(bf16[384,768]{1,0:T(8,128)(2,1)S(1)} %pad_maximum_fusion.3), channel_id=1, source_target_pairs={{0,8},{1,9},{2,10},{3,11},{4,12},{5,13},{6,14},{7,15},{8,0},{9,1},... | collective-permute-start | bytes 1769480 | tf_op jit(solution)/shard_map/ppermute | solution.py:46
  76.0 9.3 %collective-permute-start.29 = (bf16[192,768]{1,0:T(8,128)(2,1)S(1)}, bf16[192,768]{1,0:T(8,128)(2,1)S(1)}, u32[]{:S(2)}, u32[]{:S(2)}) collective-permute-start(bf16[192,768]{1,0:T(8,128)(2,1)S(1)} %collective-permute-done.27.refs_7_), channel_id=1, source_target_pairs={{0,32},{1,33},{2,34},{3,35},{4,36},{5,37},{6,38},{7,39},{8,232},{9... | collective-permute-start | bytes 884744 | tf_op jit(solution)/shard_map/ppermute | solution.py:46
  79.0 9.6 %collective-permute-start.31 = (bf16[384,768]{1,0:T(8,128)(2,1)S(1)}, bf16[384,768]{1,0:T(8,128)(2,1)S(1)}, u32[]{:S(2)}, u32[]{:S(2)}) collective-permute-start(bf16[384,768]{1,0:T(8,128)(2,1)S(1)} %pad_maximum_fusion.4), channel_id=1, source_target_pairs={{0,8},{1,9},{2,10},{3,11},{4,12},{5,13},{6,14},{7,15},{8,0},{9,1},... | collective-permute-start | bytes 1769480 | tf_op jit(solution)/shard_map/ppermute | solution.py:46
  80.8 9.0 %collective-permute-start.32 = (bf16[384,768]{1,0:T(8,128)(2,1)S(1)}, bf16[384,768]{1,0:T(8,128)(2,1)S(1)}, u32[]{:S(2)}, u32[]{:S(2)}) collective-permute-start(bf16[384,768]{1,0:T(8,128)(2,1)S(1)} %pad_maximum_fusion.5), channel_id=1, source_target_pairs={{0,8},{1,9},{2,10},{3,11},{4,12},{5,13},{6,14},{7,15},{8,0},{9,1},... | collective-permute-start | bytes 1769480 | tf_op jit(solution)/shard_map/ppermute | solution.py:46
  85.3 4.5 %collective-permute-start.33 = (bf16[192,768]{1,0:T(8,128)(2,1)S(1)}, bf16[192,768]{1,0:T(8,128)(2,1)S(1)}, u32[]{:S(2)}, u32[]{:S(2)}) collective-permute-start(bf16[192,768]{1,0:T(8,128)(2,1)S(1)} %collective-permute-done.29.a4), channel_id=1, source_target_pairs={{0,8},{1,9},{2,10},{3,11},{4,12},{5,13},{6,14},{7,15},{8,0},{9,1},... | collective-permute-start | bytes 884744 | tf_op jit(solution)/shard_map/ppermute | solution.py:46
  90.6 8.3 %collective-permute-start.34 = (bf16[192,768]{1,0:T(8,128)(2,1)S(1)}, bf16[192,768]{1,0:T(8,128)(2,1)S(1)}, u32[]{:S(2)}, u32[]{:S(2)}) collective-permute-start(bf16[192,768]{1,0:T(8,128)(2,1)S(1)} %shard_map.44), channel_id=1, source_target_pairs={{0,16},{1,17},{2,18},{3,19},{4,20},{5,21},{6,22},{7,23},{8,24},{9,... | collective-permute-start | bytes 884744 | tf_op jit(solution)/shard_map/ppermute | solution.py:46

commit v6 on v5

--- a/solution.py
+++ b/solution.py
@@ -36,6 +36,7 @@
 EAST = moves(lambda z, yl, core, yh, x: (z, yl, core, yh, x + 1))
 WEST = moves(lambda z, yl, core, yh, x: (z, yl, core, yh, x - 1))
 NORTH, SOUTH = along_y(1), along_y(-1)
+ALONG_X = moves(lambda z, yl, core, yh, x: (z, yl, core, yh, x + 1 - 2 * core))
 ACROSS = moves(lambda z, yl, core, yh, x: (z, yl, core, 1 - yh, x))
 TWIN = moves(lambda z, yl, core, yh, x: (z, 1 - yl, core, yh, x))
 CORE = moves(lambda z, yl, core, yh, x: (z, yl, 1 - core, yh, x))
@@ -96,22 +97,21 @@
 
 
 def fill_left(left, pieces):
-    own, w, e, y, x2, x2_too, yw, ye, y2 = pieces
+    own, w, e, y, x2, yw, ye, y2 = pieces
     _, _, _, col = place()
     yh, x = col // 4, col % 4
 
-    def put(ref, dx, dy, first=0):
+    def put(ref, dx, dy):
         index = lax.rem(yh + dy, 2) * 4 + lax.rem(x + dx + 4, 4)
         for core in range(2):
             columns = slice(ROWS * core, ROWS * (core + 1))
-            left[index, core, first : first + ref.shape[0], :] = ref[:, columns]
+            left[index, core] = ref[:, columns]
 
     put(own, 0, 0)
     put(w, -1, 0)
     put(e, 1, 0)
     put(y, 0, 1)
     put(x2, 2, 0)
-    put(x2_too, 2, 0, ROWS)
     put(yw, -1, 1)
     put(ye, 1, 1)
     put(y2, 2, 1)
@@ -137,23 +137,25 @@
 
 
 def square_kernel(*refs):
-    total, left = refs[17:]
-    fill_left(left, refs[:9])
-    total[...] = near_sums(left, refs[9:17])
+    total, left = refs[16:]
+    fill_left(left, refs[:8])
+    total[...] = near_sums(left, refs[8:16])
 
 
 def update_kernel(*refs):
     refs[9][...] = near_sums(refs[0], refs[1:9])
 
 
-def last_kernel(half, left, total, a4, s1, s2, s3, s4, result):
+def last_kernel(half, left, total, a4, *refs):
+    *far, s4, result = refs
     z, _, core, _ = place()
     sign = 2 * core - 1
     rows = slice(ROWS * half, ROWS * (half + 1))
     parts = [(z + 4, core, a4, 0), (z + 4, 1 - core, s4, 0)]
-    for s, ref in enumerate((s1, s2, s3)):
-        parts.append((z - sign * (s + 1), 1 - core, ref, 0))
-        parts.append((z - sign * (s + 1), core, ref, ROWS))
+    swapped = [(ref, first) for ref in far for first in range(0, ref.shape[0], 2 * ROWS)]
+    for s, (ref, first) in enumerate(swapped):
+        parts.append((z - sign * (s + 1), 1 - core, ref, first))
+        parts.append((z - sign * (s + 1), core, ref, first + ROWS))
     result[...] = (total[rows] + multiply(left, rows, parts)).astype(result.dtype)
 
 
@@ -206,16 +208,15 @@
     a3, b3 = step(a2, "a3"), step(b2, "b3")
     a4 = step(a3, "a4")
     sums = multiply_by([piece, other, a1, b1, a2, b2, a3, b3])
-    far = [send(cat(a, b), CORE) for a, b in ((a1, b1), (a2, b2), (a3, b3))]
+    far = [send(cat(a1, b1), CORE), send(after(cat(a2, b2), *awaited.get("s2", ())), CORE), send(cat(a3, b3), CORE)]
     return sums, [a4, *far, send(after(a4, sums[0]), CORE)]
 
 
 def row(piece):
     w, e, y = send(piece, EAST), send(piece, WEST), send(piece, ACROSS)
-    x2, x2_too = send(w[:ROWS], EAST), send(e[ROWS:], WEST)
+    x2 = send(jnp.where(place()[2] == 0, w, e), ALONG_X)
     yw, ye = send(y, EAST), send(y, WEST)
-    y2 = send(cat(x2, x2_too), ACROSS)
-    return [piece, w, e, y, x2, x2_too, yw, ye, y2]
+    return [piece, w, e, y, x2, yw, ye, send(x2, ACROSS)]
 
 
 FLOPS = 2 * ROWS * COLS * 6144
@@ -252,7 +253,7 @@
     def square(near):
         return call(square_kernel, [*pieces, *near], [SUMS, struct(8, 2, HALF, ROWS)], [], FLOPS // 2)
 
-    (total, left), last = ring(x, square, a2=pieces[:1], a3=pieces[1:4], b3=pieces[4:6], a4=pieces[6:8])
+    (total, left), last = ring(x, square, a2=pieces[:1], a3=pieces[1:4], b3=pieces[4:5], s2=pieces[5:])
     weight = (eye - sums(left, total, last) * kept_square).astype(BF16)
 
     def update(near):

time: 99.8 us -> 99.3 us (level)
  starting transfers between devices: 66.7 us -> 60.8 us
  waiting for transfers between devices: 22.5 us -> 28 us
    ppermute x35 -> x34, starting transfers between devices: 66.7 us -> 60.8 us  [send(): return lax.ppermute(value, AXES, pairs)]
    ppermute x35 -> x34, waiting for transfers between devices: 22.5 us -> 28 us  [send(): return lax.ppermute(value, AXES, pairs)]
  transfers between devices with their start and end apart: 35 -> 34, of which waited for: 9 -> 13; matrix products, arithmetic and copies ran while one was open for 0% -> 0% of each run, Pallas kernels for 6% -> 6%
where the time goes in v6:
time: 99.3 us; the launch traced here: 99.2 us
  starting transfers between devices  60.8 us (61%)
  waiting for transfers between devices  28 us (28%)
  Pallas kernels  8.96 us (9%)
  other arithmetic  1.19 us (1%)
    ppermute x34, starting transfers between devices, send(): return lax.ppermute(value, AXES, pairs)  60.8 us
    ppermute x34, waiting for transfers between devices, send(): return lax.ppermute(value, AXES, pairs)  28 us
    pallas_call x8, Pallas kernels, call(): pl.pallas_call(kernel, in_specs=specs or [SMEM if arg.dtype == jnp.int32...  8.96 us
  transfers between devices with their start and end apart: 34, of which 13 were waited for; matrix products, arithmetic and copies ran while one was open for 0% of the time, Pallas kernels for 6%

profile of v6, /device:TPU:1, one launch (start us, length us, event | category | flops | bytes accessed | tf_op | source)
XLA Modules:
  0.0 99.2 jit_solution(14202693196047540404)
XLA Ops:
  0.0 1.2 %shard_map.37 = (bf16[192,768]{1,0:T(8,128)(2,1)S(1)}, bf16[192,384]{1,0:T(8,128)(2,1)S(1)}, bf16[192,384]{1,0:T(8,128)(2,1)S(1)}) custom-call(s32[48,48]{1,0:T(8,128)} %pattern.3, bf16[192,768]{1,0:T(8,128)(2,1)} %matrix.1), custom_call_target="tpu_custom_call" | custom-call | tf_op jit(solution)/shard_map/pallas_call | solution.py:186
  1.2 2.2 %collective-permute-start = (bf16[192,384]{1,0:T(8,128)(2,1)S(1)}, bf16[192,384]{1,0:T(8,128)(2,1)S(1)}, u32[]{:S(2)}, u32[]{:S(2)}) collective-permute-start(bf16[192,384]{1,0:T(8,128)(2,1)S(1)} %get-tuple-element.20), channel_id=1, source_target_pairs={{0,16},{1,17},{2,18},{3,19},{4,20},{5,21},{6,22},{7,23},{8,24},{9,... | collective-permute-start | bytes 442376 | tf_op jit(solution)/shard_map/ppermute | solution.py:47
  3.4 1.2 %collective-permute-start.8 = (bf16[192,768]{1,0:T(8,128)(2,1)S(1)}, bf16[192,768]{1,0:T(8,128)(2,1)S(1)}, u32[]{:S(2)}, u32[]{:S(2)}) collective-permute-start(bf16[192,768]{1,0:T(8,128)(2,1)S(1)} %get-tuple-element.21.refs_8_), channel_id=1, source_target_pairs={{0,8},{1,9},{2,10},{3,11},{4,12},{5,13},{6,14},{7,15},{8,0},{9,1},... | collective-permute-start | bytes 884744 | tf_op jit(solution)/shard_map/ppermute | solution.py:47
  4.7 5.3 %collective-permute-start.9 = (bf16[192,768]{1,0:T(8,128)(2,1)S(1)}, bf16[192,768]{1,0:T(8,128)(2,1)S(1)}, u32[]{:S(2)}, u32[]{:S(2)}) collective-permute-start(bf16[192,768]{1,0:T(8,128)(2,1)S(1)} %get-tuple-element.21.refs_8_), channel_id=1, source_target_pairs={{0,32},{1,33},{2,34},{3,35},{4,36},{5,37},{6,38},{7,39},{8,232},{9... | collective-permute-start | bytes 884744 | tf_op jit(solution)/shard_map/ppermute | solution.py:47
  10.0 0.0 collective-permute-done
  10.0 1.3 %collective-permute-start.1 = (bf16[384,384]{1,0:T(8,128)(2,1)S(1)}, bf16[384,384]{1,0:T(8,128)(2,1)S(1)}, u32[]{:S(2)}, u32[]{:S(2)}) collective-permute-start(bf16[384,384]{1,0:T(8,128)(2,1)S(1)} %constant_dynamic-update-slice_fusion.refs_0_), channel_id=1, source_target_pairs={{0,1},{1,2},{2,3},{3,0},{4,5},{5,6},{6,7},{7,4},{8,9},{9,10},{10,1... | collective-permute-start | bytes 884744 | tf_op jit(solution)/shard_map/ppermute | solution.py:47
  11.3 1.5 %collective-permute-start.2 = (bf16[384,384]{1,0:T(8,128)(2,1)S(1)}, bf16[384,384]{1,0:T(8,128)(2,1)S(1)}, u32[]{:S(2)}, u32[]{:S(2)}) collective-permute-start(bf16[384,384]{1,0:T(8,128)(2,1)S(1)} %constant_dynamic-update-slice_fusion.refs_0_), channel_id=1, source_target_pairs={{0,3},{1,0},{2,1},{3,2},{4,7},{5,4},{6,5},{7,6},{8,11},{9,8},{10,9... | collective-permute-start | bytes 884744 | tf_op jit(solution)/shard_map/ppermute | solution.py:47
  12.8 2.4 %collective-permute-start.10 = (bf16[192,768]{1,0:T(8,128)(2,1)S(1)}, bf16[192,768]{1,0:T(8,128)(2,1)S(1)}, u32[]{:S(2)}, u32[]{:S(2)}) collective-permute-start(bf16[192,768]{1,0:T(8,128)(2,1)S(1)} %collective-permute-done.8.refs_9_), channel_id=1, source_target_pairs={{0,32},{1,33},{2,34},{3,35},{4,36},{5,37},{6,38},{7,39},{8,232},{9... | collective-permute-start | bytes 884744 | tf_op jit(solution)/shard_map/ppermute | solution.py:47
  15.2 2.9 %collective-permute-start.3 = (bf16[384,384]{1,0:T(8,128)(2,1)S(1)}, bf16[384,384]{1,0:T(8,128)(2,1)S(1)}, u32[]{:S(2)}, u32[]{:S(2)}) collective-permute-start(bf16[384,384]{1,0:T(8,128)(2,1)S(1)} %constant_dynamic-update-slice_fusion.refs_0_), channel_id=1, source_target_pairs={{0,4},{1,5},{2,6},{3,7},{4,0},{5,1},{6,2},{7,3},{8,12},{9,13},{10,... | collective-permute-start | bytes 884744 | tf_op jit(solution)/shard_map/ppermute | solution.py:47
  18.1 0.7 collective-permute-start.11
  18.9 1.3 %collective-permute-done.1.refs_1_ = bf16[384,384]{1,0:T(8,128)(2,1)S(1)} collective-permute-done((bf16[384,384]{1,0:T(8,128)(2,1)S(1)}, bf16[384,384]{1,0:T(8,128)(2,1)S(1)}, u32[]{:S(2)}, u32[]{:S(2)}) %collective-permute-start.1) | collective-permute-done | bytes 294944 | tf_op jit(solution)/shard_map/ppermute | solution.py:47
  20.2 2.6 %collective-permute-start.4 = (bf16[384,384]{1,0:T(8,128)(2,1)S(1)}, bf16[384,384]{1,0:T(8,128)(2,1)S(1)}, u32[]{:S(2)}, u32[]{:S(2)}) collective-permute-start(bf16[384,384]{1,0:T(8,128)(2,1)S(1)} %broadcast_select_fusion), channel_id=1, source_target_pairs={{0,1},{1,2},{2,3},{3,0},{4,5},{5,6},{6,7},{7,4},{8,11},{9,8},{10,9... | collective-permute-start | bytes 884744 | tf_op jit(solution)/shard_map/ppermute | solution.py:47
  22.8 0.0 collective-permute-done.10.refs_11_
  22.8 0.4 collective-permute-start.12
  23.2 1.1 %collective-permute-done.3.refs_3_ = bf16[384,384]{1,0:T(8,128)(2,1)S(1)} collective-permute-done((bf16[384,384]{1,0:T(8,128)(2,1)S(1)}, bf16[384,384]{1,0:T(8,128)(2,1)S(1)}, u32[]{:S(2)}, u32[]{:S(2)}) %collective-permute-start.3) | collective-permute-done | bytes 294944 | tf_op jit(solution)/shard_map/ppermute | solution.py:47
  24.4 1.6 %collective-permute-start.13 = (bf16[192,768]{1,0:T(8,128)(2,1)S(1)}, bf16[192,768]{1,0:T(8,128)(2,1)S(1)}, u32[]{:S(2)}, u32[]{:S(2)}) collective-permute-start(bf16[192,768]{1,0:T(8,128)(2,1)S(1)} %collective-permute-done.11.refs_12_), channel_id=1, source_target_pairs={{0,32},{1,33},{2,34},{3,35},{4,36},{5,37},{6,38},{7,39},{8,232},{9... | collective-permute-start | bytes 884744 | tf_op jit(solution)/shard_map/ppermute | solution.py:47
  26.0 0.0 collective-permute-start.5
  26.0 2.7 %collective-permute-start.6 = (bf16[384,384]{1,0:T(8,128)(2,1)S(1)}, bf16[384,384]{1,0:T(8,128)(2,1)S(1)}, u32[]{:S(2)}, u32[]{:S(2)}) collective-permute-start(bf16[384,384]{1,0:T(8,128)(2,1)S(1)} %collective-permute-done.3.refs_3_), channel_id=1, source_target_pairs={{0,3},{1,0},{2,1},{3,2},{4,7},{5,4},{6,5},{7,6},{8,11},{9,8},{10,9... | collective-permute-start | bytes 884744 | tf_op jit(solution)/shard_map/ppermute | solution.py:47
  28.6 0.0 collective-permute-done.4.refs_4_
  28.6 2.3 %collective-permute-start.7 = (bf16[384,384]{1,0:T(8,128)(2,1)S(1)}, bf16[384,384]{1,0:T(8,128)(2,1)S(1)}, u32[]{:S(2)}, u32[]{:S(2)}) collective-permute-start(bf16[384,384]{1,0:T(8,128)(2,1)S(1)} %collective-permute-done.4.refs_4_), channel_id=1, source_target_pairs={{0,4},{1,5},{2,6},{3,7},{4,0},{5,1},{6,2},{7,3},{8,12},{9,13},{10,... | collective-permute-start | bytes 884744 | tf_op jit(solution)/shard_map/ppermute | solution.py:47
  30.9 0.0 collective-permute-start.14
  31.0 0.9 collective-permute-done.13.refs_14_
  31.8 1.6 %collective-permute-start.16 = (bf16[384,768]{1,0:T(8,128)(2,1)S(1)}, bf16[384,768]{1,0:T(8,128)(2,1)S(1)}, u32[]{:S(2)}, u32[]{:S(2)}) collective-permute-start(bf16[384,768]{1,0:T(8,128)(2,1)S(1)} %pad_maximum_fusion), channel_id=1, source_target_pairs={{0,8},{1,9},{2,10},{3,11},{4,12},{5,13},{6,14},{7,15},{8,0},{9,1},... | collective-permute-start | bytes 1769480 | tf_op jit(solution)/shard_map/ppermute | solution.py:47
  33.5 2.7 %collective-permute-done.5.refs_5_ = bf16[384,384]{1,0:T(8,128)(2,1)S(1)} collective-permute-done((bf16[384,384]{1,0:T(8,128)(2,1)S(1)}, bf16[384,384]{1,0:T(8,128)(2,1)S(1)}, u32[]{:S(2)}, u32[]{:S(2)}) %collective-permute-start.5) | collective-permute-done | bytes 294944 | tf_op jit(solution)/shard_map/ppermute | solution.py:47
  36.2 0.3 collective-permute-start.15
  36.4 2.2 %collective-permute-done.7.refs_7_ = bf16[384,384]{1,0:T(8,128)(2,1)S(1)} collective-permute-done((bf16[384,384]{1,0:T(8,128)(2,1)S(1)}, bf16[384,384]{1,0:T(8,128)(2,1)S(1)}, u32[]{:S(2)}, u32[]{:S(2)}) %collective-permute-start.7) | collective-permute-done | bytes 294944 | tf_op jit(solution)/shard_map/ppermute | solution.py:47
  38.6 1.0 collective-permute-start.17
  39.6 1.5 %collective-permute-start.18 = (bf16[384,768]{1,0:T(8,128)(2,1)S(1)}, bf16[384,768]{1,0:T(8,128)(2,1)S(1)}, u32[]{:S(2)}, u32[]{:S(2)}) collective-permute-start(bf16[384,768]{1,0:T(8,128)(2,1)S(1)} %pad_maximum_fusion.2), channel_id=1, source_target_pairs={{0,8},{1,9},{2,10},{3,11},{4,12},{5,13},{6,14},{7,15},{8,0},{9,1},... | collective-permute-start | bytes 1769480 | tf_op jit(solution)/shard_map/ppermute | solution.py:47
  41.1 1.8 %shard_map.38 = (f32[384,768]{1,0:T(8,128)S(1)}, bf16[8,2,384,192]{3,2,1,0:T(8,128)(2,1)S(1)}) custom-call(bf16[384,384]{1,0:T(8,128)(2,1)S(1)} %constant_dynamic-update-slice_fusion.refs_0_, bf16[384,384]{1,0:T(8,128)(2,1)S(1)} %collective-permute-done.1.refs_1_, bf16[384,384]{1,0:T(8,128)(2,1)S(1)} %collective-permute-done.2.refs_2_, ...), custom_call_target="tpu_custom_call" | custom-call | flops 905969664 | tf_op jit(solution)/shard_map/pallas_call | solution.py:186
  42.9 0.0 collective-permute-done.15.a4
  42.9 1.6 %collective-permute-start.19 = (bf16[192,768]{1,0:T(8,128)(2,1)S(1)}, bf16[192,768]{1,0:T(8,128)(2,1)S(1)}, u32[]{:S(2)}, u32[]{:S(2)}) collective-permute-start(bf16[192,768]{1,0:T(8,128)(2,1)S(1)} %collective-permute-done.15.a4), channel_id=1, source_target_pairs={{0,8},{1,9},{2,10},{3,11},{4,12},{5,13},{6,14},{7,15},{8,0},{9,1},... | collective-permute-start | bytes 884744 | tf_op jit(solution)/shard_map/ppermute | solution.py:47
  44.5 1.2 %collective-permute-done.19.refs_3_ = bf16[192,768]{1,0:T(8,128)(2,1)S(1)} collective-permute-done((bf16[192,768]{1,0:T(8,128)(2,1)S(1)}, bf16[192,768]{1,0:T(8,128)(2,1)S(1)}, u32[]{:S(2)}, u32[]{:S(2)}) %collective-permute-start.19) | collective-permute-done | bytes 294944 | tf_op jit(solution)/shard_map/ppermute | solution.py:47
  45.7 0.0 collective-permute-done.17.refs_1_
  45.7 0.0 collective-permute-done.18.refs_2_
  45.7 0.8 shard_map.41
  46.5 0.7 collective-permute-start.20
  47.3 1.5 %shard_map.39 = (f32[192,768]{1,0:T(8,128)S(1)}, f32[192,768]{1,0:T(8,128)S(1)}, f32[192,768]{1,0:T(8,128)S(1)}) custom-call(s32[48,48]{1,0:T(8,128)S(1)} %copy-done, s32[48,48]{1,0:T(8,128)S(1)} %copy-done.1), custom_call_target="tpu_custom_call" | custom-call | flops 147456 | tf_op jit(solution)/shard_map/pallas_call | solution.py:186
  48.8 0.8 shard_map.40
  49.5 5.3 %collective-permute-done.20 = bf16[192,768]{1,0:T(8,128)(2,1)S(1)} collective-permute-done((bf16[192,768]{1,0:T(8,128)(2,1)S(1)}, bf16[192,768]{1,0:T(8,128)(2,1)S(1)}, u32[]{:S(2)}, u32[]{:S(2)}) %collective-permute-start.20) | collective-permute-done | bytes 294944 | tf_op jit(solution)/shard_map/ppermute | solution.py:47
  54.8 0.1 subtract_convert_fusion.refs_1_
  54.9 1.3 %collective-permute-start.21 = (bf16[192,768]{1,0:T(8,128)(2,1)S(1)}, bf16[192,768]{1,0:T(8,128)(2,1)S(1)}, u32[]{:S(2)}, u32[]{:S(2)}) collective-permute-start(bf16[192,768]{1,0:T(8,128)(2,1)S(1)} %subtract_convert_fusion.refs_1_), channel_id=1, source_target_pairs={{0,8},{1,9},{2,10},{3,11},{4,12},{5,13},{6,14},{7,15},{8,0},{9,1},... | collective-permute-start | bytes 884744 | tf_op jit(solution)/shard_map/ppermute | solution.py:47
  56.3 1.3 %collective-permute-start.22 = (bf16[192,768]{1,0:T(8,128)(2,1)S(1)}, bf16[192,768]{1,0:T(8,128)(2,1)S(1)}, u32[]{:S(2)}, u32[]{:S(2)}) collective-permute-start(bf16[192,768]{1,0:T(8,128)(2,1)S(1)} %subtract_convert_fusion.refs_1_), channel_id=1, source_target_pairs={{0,32},{1,33},{2,34},{3,35},{4,36},{5,37},{6,38},{7,39},{8,232},{9... | collective-permute-start | bytes 884744 | tf_op jit(solution)/shard_map/ppermute | solution.py:47
  57.6 0.0 collective-permute-done.21.refs_2_
  57.6 1.2 %collective-permute-start.23 = (bf16[192,768]{1,0:T(8,128)(2,1)S(1)}, bf16[192,768]{1,0:T(8,128)(2,1)S(1)}, u32[]{:S(2)}, u32[]{:S(2)}) collective-permute-start(bf16[192,768]{1,0:T(8,128)(2,1)S(1)} %collective-permute-done.21.refs_2_), channel_id=1, source_target_pairs={{0,32},{1,33},{2,34},{3,35},{4,36},{5,37},{6,38},{7,39},{8,232},{9... | collective-permute-start | bytes 884744 | tf_op jit(solution)/shard_map/ppermute | solution.py:47
  58.8 3.3 %collective-permute-done.22.refs_3_ = bf16[192,768]{1,0:T(8,128)(2,1)S(1)} collective-permute-done((bf16[192,768]{1,0:T(8,128)(2,1)S(1)}, bf16[192,768]{1,0:T(8,128)(2,1)S(1)}, u32[]{:S(2)}, u32[]{:S(2)}) %collective-permute-start.22) | collective-permute-done | bytes 294944 | tf_op jit(solution)/shard_map/ppermute | solution.py:47
  62.1 2.2 %collective-permute-start.24 = (bf16[192,768]{1,0:T(8,128)(2,1)S(1)}, bf16[192,768]{1,0:T(8,128)(2,1)S(1)}, u32[]{:S(2)}, u32[]{:S(2)}) collective-permute-start(bf16[192,768]{1,0:T(8,128)(2,1)S(1)} %collective-permute-done.22.refs_3_), channel_id=1, source_target_pairs={{0,32},{1,33},{2,34},{3,35},{4,36},{5,37},{6,38},{7,39},{8,232},{9... | collective-permute-start | bytes 884744 | tf_op jit(solution)/shard_map/ppermute | solution.py:47
  64.4 0.9 collective-permute-done.23.refs_4_
  65.3 2.2 %collective-permute-start.25 = (bf16[192,768]{1,0:T(8,128)(2,1)S(1)}, bf16[192,768]{1,0:T(8,128)(2,1)S(1)}, u32[]{:S(2)}, u32[]{:S(2)}) collective-permute-start(bf16[192,768]{1,0:T(8,128)(2,1)S(1)} %collective-permute-done.23.refs_4_), channel_id=1, source_target_pairs={{0,32},{1,33},{2,34},{3,35},{4,36},{5,37},{6,38},{7,39},{8,232},{9... | collective-permute-start | bytes 884744 | tf_op jit(solution)/shard_map/ppermute | solution.py:47
  67.5 0.6 collective-permute-done.24.refs_5_
  68.1 3.0 %collective-permute-start.26 = (bf16[192,768]{1,0:T(8,128)(2,1)S(1)}, bf16[192,768]{1,0:T(8,128)(2,1)S(1)}, u32[]{:S(2)}, u32[]{:S(2)}) collective-permute-start(bf16[192,768]{1,0:T(8,128)(2,1)S(1)} %collective-permute-done.24.refs_5_), channel_id=1, source_target_pairs={{0,32},{1,33},{2,34},{3,35},{4,36},{5,37},{6,38},{7,39},{8,232},{9... | collective-permute-start | bytes 884744 | tf_op jit(solution)/shard_map/ppermute | solution.py:47
  71.2 0.4 collective-permute-done.25.refs_6_
  71.6 2.7 %collective-permute-start.27 = (bf16[192,768]{1,0:T(8,128)(2,1)S(1)}, bf16[192,768]{1,0:T(8,128)(2,1)S(1)}, u32[]{:S(2)}, u32[]{:S(2)}) collective-permute-start(bf16[192,768]{1,0:T(8,128)(2,1)S(1)} %collective-permute-done.25.refs_6_), channel_id=1, source_target_pairs={{0,32},{1,33},{2,34},{3,35},{4,36},{5,37},{6,38},{7,39},{8,232},{9... | collective-permute-start | bytes 884744 | tf_op jit(solution)/shard_map/ppermute | solution.py:47
  74.4 1.2 %collective-permute-start.29 = (bf16[384,768]{1,0:T(8,128)(2,1)S(1)}, bf16[384,768]{1,0:T(8,128)(2,1)S(1)}, u32[]{:S(2)}, u32[]{:S(2)}) collective-permute-start(bf16[384,768]{1,0:T(8,128)(2,1)S(1)} %pad_maximum_fusion.3), channel_id=1, source_target_pairs={{0,8},{1,9},{2,10},{3,11},{4,12},{5,13},{6,14},{7,15},{8,0},{9,1},... | collective-permute-start | bytes 1769480 | tf_op jit(solution)/shard_map/ppermute | solution.py:47
  75.5 3.0 %collective-permute-start.28 = (bf16[192,768]{1,0:T(8,128)(2,1)S(1)}, bf16[192,768]{1,0:T(8,128)(2,1)S(1)}, u32[]{:S(2)}, u32[]{:S(2)}) collective-permute-start(bf16[192,768]{1,0:T(8,128)(2,1)S(1)} %collective-permute-done.26.refs_7_), channel_id=1, source_target_pairs={{0,32},{1,33},{2,34},{3,35},{4,36},{5,37},{6,38},{7,39},{8,232},{9... | collective-permute-start | bytes 884744 | tf_op jit(solution)/shard_map/ppermute | solution.py:47
  78.5 2.0 %collective-permute-start.30 = (bf16[384,768]{1,0:T(8,128)(2,1)S(1)}, bf16[384,768]{1,0:T(8,128)(2,1)S(1)}, u32[]{:S(2)}, u32[]{:S(2)}) collective-permute-start(bf16[384,768]{1,0:T(8,128)(2,1)S(1)} %pad_maximum_fusion.4), channel_id=1, source_target_pairs={{0,8},{1,9},{2,10},{3,11},{4,12},{5,13},{6,14},{7,15},{8,0},{9,1},... | collective-permute-start | bytes 1769480 | tf_op jit(solution)/shard_map/ppermute | solution.py:47
  80.5 2.9 %collective-permute-start.31 = (bf16[384,768]{1,0:T(8,128)(2,1)S(1)}, bf16[384,768]{1,0:T(8,128)(2,1)S(1)}, u32[]{:S(2)}, u32[]{:S(2)}) collective-permute-start(bf16[384,768]{1,0:T(8,128)(2,1)S(1)} %pad_maximum_fusion.5), channel_id=1, source_target_pairs={{0,8},{1,9},{2,10},{3,11},{4,12},{5,13},{6,14},{7,15},{8,0},{9,1},... | collective-permute-start | bytes 1769480 | tf_op jit(solution)/shard_map/ppermute | solution.py:47
  83.4 1.4 %shard_map.42.total = f32[384,768]{1,0:T(8,128)S(1)} custom-call(bf16[8,2,384,192]{3,2,1,0:T(8,128)(2,1)S(1)} %get-tuple-element.25.left.refs_0_, bf16[192,768]{1,0:T(8,128)(2,1)S(1)} %subtract_convert_fusion.refs_1_, bf16[192,768]{1,0:T(8,128)(2,1)S(1)} %collective-permute-done.21.refs_2_, bf16[192,768]{1,0:T(8,128)(2,1)S(1)} %collective-permute-done.22.refs_3_, ...), custom_call_target="tpu_custom_call" | custom-call | flops 905969664 | tf_op jit(solution)/shard_map/pallas_call | solution.py:186
  84.8 3.3 %collective-permute-start.32 = (bf16[192,768]{1,0:T(8,128)(2,1)S(1)}, bf16[192,768]{1,0:T(8,128)(2,1)S(1)}, u32[]{:S(2)}, u32[]{:S(2)}) collective-permute-start(bf16[192,768]{1,0:T(8,128)(2,1)S(1)} %collective-permute-done.28.a4), channel_id=1, source_target_pairs={{0,8},{1,9},{2,10},{3,11},{4,12},{5,13},{6,14},{7,15},{8,0},{9,1},... | collective-permute-start | bytes 884744 | tf_op jit(solution)/shard_map/ppermute | solution.py:47
  88.1 1.2 %collective-permute-done.32.refs_3_ = bf16[192,768]{1,0:T(8,128)(2,1)S(1)} collective-permute-done((bf16[192,768]{1,0:T(8,128)(2,1)S(1)}, bf16[192,768]{1,0:T(8,128)(2,1)S(1)}, u32[]{:S(2)}, u32[]{:S(2)}) %collective-permute-start.32) | collective-permute-done | bytes 294944 | tf_op jit(solution)/shard_map/ppermute | solution.py:47
  89.3 0.8 shard_map.44
  90.1 0.7 collective-permute-start.33
  90.8 0.8 shard_map.43
  91.6 6.8 %collective-permute-done.33 = bf16[192,768]{1,0:T(8,128)(2,1)S(1)} collective-permute-done((bf16[192,768]{1,0:T(8,128)(2,1)S(1)}, bf16[192,768]{1,0:T(8,128)(2,1)S(1)}, u32[]{:S(2)}, u32[]{:S(2)}) %collective-permute-start.33) | collective-permute-done | bytes 294944 | tf_op jit(solution)/shard_map/ppermute | solution.py:47
  98.4 0.8 multiply_convert_fusion
  (27 shorter events, 0.4 us)
Async XLA Ops:
  1.2 8.8 %collective-permute-start = (bf16[192,384]{1,0:T(8,128)(2,1)S(1)}, bf16[192,384]{1,0:T(8,128)(2,1)S(1)}, u32[]{:S(2)}, u32[]{:S(2)}) collective-permute-start(bf16[192,384]{1,0:T(8,128)(2,1)S(1)} %get-tuple-element.20), channel_id=1, source_target_pairs={{0,16},{1,17},{2,18},{3,19},{4,20},{5,21},{6,22},{7,23},{8,24},{9,... | collective-permute-start | bytes 442376 | tf_op jit(solution)/shard_map/ppermute | solution.py:47
  3.4 9.4 %collective-permute-start.8 = (bf16[192,768]{1,0:T(8,128)(2,1)S(1)}, bf16[192,768]{1,0:T(8,128)(2,1)S(1)}, u32[]{:S(2)}, u32[]{:S(2)}) collective-permute-start(bf16[192,768]{1,0:T(8,128)(2,1)S(1)} %get-tuple-element.21.refs_8_), channel_id=1, source_target_pairs={{0,8},{1,9},{2,10},{3,11},{4,12},{5,13},{6,14},{7,15},{8,0},{9,1},... | collective-permute-start | bytes 884744 | tf_op jit(solution)/shard_map/ppermute | solution.py:47
  4.7 13.5 %collective-permute-start.9 = (bf16[192,768]{1,0:T(8,128)(2,1)S(1)}, bf16[192,768]{1,0:T(8,128)(2,1)S(1)}, u32[]{:S(2)}, u32[]{:S(2)}) collective-permute-start(bf16[192,768]{1,0:T(8,128)(2,1)S(1)} %get-tuple-element.21.refs_8_), channel_id=1, source_target_pairs={{0,32},{1,33},{2,34},{3,35},{4,36},{5,37},{6,38},{7,39},{8,232},{9... | collective-permute-start | bytes 884744 | tf_op jit(solution)/shard_map/ppermute | solution.py:47
  10.0 10.2 %collective-permute-start.1 = (bf16[384,384]{1,0:T(8,128)(2,1)S(1)}, bf16[384,384]{1,0:T(8,128)(2,1)S(1)}, u32[]{:S(2)}, u32[]{:S(2)}) collective-permute-start(bf16[384,384]{1,0:T(8,128)(2,1)S(1)} %constant_dynamic-update-slice_fusion.refs_0_), channel_id=1, source_target_pairs={{0,1},{1,2},{2,3},{3,0},{4,5},{5,6},{6,7},{7,4},{8,9},{9,10},{10,1... | collective-permute-start | bytes 884744 | tf_op jit(solution)/shard_map/ppermute | solution.py:47
  11.3 8.9 %collective-permute-start.2 = (bf16[384,384]{1,0:T(8,128)(2,1)S(1)}, bf16[384,384]{1,0:T(8,128)(2,1)S(1)}, u32[]{:S(2)}, u32[]{:S(2)}) collective-permute-start(bf16[384,384]{1,0:T(8,128)(2,1)S(1)} %constant_dynamic-update-slice_fusion.refs_0_), channel_id=1, source_target_pairs={{0,3},{1,0},{2,1},{3,2},{4,7},{5,4},{6,5},{7,6},{8,11},{9,8},{10,9... | collective-permute-start | bytes 884744 | tf_op jit(solution)/shard_map/ppermute | solution.py:47
  12.8 10.0 %collective-permute-start.10 = (bf16[192,768]{1,0:T(8,128)(2,1)S(1)}, bf16[192,768]{1,0:T(8,128)(2,1)S(1)}, u32[]{:S(2)}, u32[]{:S(2)}) collective-permute-start(bf16[192,768]{1,0:T(8,128)(2,1)S(1)} %collective-permute-done.8.refs_9_), channel_id=1, source_target_pairs={{0,32},{1,33},{2,34},{3,35},{4,36},{5,37},{6,38},{7,39},{8,232},{9... | collective-permute-start | bytes 884744 | tf_op jit(solution)/shard_map/ppermute | solution.py:47
  15.2 9.1 %collective-permute-start.3 = (bf16[384,384]{1,0:T(8,128)(2,1)S(1)}, bf16[384,384]{1,0:T(8,128)(2,1)S(1)}, u32[]{:S(2)}, u32[]{:S(2)}) collective-permute-start(bf16[384,384]{1,0:T(8,128)(2,1)S(1)} %constant_dynamic-update-slice_fusion.refs_0_), channel_id=1, source_target_pairs={{0,4},{1,5},{2,6},{3,7},{4,0},{5,1},{6,2},{7,3},{8,12},{9,13},{10,... | collective-permute-start | bytes 884744 | tf_op jit(solution)/shard_map/ppermute | solution.py:47
  18.1 6.2 %collective-permute-start.11 = (bf16[192,768]{1,0:T(8,128)(2,1)S(1)}, bf16[192,768]{1,0:T(8,128)(2,1)S(1)}, u32[]{:S(2)}, u32[]{:S(2)}) collective-permute-start(bf16[192,768]{1,0:T(8,128)(2,1)S(1)} %collective-permute-done.9.refs_10_), channel_id=1, source_target_pairs={{0,32},{1,33},{2,34},{3,35},{4,36},{5,37},{6,38},{7,39},{8,232},{9... | collective-permute-start | bytes 884744 | tf_op jit(solution)/shard_map/ppermute | solution.py:47
  20.2 8.4 %collective-permute-start.4 = (bf16[384,384]{1,0:T(8,128)(2,1)S(1)}, bf16[384,384]{1,0:T(8,128)(2,1)S(1)}, u32[]{:S(2)}, u32[]{:S(2)}) collective-permute-start(bf16[384,384]{1,0:T(8,128)(2,1)S(1)} %broadcast_select_fusion), channel_id=1, source_target_pairs={{0,1},{1,2},{2,3},{3,0},{4,5},{5,6},{6,7},{7,4},{8,11},{9,8},{10,9... | collective-permute-start | bytes 884744 | tf_op jit(solution)/shard_map/ppermute | solution.py:47
  22.8 8.1 %collective-permute-start.12 = (bf16[192,768]{1,0:T(8,128)(2,1)S(1)}, bf16[192,768]{1,0:T(8,128)(2,1)S(1)}, u32[]{:S(2)}, u32[]{:S(2)}) collective-permute-start(bf16[192,768]{1,0:T(8,128)(2,1)S(1)} %collective-permute-done.10.refs_11_), channel_id=1, source_target_pairs={{0,32},{1,33},{2,34},{3,35},{4,36},{5,37},{6,38},{7,39},{8,232},{9... | collective-permute-start | bytes 884744 | tf_op jit(solution)/shard_map/ppermute | solution.py:47
  24.4 7.5 %collective-permute-start.13 = (bf16[192,768]{1,0:T(8,128)(2,1)S(1)}, bf16[192,768]{1,0:T(8,128)(2,1)S(1)}, u32[]{:S(2)}, u32[]{:S(2)}) collective-permute-start(bf16[192,768]{1,0:T(8,128)(2,1)S(1)} %collective-permute-done.11.refs_12_), channel_id=1, source_target_pairs={{0,32},{1,33},{2,34},{3,35},{4,36},{5,37},{6,38},{7,39},{8,232},{9... | collective-permute-start | bytes 884744 | tf_op jit(solution)/shard_map/ppermute | solution.py:47
  26.0 10.2 %collective-permute-start.5 = (bf16[384,384]{1,0:T(8,128)(2,1)S(1)}, bf16[384,384]{1,0:T(8,128)(2,1)S(1)}, u32[]{:S(2)}, u32[]{:S(2)}) collective-permute-start(bf16[384,384]{1,0:T(8,128)(2,1)S(1)} %collective-permute-done.3.refs_3_), channel_id=1, source_target_pairs={{0,1},{1,2},{2,3},{3,0},{4,5},{5,6},{6,7},{7,4},{8,9},{9,10},{10,1... | collective-permute-start | bytes 884744 | tf_op jit(solution)/shard_map/ppermute | solution.py:47
  26.0 10.5 %collective-permute-start.6 = (bf16[384,384]{1,0:T(8,128)(2,1)S(1)}, bf16[384,384]{1,0:T(8,128)(2,1)S(1)}, u32[]{:S(2)}, u32[]{:S(2)}) collective-permute-start(bf16[384,384]{1,0:T(8,128)(2,1)S(1)} %collective-permute-done.3.refs_3_), channel_id=1, source_target_pairs={{0,3},{1,0},{2,1},{3,2},{4,7},{5,4},{6,5},{7,6},{8,11},{9,8},{10,9... | collective-permute-start | bytes 884744 | tf_op jit(solution)/shard_map/ppermute | solution.py:47
  28.6 10.0 %collective-permute-start.7 = (bf16[384,384]{1,0:T(8,128)(2,1)S(1)}, bf16[384,384]{1,0:T(8,128)(2,1)S(1)}, u32[]{:S(2)}, u32[]{:S(2)}) collective-permute-start(bf16[384,384]{1,0:T(8,128)(2,1)S(1)} %collective-permute-done.4.refs_4_), channel_id=1, source_target_pairs={{0,4},{1,5},{2,6},{3,7},{4,0},{5,1},{6,2},{7,3},{8,12},{9,13},{10,... | collective-permute-start | bytes 884744 | tf_op jit(solution)/shard_map/ppermute | solution.py:47
  30.9 8.7 %collective-permute-start.14 = (bf16[192,768]{1,0:T(8,128)(2,1)S(1)}, bf16[192,768]{1,0:T(8,128)(2,1)S(1)}, u32[]{:S(2)}, u32[]{:S(2)}) collective-permute-start(bf16[192,768]{1,0:T(8,128)(2,1)S(1)} %collective-permute-done.12.refs_13_), channel_id=1, source_target_pairs={{0,32},{1,33},{2,34},{3,35},{4,36},{5,37},{6,38},{7,39},{8,232},{9... | collective-permute-start | bytes 884744 | tf_op jit(solution)/shard_map/ppermute | solution.py:47
  31.8 12.7 %collective-permute-start.16 = (bf16[384,768]{1,0:T(8,128)(2,1)S(1)}, bf16[384,768]{1,0:T(8,128)(2,1)S(1)}, u32[]{:S(2)}, u32[]{:S(2)}) collective-permute-start(bf16[384,768]{1,0:T(8,128)(2,1)S(1)} %pad_maximum_fusion), channel_id=1, source_target_pairs={{0,8},{1,9},{2,10},{3,11},{4,12},{5,13},{6,14},{7,15},{8,0},{9,1},... | collective-permute-start | bytes 1769480 | tf_op jit(solution)/shard_map/ppermute | solution.py:47
  36.2 6.7 %collective-permute-start.15 = (bf16[192,768]{1,0:T(8,128)(2,1)S(1)}, bf16[192,768]{1,0:T(8,128)(2,1)S(1)}, u32[]{:S(2)}, u32[]{:S(2)}) collective-permute-start(bf16[192,768]{1,0:T(8,128)(2,1)S(1)} %collective-permute-done.13.refs_14_), channel_id=1, source_target_pairs={{0,32},{1,33},{2,34},{3,35},{4,36},{5,37},{6,38},{7,39},{8,232},{9... | collective-permute-start | bytes 884744 | tf_op jit(solution)/shard_map/ppermute | solution.py:47
  38.6 7.1 %collective-permute-start.17 = (bf16[384,768]{1,0:T(8,128)(2,1)S(1)}, bf16[384,768]{1,0:T(8,128)(2,1)S(1)}, u32[]{:S(2)}, u32[]{:S(2)}) collective-permute-start(bf16[384,768]{1,0:T(8,128)(2,1)S(1)} %pad_maximum_fusion.1), channel_id=1, source_target_pairs={{0,8},{1,9},{2,10},{3,11},{4,12},{5,13},{6,14},{7,15},{8,0},{9,1},... | collective-permute-start | bytes 1769480 | tf_op jit(solution)/shard_map/ppermute | solution.py:47
  39.6 6.1 %collective-permute-start.18 = (bf16[384,768]{1,0:T(8,128)(2,1)S(1)}, bf16[384,768]{1,0:T(8,128)(2,1)S(1)}, u32[]{:S(2)}, u32[]{:S(2)}) collective-permute-start(bf16[384,768]{1,0:T(8,128)(2,1)S(1)} %pad_maximum_fusion.2), channel_id=1, source_target_pairs={{0,8},{1,9},{2,10},{3,11},{4,12},{5,13},{6,14},{7,15},{8,0},{9,1},... | collective-permute-start | bytes 1769480 | tf_op jit(solution)/shard_map/ppermute | solution.py:47
  42.9 2.8 %collective-permute-start.19 = (bf16[192,768]{1,0:T(8,128)(2,1)S(1)}, bf16[192,768]{1,0:T(8,128)(2,1)S(1)}, u32[]{:S(2)}, u32[]{:S(2)}) collective-permute-start(bf16[192,768]{1,0:T(8,128)(2,1)S(1)} %collective-permute-done.15.a4), channel_id=1, source_target_pairs={{0,8},{1,9},{2,10},{3,11},{4,12},{5,13},{6,14},{7,15},{8,0},{9,1},... | collective-permute-start | bytes 884744 | tf_op jit(solution)/shard_map/ppermute | solution.py:47
  45.7 1.5 %copy-start = (s32[48,48]{1,0:T(8,128)S(1)}, s32[48,48]{1,0:T(8,128)}, u32[]{:S(2)}) copy-start(s32[48,48]{1,0:T(8,128)} %pattern.3) | copy-start | bytes 27652
  45.7 1.5 %copy-start.1 = (s32[48,48]{1,0:T(8,128)S(1)}, s32[48,48]{1,0:T(8,128)}, u32[]{:S(2)}) copy-start(s32[48,48]{1,0:T(8,128)} %keep.1) | copy-start | bytes 27652
  46.5 8.3 %collective-permute-start.20 = (bf16[192,768]{1,0:T(8,128)(2,1)S(1)}, bf16[192,768]{1,0:T(8,128)(2,1)S(1)}, u32[]{:S(2)}, u32[]{:S(2)}) collective-permute-start(bf16[192,768]{1,0:T(8,128)(2,1)S(1)} %shard_map.41), channel_id=1, source_target_pairs={{0,16},{1,17},{2,18},{3,19},{4,20},{5,21},{6,22},{7,23},{8,24},{9,... | collective-permute-start | bytes 884744 | tf_op jit(solution)/shard_map/ppermute | solution.py:47
  54.9 2.6 %collective-permute-start.21 = (bf16[192,768]{1,0:T(8,128)(2,1)S(1)}, bf16[192,768]{1,0:T(8,128)(2,1)S(1)}, u32[]{:S(2)}, u32[]{:S(2)}) collective-permute-start(bf16[192,768]{1,0:T(8,128)(2,1)S(1)} %subtract_convert_fusion.refs_1_), channel_id=1, source_target_pairs={{0,8},{1,9},{2,10},{3,11},{4,12},{5,13},{6,14},{7,15},{8,0},{9,1},... | collective-permute-start | bytes 884744 | tf_op jit(solution)/shard_map/ppermute | solution.py:47
  56.3 5.9 %collective-permute-start.22 = (bf16[192,768]{1,0:T(8,128)(2,1)S(1)}, bf16[192,768]{1,0:T(8,128)(2,1)S(1)}, u32[]{:S(2)}, u32[]{:S(2)}) collective-permute-start(bf16[192,768]{1,0:T(8,128)(2,1)S(1)} %subtract_convert_fusion.refs_1_), channel_id=1, source_target_pairs={{0,32},{1,33},{2,34},{3,35},{4,36},{5,37},{6,38},{7,39},{8,232},{9... | collective-permute-start | bytes 884744 | tf_op jit(solution)/shard_map/ppermute | solution.py:47
  57.6 7.7 %collective-permute-start.23 = (bf16[192,768]{1,0:T(8,128)(2,1)S(1)}, bf16[192,768]{1,0:T(8,128)(2,1)S(1)}, u32[]{:S(2)}, u32[]{:S(2)}) collective-permute-start(bf16[192,768]{1,0:T(8,128)(2,1)S(1)} %collective-permute-done.21.refs_2_), channel_id=1, source_target_pairs={{0,32},{1,33},{2,34},{3,35},{4,36},{5,37},{6,38},{7,39},{8,232},{9... | collective-permute-start | bytes 884744 | tf_op jit(solution)/shard_map/ppermute | solution.py:47
  62.1 6.0 %collective-permute-start.24 = (bf16[192,768]{1,0:T(8,128)(2,1)S(1)}, bf16[192,768]{1,0:T(8,128)(2,1)S(1)}, u32[]{:S(2)}, u32[]{:S(2)}) collective-permute-start(bf16[192,768]{1,0:T(8,128)(2,1)S(1)} %collective-permute-done.22.refs_3_), channel_id=1, source_target_pairs={{0,32},{1,33},{2,34},{3,35},{4,36},{5,37},{6,38},{7,39},{8,232},{9... | collective-permute-start | bytes 884744 | tf_op jit(solution)/shard_map/ppermute | solution.py:47
  65.3 6.3 %collective-permute-start.25 = (bf16[192,768]{1,0:T(8,128)(2,1)S(1)}, bf16[192,768]{1,0:T(8,128)(2,1)S(1)}, u32[]{:S(2)}, u32[]{:S(2)}) collective-permute-start(bf16[192,768]{1,0:T(8,128)(2,1)S(1)} %collective-permute-done.23.refs_4_), channel_id=1, source_target_pairs={{0,32},{1,33},{2,34},{3,35},{4,36},{5,37},{6,38},{7,39},{8,232},{9... | collective-permute-start | bytes 884744 | tf_op jit(solution)/shard_map/ppermute | solution.py:47
  68.1 7.4 %collective-permute-start.26 = (bf16[192,768]{1,0:T(8,128)(2,1)S(1)}, bf16[192,768]{1,0:T(8,128)(2,1)S(1)}, u32[]{:S(2)}, u32[]{:S(2)}) collective-permute-start(bf16[192,768]{1,0:T(8,128)(2,1)S(1)} %collective-permute-done.24.refs_5_), channel_id=1, source_target_pairs={{0,32},{1,33},{2,34},{3,35},{4,36},{5,37},{6,38},{7,39},{8,232},{9... | collective-permute-start | bytes 884744 | tf_op jit(solution)/shard_map/ppermute | solution.py:47
  71.6 8.9 %collective-permute-start.27 = (bf16[192,768]{1,0:T(8,128)(2,1)S(1)}, bf16[192,768]{1,0:T(8,128)(2,1)S(1)}, u32[]{:S(2)}, u32[]{:S(2)}) collective-permute-start(bf16[192,768]{1,0:T(8,128)(2,1)S(1)} %collective-permute-done.25.refs_6_), channel_id=1, source_target_pairs={{0,32},{1,33},{2,34},{3,35},{4,36},{5,37},{6,38},{7,39},{8,232},{9... | collective-permute-start | bytes 884744 | tf_op jit(solution)/shard_map/ppermute | solution.py:47
  74.4 13.7 %collective-permute-start.29 = (bf16[384,768]{1,0:T(8,128)(2,1)S(1)}, bf16[384,768]{1,0:T(8,128)(2,1)S(1)}, u32[]{:S(2)}, u32[]{:S(2)}) collective-permute-start(bf16[384,768]{1,0:T(8,128)(2,1)S(1)} %pad_maximum_fusion.3), channel_id=1, source_target_pairs={{0,8},{1,9},{2,10},{3,11},{4,12},{5,13},{6,14},{7,15},{8,0},{9,1},... | collective-permute-start | bytes 1769480 | tf_op jit(solution)/shard_map/ppermute | solution.py:47
  75.5 9.3 %collective-permute-start.28 = (bf16[192,768]{1,0:T(8,128)(2,1)S(1)}, bf16[192,768]{1,0:T(8,128)(2,1)S(1)}, u32[]{:S(2)}, u32[]{:S(2)}) collective-permute-start(bf16[192,768]{1,0:T(8,128)(2,1)S(1)} %collective-permute-done.26.refs_7_), channel_id=1, source_target_pairs={{0,32},{1,33},{2,34},{3,35},{4,36},{5,37},{6,38},{7,39},{8,232},{9... | collective-permute-start | bytes 884744 | tf_op jit(solution)/shard_map/ppermute | solution.py:47
  78.5 9.6 %collective-permute-start.30 = (bf16[384,768]{1,0:T(8,128)(2,1)S(1)}, bf16[384,768]{1,0:T(8,128)(2,1)S(1)}, u32[]{:S(2)}, u32[]{:S(2)}) collective-permute-start(bf16[384,768]{1,0:T(8,128)(2,1)S(1)} %pad_maximum_fusion.4), channel_id=1, source_target_pairs={{0,8},{1,9},{2,10},{3,11},{4,12},{5,13},{6,14},{7,15},{8,0},{9,1},... | collective-permute-start | bytes 1769480 | tf_op jit(solution)/shard_map/ppermute | solution.py:47
  80.5 8.7 %collective-permute-start.31 = (bf16[384,768]{1,0:T(8,128)(2,1)S(1)}, bf16[384,768]{1,0:T(8,128)(2,1)S(1)}, u32[]{:S(2)}, u32[]{:S(2)}) collective-permute-start(bf16[384,768]{1,0:T(8,128)(2,1)S(1)} %pad_maximum_fusion.5), channel_id=1, source_target_pairs={{0,8},{1,9},{2,10},{3,11},{4,12},{5,13},{6,14},{7,15},{8,0},{9,1},... | collective-permute-start | bytes 1769480 | tf_op jit(solution)/shard_map/ppermute | solution.py:47
  84.8 4.5 %collective-permute-start.32 = (bf16[192,768]{1,0:T(8,128)(2,1)S(1)}, bf16[192,768]{1,0:T(8,128)(2,1)S(1)}, u32[]{:S(2)}, u32[]{:S(2)}) collective-permute-start(bf16[192,768]{1,0:T(8,128)(2,1)S(1)} %collective-permute-done.28.a4), channel_id=1, source_target_pairs={{0,8},{1,9},{2,10},{3,11},{4,12},{5,13},{6,14},{7,15},{8,0},{9,1},... | collective-permute-start | bytes 884744 | tf_op jit(solution)/shard_map/ppermute | solution.py:47
  90.1 8.3 %collective-permute-start.33 = (bf16[192,768]{1,0:T(8,128)(2,1)S(1)}, bf16[192,768]{1,0:T(8,128)(2,1)S(1)}, u32[]{:S(2)}, u32[]{:S(2)}) collective-permute-start(bf16[192,768]{1,0:T(8,128)(2,1)S(1)} %shard_map.44), channel_id=1, source_target_pairs={{0,16},{1,17},{2,18},{3,19},{4,20},{5,21},{6,22},{7,23},{8,24},{9,... | collective-permute-start | bytes 884744 | tf_op jit(solution)/shard_map/ppermute | solution.py:47

commit v7 on v6

--- a/solution.py
+++ b/solution.py
@@ -166,11 +166,11 @@
         shape = (SLAB, BLOCK)
         down = lax.broadcasted_iota(jnp.int32, shape, 0) + (row * ROWS + rows.start)
         over = lax.broadcasted_iota(jnp.int32, shape, 1) + (col * COLS + cols.start)
-        eye[rows, cols] = jnp.where(down == over, 1.5, 0.0).astype(F32)
+        eye[rows, cols] = jnp.where(down == over, 1.5, 0.0).astype(F32).astype(BF16)
         square_factor = jnp.where(listed(keep, a, b), 0.5, 0.0).astype(F32)
-        kept_square[rows, cols] = jnp.full(shape, square_factor, F32)
+        kept_square[rows, cols] = jnp.full(shape, square_factor, F32).astype(BF16)
         result_factor = jnp.where(listed(pattern, a, b) | (a == b), 1.0, 0.0).astype(F32)
-        kept_result[rows, cols] = jnp.full(shape, result_factor, F32)
+        kept_result[rows, cols] = jnp.full(shape, result_factor, F32).astype(BF16)
 
     tiles(body)
 
@@ -246,7 +246,7 @@
         [pl.BlockSpec(memory_space=pltpu.HBM)] * 2,
     )
     kept_square, eye, kept_result = call(
-        factor_kernel, [pattern, keep], [struct(ROWS, COLS, dtype=F32)] * 3, [], ROWS * COLS
+        factor_kernel, [pattern, keep], [struct(ROWS, COLS)] * 3, [], ROWS * COLS
     )
     pieces = row(cat(kept, send(away, TWIN)))
 

time: 99.3 us -> 99.3 us (level)
  no operation moved by 1% of the time
where the time goes in v7:
time: 99.3 us; the launch traced here: 99.2 us
  starting transfers between devices  60.8 us (61%)
  waiting for transfers between devices  28 us (28%)
  Pallas kernels  8.96 us (9%)
  other arithmetic  1.2 us (1%)
    ppermute x34, starting transfers between devices, send(): return lax.ppermute(value, AXES, pairs)  60.8 us
    ppermute x34, waiting for transfers between devices, send(): return lax.ppermute(value, AXES, pairs)  28 us
    pallas_call x8, Pallas kernels, call(): pl.pallas_call(kernel, in_specs=specs or [SMEM if arg.dtype == jnp.int32...  8.96 us
  transfers between devices with their start and end apart: 34, of which 13 were waited for; matrix products, arithmetic and copies ran while one was open for 0% of the time, Pallas kernels for 6%

profile of v7, /device:TPU:1, one launch (start us, length us, event | category | flops | bytes accessed | tf_op | source)
XLA Modules:
  0.0 99.2 jit_solution(16381326809368755082)
XLA Ops:
  0.0 1.2 %shard_map.37 = (bf16[192,768]{1,0:T(8,128)(2,1)S(1)}, bf16[192,384]{1,0:T(8,128)(2,1)S(1)}, bf16[192,384]{1,0:T(8,128)(2,1)S(1)}) custom-call(s32[48,48]{1,0:T(8,128)} %pattern.3, bf16[192,768]{1,0:T(8,128)(2,1)} %matrix.1), custom_call_target="tpu_custom_call" | custom-call | tf_op jit(solution)/shard_map/pallas_call | solution.py:186
  1.2 2.2 %collective-permute-start = (bf16[192,384]{1,0:T(8,128)(2,1)S(1)}, bf16[192,384]{1,0:T(8,128)(2,1)S(1)}, u32[]{:S(2)}, u32[]{:S(2)}) collective-permute-start(bf16[192,384]{1,0:T(8,128)(2,1)S(1)} %get-tuple-element.20), channel_id=1, source_target_pairs={{0,16},{1,17},{2,18},{3,19},{4,20},{5,21},{6,22},{7,23},{8,24},{9,... | collective-permute-start | bytes 442376 | tf_op jit(solution)/shard_map/ppermute | solution.py:47
  3.4 1.2 %collective-permute-start.8 = (bf16[192,768]{1,0:T(8,128)(2,1)S(1)}, bf16[192,768]{1,0:T(8,128)(2,1)S(1)}, u32[]{:S(2)}, u32[]{:S(2)}) collective-permute-start(bf16[192,768]{1,0:T(8,128)(2,1)S(1)} %get-tuple-element.21.refs_8_), channel_id=1, source_target_pairs={{0,8},{1,9},{2,10},{3,11},{4,12},{5,13},{6,14},{7,15},{8,0},{9,1},... | collective-permute-start | bytes 884744 | tf_op jit(solution)/shard_map/ppermute | solution.py:47
  4.7 5.3 %collective-permute-start.9 = (bf16[192,768]{1,0:T(8,128)(2,1)S(1)}, bf16[192,768]{1,0:T(8,128)(2,1)S(1)}, u32[]{:S(2)}, u32[]{:S(2)}) collective-permute-start(bf16[192,768]{1,0:T(8,128)(2,1)S(1)} %get-tuple-element.21.refs_8_), channel_id=1, source_target_pairs={{0,32},{1,33},{2,34},{3,35},{4,36},{5,37},{6,38},{7,39},{8,232},{9... | collective-permute-start | bytes 884744 | tf_op jit(solution)/shard_map/ppermute | solution.py:47
  10.0 0.0 collective-permute-done
  10.0 1.3 %collective-permute-start.1 = (bf16[384,384]{1,0:T(8,128)(2,1)S(1)}, bf16[384,384]{1,0:T(8,128)(2,1)S(1)}, u32[]{:S(2)}, u32[]{:S(2)}) collective-permute-start(bf16[384,384]{1,0:T(8,128)(2,1)S(1)} %constant_dynamic-update-slice_fusion.refs_0_), channel_id=1, source_target_pairs={{0,1},{1,2},{2,3},{3,0},{4,5},{5,6},{6,7},{7,4},{8,9},{9,10},{10,1... | collective-permute-start | bytes 884744 | tf_op jit(solution)/shard_map/ppermute | solution.py:47
  11.3 1.5 %collective-permute-start.2 = (bf16[384,384]{1,0:T(8,128)(2,1)S(1)}, bf16[384,384]{1,0:T(8,128)(2,1)S(1)}, u32[]{:S(2)}, u32[]{:S(2)}) collective-permute-start(bf16[384,384]{1,0:T(8,128)(2,1)S(1)} %constant_dynamic-update-slice_fusion.refs_0_), channel_id=1, source_target_pairs={{0,3},{1,0},{2,1},{3,2},{4,7},{5,4},{6,5},{7,6},{8,11},{9,8},{10,9... | collective-permute-start | bytes 884744 | tf_op jit(solution)/shard_map/ppermute | solution.py:47
  12.8 0.0 collective-permute-done.8.refs_9_
  12.8 2.4 %collective-permute-start.10 = (bf16[192,768]{1,0:T(8,128)(2,1)S(1)}, bf16[192,768]{1,0:T(8,128)(2,1)S(1)}, u32[]{:S(2)}, u32[]{:S(2)}) collective-permute-start(bf16[192,768]{1,0:T(8,128)(2,1)S(1)} %collective-permute-done.8.refs_9_), channel_id=1, source_target_pairs={{0,32},{1,33},{2,34},{3,35},{4,36},{5,37},{6,38},{7,39},{8,232},{9... | collective-permute-start | bytes 884744 | tf_op jit(solution)/shard_map/ppermute | solution.py:47
  15.2 2.9 %collective-permute-start.3 = (bf16[384,384]{1,0:T(8,128)(2,1)S(1)}, bf16[384,384]{1,0:T(8,128)(2,1)S(1)}, u32[]{:S(2)}, u32[]{:S(2)}) collective-permute-start(bf16[384,384]{1,0:T(8,128)(2,1)S(1)} %constant_dynamic-update-slice_fusion.refs_0_), channel_id=1, source_target_pairs={{0,4},{1,5},{2,6},{3,7},{4,0},{5,1},{6,2},{7,3},{8,12},{9,13},{10,... | collective-permute-start | bytes 884744 | tf_op jit(solution)/shard_map/ppermute | solution.py:47
  18.1 0.7 collective-permute-start.11
  18.9 1.3 %collective-permute-done.1.refs_1_ = bf16[384,384]{1,0:T(8,128)(2,1)S(1)} collective-permute-done((bf16[384,384]{1,0:T(8,128)(2,1)S(1)}, bf16[384,384]{1,0:T(8,128)(2,1)S(1)}, u32[]{:S(2)}, u32[]{:S(2)}) %collective-permute-start.1) | collective-permute-done | bytes 294944 | tf_op jit(solution)/shard_map/ppermute | solution.py:47
  20.2 0.0 collective-permute-done.2.refs_2_
  20.2 2.6 %collective-permute-start.4 = (bf16[384,384]{1,0:T(8,128)(2,1)S(1)}, bf16[384,384]{1,0:T(8,128)(2,1)S(1)}, u32[]{:S(2)}, u32[]{:S(2)}) collective-permute-start(bf16[384,384]{1,0:T(8,128)(2,1)S(1)} %broadcast_select_fusion), channel_id=1, source_target_pairs={{0,1},{1,2},{2,3},{3,0},{4,5},{5,6},{6,7},{7,4},{8,11},{9,8},{10,9... | collective-permute-start | bytes 884744 | tf_op jit(solution)/shard_map/ppermute | solution.py:47
  22.8 0.0 collective-permute-done.10.refs_11_
  22.8 0.4 collective-permute-start.12
  23.2 1.1 %collective-permute-done.3.refs_3_ = bf16[384,384]{1,0:T(8,128)(2,1)S(1)} collective-permute-done((bf16[384,384]{1,0:T(8,128)(2,1)S(1)}, bf16[384,384]{1,0:T(8,128)(2,1)S(1)}, u32[]{:S(2)}, u32[]{:S(2)}) %collective-permute-start.3) | collective-permute-done | bytes 294944 | tf_op jit(solution)/shard_map/ppermute | solution.py:47
  24.4 0.0 collective-permute-done.11.refs_12_
  24.4 1.6 %collective-permute-start.13 = (bf16[192,768]{1,0:T(8,128)(2,1)S(1)}, bf16[192,768]{1,0:T(8,128)(2,1)S(1)}, u32[]{:S(2)}, u32[]{:S(2)}) collective-permute-start(bf16[192,768]{1,0:T(8,128)(2,1)S(1)} %collective-permute-done.11.refs_12_), channel_id=1, source_target_pairs={{0,32},{1,33},{2,34},{3,35},{4,36},{5,37},{6,38},{7,39},{8,232},{9... | collective-permute-start | bytes 884744 | tf_op jit(solution)/shard_map/ppermute | solution.py:47
  26.0 2.7 %collective-permute-start.6 = (bf16[384,384]{1,0:T(8,128)(2,1)S(1)}, bf16[384,384]{1,0:T(8,128)(2,1)S(1)}, u32[]{:S(2)}, u32[]{:S(2)}) collective-permute-start(bf16[384,384]{1,0:T(8,128)(2,1)S(1)} %collective-permute-done.3.refs_3_), channel_id=1, source_target_pairs={{0,3},{1,0},{2,1},{3,2},{4,7},{5,4},{6,5},{7,6},{8,11},{9,8},{10,9... | collective-permute-start | bytes 884744 | tf_op jit(solution)/shard_map/ppermute | solution.py:47
  28.6 0.0 collective-permute-done.4.refs_4_
  28.6 2.3 %collective-permute-start.7 = (bf16[384,384]{1,0:T(8,128)(2,1)S(1)}, bf16[384,384]{1,0:T(8,128)(2,1)S(1)}, u32[]{:S(2)}, u32[]{:S(2)}) collective-permute-start(bf16[384,384]{1,0:T(8,128)(2,1)S(1)} %collective-permute-done.4.refs_4_), channel_id=1, source_target_pairs={{0,4},{1,5},{2,6},{3,7},{4,0},{5,1},{6,2},{7,3},{8,12},{9,13},{10,... | collective-permute-start | bytes 884744 | tf_op jit(solution)/shard_map/ppermute | solution.py:47
  30.9 0.0 collective-permute-done.12.refs_13_
  30.9 0.0 collective-permute-start.14
  31.0 0.9 collective-permute-done.13.refs_14_
  31.8 1.6 %collective-permute-start.16 = (bf16[384,768]{1,0:T(8,128)(2,1)S(1)}, bf16[384,768]{1,0:T(8,128)(2,1)S(1)}, u32[]{:S(2)}, u32[]{:S(2)}) collective-permute-start(bf16[384,768]{1,0:T(8,128)(2,1)S(1)} %pad_maximum_fusion), channel_id=1, source_target_pairs={{0,8},{1,9},{2,10},{3,11},{4,12},{5,13},{6,14},{7,15},{8,0},{9,1},... | collective-permute-start | bytes 1769480 | tf_op jit(solution)/shard_map/ppermute | solution.py:47
  33.5 2.7 %collective-permute-done.5.refs_5_ = bf16[384,384]{1,0:T(8,128)(2,1)S(1)} collective-permute-done((bf16[384,384]{1,0:T(8,128)(2,1)S(1)}, bf16[384,384]{1,0:T(8,128)(2,1)S(1)}, u32[]{:S(2)}, u32[]{:S(2)}) %collective-permute-start.5) | collective-permute-done | bytes 294944 | tf_op jit(solution)/shard_map/ppermute | solution.py:47
  36.2 0.3 collective-permute-start.15
  36.4 0.0 collective-permute-done.6.refs_6_
  36.4 2.2 %collective-permute-done.7.refs_7_ = bf16[384,384]{1,0:T(8,128)(2,1)S(1)} collective-permute-done((bf16[384,384]{1,0:T(8,128)(2,1)S(1)}, bf16[384,384]{1,0:T(8,128)(2,1)S(1)}, u32[]{:S(2)}, u32[]{:S(2)}) %collective-permute-start.7) | collective-permute-done | bytes 294944 | tf_op jit(solution)/shard_map/ppermute | solution.py:47
  38.6 1.0 collective-permute-start.17
  39.6 1.5 %collective-permute-start.18 = (bf16[384,768]{1,0:T(8,128)(2,1)S(1)}, bf16[384,768]{1,0:T(8,128)(2,1)S(1)}, u32[]{:S(2)}, u32[]{:S(2)}) collective-permute-start(bf16[384,768]{1,0:T(8,128)(2,1)S(1)} %pad_maximum_fusion.2), channel_id=1, source_target_pairs={{0,8},{1,9},{2,10},{3,11},{4,12},{5,13},{6,14},{7,15},{8,0},{9,1},... | collective-permute-start | bytes 1769480 | tf_op jit(solution)/shard_map/ppermute | solution.py:47
  41.1 1.8 %shard_map.38 = (f32[384,768]{1,0:T(8,128)S(1)}, bf16[8,2,384,192]{3,2,1,0:T(8,128)(2,1)S(1)}) custom-call(bf16[384,384]{1,0:T(8,128)(2,1)S(1)} %constant_dynamic-update-slice_fusion.refs_0_, bf16[384,384]{1,0:T(8,128)(2,1)S(1)} %collective-permute-done.1.refs_1_, bf16[384,384]{1,0:T(8,128)(2,1)S(1)} %collective-permute-done.2.refs_2_, ...), custom_call_target="tpu_custom_call" | custom-call | flops 905969664 | tf_op jit(solution)/shard_map/pallas_call | solution.py:186
  42.9 1.6 %collective-permute-start.19 = (bf16[192,768]{1,0:T(8,128)(2,1)S(1)}, bf16[192,768]{1,0:T(8,128)(2,1)S(1)}, u32[]{:S(2)}, u32[]{:S(2)}) collective-permute-start(bf16[192,768]{1,0:T(8,128)(2,1)S(1)} %collective-permute-done.15.a4), channel_id=1, source_target_pairs={{0,8},{1,9},{2,10},{3,11},{4,12},{5,13},{6,14},{7,15},{8,0},{9,1},... | collective-permute-start | bytes 884744 | tf_op jit(solution)/shard_map/ppermute | solution.py:47
  44.5 1.2 %collective-permute-done.19.refs_3_ = bf16[192,768]{1,0:T(8,128)(2,1)S(1)} collective-permute-done((bf16[192,768]{1,0:T(8,128)(2,1)S(1)}, bf16[192,768]{1,0:T(8,128)(2,1)S(1)}, u32[]{:S(2)}, u32[]{:S(2)}) %collective-permute-start.19) | collective-permute-done | bytes 294944 | tf_op jit(solution)/shard_map/ppermute | solution.py:47
  45.7 0.8 shard_map.41
  46.5 0.7 collective-permute-start.20
  47.3 1.5 %shard_map.39 = (bf16[192,768]{1,0:T(8,128)(2,1)S(1)}, bf16[192,768]{1,0:T(8,128)(2,1)S(1)}, bf16[192,768]{1,0:T(8,128)(2,1)S(1)}) custom-call(s32[48,48]{1,0:T(8,128)S(1)} %copy-done, s32[48,48]{1,0:T(8,128)S(1)} %copy-done.1), custom_call_target="tpu_custom_call" | custom-call | flops 147456 | tf_op jit(solution)/shard_map/pallas_call | solution.py:186
  48.8 0.8 shard_map.40
  49.5 5.3 %collective-permute-done.20 = bf16[192,768]{1,0:T(8,128)(2,1)S(1)} collective-permute-done((bf16[192,768]{1,0:T(8,128)(2,1)S(1)}, bf16[192,768]{1,0:T(8,128)(2,1)S(1)}, u32[]{:S(2)}, u32[]{:S(2)}) %collective-permute-start.20) | collective-permute-done | bytes 294944 | tf_op jit(solution)/shard_map/ppermute | solution.py:47
  54.8 0.1 subtract_convert_fusion.refs_1_
  54.9 1.3 %collective-permute-start.21 = (bf16[192,768]{1,0:T(8,128)(2,1)S(1)}, bf16[192,768]{1,0:T(8,128)(2,1)S(1)}, u32[]{:S(2)}, u32[]{:S(2)}) collective-permute-start(bf16[192,768]{1,0:T(8,128)(2,1)S(1)} %subtract_convert_fusion.refs_1_), channel_id=1, source_target_pairs={{0,8},{1,9},{2,10},{3,11},{4,12},{5,13},{6,14},{7,15},{8,0},{9,1},... | collective-permute-start | bytes 884744 | tf_op jit(solution)/shard_map/ppermute | solution.py:47
  56.3 1.3 %collective-permute-start.22 = (bf16[192,768]{1,0:T(8,128)(2,1)S(1)}, bf16[192,768]{1,0:T(8,128)(2,1)S(1)}, u32[]{:S(2)}, u32[]{:S(2)}) collective-permute-start(bf16[192,768]{1,0:T(8,128)(2,1)S(1)} %subtract_convert_fusion.refs_1_), channel_id=1, source_target_pairs={{0,32},{1,33},{2,34},{3,35},{4,36},{5,37},{6,38},{7,39},{8,232},{9... | collective-permute-start | bytes 884744 | tf_op jit(solution)/shard_map/ppermute | solution.py:47
  57.6 1.2 %collective-permute-start.23 = (bf16[192,768]{1,0:T(8,128)(2,1)S(1)}, bf16[192,768]{1,0:T(8,128)(2,1)S(1)}, u32[]{:S(2)}, u32[]{:S(2)}) collective-permute-start(bf16[192,768]{1,0:T(8,128)(2,1)S(1)} %collective-permute-done.21.refs_2_), channel_id=1, source_target_pairs={{0,32},{1,33},{2,34},{3,35},{4,36},{5,37},{6,38},{7,39},{8,232},{9... | collective-permute-start | bytes 884744 | tf_op jit(solution)/shard_map/ppermute | solution.py:47
  58.8 3.3 %collective-permute-done.22.refs_3_ = bf16[192,768]{1,0:T(8,128)(2,1)S(1)} collective-permute-done((bf16[192,768]{1,0:T(8,128)(2,1)S(1)}, bf16[192,768]{1,0:T(8,128)(2,1)S(1)}, u32[]{:S(2)}, u32[]{:S(2)}) %collective-permute-start.22) | collective-permute-done | bytes 294944 | tf_op jit(solution)/shard_map/ppermute | solution.py:47
  62.1 2.2 %collective-permute-start.24 = (bf16[192,768]{1,0:T(8,128)(2,1)S(1)}, bf16[192,768]{1,0:T(8,128)(2,1)S(1)}, u32[]{:S(2)}, u32[]{:S(2)}) collective-permute-start(bf16[192,768]{1,0:T(8,128)(2,1)S(1)} %collective-permute-done.22.refs_3_), channel_id=1, source_target_pairs={{0,32},{1,33},{2,34},{3,35},{4,36},{5,37},{6,38},{7,39},{8,232},{9... | collective-permute-start | bytes 884744 | tf_op jit(solution)/shard_map/ppermute | solution.py:47
  64.4 0.9 collective-permute-done.23.refs_4_
  65.3 2.2 %collective-permute-start.25 = (bf16[192,768]{1,0:T(8,128)(2,1)S(1)}, bf16[192,768]{1,0:T(8,128)(2,1)S(1)}, u32[]{:S(2)}, u32[]{:S(2)}) collective-permute-start(bf16[192,768]{1,0:T(8,128)(2,1)S(1)} %collective-permute-done.23.refs_4_), channel_id=1, source_target_pairs={{0,32},{1,33},{2,34},{3,35},{4,36},{5,37},{6,38},{7,39},{8,232},{9... | collective-permute-start | bytes 884744 | tf_op jit(solution)/shard_map/ppermute | solution.py:47
  67.5 0.6 collective-permute-done.24.refs_5_
  68.1 3.0 %collective-permute-start.26 = (bf16[192,768]{1,0:T(8,128)(2,1)S(1)}, bf16[192,768]{1,0:T(8,128)(2,1)S(1)}, u32[]{:S(2)}, u32[]{:S(2)}) collective-permute-start(bf16[192,768]{1,0:T(8,128)(2,1)S(1)} %collective-permute-done.24.refs_5_), channel_id=1, source_target_pairs={{0,32},{1,33},{2,34},{3,35},{4,36},{5,37},{6,38},{7,39},{8,232},{9... | collective-permute-start | bytes 884744 | tf_op jit(solution)/shard_map/ppermute | solution.py:47
  71.2 0.4 collective-permute-done.25.refs_6_
  71.6 2.7 %collective-permute-start.27 = (bf16[192,768]{1,0:T(8,128)(2,1)S(1)}, bf16[192,768]{1,0:T(8,128)(2,1)S(1)}, u32[]{:S(2)}, u32[]{:S(2)}) collective-permute-start(bf16[192,768]{1,0:T(8,128)(2,1)S(1)} %collective-permute-done.25.refs_6_), channel_id=1, source_target_pairs={{0,32},{1,33},{2,34},{3,35},{4,36},{5,37},{6,38},{7,39},{8,232},{9... | collective-permute-start | bytes 884744 | tf_op jit(solution)/shard_map/ppermute | solution.py:47
  74.4 1.2 %collective-permute-start.29 = (bf16[384,768]{1,0:T(8,128)(2,1)S(1)}, bf16[384,768]{1,0:T(8,128)(2,1)S(1)}, u32[]{:S(2)}, u32[]{:S(2)}) collective-permute-start(bf16[384,768]{1,0:T(8,128)(2,1)S(1)} %pad_maximum_fusion.3), channel_id=1, source_target_pairs={{0,8},{1,9},{2,10},{3,11},{4,12},{5,13},{6,14},{7,15},{8,0},{9,1},... | collective-permute-start | bytes 1769480 | tf_op jit(solution)/shard_map/ppermute | solution.py:47
  75.5 3.0 %collective-permute-start.28 = (bf16[192,768]{1,0:T(8,128)(2,1)S(1)}, bf16[192,768]{1,0:T(8,128)(2,1)S(1)}, u32[]{:S(2)}, u32[]{:S(2)}) collective-permute-start(bf16[192,768]{1,0:T(8,128)(2,1)S(1)} %collective-permute-done.26.refs_7_), channel_id=1, source_target_pairs={{0,32},{1,33},{2,34},{3,35},{4,36},{5,37},{6,38},{7,39},{8,232},{9... | collective-permute-start | bytes 884744 | tf_op jit(solution)/shard_map/ppermute | solution.py:47
  78.5 2.0 %collective-permute-start.30 = (bf16[384,768]{1,0:T(8,128)(2,1)S(1)}, bf16[384,768]{1,0:T(8,128)(2,1)S(1)}, u32[]{:S(2)}, u32[]{:S(2)}) collective-permute-start(bf16[384,768]{1,0:T(8,128)(2,1)S(1)} %pad_maximum_fusion.4), channel_id=1, source_target_pairs={{0,8},{1,9},{2,10},{3,11},{4,12},{5,13},{6,14},{7,15},{8,0},{9,1},... | collective-permute-start | bytes 1769480 | tf_op jit(solution)/shard_map/ppermute | solution.py:47
  80.5 2.9 %collective-permute-start.31 = (bf16[384,768]{1,0:T(8,128)(2,1)S(1)}, bf16[384,768]{1,0:T(8,128)(2,1)S(1)}, u32[]{:S(2)}, u32[]{:S(2)}) collective-permute-start(bf16[384,768]{1,0:T(8,128)(2,1)S(1)} %pad_maximum_fusion.5), channel_id=1, source_target_pairs={{0,8},{1,9},{2,10},{3,11},{4,12},{5,13},{6,14},{7,15},{8,0},{9,1},... | collective-permute-start | bytes 1769480 | tf_op jit(solution)/shard_map/ppermute | solution.py:47
  83.4 1.4 %shard_map.42.total = f32[384,768]{1,0:T(8,128)S(1)} custom-call(bf16[8,2,384,192]{3,2,1,0:T(8,128)(2,1)S(1)} %get-tuple-element.25.left.refs_0_, bf16[192,768]{1,0:T(8,128)(2,1)S(1)} %subtract_convert_fusion.refs_1_, bf16[192,768]{1,0:T(8,128)(2,1)S(1)} %collective-permute-done.21.refs_2_, bf16[192,768]{1,0:T(8,128)(2,1)S(1)} %collective-permute-done.22.refs_3_, ...), custom_call_target="tpu_custom_call" | custom-call | flops 905969664 | tf_op jit(solution)/shard_map/pallas_call | solution.py:186
  84.8 3.3 %collective-permute-start.32 = (bf16[192,768]{1,0:T(8,128)(2,1)S(1)}, bf16[192,768]{1,0:T(8,128)(2,1)S(1)}, u32[]{:S(2)}, u32[]{:S(2)}) collective-permute-start(bf16[192,768]{1,0:T(8,128)(2,1)S(1)} %collective-permute-done.28.a4), channel_id=1, source_target_pairs={{0,8},{1,9},{2,10},{3,11},{4,12},{5,13},{6,14},{7,15},{8,0},{9,1},... | collective-permute-start | bytes 884744 | tf_op jit(solution)/shard_map/ppermute | solution.py:47
  88.1 1.2 %collective-permute-done.32.refs_3_ = bf16[192,768]{1,0:T(8,128)(2,1)S(1)} collective-permute-done((bf16[192,768]{1,0:T(8,128)(2,1)S(1)}, bf16[192,768]{1,0:T(8,128)(2,1)S(1)}, u32[]{:S(2)}, u32[]{:S(2)}) %collective-permute-start.32) | collective-permute-done | bytes 294944 | tf_op jit(solution)/shard_map/ppermute | solution.py:47
  89.3 0.8 shard_map.44
  90.1 0.7 collective-permute-start.33
  90.8 0.8 shard_map.43
  91.6 6.8 %collective-permute-done.33 = bf16[192,768]{1,0:T(8,128)(2,1)S(1)} collective-permute-done((bf16[192,768]{1,0:T(8,128)(2,1)S(1)}, bf16[192,768]{1,0:T(8,128)(2,1)S(1)}, u32[]{:S(2)}, u32[]{:S(2)}) %collective-permute-start.33) | collective-permute-done | bytes 294944 | tf_op jit(solution)/shard_map/ppermute | solution.py:47
  98.4 0.8 multiply_convert_fusion
  (27 shorter events, 0.4 us)
Async XLA Ops:
  1.2 8.8 %collective-permute-start = (bf16[192,384]{1,0:T(8,128)(2,1)S(1)}, bf16[192,384]{1,0:T(8,128)(2,1)S(1)}, u32[]{:S(2)}, u32[]{:S(2)}) collective-permute-start(bf16[192,384]{1,0:T(8,128)(2,1)S(1)} %get-tuple-element.20), channel_id=1, source_target_pairs={{0,16},{1,17},{2,18},{3,19},{4,20},{5,21},{6,22},{7,23},{8,24},{9,... | collective-permute-start | bytes 442376 | tf_op jit(solution)/shard_map/ppermute | solution.py:47
  3.4 9.4 %collective-permute-start.8 = (bf16[192,768]{1,0:T(8,128)(2,1)S(1)}, bf16[192,768]{1,0:T(8,128)(2,1)S(1)}, u32[]{:S(2)}, u32[]{:S(2)}) collective-permute-start(bf16[192,768]{1,0:T(8,128)(2,1)S(1)} %get-tuple-element.21.refs_8_), channel_id=1, source_target_pairs={{0,8},{1,9},{2,10},{3,11},{4,12},{5,13},{6,14},{7,15},{8,0},{9,1},... | collective-permute-start | bytes 884744 | tf_op jit(solution)/shard_map/ppermute | solution.py:47
  4.7 13.5 %collective-permute-start.9 = (bf16[192,768]{1,0:T(8,128)(2,1)S(1)}, bf16[192,768]{1,0:T(8,128)(2,1)S(1)}, u32[]{:S(2)}, u32[]{:S(2)}) collective-permute-start(bf16[192,768]{1,0:T(8,128)(2,1)S(1)} %get-tuple-element.21.refs_8_), channel_id=1, source_target_pairs={{0,32},{1,33},{2,34},{3,35},{4,36},{5,37},{6,38},{7,39},{8,232},{9... | collective-permute-start | bytes 884744 | tf_op jit(solution)/shard_map/ppermute | solution.py:47
  10.0 10.2 %collective-permute-start.1 = (bf16[384,384]{1,0:T(8,128)(2,1)S(1)}, bf16[384,384]{1,0:T(8,128)(2,1)S(1)}, u32[]{:S(2)}, u32[]{:S(2)}) collective-permute-start(bf16[384,384]{1,0:T(8,128)(2,1)S(1)} %constant_dynamic-update-slice_fusion.refs_0_), channel_id=1, source_target_pairs={{0,1},{1,2},{2,3},{3,0},{4,5},{5,6},{6,7},{7,4},{8,9},{9,10},{10,1... | collective-permute-start | bytes 884744 | tf_op jit(solution)/shard_map/ppermute | solution.py:47
  11.3 8.9 %collective-permute-start.2 = (bf16[384,384]{1,0:T(8,128)(2,1)S(1)}, bf16[384,384]{1,0:T(8,128)(2,1)S(1)}, u32[]{:S(2)}, u32[]{:S(2)}) collective-permute-start(bf16[384,384]{1,0:T(8,128)(2,1)S(1)} %constant_dynamic-update-slice_fusion.refs_0_), channel_id=1, source_target_pairs={{0,3},{1,0},{2,1},{3,2},{4,7},{5,4},{6,5},{7,6},{8,11},{9,8},{10,9... | collective-permute-start | bytes 884744 | tf_op jit(solution)/shard_map/ppermute | solution.py:47
  12.8 10.0 %collective-permute-start.10 = (bf16[192,768]{1,0:T(8,128)(2,1)S(1)}, bf16[192,768]{1,0:T(8,128)(2,1)S(1)}, u32[]{:S(2)}, u32[]{:S(2)}) collective-permute-start(bf16[192,768]{1,0:T(8,128)(2,1)S(1)} %collective-permute-done.8.refs_9_), channel_id=1, source_target_pairs={{0,32},{1,33},{2,34},{3,35},{4,36},{5,37},{6,38},{7,39},{8,232},{9... | collective-permute-start | bytes 884744 | tf_op jit(solution)/shard_map/ppermute | solution.py:47
  15.2 9.1 %collective-permute-start.3 = (bf16[384,384]{1,0:T(8,128)(2,1)S(1)}, bf16[384,384]{1,0:T(8,128)(2,1)S(1)}, u32[]{:S(2)}, u32[]{:S(2)}) collective-permute-start(bf16[384,384]{1,0:T(8,128)(2,1)S(1)} %constant_dynamic-update-slice_fusion.refs_0_), channel_id=1, source_target_pairs={{0,4},{1,5},{2,6},{3,7},{4,0},{5,1},{6,2},{7,3},{8,12},{9,13},{10,... | collective-permute-start | bytes 884744 | tf_op jit(solution)/shard_map/ppermute | solution.py:47
  18.1 6.2 %collective-permute-start.11 = (bf16[192,768]{1,0:T(8,128)(2,1)S(1)}, bf16[192,768]{1,0:T(8,128)(2,1)S(1)}, u32[]{:S(2)}, u32[]{:S(2)}) collective-permute-start(bf16[192,768]{1,0:T(8,128)(2,1)S(1)} %collective-permute-done.9.refs_10_), channel_id=1, source_target_pairs={{0,32},{1,33},{2,34},{3,35},{4,36},{5,37},{6,38},{7,39},{8,232},{9... | collective-permute-start | bytes 884744 | tf_op jit(solution)/shard_map/ppermute | solution.py:47
  20.2 8.4 %collective-permute-start.4 = (bf16[384,384]{1,0:T(8,128)(2,1)S(1)}, bf16[384,384]{1,0:T(8,128)(2,1)S(1)}, u32[]{:S(2)}, u32[]{:S(2)}) collective-permute-start(bf16[384,384]{1,0:T(8,128)(2,1)S(1)} %broadcast_select_fusion), channel_id=1, source_target_pairs={{0,1},{1,2},{2,3},{3,0},{4,5},{5,6},{6,7},{7,4},{8,11},{9,8},{10,9... | collective-permute-start | bytes 884744 | tf_op jit(solution)/shard_map/ppermute | solution.py:47
  22.8 8.1 %collective-permute-start.12 = (bf16[192,768]{1,0:T(8,128)(2,1)S(1)}, bf16[192,768]{1,0:T(8,128)(2,1)S(1)}, u32[]{:S(2)}, u32[]{:S(2)}) collective-permute-start(bf16[192,768]{1,0:T(8,128)(2,1)S(1)} %collective-permute-done.10.refs_11_), channel_id=1, source_target_pairs={{0,32},{1,33},{2,34},{3,35},{4,36},{5,37},{6,38},{7,39},{8,232},{9... | collective-permute-start | bytes 884744 | tf_op jit(solution)/shard_map/ppermute | solution.py:47
  24.4 7.5 %collective-permute-start.13 = (bf16[192,768]{1,0:T(8,128)(2,1)S(1)}, bf16[192,768]{1,0:T(8,128)(2,1)S(1)}, u32[]{:S(2)}, u32[]{:S(2)}) collective-permute-start(bf16[192,768]{1,0:T(8,128)(2,1)S(1)} %collective-permute-done.11.refs_12_), channel_id=1, source_target_pairs={{0,32},{1,33},{2,34},{3,35},{4,36},{5,37},{6,38},{7,39},{8,232},{9... | collective-permute-start | bytes 884744 | tf_op jit(solution)/shard_map/ppermute | solution.py:47
  26.0 10.2 %collective-permute-start.5 = (bf16[384,384]{1,0:T(8,128)(2,1)S(1)}, bf16[384,384]{1,0:T(8,128)(2,1)S(1)}, u32[]{:S(2)}, u32[]{:S(2)}) collective-permute-start(bf16[384,384]{1,0:T(8,128)(2,1)S(1)} %collective-permute-done.3.refs_3_), channel_id=1, source_target_pairs={{0,1},{1,2},{2,3},{3,0},{4,5},{5,6},{6,7},{7,4},{8,9},{9,10},{10,1... | collective-permute-start | bytes 884744 | tf_op jit(solution)/shard_map/ppermute | solution.py:47
  26.0 10.5 %collective-permute-start.6 = (bf16[384,384]{1,0:T(8,128)(2,1)S(1)}, bf16[384,384]{1,0:T(8,128)(2,1)S(1)}, u32[]{:S(2)}, u32[]{:S(2)}) collective-permute-start(bf16[384,384]{1,0:T(8,128)(2,1)S(1)} %collective-permute-done.3.refs_3_), channel_id=1, source_target_pairs={{0,3},{1,0},{2,1},{3,2},{4,7},{5,4},{6,5},{7,6},{8,11},{9,8},{10,9... | collective-permute-start | bytes 884744 | tf_op jit(solution)/shard_map/ppermute | solution.py:47
  28.6 10.0 %collective-permute-start.7 = (bf16[384,384]{1,0:T(8,128)(2,1)S(1)}, bf16[384,384]{1,0:T(8,128)(2,1)S(1)}, u32[]{:S(2)}, u32[]{:S(2)}) collective-permute-start(bf16[384,384]{1,0:T(8,128)(2,1)S(1)} %collective-permute-done.4.refs_4_), channel_id=1, source_target_pairs={{0,4},{1,5},{2,6},{3,7},{4,0},{5,1},{6,2},{7,3},{8,12},{9,13},{10,... | collective-permute-start | bytes 884744 | tf_op jit(solution)/shard_map/ppermute | solution.py:47
  30.9 8.7 %collective-permute-start.14 = (bf16[192,768]{1,0:T(8,128)(2,1)S(1)}, bf16[192,768]{1,0:T(8,128)(2,1)S(1)}, u32[]{:S(2)}, u32[]{:S(2)}) collective-permute-start(bf16[192,768]{1,0:T(8,128)(2,1)S(1)} %collective-permute-done.12.refs_13_), channel_id=1, source_target_pairs={{0,32},{1,33},{2,34},{3,35},{4,36},{5,37},{6,38},{7,39},{8,232},{9... | collective-permute-start | bytes 884744 | tf_op jit(solution)/shard_map/ppermute | solution.py:47
  31.8 12.7 %collective-permute-start.16 = (bf16[384,768]{1,0:T(8,128)(2,1)S(1)}, bf16[384,768]{1,0:T(8,128)(2,1)S(1)}, u32[]{:S(2)}, u32[]{:S(2)}) collective-permute-start(bf16[384,768]{1,0:T(8,128)(2,1)S(1)} %pad_maximum_fusion), channel_id=1, source_target_pairs={{0,8},{1,9},{2,10},{3,11},{4,12},{5,13},{6,14},{7,15},{8,0},{9,1},... | collective-permute-start | bytes 1769480 | tf_op jit(solution)/shard_map/ppermute | solution.py:47
  36.2 6.7 %collective-permute-start.15 = (bf16[192,768]{1,0:T(8,128)(2,1)S(1)}, bf16[192,768]{1,0:T(8,128)(2,1)S(1)}, u32[]{:S(2)}, u32[]{:S(2)}) collective-permute-start(bf16[192,768]{1,0:T(8,128)(2,1)S(1)} %collective-permute-done.13.refs_14_), channel_id=1, source_target_pairs={{0,32},{1,33},{2,34},{3,35},{4,36},{5,37},{6,38},{7,39},{8,232},{9... | collective-permute-start | bytes 884744 | tf_op jit(solution)/shard_map/ppermute | solution.py:47
  38.6 7.1 %collective-permute-start.17 = (bf16[384,768]{1,0:T(8,128)(2,1)S(1)}, bf16[384,768]{1,0:T(8,128)(2,1)S(1)}, u32[]{:S(2)}, u32[]{:S(2)}) collective-permute-start(bf16[384,768]{1,0:T(8,128)(2,1)S(1)} %pad_maximum_fusion.1), channel_id=1, source_target_pairs={{0,8},{1,9},{2,10},{3,11},{4,12},{5,13},{6,14},{7,15},{8,0},{9,1},... | collective-permute-start | bytes 1769480 | tf_op jit(solution)/shard_map/ppermute | solution.py:47
  39.6 6.1 %collective-permute-start.18 = (bf16[384,768]{1,0:T(8,128)(2,1)S(1)}, bf16[384,768]{1,0:T(8,128)(2,1)S(1)}, u32[]{:S(2)}, u32[]{:S(2)}) collective-permute-start(bf16[384,768]{1,0:T(8,128)(2,1)S(1)} %pad_maximum_fusion.2), channel_id=1, source_target_pairs={{0,8},{1,9},{2,10},{3,11},{4,12},{5,13},{6,14},{7,15},{8,0},{9,1},... | collective-permute-start | bytes 1769480 | tf_op jit(solution)/shard_map/ppermute | solution.py:47
  42.9 2.8 %collective-permute-start.19 = (bf16[192,768]{1,0:T(8,128)(2,1)S(1)}, bf16[192,768]{1,0:T(8,128)(2,1)S(1)}, u32[]{:S(2)}, u32[]{:S(2)}) collective-permute-start(bf16[192,768]{1,0:T(8,128)(2,1)S(1)} %collective-permute-done.15.a4), channel_id=1, source_target_pairs={{0,8},{1,9},{2,10},{3,11},{4,12},{5,13},{6,14},{7,15},{8,0},{9,1},... | collective-permute-start | bytes 884744 | tf_op jit(solution)/shard_map/ppermute | solution.py:47
  45.7 1.5 %copy-start = (s32[48,48]{1,0:T(8,128)S(1)}, s32[48,48]{1,0:T(8,128)}, u32[]{:S(2)}) copy-start(s32[48,48]{1,0:T(8,128)} %pattern.3) | copy-start | bytes 27652
  45.7 1.5 %copy-start.1 = (s32[48,48]{1,0:T(8,128)S(1)}, s32[48,48]{1,0:T(8,128)}, u32[]{:S(2)}) copy-start(s32[48,48]{1,0:T(8,128)} %keep.1) | copy-start | bytes 27652
  46.5 8.3 %collective-permute-start.20 = (bf16[192,768]{1,0:T(8,128)(2,1)S(1)}, bf16[192,768]{1,0:T(8,128)(2,1)S(1)}, u32[]{:S(2)}, u32[]{:S(2)}) collective-permute-start(bf16[192,768]{1,0:T(8,128)(2,1)S(1)} %shard_map.41), channel_id=1, source_target_pairs={{0,16},{1,17},{2,18},{3,19},{4,20},{5,21},{6,22},{7,23},{8,24},{9,... | collective-permute-start | bytes 884744 | tf_op jit(solution)/shard_map/ppermute | solution.py:47
  54.9 2.6 %collective-permute-start.21 = (bf16[192,768]{1,0:T(8,128)(2,1)S(1)}, bf16[192,768]{1,0:T(8,128)(2,1)S(1)}, u32[]{:S(2)}, u32[]{:S(2)}) collective-permute-start(bf16[192,768]{1,0:T(8,128)(2,1)S(1)} %subtract_convert_fusion.refs_1_), channel_id=1, source_target_pairs={{0,8},{1,9},{2,10},{3,11},{4,12},{5,13},{6,14},{7,15},{8,0},{9,1},... | collective-permute-start | bytes 884744 | tf_op jit(solution)/shard_map/ppermute | solution.py:47
  56.3 5.9 %collective-permute-start.22 = (bf16[192,768]{1,0:T(8,128)(2,1)S(1)}, bf16[192,768]{1,0:T(8,128)(2,1)S(1)}, u32[]{:S(2)}, u32[]{:S(2)}) collective-permute-start(bf16[192,768]{1,0:T(8,128)(2,1)S(1)} %subtract_convert_fusion.refs_1_), channel_id=1, source_target_pairs={{0,32},{1,33},{2,34},{3,35},{4,36},{5,37},{6,38},{7,39},{8,232},{9... | collective-permute-start | bytes 884744 | tf_op jit(solution)/shard_map/ppermute | solution.py:47
  57.6 7.7 %collective-permute-start.23 = (bf16[192,768]{1,0:T(8,128)(2,1)S(1)}, bf16[192,768]{1,0:T(8,128)(2,1)S(1)}, u32[]{:S(2)}, u32[]{:S(2)}) collective-permute-start(bf16[192,768]{1,0:T(8,128)(2,1)S(1)} %collective-permute-done.21.refs_2_), channel_id=1, source_target_pairs={{0,32},{1,33},{2,34},{3,35},{4,36},{5,37},{6,38},{7,39},{8,232},{9... | collective-permute-start | bytes 884744 | tf_op jit(solution)/shard_map/ppermute | solution.py:47
  62.1 6.0 %collective-permute-start.24 = (bf16[192,768]{1,0:T(8,128)(2,1)S(1)}, bf16[192,768]{1,0:T(8,128)(2,1)S(1)}, u32[]{:S(2)}, u32[]{:S(2)}) collective-permute-start(bf16[192,768]{1,0:T(8,128)(2,1)S(1)} %collective-permute-done.22.refs_3_), channel_id=1, source_target_pairs={{0,32},{1,33},{2,34},{3,35},{4,36},{5,37},{6,38},{7,39},{8,232},{9... | collective-permute-start | bytes 884744 | tf_op jit(solution)/shard_map/ppermute | solution.py:47
  65.3 6.3 %collective-permute-start.25 = (bf16[192,768]{1,0:T(8,128)(2,1)S(1)}, bf16[192,768]{1,0:T(8,128)(2,1)S(1)}, u32[]{:S(2)}, u32[]{:S(2)}) collective-permute-start(bf16[192,768]{1,0:T(8,128)(2,1)S(1)} %collective-permute-done.23.refs_4_), channel_id=1, source_target_pairs={{0,32},{1,33},{2,34},{3,35},{4,36},{5,37},{6,38},{7,39},{8,232},{9... | collective-permute-start | bytes 884744 | tf_op jit(solution)/shard_map/ppermute | solution.py:47
  68.1 7.4 %collective-permute-start.26 = (bf16[192,768]{1,0:T(8,128)(2,1)S(1)}, bf16[192,768]{1,0:T(8,128)(2,1)S(1)}, u32[]{:S(2)}, u32[]{:S(2)}) collective-permute-start(bf16[192,768]{1,0:T(8,128)(2,1)S(1)} %collective-permute-done.24.refs_5_), channel_id=1, source_target_pairs={{0,32},{1,33},{2,34},{3,35},{4,36},{5,37},{6,38},{7,39},{8,232},{9... | collective-permute-start | bytes 884744 | tf_op jit(solution)/shard_map/ppermute | solution.py:47
  71.6 8.9 %collective-permute-start.27 = (bf16[192,768]{1,0:T(8,128)(2,1)S(1)}, bf16[192,768]{1,0:T(8,128)(2,1)S(1)}, u32[]{:S(2)}, u32[]{:S(2)}) collective-permute-start(bf16[192,768]{1,0:T(8,128)(2,1)S(1)} %collective-permute-done.25.refs_6_), channel_id=1, source_target_pairs={{0,32},{1,33},{2,34},{3,35},{4,36},{5,37},{6,38},{7,39},{8,232},{9... | collective-permute-start | bytes 884744 | tf_op jit(solution)/shard_map/ppermute | solution.py:47
  74.4 13.7 %collective-permute-start.29 = (bf16[384,768]{1,0:T(8,128)(2,1)S(1)}, bf16[384,768]{1,0:T(8,128)(2,1)S(1)}, u32[]{:S(2)}, u32[]{:S(2)}) collective-permute-start(bf16[384,768]{1,0:T(8,128)(2,1)S(1)} %pad_maximum_fusion.3), channel_id=1, source_target_pairs={{0,8},{1,9},{2,10},{3,11},{4,12},{5,13},{6,14},{7,15},{8,0},{9,1},... | collective-permute-start | bytes 1769480 | tf_op jit(solution)/shard_map/ppermute | solution.py:47
  75.5 9.3 %collective-permute-start.28 = (bf16[192,768]{1,0:T(8,128)(2,1)S(1)}, bf16[192,768]{1,0:T(8,128)(2,1)S(1)}, u32[]{:S(2)}, u32[]{:S(2)}) collective-permute-start(bf16[192,768]{1,0:T(8,128)(2,1)S(1)} %collective-permute-done.26.refs_7_), channel_id=1, source_target_pairs={{0,32},{1,33},{2,34},{3,35},{4,36},{5,37},{6,38},{7,39},{8,232},{9... | collective-permute-start | bytes 884744 | tf_op jit(solution)/shard_map/ppermute | solution.py:47
  78.5 9.6 %collective-permute-start.30 = (bf16[384,768]{1,0:T(8,128)(2,1)S(1)}, bf16[384,768]{1,0:T(8,128)(2,1)S(1)}, u32[]{:S(2)}, u32[]{:S(2)}) collective-permute-start(bf16[384,768]{1,0:T(8,128)(2,1)S(1)} %pad_maximum_fusion.4), channel_id=1, source_target_pairs={{0,8},{1,9},{2,10},{3,11},{4,12},{5,13},{6,14},{7,15},{8,0},{9,1},... | collective-permute-start | bytes 1769480 | tf_op jit(solution)/shard_map/ppermute | solution.py:47
  80.5 8.7 %collective-permute-start.31 = (bf16[384,768]{1,0:T(8,128)(2,1)S(1)}, bf16[384,768]{1,0:T(8,128)(2,1)S(1)}, u32[]{:S(2)}, u32[]{:S(2)}) collective-permute-start(bf16[384,768]{1,0:T(8,128)(2,1)S(1)} %pad_maximum_fusion.5), channel_id=1, source_target_pairs={{0,8},{1,9},{2,10},{3,11},{4,12},{5,13},{6,14},{7,15},{8,0},{9,1},... | collective-permute-start | bytes 1769480 | tf_op jit(solution)/shard_map/ppermute | solution.py:47
  84.8 4.5 %collective-permute-start.32 = (bf16[192,768]{1,0:T(8,128)(2,1)S(1)}, bf16[192,768]{1,0:T(8,128)(2,1)S(1)}, u32[]{:S(2)}, u32[]{:S(2)}) collective-permute-start(bf16[192,768]{1,0:T(8,128)(2,1)S(1)} %collective-permute-done.28.a4), channel_id=1, source_target_pairs={{0,8},{1,9},{2,10},{3,11},{4,12},{5,13},{6,14},{7,15},{8,0},{9,1},... | collective-permute-start | bytes 884744 | tf_op jit(solution)/shard_map/ppermute | solution.py:47
  90.1 8.3 %collective-permute-start.33 = (bf16[192,768]{1,0:T(8,128)(2,1)S(1)}, bf16[192,768]{1,0:T(8,128)(2,1)S(1)}, u32[]{:S(2)}, u32[]{:S(2)}) collective-permute-start(bf16[192,768]{1,0:T(8,128)(2,1)S(1)} %shard_map.44), channel_id=1, source_target_pairs={{0,16},{1,17},{2,18},{3,19},{4,20},{5,21},{6,22},{7,23},{8,24},{9,... | collective-permute-start | bytes 884744 | tf_op jit(solution)/shard_map/ppermute | solution.py:47

commit v8 on v6

--- a/solution.py
+++ b/solution.py
@@ -159,6 +159,12 @@
     result[...] = (total[rows] + multiply(left, rows, parts)).astype(result.dtype)
 
 
+def keep_kernel(left, total, scale, offset, *refs):
+    result = refs[-1]
+    last_kernel(0, left, total, *refs)
+    result[...] = offset[...] + scale[...] * result[...]
+
+
 def factor_kernel(pattern, keep, kept_square, eye, kept_result):
     row, col = lax.axis_index("row"), lax.axis_index("col")
 
@@ -167,7 +173,7 @@
         down = lax.broadcasted_iota(jnp.int32, shape, 0) + (row * ROWS + rows.start)
         over = lax.broadcasted_iota(jnp.int32, shape, 1) + (col * COLS + cols.start)
         eye[rows, cols] = jnp.where(down == over, 1.5, 0.0).astype(F32)
-        square_factor = jnp.where(listed(keep, a, b), 0.5, 0.0).astype(F32)
+        square_factor = jnp.where(listed(keep, a, b), -0.5, 0.0).astype(F32)
         kept_square[rows, cols] = jnp.full(shape, square_factor, F32)
         result_factor = jnp.where(listed(pattern, a, b) | (a == b), 1.0, 0.0).astype(F32)
         kept_result[rows, cols] = jnp.full(shape, result_factor, F32)
@@ -223,13 +229,14 @@
 SUMS = struct(HALF, COLS, dtype=F32)
 
 
-def sums(left, total, last):
-    args = [left, total, *last]
-    away_kernel, keep_kernel = functools.partial(last_kernel, 1), functools.partial(last_kernel, 0)
-    (away,) = call(away_kernel, args, [struct(ROWS, COLS)], [], FLOPS // 4)
+def scaled_sums(left, total, last, scale, offset):
+    (away,) = call(
+        functools.partial(last_kernel, 1), [left, total, *last], [struct(ROWS, COLS)], [], FLOPS // 4
+    )
     theirs = send(away, TWIN)
+    args = [left, total, scale, offset, *last]
     (kept,) = call(keep_kernel, args, [struct(ROWS, COLS, dtype=F32)], [], FLOPS // 4)
-    return kept + theirs.astype(F32)
+    return (kept + scale * theirs.astype(F32)).astype(BF16)
 
 
 def in_hbm(value):
@@ -254,13 +261,13 @@
         return call(square_kernel, [*pieces, *near], [SUMS, struct(8, 2, HALF, ROWS)], [], FLOPS // 2)
 
     (total, left), last = ring(x, square, a2=pieces[:1], a3=pieces[1:4], b3=pieces[4:5], s2=pieces[5:])
-    weight = (eye - sums(left, total, last) * kept_square).astype(BF16)
+    weight = scaled_sums(left, total, last, kept_square, eye)
 
     def update(near):
         return call(update_kernel, [left, *near], [SUMS], [], FLOPS // 2)
 
     (total,), last = ring(weight, update)
-    return (sums(left, total, last) * kept_result).astype(BF16)
+    return scaled_sums(left, total, last, kept_result, jnp.zeros_like(eye))
 
 
 def solution(mesh):

time: 99.3 us -> 99.2 us (level)
  no operation moved by 1% of the time
where the time goes in v8:
time: 99.2 us; the launch traced here: 99.1 us
  starting transfers between devices  60.8 us (61%)
  waiting for transfers between devices  28 us (28%)
  Pallas kernels  8.99 us (9%)
  other arithmetic  1.14 us (1%)
    ppermute x34, starting transfers between devices, send(): return lax.ppermute(value, AXES, pairs)  60.8 us
    ppermute x34, waiting for transfers between devices, send(): return lax.ppermute(value, AXES, pairs)  28 us
    pallas_call x8, Pallas kernels, call(): pl.pallas_call(kernel, in_specs=specs or [SMEM if arg.dtype == jnp.int32...  8.99 us
  transfers between devices with their start and end apart: 34, of which 13 were waited for; matrix products, arithmetic and copies ran while one was open for 0% of the time, Pallas kernels for 6%

profile of v8, /device:TPU:1, one launch (start us, length us, event | category | flops | bytes accessed | tf_op | source)
XLA Modules:
  0.0 99.1 jit_solution(14281814866732131896)
XLA Ops:
  0.0 1.2 %shard_map.37 = (bf16[192,768]{1,0:T(8,128)(2,1)S(1)}, bf16[192,384]{1,0:T(8,128)(2,1)S(1)}, bf16[192,384]{1,0:T(8,128)(2,1)S(1)}) custom-call(s32[48,48]{1,0:T(8,128)} %pattern.3, bf16[192,768]{1,0:T(8,128)(2,1)} %matrix.1), custom_call_target="tpu_custom_call" | custom-call | tf_op jit(solution)/shard_map/pallas_call | solution.py:192
  1.2 2.2 %collective-permute-start = (bf16[192,384]{1,0:T(8,128)(2,1)S(1)}, bf16[192,384]{1,0:T(8,128)(2,1)S(1)}, u32[]{:S(2)}, u32[]{:S(2)}) collective-permute-start(bf16[192,384]{1,0:T(8,128)(2,1)S(1)} %get-tuple-element.20), channel_id=1, source_target_pairs={{0,16},{1,17},{2,18},{3,19},{4,20},{5,21},{6,22},{7,23},{8,24},{9,... | collective-permute-start | bytes 442376 | tf_op jit(solution)/shard_map/ppermute | solution.py:47
  3.4 1.2 %collective-permute-start.8 = (bf16[192,768]{1,0:T(8,128)(2,1)S(1)}, bf16[192,768]{1,0:T(8,128)(2,1)S(1)}, u32[]{:S(2)}, u32[]{:S(2)}) collective-permute-start(bf16[192,768]{1,0:T(8,128)(2,1)S(1)} %get-tuple-element.21.refs_8_), channel_id=1, source_target_pairs={{0,8},{1,9},{2,10},{3,11},{4,12},{5,13},{6,14},{7,15},{8,0},{9,1},... | collective-permute-start | bytes 884744 | tf_op jit(solution)/shard_map/ppermute | solution.py:47
  4.7 5.3 %collective-permute-start.9 = (bf16[192,768]{1,0:T(8,128)(2,1)S(1)}, bf16[192,768]{1,0:T(8,128)(2,1)S(1)}, u32[]{:S(2)}, u32[]{:S(2)}) collective-permute-start(bf16[192,768]{1,0:T(8,128)(2,1)S(1)} %get-tuple-element.21.refs_8_), channel_id=1, source_target_pairs={{0,32},{1,33},{2,34},{3,35},{4,36},{5,37},{6,38},{7,39},{8,232},{9... | collective-permute-start | bytes 884744 | tf_op jit(solution)/shard_map/ppermute | solution.py:47
  10.0 0.0 collective-permute-done
  10.0 1.3 %collective-permute-start.1 = (bf16[384,384]{1,0:T(8,128)(2,1)S(1)}, bf16[384,384]{1,0:T(8,128)(2,1)S(1)}, u32[]{:S(2)}, u32[]{:S(2)}) collective-permute-start(bf16[384,384]{1,0:T(8,128)(2,1)S(1)} %constant_dynamic-update-slice_fusion.refs_0_), channel_id=1, source_target_pairs={{0,1},{1,2},{2,3},{3,0},{4,5},{5,6},{6,7},{7,4},{8,9},{9,10},{10,1... | collective-permute-start | bytes 884744 | tf_op jit(solution)/shard_map/ppermute | solution.py:47
  11.3 1.5 %collective-permute-start.2 = (bf16[384,384]{1,0:T(8,128)(2,1)S(1)}, bf16[384,384]{1,0:T(8,128)(2,1)S(1)}, u32[]{:S(2)}, u32[]{:S(2)}) collective-permute-start(bf16[384,384]{1,0:T(8,128)(2,1)S(1)} %constant_dynamic-update-slice_fusion.refs_0_), channel_id=1, source_target_pairs={{0,3},{1,0},{2,1},{3,2},{4,7},{5,4},{6,5},{7,6},{8,11},{9,8},{10,9... | collective-permute-start | bytes 884744 | tf_op jit(solution)/shard_map/ppermute | solution.py:47
  12.8 0.0 collective-permute-done.8.refs_9_
  12.8 2.4 %collective-permute-start.10 = (bf16[192,768]{1,0:T(8,128)(2,1)S(1)}, bf16[192,768]{1,0:T(8,128)(2,1)S(1)}, u32[]{:S(2)}, u32[]{:S(2)}) collective-permute-start(bf16[192,768]{1,0:T(8,128)(2,1)S(1)} %collective-permute-done.8.refs_9_), channel_id=1, source_target_pairs={{0,32},{1,33},{2,34},{3,35},{4,36},{5,37},{6,38},{7,39},{8,232},{9... | collective-permute-start | bytes 884744 | tf_op jit(solution)/shard_map/ppermute | solution.py:47
  15.2 2.9 %collective-permute-start.3 = (bf16[384,384]{1,0:T(8,128)(2,1)S(1)}, bf16[384,384]{1,0:T(8,128)(2,1)S(1)}, u32[]{:S(2)}, u32[]{:S(2)}) collective-permute-start(bf16[384,384]{1,0:T(8,128)(2,1)S(1)} %constant_dynamic-update-slice_fusion.refs_0_), channel_id=1, source_target_pairs={{0,4},{1,5},{2,6},{3,7},{4,0},{5,1},{6,2},{7,3},{8,12},{9,13},{10,... | collective-permute-start | bytes 884744 | tf_op jit(solution)/shard_map/ppermute | solution.py:47
  18.1 0.0 collective-permute-done.9.refs_10_
  18.1 0.7 collective-permute-start.11
  18.9 1.3 %collective-permute-done.1.refs_1_ = bf16[384,384]{1,0:T(8,128)(2,1)S(1)} collective-permute-done((bf16[384,384]{1,0:T(8,128)(2,1)S(1)}, bf16[384,384]{1,0:T(8,128)(2,1)S(1)}, u32[]{:S(2)}, u32[]{:S(2)}) %collective-permute-start.1) | collective-permute-done | bytes 294944 | tf_op jit(solution)/shard_map/ppermute | solution.py:47
  20.2 0.0 collective-permute-done.2.refs_2_
  20.2 2.6 %collective-permute-start.4 = (bf16[384,384]{1,0:T(8,128)(2,1)S(1)}, bf16[384,384]{1,0:T(8,128)(2,1)S(1)}, u32[]{:S(2)}, u32[]{:S(2)}) collective-permute-start(bf16[384,384]{1,0:T(8,128)(2,1)S(1)} %broadcast_select_fusion), channel_id=1, source_target_pairs={{0,1},{1,2},{2,3},{3,0},{4,5},{5,6},{6,7},{7,4},{8,11},{9,8},{10,9... | collective-permute-start | bytes 884744 | tf_op jit(solution)/shard_map/ppermute | solution.py:47
  22.8 0.4 collective-permute-start.12
  23.2 1.1 %collective-permute-done.3.refs_3_ = bf16[384,384]{1,0:T(8,128)(2,1)S(1)} collective-permute-done((bf16[384,384]{1,0:T(8,128)(2,1)S(1)}, bf16[384,384]{1,0:T(8,128)(2,1)S(1)}, u32[]{:S(2)}, u32[]{:S(2)}) %collective-permute-start.3) | collective-permute-done | bytes 294944 | tf_op jit(solution)/shard_map/ppermute | solution.py:47
  24.4 1.6 %collective-permute-start.13 = (bf16[192,768]{1,0:T(8,128)(2,1)S(1)}, bf16[192,768]{1,0:T(8,128)(2,1)S(1)}, u32[]{:S(2)}, u32[]{:S(2)}) collective-permute-start(bf16[192,768]{1,0:T(8,128)(2,1)S(1)} %collective-permute-done.11.refs_12_), channel_id=1, source_target_pairs={{0,32},{1,33},{2,34},{3,35},{4,36},{5,37},{6,38},{7,39},{8,232},{9... | collective-permute-start | bytes 884744 | tf_op jit(solution)/shard_map/ppermute | solution.py:47
  26.0 0.0 collective-permute-start.5
  26.0 2.7 %collective-permute-start.6 = (bf16[384,384]{1,0:T(8,128)(2,1)S(1)}, bf16[384,384]{1,0:T(8,128)(2,1)S(1)}, u32[]{:S(2)}, u32[]{:S(2)}) collective-permute-start(bf16[384,384]{1,0:T(8,128)(2,1)S(1)} %collective-permute-done.3.refs_3_), channel_id=1, source_target_pairs={{0,3},{1,0},{2,1},{3,2},{4,7},{5,4},{6,5},{7,6},{8,11},{9,8},{10,9... | collective-permute-start | bytes 884744 | tf_op jit(solution)/shard_map/ppermute | solution.py:47
  28.6 2.3 %collective-permute-start.7 = (bf16[384,384]{1,0:T(8,128)(2,1)S(1)}, bf16[384,384]{1,0:T(8,128)(2,1)S(1)}, u32[]{:S(2)}, u32[]{:S(2)}) collective-permute-start(bf16[384,384]{1,0:T(8,128)(2,1)S(1)} %collective-permute-done.4.refs_4_), channel_id=1, source_target_pairs={{0,4},{1,5},{2,6},{3,7},{4,0},{5,1},{6,2},{7,3},{8,12},{9,13},{10,... | collective-permute-start | bytes 884744 | tf_op jit(solution)/shard_map/ppermute | solution.py:47
  30.9 0.0 collective-permute-start.14
  31.0 0.9 collective-permute-done.13.refs_14_
  31.8 1.6 %collective-permute-start.16 = (bf16[384,768]{1,0:T(8,128)(2,1)S(1)}, bf16[384,768]{1,0:T(8,128)(2,1)S(1)}, u32[]{:S(2)}, u32[]{:S(2)}) collective-permute-start(bf16[384,768]{1,0:T(8,128)(2,1)S(1)} %pad_maximum_fusion), channel_id=1, source_target_pairs={{0,8},{1,9},{2,10},{3,11},{4,12},{5,13},{6,14},{7,15},{8,0},{9,1},... | collective-permute-start | bytes 1769480 | tf_op jit(solution)/shard_map/ppermute | solution.py:47
  33.5 2.7 %collective-permute-done.5.refs_5_ = bf16[384,384]{1,0:T(8,128)(2,1)S(1)} collective-permute-done((bf16[384,384]{1,0:T(8,128)(2,1)S(1)}, bf16[384,384]{1,0:T(8,128)(2,1)S(1)}, u32[]{:S(2)}, u32[]{:S(2)}) %collective-permute-start.5) | collective-permute-done | bytes 294944 | tf_op jit(solution)/shard_map/ppermute | solution.py:47
  36.2 0.3 collective-permute-start.15
  36.4 2.2 %collective-permute-done.7.refs_7_ = bf16[384,384]{1,0:T(8,128)(2,1)S(1)} collective-permute-done((bf16[384,384]{1,0:T(8,128)(2,1)S(1)}, bf16[384,384]{1,0:T(8,128)(2,1)S(1)}, u32[]{:S(2)}, u32[]{:S(2)}) %collective-permute-start.7) | collective-permute-done | bytes 294944 | tf_op jit(solution)/shard_map/ppermute | solution.py:47
  38.6 1.0 collective-permute-start.17
  39.6 1.5 %collective-permute-start.18 = (bf16[384,768]{1,0:T(8,128)(2,1)S(1)}, bf16[384,768]{1,0:T(8,128)(2,1)S(1)}, u32[]{:S(2)}, u32[]{:S(2)}) collective-permute-start(bf16[384,768]{1,0:T(8,128)(2,1)S(1)} %pad_maximum_fusion.2), channel_id=1, source_target_pairs={{0,8},{1,9},{2,10},{3,11},{4,12},{5,13},{6,14},{7,15},{8,0},{9,1},... | collective-permute-start | bytes 1769480 | tf_op jit(solution)/shard_map/ppermute | solution.py:47
  41.1 1.8 %shard_map.38 = (f32[384,768]{1,0:T(8,128)S(1)}, bf16[8,2,384,192]{3,2,1,0:T(8,128)(2,1)S(1)}) custom-call(bf16[384,384]{1,0:T(8,128)(2,1)S(1)} %constant_dynamic-update-slice_fusion.refs_0_, bf16[384,384]{1,0:T(8,128)(2,1)S(1)} %collective-permute-done.1.refs_1_, bf16[384,384]{1,0:T(8,128)(2,1)S(1)} %collective-permute-done.2.refs_2_, ...), custom_call_target="tpu_custom_call" | custom-call | flops 905969664 | tf_op jit(solution)/shard_map/pallas_call | solution.py:192
  42.9 0.0 collective-permute-done.15.refs_0_.a4
  42.9 1.6 %collective-permute-start.19 = (bf16[192,768]{1,0:T(8,128)(2,1)S(1)}, bf16[192,768]{1,0:T(8,128)(2,1)S(1)}, u32[]{:S(2)}, u32[]{:S(2)}) collective-permute-start(bf16[192,768]{1,0:T(8,128)(2,1)S(1)} %collective-permute-done.15.refs_0_.a4), channel_id=1, source_target_pairs={{0,8},{1,9},{2,10},{3,11},{4,12},{5,13},{6,14},{7,15},{8,0},{9,1},... | collective-permute-start | bytes 884744 | tf_op jit(solution)/shard_map/ppermute | solution.py:47
  44.5 1.2 %collective-permute-done.19.refs_4_.refs_3_ = bf16[192,768]{1,0:T(8,128)(2,1)S(1)} collective-permute-done((bf16[192,768]{1,0:T(8,128)(2,1)S(1)}, bf16[192,768]{1,0:T(8,128)(2,1)S(1)}, u32[]{:S(2)}, u32[]{:S(2)}) %collective-permute-start.19) | collective-permute-done | bytes 294944 | tf_op jit(solution)/shard_map/ppermute | solution.py:47
  45.7 0.0 collective-permute-done.18.refs_3_.refs_2_
  45.7 0.8 shard_map.41
  46.5 0.7 collective-permute-start.20
  47.3 1.5 %shard_map.39 = (f32[192,768]{1,0:T(8,128)S(1)}, f32[192,768]{1,0:T(8,128)S(1)}, f32[192,768]{1,0:T(8,128)S(1)}) custom-call(s32[48,48]{1,0:T(8,128)S(1)} %copy-done, s32[48,48]{1,0:T(8,128)S(1)} %copy-done.1), custom_call_target="tpu_custom_call" | custom-call | flops 147456 | tf_op jit(solution)/shard_map/pallas_call | solution.py:192
  48.8 0.8 shard_map.40
  49.5 5.3 %collective-permute-done.20 = bf16[192,768]{1,0:T(8,128)(2,1)S(1)} collective-permute-done((bf16[192,768]{1,0:T(8,128)(2,1)S(1)}, bf16[192,768]{1,0:T(8,128)(2,1)S(1)}, u32[]{:S(2)}, u32[]{:S(2)}) %collective-permute-start.20) | collective-permute-done | bytes 294944 | tf_op jit(solution)/shard_map/ppermute | solution.py:47
  54.8 0.1 add_convert_fusion.1.refs_1_
  54.9 1.3 %collective-permute-start.21 = (bf16[192,768]{1,0:T(8,128)(2,1)S(1)}, bf16[192,768]{1,0:T(8,128)(2,1)S(1)}, u32[]{:S(2)}, u32[]{:S(2)}) collective-permute-start(bf16[192,768]{1,0:T(8,128)(2,1)S(1)} %add_convert_fusion.1.refs_1_), channel_id=1, source_target_pairs={{0,8},{1,9},{2,10},{3,11},{4,12},{5,13},{6,14},{7,15},{8,0},{9,1},... | collective-permute-start | bytes 884744 | tf_op jit(solution)/shard_map/ppermute | solution.py:47
  56.2 1.3 %collective-permute-start.22 = (bf16[192,768]{1,0:T(8,128)(2,1)S(1)}, bf16[192,768]{1,0:T(8,128)(2,1)S(1)}, u32[]{:S(2)}, u32[]{:S(2)}) collective-permute-start(bf16[192,768]{1,0:T(8,128)(2,1)S(1)} %add_convert_fusion.1.refs_1_), channel_id=1, source_target_pairs={{0,32},{1,33},{2,34},{3,35},{4,36},{5,37},{6,38},{7,39},{8,232},{9... | collective-permute-start | bytes 884744 | tf_op jit(solution)/shard_map/ppermute | solution.py:47
  57.5 1.2 %collective-permute-start.23 = (bf16[192,768]{1,0:T(8,128)(2,1)S(1)}, bf16[192,768]{1,0:T(8,128)(2,1)S(1)}, u32[]{:S(2)}, u32[]{:S(2)}) collective-permute-start(bf16[192,768]{1,0:T(8,128)(2,1)S(1)} %collective-permute-done.21.refs_2_), channel_id=1, source_target_pairs={{0,32},{1,33},{2,34},{3,35},{4,36},{5,37},{6,38},{7,39},{8,232},{9... | collective-permute-start | bytes 884744 | tf_op jit(solution)/shard_map/ppermute | solution.py:47
  58.7 3.3 %collective-permute-done.22.refs_3_ = bf16[192,768]{1,0:T(8,128)(2,1)S(1)} collective-permute-done((bf16[192,768]{1,0:T(8,128)(2,1)S(1)}, bf16[192,768]{1,0:T(8,128)(2,1)S(1)}, u32[]{:S(2)}, u32[]{:S(2)}) %collective-permute-start.22) | collective-permute-done | bytes 294944 | tf_op jit(solution)/shard_map/ppermute | solution.py:47
  62.1 2.2 %collective-permute-start.24 = (bf16[192,768]{1,0:T(8,128)(2,1)S(1)}, bf16[192,768]{1,0:T(8,128)(2,1)S(1)}, u32[]{:S(2)}, u32[]{:S(2)}) collective-permute-start(bf16[192,768]{1,0:T(8,128)(2,1)S(1)} %collective-permute-done.22.refs_3_), channel_id=1, source_target_pairs={{0,32},{1,33},{2,34},{3,35},{4,36},{5,37},{6,38},{7,39},{8,232},{9... | collective-permute-start | bytes 884744 | tf_op jit(solution)/shard_map/ppermute | solution.py:47
  64.3 0.9 collective-permute-done.23.refs_4_
  65.2 2.2 %collective-permute-start.25 = (bf16[192,768]{1,0:T(8,128)(2,1)S(1)}, bf16[192,768]{1,0:T(8,128)(2,1)S(1)}, u32[]{:S(2)}, u32[]{:S(2)}) collective-permute-start(bf16[192,768]{1,0:T(8,128)(2,1)S(1)} %collective-permute-done.23.refs_4_), channel_id=1, source_target_pairs={{0,32},{1,33},{2,34},{3,35},{4,36},{5,37},{6,38},{7,39},{8,232},{9... | collective-permute-start | bytes 884744 | tf_op jit(solution)/shard_map/ppermute | solution.py:47
  67.5 0.6 collective-permute-done.24.refs_5_
  68.1 3.0 %collective-permute-start.26 = (bf16[192,768]{1,0:T(8,128)(2,1)S(1)}, bf16[192,768]{1,0:T(8,128)(2,1)S(1)}, u32[]{:S(2)}, u32[]{:S(2)}) collective-permute-start(bf16[192,768]{1,0:T(8,128)(2,1)S(1)} %collective-permute-done.24.refs_5_), channel_id=1, source_target_pairs={{0,32},{1,33},{2,34},{3,35},{4,36},{5,37},{6,38},{7,39},{8,232},{9... | collective-permute-start | bytes 884744 | tf_op jit(solution)/shard_map/ppermute | solution.py:47
  71.1 0.4 collective-permute-done.25.refs_6_
  71.6 2.7 %collective-permute-start.27 = (bf16[192,768]{1,0:T(8,128)(2,1)S(1)}, bf16[192,768]{1,0:T(8,128)(2,1)S(1)}, u32[]{:S(2)}, u32[]{:S(2)}) collective-permute-start(bf16[192,768]{1,0:T(8,128)(2,1)S(1)} %collective-permute-done.25.refs_6_), channel_id=1, source_target_pairs={{0,32},{1,33},{2,34},{3,35},{4,36},{5,37},{6,38},{7,39},{8,232},{9... | collective-permute-start | bytes 884744 | tf_op jit(solution)/shard_map/ppermute | solution.py:47
  74.3 1.2 %collective-permute-start.29 = (bf16[384,768]{1,0:T(8,128)(2,1)S(1)}, bf16[384,768]{1,0:T(8,128)(2,1)S(1)}, u32[]{:S(2)}, u32[]{:S(2)}) collective-permute-start(bf16[384,768]{1,0:T(8,128)(2,1)S(1)} %pad_maximum_fusion.3), channel_id=1, source_target_pairs={{0,8},{1,9},{2,10},{3,11},{4,12},{5,13},{6,14},{7,15},{8,0},{9,1},... | collective-permute-start | bytes 1769480 | tf_op jit(solution)/shard_map/ppermute | solution.py:47
  75.5 3.0 %collective-permute-start.28 = (bf16[192,768]{1,0:T(8,128)(2,1)S(1)}, bf16[192,768]{1,0:T(8,128)(2,1)S(1)}, u32[]{:S(2)}, u32[]{:S(2)}) collective-permute-start(bf16[192,768]{1,0:T(8,128)(2,1)S(1)} %collective-permute-done.26.refs_7_), channel_id=1, source_target_pairs={{0,32},{1,33},{2,34},{3,35},{4,36},{5,37},{6,38},{7,39},{8,232},{9... | collective-permute-start | bytes 884744 | tf_op jit(solution)/shard_map/ppermute | solution.py:47
  78.5 2.0 %collective-permute-start.30 = (bf16[384,768]{1,0:T(8,128)(2,1)S(1)}, bf16[384,768]{1,0:T(8,128)(2,1)S(1)}, u32[]{:S(2)}, u32[]{:S(2)}) collective-permute-start(bf16[384,768]{1,0:T(8,128)(2,1)S(1)} %pad_maximum_fusion.4), channel_id=1, source_target_pairs={{0,8},{1,9},{2,10},{3,11},{4,12},{5,13},{6,14},{7,15},{8,0},{9,1},... | collective-permute-start | bytes 1769480 | tf_op jit(solution)/shard_map/ppermute | solution.py:47
  80.5 2.9 %collective-permute-start.31 = (bf16[384,768]{1,0:T(8,128)(2,1)S(1)}, bf16[384,768]{1,0:T(8,128)(2,1)S(1)}, u32[]{:S(2)}, u32[]{:S(2)}) collective-permute-start(bf16[384,768]{1,0:T(8,128)(2,1)S(1)} %pad_maximum_fusion.5), channel_id=1, source_target_pairs={{0,8},{1,9},{2,10},{3,11},{4,12},{5,13},{6,14},{7,15},{8,0},{9,1},... | collective-permute-start | bytes 1769480 | tf_op jit(solution)/shard_map/ppermute | solution.py:47
  83.4 1.4 %shard_map.42.total = f32[384,768]{1,0:T(8,128)S(1)} custom-call(bf16[8,2,384,192]{3,2,1,0:T(8,128)(2,1)S(1)} %get-tuple-element.25.left.refs_0_, bf16[192,768]{1,0:T(8,128)(2,1)S(1)} %add_convert_fusion.1.refs_1_, bf16[192,768]{1,0:T(8,128)(2,1)S(1)} %collective-permute-done.21.refs_2_, bf16[192,768]{1,0:T(8,128)(2,1)S(1)} %collective-permute-done.22.refs_3_, ...), custom_call_target="tpu_custom_call" | custom-call | flops 905969664 | tf_op jit(solution)/shard_map/pallas_call | solution.py:192
  84.8 0.0 collective-permute-done.28.refs_0_.a4
  84.8 3.3 %collective-permute-start.32 = (bf16[192,768]{1,0:T(8,128)(2,1)S(1)}, bf16[192,768]{1,0:T(8,128)(2,1)S(1)}, u32[]{:S(2)}, u32[]{:S(2)}) collective-permute-start(bf16[192,768]{1,0:T(8,128)(2,1)S(1)} %collective-permute-done.28.refs_0_.a4), channel_id=1, source_target_pairs={{0,8},{1,9},{2,10},{3,11},{4,12},{5,13},{6,14},{7,15},{8,0},{9,1},... | collective-permute-start | bytes 884744 | tf_op jit(solution)/shard_map/ppermute | solution.py:47
  88.0 1.2 %collective-permute-done.32.refs_4_.refs_3_ = bf16[192,768]{1,0:T(8,128)(2,1)S(1)} collective-permute-done((bf16[192,768]{1,0:T(8,128)(2,1)S(1)}, bf16[192,768]{1,0:T(8,128)(2,1)S(1)}, u32[]{:S(2)}, u32[]{:S(2)}) %collective-permute-start.32) | collective-permute-done | bytes 294944 | tf_op jit(solution)/shard_map/ppermute | solution.py:47
  89.2 0.8 shard_map.44
  90.0 0.7 collective-permute-start.33
  90.8 0.8 shard_map.43
  91.6 6.7 %collective-permute-done.33 = bf16[192,768]{1,0:T(8,128)(2,1)S(1)} collective-permute-done((bf16[192,768]{1,0:T(8,128)(2,1)S(1)}, bf16[192,768]{1,0:T(8,128)(2,1)S(1)}, u32[]{:S(2)}, u32[]{:S(2)}) %collective-permute-start.33) | collective-permute-done | bytes 294944 | tf_op jit(solution)/shard_map/ppermute | solution.py:47
  98.3 0.8 add_convert_fusion
  (28 shorter events, 0.4 us)
Async XLA Ops:
  1.2 8.8 %collective-permute-start = (bf16[192,384]{1,0:T(8,128)(2,1)S(1)}, bf16[192,384]{1,0:T(8,128)(2,1)S(1)}, u32[]{:S(2)}, u32[]{:S(2)}) collective-permute-start(bf16[192,384]{1,0:T(8,128)(2,1)S(1)} %get-tuple-element.20), channel_id=1, source_target_pairs={{0,16},{1,17},{2,18},{3,19},{4,20},{5,21},{6,22},{7,23},{8,24},{9,... | collective-permute-start | bytes 442376 | tf_op jit(solution)/shard_map/ppermute | solution.py:47
  3.4 9.4 %collective-permute-start.8 = (bf16[192,768]{1,0:T(8,128)(2,1)S(1)}, bf16[192,768]{1,0:T(8,128)(2,1)S(1)}, u32[]{:S(2)}, u32[]{:S(2)}) collective-permute-start(bf16[192,768]{1,0:T(8,128)(2,1)S(1)} %get-tuple-element.21.refs_8_), channel_id=1, source_target_pairs={{0,8},{1,9},{2,10},{3,11},{4,12},{5,13},{6,14},{7,15},{8,0},{9,1},... | collective-permute-start | bytes 884744 | tf_op jit(solution)/shard_map/ppermute | solution.py:47
  4.7 13.5 %collective-permute-start.9 = (bf16[192,768]{1,0:T(8,128)(2,1)S(1)}, bf16[192,768]{1,0:T(8,128)(2,1)S(1)}, u32[]{:S(2)}, u32[]{:S(2)}) collective-permute-start(bf16[192,768]{1,0:T(8,128)(2,1)S(1)} %get-tuple-element.21.refs_8_), channel_id=1, source_target_pairs={{0,32},{1,33},{2,34},{3,35},{4,36},{5,37},{6,38},{7,39},{8,232},{9... | collective-permute-start | bytes 884744 | tf_op jit(solution)/shard_map/ppermute | solution.py:47
  10.0 10.2 %collective-permute-start.1 = (bf16[384,384]{1,0:T(8,128)(2,1)S(1)}, bf16[384,384]{1,0:T(8,128)(2,1)S(1)}, u32[]{:S(2)}, u32[]{:S(2)}) collective-permute-start(bf16[384,384]{1,0:T(8,128)(2,1)S(1)} %constant_dynamic-update-slice_fusion.refs_0_), channel_id=1, source_target_pairs={{0,1},{1,2},{2,3},{3,0},{4,5},{5,6},{6,7},{7,4},{8,9},{9,10},{10,1... | collective-permute-start | bytes 884744 | tf_op jit(solution)/shard_map/ppermute | solution.py:47
  11.3 8.9 %collective-permute-start.2 = (bf16[384,384]{1,0:T(8,128)(2,1)S(1)}, bf16[384,384]{1,0:T(8,128)(2,1)S(1)}, u32[]{:S(2)}, u32[]{:S(2)}) collective-permute-start(bf16[384,384]{1,0:T(8,128)(2,1)S(1)} %constant_dynamic-update-slice_fusion.refs_0_), channel_id=1, source_target_pairs={{0,3},{1,0},{2,1},{3,2},{4,7},{5,4},{6,5},{7,6},{8,11},{9,8},{10,9... | collective-permute-start | bytes 884744 | tf_op jit(solution)/shard_map/ppermute | solution.py:47
  12.8 10.0 %collective-permute-start.10 = (bf16[192,768]{1,0:T(8,128)(2,1)S(1)}, bf16[192,768]{1,0:T(8,128)(2,1)S(1)}, u32[]{:S(2)}, u32[]{:S(2)}) collective-permute-start(bf16[192,768]{1,0:T(8,128)(2,1)S(1)} %collective-permute-done.8.refs_9_), channel_id=1, source_target_pairs={{0,32},{1,33},{2,34},{3,35},{4,36},{5,37},{6,38},{7,39},{8,232},{9... | collective-permute-start | bytes 884744 | tf_op jit(solution)/shard_map/ppermute | solution.py:47
  15.2 9.1 %collective-permute-start.3 = (bf16[384,384]{1,0:T(8,128)(2,1)S(1)}, bf16[384,384]{1,0:T(8,128)(2,1)S(1)}, u32[]{:S(2)}, u32[]{:S(2)}) collective-permute-start(bf16[384,384]{1,0:T(8,128)(2,1)S(1)} %constant_dynamic-update-slice_fusion.refs_0_), channel_id=1, source_target_pairs={{0,4},{1,5},{2,6},{3,7},{4,0},{5,1},{6,2},{7,3},{8,12},{9,13},{10,... | collective-permute-start | bytes 884744 | tf_op jit(solution)/shard_map/ppermute | solution.py:47
  18.1 6.2 %collective-permute-start.11 = (bf16[192,768]{1,0:T(8,128)(2,1)S(1)}, bf16[192,768]{1,0:T(8,128)(2,1)S(1)}, u32[]{:S(2)}, u32[]{:S(2)}) collective-permute-start(bf16[192,768]{1,0:T(8,128)(2,1)S(1)} %collective-permute-done.9.refs_10_), channel_id=1, source_target_pairs={{0,32},{1,33},{2,34},{3,35},{4,36},{5,37},{6,38},{7,39},{8,232},{9... | collective-permute-start | bytes 884744 | tf_op jit(solution)/shard_map/ppermute | solution.py:47
  20.2 8.4 %collective-permute-start.4 = (bf16[384,384]{1,0:T(8,128)(2,1)S(1)}, bf16[384,384]{1,0:T(8,128)(2,1)S(1)}, u32[]{:S(2)}, u32[]{:S(2)}) collective-permute-start(bf16[384,384]{1,0:T(8,128)(2,1)S(1)} %broadcast_select_fusion), channel_id=1, source_target_pairs={{0,1},{1,2},{2,3},{3,0},{4,5},{5,6},{6,7},{7,4},{8,11},{9,8},{10,9... | collective-permute-start | bytes 884744 | tf_op jit(solution)/shard_map/ppermute | solution.py:47
  22.8 8.1 %collective-permute-start.12 = (bf16[192,768]{1,0:T(8,128)(2,1)S(1)}, bf16[192,768]{1,0:T(8,128)(2,1)S(1)}, u32[]{:S(2)}, u32[]{:S(2)}) collective-permute-start(bf16[192,768]{1,0:T(8,128)(2,1)S(1)} %collective-permute-done.10.refs_11_), channel_id=1, source_target_pairs={{0,32},{1,33},{2,34},{3,35},{4,36},{5,37},{6,38},{7,39},{8,232},{9... | collective-permute-start | bytes 884744 | tf_op jit(solution)/shard_map/ppermute | solution.py:47
  24.4 7.5 %collective-permute-start.13 = (bf16[192,768]{1,0:T(8,128)(2,1)S(1)}, bf16[192,768]{1,0:T(8,128)(2,1)S(1)}, u32[]{:S(2)}, u32[]{:S(2)}) collective-permute-start(bf16[192,768]{1,0:T(8,128)(2,1)S(1)} %collective-permute-done.11.refs_12_), channel_id=1, source_target_pairs={{0,32},{1,33},{2,34},{3,35},{4,36},{5,37},{6,38},{7,39},{8,232},{9... | collective-permute-start | bytes 884744 | tf_op jit(solution)/shard_map/ppermute | solution.py:47
  26.0 10.2 %collective-permute-start.5 = (bf16[384,384]{1,0:T(8,128)(2,1)S(1)}, bf16[384,384]{1,0:T(8,128)(2,1)S(1)}, u32[]{:S(2)}, u32[]{:S(2)}) collective-permute-start(bf16[384,384]{1,0:T(8,128)(2,1)S(1)} %collective-permute-done.3.refs_3_), channel_id=1, source_target_pairs={{0,1},{1,2},{2,3},{3,0},{4,5},{5,6},{6,7},{7,4},{8,9},{9,10},{10,1... | collective-permute-start | bytes 884744 | tf_op jit(solution)/shard_map/ppermute | solution.py:47
  26.0 10.5 %collective-permute-start.6 = (bf16[384,384]{1,0:T(8,128)(2,1)S(1)}, bf16[384,384]{1,0:T(8,128)(2,1)S(1)}, u32[]{:S(2)}, u32[]{:S(2)}) collective-permute-start(bf16[384,384]{1,0:T(8,128)(2,1)S(1)} %collective-permute-done.3.refs_3_), channel_id=1, source_target_pairs={{0,3},{1,0},{2,1},{3,2},{4,7},{5,4},{6,5},{7,6},{8,11},{9,8},{10,9... | collective-permute-start | bytes 884744 | tf_op jit(solution)/shard_map/ppermute | solution.py:47
  28.6 10.0 %collective-permute-start.7 = (bf16[384,384]{1,0:T(8,128)(2,1)S(1)}, bf16[384,384]{1,0:T(8,128)(2,1)S(1)}, u32[]{:S(2)}, u32[]{:S(2)}) collective-permute-start(bf16[384,384]{1,0:T(8,128)(2,1)S(1)} %collective-permute-done.4.refs_4_), channel_id=1, source_target_pairs={{0,4},{1,5},{2,6},{3,7},{4,0},{5,1},{6,2},{7,3},{8,12},{9,13},{10,... | collective-permute-start | bytes 884744 | tf_op jit(solution)/shard_map/ppermute | solution.py:47
  30.9 8.7 %collective-permute-start.14 = (bf16[192,768]{1,0:T(8,128)(2,1)S(1)}, bf16[192,768]{1,0:T(8,128)(2,1)S(1)}, u32[]{:S(2)}, u32[]{:S(2)}) collective-permute-start(bf16[192,768]{1,0:T(8,128)(2,1)S(1)} %collective-permute-done.12.refs_13_), channel_id=1, source_target_pairs={{0,32},{1,33},{2,34},{3,35},{4,36},{5,37},{6,38},{7,39},{8,232},{9... | collective-permute-start | bytes 884744 | tf_op jit(solution)/shard_map/ppermute | solution.py:47
  31.8 12.7 %collective-permute-start.16 = (bf16[384,768]{1,0:T(8,128)(2,1)S(1)}, bf16[384,768]{1,0:T(8,128)(2,1)S(1)}, u32[]{:S(2)}, u32[]{:S(2)}) collective-permute-start(bf16[384,768]{1,0:T(8,128)(2,1)S(1)} %pad_maximum_fusion), channel_id=1, source_target_pairs={{0,8},{1,9},{2,10},{3,11},{4,12},{5,13},{6,14},{7,15},{8,0},{9,1},... | collective-permute-start | bytes 1769480 | tf_op jit(solution)/shard_map/ppermute | solution.py:47
  36.2 6.7 %collective-permute-start.15 = (bf16[192,768]{1,0:T(8,128)(2,1)S(1)}, bf16[192,768]{1,0:T(8,128)(2,1)S(1)}, u32[]{:S(2)}, u32[]{:S(2)}) collective-permute-start(bf16[192,768]{1,0:T(8,128)(2,1)S(1)} %collective-permute-done.13.refs_14_), channel_id=1, source_target_pairs={{0,32},{1,33},{2,34},{3,35},{4,36},{5,37},{6,38},{7,39},{8,232},{9... | collective-permute-start | bytes 884744 | tf_op jit(solution)/shard_map/ppermute | solution.py:47
  38.6 7.1 %collective-permute-start.17 = (bf16[384,768]{1,0:T(8,128)(2,1)S(1)}, bf16[384,768]{1,0:T(8,128)(2,1)S(1)}, u32[]{:S(2)}, u32[]{:S(2)}) collective-permute-start(bf16[384,768]{1,0:T(8,128)(2,1)S(1)} %pad_maximum_fusion.1), channel_id=1, source_target_pairs={{0,8},{1,9},{2,10},{3,11},{4,12},{5,13},{6,14},{7,15},{8,0},{9,1},... | collective-permute-start | bytes 1769480 | tf_op jit(solution)/shard_map/ppermute | solution.py:47
  39.6 6.1 %collective-permute-start.18 = (bf16[384,768]{1,0:T(8,128)(2,1)S(1)}, bf16[384,768]{1,0:T(8,128)(2,1)S(1)}, u32[]{:S(2)}, u32[]{:S(2)}) collective-permute-start(bf16[384,768]{1,0:T(8,128)(2,1)S(1)} %pad_maximum_fusion.2), channel_id=1, source_target_pairs={{0,8},{1,9},{2,10},{3,11},{4,12},{5,13},{6,14},{7,15},{8,0},{9,1},... | collective-permute-start | bytes 1769480 | tf_op jit(solution)/shard_map/ppermute | solution.py:47
  42.9 2.8 %collective-permute-start.19 = (bf16[192,768]{1,0:T(8,128)(2,1)S(1)}, bf16[192,768]{1,0:T(8,128)(2,1)S(1)}, u32[]{:S(2)}, u32[]{:S(2)}) collective-permute-start(bf16[192,768]{1,0:T(8,128)(2,1)S(1)} %collective-permute-done.15.refs_0_.a4), channel_id=1, source_target_pairs={{0,8},{1,9},{2,10},{3,11},{4,12},{5,13},{6,14},{7,15},{8,0},{9,1},... | collective-permute-start | bytes 884744 | tf_op jit(solution)/shard_map/ppermute | solution.py:47
  45.7 1.5 %copy-start = (s32[48,48]{1,0:T(8,128)S(1)}, s32[48,48]{1,0:T(8,128)}, u32[]{:S(2)}) copy-start(s32[48,48]{1,0:T(8,128)} %pattern.3) | copy-start | bytes 27652
  45.7 1.5 %copy-start.1 = (s32[48,48]{1,0:T(8,128)S(1)}, s32[48,48]{1,0:T(8,128)}, u32[]{:S(2)}) copy-start(s32[48,48]{1,0:T(8,128)} %keep.1) | copy-start | bytes 27652
  46.5 8.3 %collective-permute-start.20 = (bf16[192,768]{1,0:T(8,128)(2,1)S(1)}, bf16[192,768]{1,0:T(8,128)(2,1)S(1)}, u32[]{:S(2)}, u32[]{:S(2)}) collective-permute-start(bf16[192,768]{1,0:T(8,128)(2,1)S(1)} %shard_map.41), channel_id=1, source_target_pairs={{0,16},{1,17},{2,18},{3,19},{4,20},{5,21},{6,22},{7,23},{8,24},{9,... | collective-permute-start | bytes 884744 | tf_op jit(solution)/shard_map/ppermute | solution.py:47
  54.9 2.6 %collective-permute-start.21 = (bf16[192,768]{1,0:T(8,128)(2,1)S(1)}, bf16[192,768]{1,0:T(8,128)(2,1)S(1)}, u32[]{:S(2)}, u32[]{:S(2)}) collective-permute-start(bf16[192,768]{1,0:T(8,128)(2,1)S(1)} %add_convert_fusion.1.refs_1_), channel_id=1, source_target_pairs={{0,8},{1,9},{2,10},{3,11},{4,12},{5,13},{6,14},{7,15},{8,0},{9,1},... | collective-permute-start | bytes 884744 | tf_op jit(solution)/shard_map/ppermute | solution.py:47
  56.2 5.9 %collective-permute-start.22 = (bf16[192,768]{1,0:T(8,128)(2,1)S(1)}, bf16[192,768]{1,0:T(8,128)(2,1)S(1)}, u32[]{:S(2)}, u32[]{:S(2)}) collective-permute-start(bf16[192,768]{1,0:T(8,128)(2,1)S(1)} %add_convert_fusion.1.refs_1_), channel_id=1, source_target_pairs={{0,32},{1,33},{2,34},{3,35},{4,36},{5,37},{6,38},{7,39},{8,232},{9... | collective-permute-start | bytes 884744 | tf_op jit(solution)/shard_map/ppermute | solution.py:47
  57.5 7.7 %collective-permute-start.23 = (bf16[192,768]{1,0:T(8,128)(2,1)S(1)}, bf16[192,768]{1,0:T(8,128)(2,1)S(1)}, u32[]{:S(2)}, u32[]{:S(2)}) collective-permute-start(bf16[192,768]{1,0:T(8,128)(2,1)S(1)} %collective-permute-done.21.refs_2_), channel_id=1, source_target_pairs={{0,32},{1,33},{2,34},{3,35},{4,36},{5,37},{6,38},{7,39},{8,232},{9... | collective-permute-start | bytes 884744 | tf_op jit(solution)/shard_map/ppermute | solution.py:47
  62.1 6.0 %collective-permute-start.24 = (bf16[192,768]{1,0:T(8,128)(2,1)S(1)}, bf16[192,768]{1,0:T(8,128)(2,1)S(1)}, u32[]{:S(2)}, u32[]{:S(2)}) collective-permute-start(bf16[192,768]{1,0:T(8,128)(2,1)S(1)} %collective-permute-done.22.refs_3_), channel_id=1, source_target_pairs={{0,32},{1,33},{2,34},{3,35},{4,36},{5,37},{6,38},{7,39},{8,232},{9... | collective-permute-start | bytes 884744 | tf_op jit(solution)/shard_map/ppermute | solution.py:47
  65.2 6.3 %collective-permute-start.25 = (bf16[192,768]{1,0:T(8,128)(2,1)S(1)}, bf16[192,768]{1,0:T(8,128)(2,1)S(1)}, u32[]{:S(2)}, u32[]{:S(2)}) collective-permute-start(bf16[192,768]{1,0:T(8,128)(2,1)S(1)} %collective-permute-done.23.refs_4_), channel_id=1, source_target_pairs={{0,32},{1,33},{2,34},{3,35},{4,36},{5,37},{6,38},{7,39},{8,232},{9... | collective-permute-start | bytes 884744 | tf_op jit(solution)/shard_map/ppermute | solution.py:47
  68.1 7.4 %collective-permute-start.26 = (bf16[192,768]{1,0:T(8,128)(2,1)S(1)}, bf16[192,768]{1,0:T(8,128)(2,1)S(1)}, u32[]{:S(2)}, u32[]{:S(2)}) collective-permute-start(bf16[192,768]{1,0:T(8,128)(2,1)S(1)} %collective-permute-done.24.refs_5_), channel_id=1, source_target_pairs={{0,32},{1,33},{2,34},{3,35},{4,36},{5,37},{6,38},{7,39},{8,232},{9... | collective-permute-start | bytes 884744 | tf_op jit(solution)/shard_map/ppermute | solution.py:47
  71.6 8.9 %collective-permute-start.27 = (bf16[192,768]{1,0:T(8,128)(2,1)S(1)}, bf16[192,768]{1,0:T(8,128)(2,1)S(1)}, u32[]{:S(2)}, u32[]{:S(2)}) collective-permute-start(bf16[192,768]{1,0:T(8,128)(2,1)S(1)} %collective-permute-done.25.refs_6_), channel_id=1, source_target_pairs={{0,32},{1,33},{2,34},{3,35},{4,36},{5,37},{6,38},{7,39},{8,232},{9... | collective-permute-start | bytes 884744 | tf_op jit(solution)/shard_map/ppermute | solution.py:47
  74.3 13.7 %collective-permute-start.29 = (bf16[384,768]{1,0:T(8,128)(2,1)S(1)}, bf16[384,768]{1,0:T(8,128)(2,1)S(1)}, u32[]{:S(2)}, u32[]{:S(2)}) collective-permute-start(bf16[384,768]{1,0:T(8,128)(2,1)S(1)} %pad_maximum_fusion.3), channel_id=1, source_target_pairs={{0,8},{1,9},{2,10},{3,11},{4,12},{5,13},{6,14},{7,15},{8,0},{9,1},... | collective-permute-start | bytes 1769480 | tf_op jit(solution)/shard_map/ppermute | solution.py:47
  75.5 9.3 %collective-permute-start.28 = (bf16[192,768]{1,0:T(8,128)(2,1)S(1)}, bf16[192,768]{1,0:T(8,128)(2,1)S(1)}, u32[]{:S(2)}, u32[]{:S(2)}) collective-permute-start(bf16[192,768]{1,0:T(8,128)(2,1)S(1)} %collective-permute-done.26.refs_7_), channel_id=1, source_target_pairs={{0,32},{1,33},{2,34},{3,35},{4,36},{5,37},{6,38},{7,39},{8,232},{9... | collective-permute-start | bytes 884744 | tf_op jit(solution)/shard_map/ppermute | solution.py:47
  78.5 9.6 %collective-permute-start.30 = (bf16[384,768]{1,0:T(8,128)(2,1)S(1)}, bf16[384,768]{1,0:T(8,128)(2,1)S(1)}, u32[]{:S(2)}, u32[]{:S(2)}) collective-permute-start(bf16[384,768]{1,0:T(8,128)(2,1)S(1)} %pad_maximum_fusion.4), channel_id=1, source_target_pairs={{0,8},{1,9},{2,10},{3,11},{4,12},{5,13},{6,14},{7,15},{8,0},{9,1},... | collective-permute-start | bytes 1769480 | tf_op jit(solution)/shard_map/ppermute | solution.py:47
  80.5 8.7 %collective-permute-start.31 = (bf16[384,768]{1,0:T(8,128)(2,1)S(1)}, bf16[384,768]{1,0:T(8,128)(2,1)S(1)}, u32[]{:S(2)}, u32[]{:S(2)}) collective-permute-start(bf16[384,768]{1,0:T(8,128)(2,1)S(1)} %pad_maximum_fusion.5), channel_id=1, source_target_pairs={{0,8},{1,9},{2,10},{3,11},{4,12},{5,13},{6,14},{7,15},{8,0},{9,1},... | collective-permute-start | bytes 1769480 | tf_op jit(solution)/shard_map/ppermute | solution.py:47
  84.8 4.5 %collective-permute-start.32 = (bf16[192,768]{1,0:T(8,128)(2,1)S(1)}, bf16[192,768]{1,0:T(8,128)(2,1)S(1)}, u32[]{:S(2)}, u32[]{:S(2)}) collective-permute-start(bf16[192,768]{1,0:T(8,128)(2,1)S(1)} %collective-permute-done.28.refs_0_.a4), channel_id=1, source_target_pairs={{0,8},{1,9},{2,10},{3,11},{4,12},{5,13},{6,14},{7,15},{8,0},{9,1},... | collective-permute-start | bytes 884744 | tf_op jit(solution)/shard_map/ppermute | solution.py:47
  90.0 8.3 %collective-permute-start.33 = (bf16[192,768]{1,0:T(8,128)(2,1)S(1)}, bf16[192,768]{1,0:T(8,128)(2,1)S(1)}, u32[]{:S(2)}, u32[]{:S(2)}) collective-permute-start(bf16[192,768]{1,0:T(8,128)(2,1)S(1)} %shard_map.44), channel_id=1, source_target_pairs={{0,16},{1,17},{2,18},{3,19},{4,20},{5,21},{6,22},{7,23},{8,24},{9,... | collective-permute-start | bytes 884744 | tf_op jit(solution)/shard_map/ppermute | solution.py:47

commit v9 on v6

--- a/solution.py
+++ b/solution.py
@@ -253,7 +253,7 @@
     def square(near):
         return call(square_kernel, [*pieces, *near], [SUMS, struct(8, 2, HALF, ROWS)], [], FLOPS // 2)
 
-    (total, left), last = ring(x, square, a2=pieces[:1], a3=pieces[1:4], b3=pieces[4:5], s2=pieces[5:])
+    (total, left), last = ring(x, square, a2=pieces[:1], a3=pieces[1:3], b3=pieces[3:5], s2=pieces[5:])
     weight = (eye - sums(left, total, last) * kept_square).astype(BF16)
 
     def update(near):

time: 99.3 us -> 99.3 us (level)
  no operation moved by 1% of the time
where the time goes in v9:
time: 99.3 us; the launch traced here: 99.2 us
  starting transfers between devices  61.1 us (62%)
  waiting for transfers between devices  27.7 us (28%)
  Pallas kernels  8.96 us (9%)
  other arithmetic  1.19 us (1%)
    ppermute x34, starting transfers between devices, send(): return lax.ppermute(value, AXES, pairs)  61.1 us
    ppermute x34, waiting for transfers between devices, send(): return lax.ppermute(value, AXES, pairs)  27.7 us
    pallas_call x8, Pallas kernels, call(): pl.pallas_call(kernel, in_specs=specs or [SMEM if arg.dtype == jnp.int32...  8.96 us
  transfers between devices with their start and end apart: 34, of which 13 were waited for; matrix products, arithmetic and copies ran while one was open for 0% of the time, Pallas kernels for 6%

profile of v9, /device:TPU:1, one launch (start us, length us, event | category | flops | bytes accessed | tf_op | source)
XLA Modules:
  0.0 99.2 jit_solution(15866666839044283850)
XLA Ops:
  0.0 1.2 %shard_map.37 = (bf16[192,768]{1,0:T(8,128)(2,1)S(1)}, bf16[192,384]{1,0:T(8,128)(2,1)S(1)}, bf16[192,384]{1,0:T(8,128)(2,1)S(1)}) custom-call(s32[48,48]{1,0:T(8,128)} %pattern.3, bf16[192,768]{1,0:T(8,128)(2,1)} %matrix.1), custom_call_target="tpu_custom_call" | custom-call | tf_op jit(solution)/shard_map/pallas_call | solution.py:186
  1.2 2.2 %collective-permute-start = (bf16[192,384]{1,0:T(8,128)(2,1)S(1)}, bf16[192,384]{1,0:T(8,128)(2,1)S(1)}, u32[]{:S(2)}, u32[]{:S(2)}) collective-permute-start(bf16[192,384]{1,0:T(8,128)(2,1)S(1)} %get-tuple-element.20), channel_id=1, source_target_pairs={{0,16},{1,17},{2,18},{3,19},{4,20},{5,21},{6,22},{7,23},{8,24},{9,... | collective-permute-start | bytes 442376 | tf_op jit(solution)/shard_map/ppermute | solution.py:47
  3.4 1.2 %collective-permute-start.8 = (bf16[192,768]{1,0:T(8,128)(2,1)S(1)}, bf16[192,768]{1,0:T(8,128)(2,1)S(1)}, u32[]{:S(2)}, u32[]{:S(2)}) collective-permute-start(bf16[192,768]{1,0:T(8,128)(2,1)S(1)} %get-tuple-element.21.refs_8_), channel_id=1, source_target_pairs={{0,8},{1,9},{2,10},{3,11},{4,12},{5,13},{6,14},{7,15},{8,0},{9,1},... | collective-permute-start | bytes 884744 | tf_op jit(solution)/shard_map/ppermute | solution.py:47
  4.7 5.3 %collective-permute-start.9 = (bf16[192,768]{1,0:T(8,128)(2,1)S(1)}, bf16[192,768]{1,0:T(8,128)(2,1)S(1)}, u32[]{:S(2)}, u32[]{:S(2)}) collective-permute-start(bf16[192,768]{1,0:T(8,128)(2,1)S(1)} %get-tuple-element.21.refs_8_), channel_id=1, source_target_pairs={{0,32},{1,33},{2,34},{3,35},{4,36},{5,37},{6,38},{7,39},{8,232},{9... | collective-permute-start | bytes 884744 | tf_op jit(solution)/shard_map/ppermute | solution.py:47
  10.0 0.0 collective-permute-done
  10.0 1.3 %collective-permute-start.1 = (bf16[384,384]{1,0:T(8,128)(2,1)S(1)}, bf16[384,384]{1,0:T(8,128)(2,1)S(1)}, u32[]{:S(2)}, u32[]{:S(2)}) collective-permute-start(bf16[384,384]{1,0:T(8,128)(2,1)S(1)} %constant_dynamic-update-slice_fusion.refs_0_), channel_id=1, source_target_pairs={{0,1},{1,2},{2,3},{3,0},{4,5},{5,6},{6,7},{7,4},{8,9},{9,10},{10,1... | collective-permute-start | bytes 884744 | tf_op jit(solution)/shard_map/ppermute | solution.py:47
  11.3 1.5 %collective-permute-start.2 = (bf16[384,384]{1,0:T(8,128)(2,1)S(1)}, bf16[384,384]{1,0:T(8,128)(2,1)S(1)}, u32[]{:S(2)}, u32[]{:S(2)}) collective-permute-start(bf16[384,384]{1,0:T(8,128)(2,1)S(1)} %constant_dynamic-update-slice_fusion.refs_0_), channel_id=1, source_target_pairs={{0,3},{1,0},{2,1},{3,2},{4,7},{5,4},{6,5},{7,6},{8,11},{9,8},{10,9... | collective-permute-start | bytes 884744 | tf_op jit(solution)/shard_map/ppermute | solution.py:47
  12.8 2.4 %collective-permute-start.10 = (bf16[192,768]{1,0:T(8,128)(2,1)S(1)}, bf16[192,768]{1,0:T(8,128)(2,1)S(1)}, u32[]{:S(2)}, u32[]{:S(2)}) collective-permute-start(bf16[192,768]{1,0:T(8,128)(2,1)S(1)} %collective-permute-done.8.refs_9_), channel_id=1, source_target_pairs={{0,32},{1,33},{2,34},{3,35},{4,36},{5,37},{6,38},{7,39},{8,232},{9... | collective-permute-start | bytes 884744 | tf_op jit(solution)/shard_map/ppermute | solution.py:47
  15.2 2.9 %collective-permute-start.3 = (bf16[384,384]{1,0:T(8,128)(2,1)S(1)}, bf16[384,384]{1,0:T(8,128)(2,1)S(1)}, u32[]{:S(2)}, u32[]{:S(2)}) collective-permute-start(bf16[384,384]{1,0:T(8,128)(2,1)S(1)} %constant_dynamic-update-slice_fusion.refs_0_), channel_id=1, source_target_pairs={{0,4},{1,5},{2,6},{3,7},{4,0},{5,1},{6,2},{7,3},{8,12},{9,13},{10,... | collective-permute-start | bytes 884744 | tf_op jit(solution)/shard_map/ppermute | solution.py:47
  18.1 0.7 collective-permute-start.11
  18.9 1.3 %collective-permute-done.1.refs_1_ = bf16[384,384]{1,0:T(8,128)(2,1)S(1)} collective-permute-done((bf16[384,384]{1,0:T(8,128)(2,1)S(1)}, bf16[384,384]{1,0:T(8,128)(2,1)S(1)}, u32[]{:S(2)}, u32[]{:S(2)}) %collective-permute-start.1) | collective-permute-done | bytes 294944 | tf_op jit(solution)/shard_map/ppermute | solution.py:47
  20.2 2.6 %collective-permute-start.4 = (bf16[384,384]{1,0:T(8,128)(2,1)S(1)}, bf16[384,384]{1,0:T(8,128)(2,1)S(1)}, u32[]{:S(2)}, u32[]{:S(2)}) collective-permute-start(bf16[384,384]{1,0:T(8,128)(2,1)S(1)} %broadcast_select_fusion), channel_id=1, source_target_pairs={{0,1},{1,2},{2,3},{3,0},{4,5},{5,6},{6,7},{7,4},{8,11},{9,8},{10,9... | collective-permute-start | bytes 884744 | tf_op jit(solution)/shard_map/ppermute | solution.py:47
  22.8 0.4 collective-permute-start.12
  23.2 0.8 collective-permute-done.11.refs_12_
  24.0 1.9 %collective-permute-start.13 = (bf16[192,768]{1,0:T(8,128)(2,1)S(1)}, bf16[192,768]{1,0:T(8,128)(2,1)S(1)}, u32[]{:S(2)}, u32[]{:S(2)}) collective-permute-start(bf16[192,768]{1,0:T(8,128)(2,1)S(1)} %collective-permute-done.11.refs_12_), channel_id=1, source_target_pairs={{0,32},{1,33},{2,34},{3,35},{4,36},{5,37},{6,38},{7,39},{8,232},{9... | collective-permute-start | bytes 884744 | tf_op jit(solution)/shard_map/ppermute | solution.py:47
  26.0 0.0 collective-permute-done.3.refs_3_
  26.0 0.0 collective-permute-start.5
  26.0 2.7 %collective-permute-start.6 = (bf16[384,384]{1,0:T(8,128)(2,1)S(1)}, bf16[384,384]{1,0:T(8,128)(2,1)S(1)}, u32[]{:S(2)}, u32[]{:S(2)}) collective-permute-start(bf16[384,384]{1,0:T(8,128)(2,1)S(1)} %collective-permute-done.3.refs_3_), channel_id=1, source_target_pairs={{0,3},{1,0},{2,1},{3,2},{4,7},{5,4},{6,5},{7,6},{8,11},{9,8},{10,9... | collective-permute-start | bytes 884744 | tf_op jit(solution)/shard_map/ppermute | solution.py:47
  28.6 2.3 %collective-permute-start.7 = (bf16[384,384]{1,0:T(8,128)(2,1)S(1)}, bf16[384,384]{1,0:T(8,128)(2,1)S(1)}, u32[]{:S(2)}, u32[]{:S(2)}) collective-permute-start(bf16[384,384]{1,0:T(8,128)(2,1)S(1)} %collective-permute-done.4.refs_4_), channel_id=1, source_target_pairs={{0,4},{1,5},{2,6},{3,7},{4,0},{5,1},{6,2},{7,3},{8,12},{9,13},{10,... | collective-permute-start | bytes 884744 | tf_op jit(solution)/shard_map/ppermute | solution.py:47
  30.9 0.0 collective-permute-start.14
  31.0 0.9 collective-permute-done.13.refs_14_
  31.8 1.6 %collective-permute-start.16 = (bf16[384,768]{1,0:T(8,128)(2,1)S(1)}, bf16[384,768]{1,0:T(8,128)(2,1)S(1)}, u32[]{:S(2)}, u32[]{:S(2)}) collective-permute-start(bf16[384,768]{1,0:T(8,128)(2,1)S(1)} %pad_maximum_fusion), channel_id=1, source_target_pairs={{0,8},{1,9},{2,10},{3,11},{4,12},{5,13},{6,14},{7,15},{8,0},{9,1},... | collective-permute-start | bytes 1769480 | tf_op jit(solution)/shard_map/ppermute | solution.py:47
  33.5 2.7 %collective-permute-done.5.refs_5_ = bf16[384,384]{1,0:T(8,128)(2,1)S(1)} collective-permute-done((bf16[384,384]{1,0:T(8,128)(2,1)S(1)}, bf16[384,384]{1,0:T(8,128)(2,1)S(1)}, u32[]{:S(2)}, u32[]{:S(2)}) %collective-permute-start.5) | collective-permute-done | bytes 294944 | tf_op jit(solution)/shard_map/ppermute | solution.py:47
  36.2 0.3 collective-permute-start.15
  36.4 2.2 %collective-permute-done.7.refs_7_ = bf16[384,384]{1,0:T(8,128)(2,1)S(1)} collective-permute-done((bf16[384,384]{1,0:T(8,128)(2,1)S(1)}, bf16[384,384]{1,0:T(8,128)(2,1)S(1)}, u32[]{:S(2)}, u32[]{:S(2)}) %collective-permute-start.7) | collective-permute-done | bytes 294944 | tf_op jit(solution)/shard_map/ppermute | solution.py:47
  38.6 1.0 collective-permute-start.17
  39.6 0.0 collective-permute-done.14.refs_15_
  39.6 1.5 %collective-permute-start.18 = (bf16[384,768]{1,0:T(8,128)(2,1)S(1)}, bf16[384,768]{1,0:T(8,128)(2,1)S(1)}, u32[]{:S(2)}, u32[]{:S(2)}) collective-permute-start(bf16[384,768]{1,0:T(8,128)(2,1)S(1)} %pad_maximum_fusion.2), channel_id=1, source_target_pairs={{0,8},{1,9},{2,10},{3,11},{4,12},{5,13},{6,14},{7,15},{8,0},{9,1},... | collective-permute-start | bytes 1769480 | tf_op jit(solution)/shard_map/ppermute | solution.py:47
  41.1 1.8 %shard_map.38 = (f32[384,768]{1,0:T(8,128)S(1)}, bf16[8,2,384,192]{3,2,1,0:T(8,128)(2,1)S(1)}) custom-call(bf16[384,384]{1,0:T(8,128)(2,1)S(1)} %constant_dynamic-update-slice_fusion.refs_0_, bf16[384,384]{1,0:T(8,128)(2,1)S(1)} %collective-permute-done.1.refs_1_, bf16[384,384]{1,0:T(8,128)(2,1)S(1)} %collective-permute-done.2.refs_2_, ...), custom_call_target="tpu_custom_call" | custom-call | flops 905969664 | tf_op jit(solution)/shard_map/pallas_call | solution.py:186
  42.9 0.0 collective-permute-done.15.a4
  42.9 1.6 %collective-permute-start.19 = (bf16[192,768]{1,0:T(8,128)(2,1)S(1)}, bf16[192,768]{1,0:T(8,128)(2,1)S(1)}, u32[]{:S(2)}, u32[]{:S(2)}) collective-permute-start(bf16[192,768]{1,0:T(8,128)(2,1)S(1)} %collective-permute-done.15.a4), channel_id=1, source_target_pairs={{0,8},{1,9},{2,10},{3,11},{4,12},{5,13},{6,14},{7,15},{8,0},{9,1},... | collective-permute-start | bytes 884744 | tf_op jit(solution)/shard_map/ppermute | solution.py:47
  44.5 0.0 collective-permute-done.16.refs_0_
  44.5 1.2 %collective-permute-done.19.refs_3_ = bf16[192,768]{1,0:T(8,128)(2,1)S(1)} collective-permute-done((bf16[192,768]{1,0:T(8,128)(2,1)S(1)}, bf16[192,768]{1,0:T(8,128)(2,1)S(1)}, u32[]{:S(2)}, u32[]{:S(2)}) %collective-permute-start.19) | collective-permute-done | bytes 294944 | tf_op jit(solution)/shard_map/ppermute | solution.py:47
  45.8 0.8 shard_map.41
  46.5 0.7 collective-permute-start.20
  47.3 1.5 %shard_map.39 = (f32[192,768]{1,0:T(8,128)S(1)}, f32[192,768]{1,0:T(8,128)S(1)}, f32[192,768]{1,0:T(8,128)S(1)}) custom-call(s32[48,48]{1,0:T(8,128)S(1)} %copy-done, s32[48,48]{1,0:T(8,128)S(1)} %copy-done.1), custom_call_target="tpu_custom_call" | custom-call | flops 147456 | tf_op jit(solution)/shard_map/pallas_call | solution.py:186
  48.8 0.8 shard_map.40
  49.5 5.3 %collective-permute-done.20 = bf16[192,768]{1,0:T(8,128)(2,1)S(1)} collective-permute-done((bf16[192,768]{1,0:T(8,128)(2,1)S(1)}, bf16[192,768]{1,0:T(8,128)(2,1)S(1)}, u32[]{:S(2)}, u32[]{:S(2)}) %collective-permute-start.20) | collective-permute-done | bytes 294944 | tf_op jit(solution)/shard_map/ppermute | solution.py:47
  54.8 0.1 subtract_convert_fusion.refs_1_
  55.0 1.3 %collective-permute-start.21 = (bf16[192,768]{1,0:T(8,128)(2,1)S(1)}, bf16[192,768]{1,0:T(8,128)(2,1)S(1)}, u32[]{:S(2)}, u32[]{:S(2)}) collective-permute-start(bf16[192,768]{1,0:T(8,128)(2,1)S(1)} %subtract_convert_fusion.refs_1_), channel_id=1, source_target_pairs={{0,8},{1,9},{2,10},{3,11},{4,12},{5,13},{6,14},{7,15},{8,0},{9,1},... | collective-permute-start | bytes 884744 | tf_op jit(solution)/shard_map/ppermute | solution.py:47
  56.3 1.3 %collective-permute-start.22 = (bf16[192,768]{1,0:T(8,128)(2,1)S(1)}, bf16[192,768]{1,0:T(8,128)(2,1)S(1)}, u32[]{:S(2)}, u32[]{:S(2)}) collective-permute-start(bf16[192,768]{1,0:T(8,128)(2,1)S(1)} %subtract_convert_fusion.refs_1_), channel_id=1, source_target_pairs={{0,32},{1,33},{2,34},{3,35},{4,36},{5,37},{6,38},{7,39},{8,232},{9... | collective-permute-start | bytes 884744 | tf_op jit(solution)/shard_map/ppermute | solution.py:47
  57.6 0.0 collective-permute-done.21.refs_2_
  57.6 1.2 %collective-permute-start.23 = (bf16[192,768]{1,0:T(8,128)(2,1)S(1)}, bf16[192,768]{1,0:T(8,128)(2,1)S(1)}, u32[]{:S(2)}, u32[]{:S(2)}) collective-permute-start(bf16[192,768]{1,0:T(8,128)(2,1)S(1)} %collective-permute-done.21.refs_2_), channel_id=1, source_target_pairs={{0,32},{1,33},{2,34},{3,35},{4,36},{5,37},{6,38},{7,39},{8,232},{9... | collective-permute-start | bytes 884744 | tf_op jit(solution)/shard_map/ppermute | solution.py:47
  58.8 3.3 %collective-permute-done.22.refs_3_ = bf16[192,768]{1,0:T(8,128)(2,1)S(1)} collective-permute-done((bf16[192,768]{1,0:T(8,128)(2,1)S(1)}, bf16[192,768]{1,0:T(8,128)(2,1)S(1)}, u32[]{:S(2)}, u32[]{:S(2)}) %collective-permute-start.22) | collective-permute-done | bytes 294944 | tf_op jit(solution)/shard_map/ppermute | solution.py:47
  62.1 2.2 %collective-permute-start.24 = (bf16[192,768]{1,0:T(8,128)(2,1)S(1)}, bf16[192,768]{1,0:T(8,128)(2,1)S(1)}, u32[]{:S(2)}, u32[]{:S(2)}) collective-permute-start(bf16[192,768]{1,0:T(8,128)(2,1)S(1)} %collective-permute-done.22.refs_3_), channel_id=1, source_target_pairs={{0,32},{1,33},{2,34},{3,35},{4,36},{5,37},{6,38},{7,39},{8,232},{9... | collective-permute-start | bytes 884744 | tf_op jit(solution)/shard_map/ppermute | solution.py:47
  64.4 0.9 collective-permute-done.23.refs_4_
  65.3 2.2 %collective-permute-start.25 = (bf16[192,768]{1,0:T(8,128)(2,1)S(1)}, bf16[192,768]{1,0:T(8,128)(2,1)S(1)}, u32[]{:S(2)}, u32[]{:S(2)}) collective-permute-start(bf16[192,768]{1,0:T(8,128)(2,1)S(1)} %collective-permute-done.23.refs_4_), channel_id=1, source_target_pairs={{0,32},{1,33},{2,34},{3,35},{4,36},{5,37},{6,38},{7,39},{8,232},{9... | collective-permute-start | bytes 884744 | tf_op jit(solution)/shard_map/ppermute | solution.py:47
  67.5 0.6 collective-permute-done.24.refs_5_
  68.2 3.0 %collective-permute-start.26 = (bf16[192,768]{1,0:T(8,128)(2,1)S(1)}, bf16[192,768]{1,0:T(8,128)(2,1)S(1)}, u32[]{:S(2)}, u32[]{:S(2)}) collective-permute-start(bf16[192,768]{1,0:T(8,128)(2,1)S(1)} %collective-permute-done.24.refs_5_), channel_id=1, source_target_pairs={{0,32},{1,33},{2,34},{3,35},{4,36},{5,37},{6,38},{7,39},{8,232},{9... | collective-permute-start | bytes 884744 | tf_op jit(solution)/shard_map/ppermute | solution.py:47
  71.2 0.5 collective-permute-done.25.refs_6_
  71.6 2.7 %collective-permute-start.27 = (bf16[192,768]{1,0:T(8,128)(2,1)S(1)}, bf16[192,768]{1,0:T(8,128)(2,1)S(1)}, u32[]{:S(2)}, u32[]{:S(2)}) collective-permute-start(bf16[192,768]{1,0:T(8,128)(2,1)S(1)} %collective-permute-done.25.refs_6_), channel_id=1, source_target_pairs={{0,32},{1,33},{2,34},{3,35},{4,36},{5,37},{6,38},{7,39},{8,232},{9... | collective-permute-start | bytes 884744 | tf_op jit(solution)/shard_map/ppermute | solution.py:47
  74.4 1.2 %collective-permute-start.29 = (bf16[384,768]{1,0:T(8,128)(2,1)S(1)}, bf16[384,768]{1,0:T(8,128)(2,1)S(1)}, u32[]{:S(2)}, u32[]{:S(2)}) collective-permute-start(bf16[384,768]{1,0:T(8,128)(2,1)S(1)} %pad_maximum_fusion.3), channel_id=1, source_target_pairs={{0,8},{1,9},{2,10},{3,11},{4,12},{5,13},{6,14},{7,15},{8,0},{9,1},... | collective-permute-start | bytes 1769480 | tf_op jit(solution)/shard_map/ppermute | solution.py:47
  75.5 3.0 %collective-permute-start.28 = (bf16[192,768]{1,0:T(8,128)(2,1)S(1)}, bf16[192,768]{1,0:T(8,128)(2,1)S(1)}, u32[]{:S(2)}, u32[]{:S(2)}) collective-permute-start(bf16[192,768]{1,0:T(8,128)(2,1)S(1)} %collective-permute-done.26.refs_7_), channel_id=1, source_target_pairs={{0,32},{1,33},{2,34},{3,35},{4,36},{5,37},{6,38},{7,39},{8,232},{9... | collective-permute-start | bytes 884744 | tf_op jit(solution)/shard_map/ppermute | solution.py:47
  78.5 2.0 %collective-permute-start.30 = (bf16[384,768]{1,0:T(8,128)(2,1)S(1)}, bf16[384,768]{1,0:T(8,128)(2,1)S(1)}, u32[]{:S(2)}, u32[]{:S(2)}) collective-permute-start(bf16[384,768]{1,0:T(8,128)(2,1)S(1)} %pad_maximum_fusion.4), channel_id=1, source_target_pairs={{0,8},{1,9},{2,10},{3,11},{4,12},{5,13},{6,14},{7,15},{8,0},{9,1},... | collective-permute-start | bytes 1769480 | tf_op jit(solution)/shard_map/ppermute | solution.py:47
  80.6 2.9 %collective-permute-start.31 = (bf16[384,768]{1,0:T(8,128)(2,1)S(1)}, bf16[384,768]{1,0:T(8,128)(2,1)S(1)}, u32[]{:S(2)}, u32[]{:S(2)}) collective-permute-start(bf16[384,768]{1,0:T(8,128)(2,1)S(1)} %pad_maximum_fusion.5), channel_id=1, source_target_pairs={{0,8},{1,9},{2,10},{3,11},{4,12},{5,13},{6,14},{7,15},{8,0},{9,1},... | collective-permute-start | bytes 1769480 | tf_op jit(solution)/shard_map/ppermute | solution.py:47
  83.4 1.4 %shard_map.42.total = f32[384,768]{1,0:T(8,128)S(1)} custom-call(bf16[8,2,384,192]{3,2,1,0:T(8,128)(2,1)S(1)} %get-tuple-element.25.left.refs_0_, bf16[192,768]{1,0:T(8,128)(2,1)S(1)} %subtract_convert_fusion.refs_1_, bf16[192,768]{1,0:T(8,128)(2,1)S(1)} %collective-permute-done.21.refs_2_, bf16[192,768]{1,0:T(8,128)(2,1)S(1)} %collective-permute-done.22.refs_3_, ...), custom_call_target="tpu_custom_call" | custom-call | flops 905969664 | tf_op jit(solution)/shard_map/pallas_call | solution.py:186
  84.8 3.3 %collective-permute-start.32 = (bf16[192,768]{1,0:T(8,128)(2,1)S(1)}, bf16[192,768]{1,0:T(8,128)(2,1)S(1)}, u32[]{:S(2)}, u32[]{:S(2)}) collective-permute-start(bf16[192,768]{1,0:T(8,128)(2,1)S(1)} %collective-permute-done.28.a4), channel_id=1, source_target_pairs={{0,8},{1,9},{2,10},{3,11},{4,12},{5,13},{6,14},{7,15},{8,0},{9,1},... | collective-permute-start | bytes 884744 | tf_op jit(solution)/shard_map/ppermute | solution.py:47
  88.1 0.0 collective-permute-done.29.refs_0_
  88.1 1.2 %collective-permute-done.32.refs_3_ = bf16[192,768]{1,0:T(8,128)(2,1)S(1)} collective-permute-done((bf16[192,768]{1,0:T(8,128)(2,1)S(1)}, bf16[192,768]{1,0:T(8,128)(2,1)S(1)}, u32[]{:S(2)}, u32[]{:S(2)}) %collective-permute-start.32) | collective-permute-done | bytes 294944 | tf_op jit(solution)/shard_map/ppermute | solution.py:47
  89.3 0.8 shard_map.44
  90.1 0.7 collective-permute-start.33
  90.8 0.8 shard_map.43
  91.6 6.8 %collective-permute-done.33 = bf16[192,768]{1,0:T(8,128)(2,1)S(1)} collective-permute-done((bf16[192,768]{1,0:T(8,128)(2,1)S(1)}, bf16[192,768]{1,0:T(8,128)(2,1)S(1)}, u32[]{:S(2)}, u32[]{:S(2)}) %collective-permute-start.33) | collective-permute-done | bytes 294944 | tf_op jit(solution)/shard_map/ppermute | solution.py:47
  98.4 0.8 multiply_convert_fusion
  (27 shorter events, 0.4 us)
Async XLA Ops:
  1.2 8.8 %collective-permute-start = (bf16[192,384]{1,0:T(8,128)(2,1)S(1)}, bf16[192,384]{1,0:T(8,128)(2,1)S(1)}, u32[]{:S(2)}, u32[]{:S(2)}) collective-permute-start(bf16[192,384]{1,0:T(8,128)(2,1)S(1)} %get-tuple-element.20), channel_id=1, source_target_pairs={{0,16},{1,17},{2,18},{3,19},{4,20},{5,21},{6,22},{7,23},{8,24},{9,... | collective-permute-start | bytes 442376 | tf_op jit(solution)/shard_map/ppermute | solution.py:47
  3.4 9.4 %collective-permute-start.8 = (bf16[192,768]{1,0:T(8,128)(2,1)S(1)}, bf16[192,768]{1,0:T(8,128)(2,1)S(1)}, u32[]{:S(2)}, u32[]{:S(2)}) collective-permute-start(bf16[192,768]{1,0:T(8,128)(2,1)S(1)} %get-tuple-element.21.refs_8_), channel_id=1, source_target_pairs={{0,8},{1,9},{2,10},{3,11},{4,12},{5,13},{6,14},{7,15},{8,0},{9,1},... | collective-permute-start | bytes 884744 | tf_op jit(solution)/shard_map/ppermute | solution.py:47
  4.7 13.5 %collective-permute-start.9 = (bf16[192,768]{1,0:T(8,128)(2,1)S(1)}, bf16[192,768]{1,0:T(8,128)(2,1)S(1)}, u32[]{:S(2)}, u32[]{:S(2)}) collective-permute-start(bf16[192,768]{1,0:T(8,128)(2,1)S(1)} %get-tuple-element.21.refs_8_), channel_id=1, source_target_pairs={{0,32},{1,33},{2,34},{3,35},{4,36},{5,37},{6,38},{7,39},{8,232},{9... | collective-permute-start | bytes 884744 | tf_op jit(solution)/shard_map/ppermute | solution.py:47
  10.0 10.2 %collective-permute-start.1 = (bf16[384,384]{1,0:T(8,128)(2,1)S(1)}, bf16[384,384]{1,0:T(8,128)(2,1)S(1)}, u32[]{:S(2)}, u32[]{:S(2)}) collective-permute-start(bf16[384,384]{1,0:T(8,128)(2,1)S(1)} %constant_dynamic-update-slice_fusion.refs_0_), channel_id=1, source_target_pairs={{0,1},{1,2},{2,3},{3,0},{4,5},{5,6},{6,7},{7,4},{8,9},{9,10},{10,1... | collective-permute-start | bytes 884744 | tf_op jit(solution)/shard_map/ppermute | solution.py:47
  11.3 8.9 %collective-permute-start.2 = (bf16[384,384]{1,0:T(8,128)(2,1)S(1)}, bf16[384,384]{1,0:T(8,128)(2,1)S(1)}, u32[]{:S(2)}, u32[]{:S(2)}) collective-permute-start(bf16[384,384]{1,0:T(8,128)(2,1)S(1)} %constant_dynamic-update-slice_fusion.refs_0_), channel_id=1, source_target_pairs={{0,3},{1,0},{2,1},{3,2},{4,7},{5,4},{6,5},{7,6},{8,11},{9,8},{10,9... | collective-permute-start | bytes 884744 | tf_op jit(solution)/shard_map/ppermute | solution.py:47
  12.8 10.0 %collective-permute-start.10 = (bf16[192,768]{1,0:T(8,128)(2,1)S(1)}, bf16[192,768]{1,0:T(8,128)(2,1)S(1)}, u32[]{:S(2)}, u32[]{:S(2)}) collective-permute-start(bf16[192,768]{1,0:T(8,128)(2,1)S(1)} %collective-permute-done.8.refs_9_), channel_id=1, source_target_pairs={{0,32},{1,33},{2,34},{3,35},{4,36},{5,37},{6,38},{7,39},{8,232},{9... | collective-permute-start | bytes 884744 | tf_op jit(solution)/shard_map/ppermute | solution.py:47
  15.2 10.7 %collective-permute-start.3 = (bf16[384,384]{1,0:T(8,128)(2,1)S(1)}, bf16[384,384]{1,0:T(8,128)(2,1)S(1)}, u32[]{:S(2)}, u32[]{:S(2)}) collective-permute-start(bf16[384,384]{1,0:T(8,128)(2,1)S(1)} %constant_dynamic-update-slice_fusion.refs_0_), channel_id=1, source_target_pairs={{0,4},{1,5},{2,6},{3,7},{4,0},{5,1},{6,2},{7,3},{8,12},{9,13},{10,... | collective-permute-start | bytes 884744 | tf_op jit(solution)/shard_map/ppermute | solution.py:47
  18.1 5.9 %collective-permute-start.11 = (bf16[192,768]{1,0:T(8,128)(2,1)S(1)}, bf16[192,768]{1,0:T(8,128)(2,1)S(1)}, u32[]{:S(2)}, u32[]{:S(2)}) collective-permute-start(bf16[192,768]{1,0:T(8,128)(2,1)S(1)} %collective-permute-done.9.refs_10_), channel_id=1, source_target_pairs={{0,32},{1,33},{2,34},{3,35},{4,36},{5,37},{6,38},{7,39},{8,232},{9... | collective-permute-start | bytes 884744 | tf_op jit(solution)/shard_map/ppermute | solution.py:47
  20.2 8.4 %collective-permute-start.4 = (bf16[384,384]{1,0:T(8,128)(2,1)S(1)}, bf16[384,384]{1,0:T(8,128)(2,1)S(1)}, u32[]{:S(2)}, u32[]{:S(2)}) collective-permute-start(bf16[384,384]{1,0:T(8,128)(2,1)S(1)} %broadcast_select_fusion), channel_id=1, source_target_pairs={{0,1},{1,2},{2,3},{3,0},{4,5},{5,6},{6,7},{7,4},{8,11},{9,8},{10,9... | collective-permute-start | bytes 884744 | tf_op jit(solution)/shard_map/ppermute | solution.py:47
  22.8 8.1 %collective-permute-start.12 = (bf16[192,768]{1,0:T(8,128)(2,1)S(1)}, bf16[192,768]{1,0:T(8,128)(2,1)S(1)}, u32[]{:S(2)}, u32[]{:S(2)}) collective-permute-start(bf16[192,768]{1,0:T(8,128)(2,1)S(1)} %collective-permute-done.10.refs_11_), channel_id=1, source_target_pairs={{0,32},{1,33},{2,34},{3,35},{4,36},{5,37},{6,38},{7,39},{8,232},{9... | collective-permute-start | bytes 884744 | tf_op jit(solution)/shard_map/ppermute | solution.py:47
  24.0 7.8 %collective-permute-start.13 = (bf16[192,768]{1,0:T(8,128)(2,1)S(1)}, bf16[192,768]{1,0:T(8,128)(2,1)S(1)}, u32[]{:S(2)}, u32[]{:S(2)}) collective-permute-start(bf16[192,768]{1,0:T(8,128)(2,1)S(1)} %collective-permute-done.11.refs_12_), channel_id=1, source_target_pairs={{0,32},{1,33},{2,34},{3,35},{4,36},{5,37},{6,38},{7,39},{8,232},{9... | collective-permute-start | bytes 884744 | tf_op jit(solution)/shard_map/ppermute | solution.py:47
  26.0 10.2 %collective-permute-start.5 = (bf16[384,384]{1,0:T(8,128)(2,1)S(1)}, bf16[384,384]{1,0:T(8,128)(2,1)S(1)}, u32[]{:S(2)}, u32[]{:S(2)}) collective-permute-start(bf16[384,384]{1,0:T(8,128)(2,1)S(1)} %collective-permute-done.3.refs_3_), channel_id=1, source_target_pairs={{0,1},{1,2},{2,3},{3,0},{4,5},{5,6},{6,7},{7,4},{8,9},{9,10},{10,1... | collective-permute-start | bytes 884744 | tf_op jit(solution)/shard_map/ppermute | solution.py:47
  26.0 10.5 %collective-permute-start.6 = (bf16[384,384]{1,0:T(8,128)(2,1)S(1)}, bf16[384,384]{1,0:T(8,128)(2,1)S(1)}, u32[]{:S(2)}, u32[]{:S(2)}) collective-permute-start(bf16[384,384]{1,0:T(8,128)(2,1)S(1)} %collective-permute-done.3.refs_3_), channel_id=1, source_target_pairs={{0,3},{1,0},{2,1},{3,2},{4,7},{5,4},{6,5},{7,6},{8,11},{9,8},{10,9... | collective-permute-start | bytes 884744 | tf_op jit(solution)/shard_map/ppermute | solution.py:47
  28.6 10.0 %collective-permute-start.7 = (bf16[384,384]{1,0:T(8,128)(2,1)S(1)}, bf16[384,384]{1,0:T(8,128)(2,1)S(1)}, u32[]{:S(2)}, u32[]{:S(2)}) collective-permute-start(bf16[384,384]{1,0:T(8,128)(2,1)S(1)} %collective-permute-done.4.refs_4_), channel_id=1, source_target_pairs={{0,4},{1,5},{2,6},{3,7},{4,0},{5,1},{6,2},{7,3},{8,12},{9,13},{10,... | collective-permute-start | bytes 884744 | tf_op jit(solution)/shard_map/ppermute | solution.py:47
  30.9 8.7 %collective-permute-start.14 = (bf16[192,768]{1,0:T(8,128)(2,1)S(1)}, bf16[192,768]{1,0:T(8,128)(2,1)S(1)}, u32[]{:S(2)}, u32[]{:S(2)}) collective-permute-start(bf16[192,768]{1,0:T(8,128)(2,1)S(1)} %collective-permute-done.12.refs_13_), channel_id=1, source_target_pairs={{0,32},{1,33},{2,34},{3,35},{4,36},{5,37},{6,38},{7,39},{8,232},{9... | collective-permute-start | bytes 884744 | tf_op jit(solution)/shard_map/ppermute | solution.py:47
  31.8 12.7 %collective-permute-start.16 = (bf16[384,768]{1,0:T(8,128)(2,1)S(1)}, bf16[384,768]{1,0:T(8,128)(2,1)S(1)}, u32[]{:S(2)}, u32[]{:S(2)}) collective-permute-start(bf16[384,768]{1,0:T(8,128)(2,1)S(1)} %pad_maximum_fusion), channel_id=1, source_target_pairs={{0,8},{1,9},{2,10},{3,11},{4,12},{5,13},{6,14},{7,15},{8,0},{9,1},... | collective-permute-start | bytes 1769480 | tf_op jit(solution)/shard_map/ppermute | solution.py:47
  36.2 6.7 %collective-permute-start.15 = (bf16[192,768]{1,0:T(8,128)(2,1)S(1)}, bf16[192,768]{1,0:T(8,128)(2,1)S(1)}, u32[]{:S(2)}, u32[]{:S(2)}) collective-permute-start(bf16[192,768]{1,0:T(8,128)(2,1)S(1)} %collective-permute-done.13.refs_14_), channel_id=1, source_target_pairs={{0,32},{1,33},{2,34},{3,35},{4,36},{5,37},{6,38},{7,39},{8,232},{9... | collective-permute-start | bytes 884744 | tf_op jit(solution)/shard_map/ppermute | solution.py:47
  38.6 7.1 %collective-permute-start.17 = (bf16[384,768]{1,0:T(8,128)(2,1)S(1)}, bf16[384,768]{1,0:T(8,128)(2,1)S(1)}, u32[]{:S(2)}, u32[]{:S(2)}) collective-permute-start(bf16[384,768]{1,0:T(8,128)(2,1)S(1)} %pad_maximum_fusion.1), channel_id=1, source_target_pairs={{0,8},{1,9},{2,10},{3,11},{4,12},{5,13},{6,14},{7,15},{8,0},{9,1},... | collective-permute-start | bytes 1769480 | tf_op jit(solution)/shard_map/ppermute | solution.py:47
  39.6 6.1 %collective-permute-start.18 = (bf16[384,768]{1,0:T(8,128)(2,1)S(1)}, bf16[384,768]{1,0:T(8,128)(2,1)S(1)}, u32[]{:S(2)}, u32[]{:S(2)}) collective-permute-start(bf16[384,768]{1,0:T(8,128)(2,1)S(1)} %pad_maximum_fusion.2), channel_id=1, source_target_pairs={{0,8},{1,9},{2,10},{3,11},{4,12},{5,13},{6,14},{7,15},{8,0},{9,1},... | collective-permute-start | bytes 1769480 | tf_op jit(solution)/shard_map/ppermute | solution.py:47
  42.9 2.8 %collective-permute-start.19 = (bf16[192,768]{1,0:T(8,128)(2,1)S(1)}, bf16[192,768]{1,0:T(8,128)(2,1)S(1)}, u32[]{:S(2)}, u32[]{:S(2)}) collective-permute-start(bf16[192,768]{1,0:T(8,128)(2,1)S(1)} %collective-permute-done.15.a4), channel_id=1, source_target_pairs={{0,8},{1,9},{2,10},{3,11},{4,12},{5,13},{6,14},{7,15},{8,0},{9,1},... | collective-permute-start | bytes 884744 | tf_op jit(solution)/shard_map/ppermute | solution.py:47
  45.7 1.5 %copy-start = (s32[48,48]{1,0:T(8,128)S(1)}, s32[48,48]{1,0:T(8,128)}, u32[]{:S(2)}) copy-start(s32[48,48]{1,0:T(8,128)} %pattern.3) | copy-start | bytes 27652
  45.7 1.5 %copy-start.1 = (s32[48,48]{1,0:T(8,128)S(1)}, s32[48,48]{1,0:T(8,128)}, u32[]{:S(2)}) copy-start(s32[48,48]{1,0:T(8,128)} %keep.1) | copy-start | bytes 27652
  46.5 8.3 %collective-permute-start.20 = (bf16[192,768]{1,0:T(8,128)(2,1)S(1)}, bf16[192,768]{1,0:T(8,128)(2,1)S(1)}, u32[]{:S(2)}, u32[]{:S(2)}) collective-permute-start(bf16[192,768]{1,0:T(8,128)(2,1)S(1)} %shard_map.41), channel_id=1, source_target_pairs={{0,16},{1,17},{2,18},{3,19},{4,20},{5,21},{6,22},{7,23},{8,24},{9,... | collective-permute-start | bytes 884744 | tf_op jit(solution)/shard_map/ppermute | solution.py:47
  55.0 2.6 %collective-permute-start.21 = (bf16[192,768]{1,0:T(8,128)(2,1)S(1)}, bf16[192,768]{1,0:T(8,128)(2,1)S(1)}, u32[]{:S(2)}, u32[]{:S(2)}) collective-permute-start(bf16[192,768]{1,0:T(8,128)(2,1)S(1)} %subtract_convert_fusion.refs_1_), channel_id=1, source_target_pairs={{0,8},{1,9},{2,10},{3,11},{4,12},{5,13},{6,14},{7,15},{8,0},{9,1},... | collective-permute-start | bytes 884744 | tf_op jit(solution)/shard_map/ppermute | solution.py:47
  56.3 5.9 %collective-permute-start.22 = (bf16[192,768]{1,0:T(8,128)(2,1)S(1)}, bf16[192,768]{1,0:T(8,128)(2,1)S(1)}, u32[]{:S(2)}, u32[]{:S(2)}) collective-permute-start(bf16[192,768]{1,0:T(8,128)(2,1)S(1)} %subtract_convert_fusion.refs_1_), channel_id=1, source_target_pairs={{0,32},{1,33},{2,34},{3,35},{4,36},{5,37},{6,38},{7,39},{8,232},{9... | collective-permute-start | bytes 884744 | tf_op jit(solution)/shard_map/ppermute | solution.py:47
  57.6 7.7 %collective-permute-start.23 = (bf16[192,768]{1,0:T(8,128)(2,1)S(1)}, bf16[192,768]{1,0:T(8,128)(2,1)S(1)}, u32[]{:S(2)}, u32[]{:S(2)}) collective-permute-start(bf16[192,768]{1,0:T(8,128)(2,1)S(1)} %collective-permute-done.21.refs_2_), channel_id=1, source_target_pairs={{0,32},{1,33},{2,34},{3,35},{4,36},{5,37},{6,38},{7,39},{8,232},{9... | collective-permute-start | bytes 884744 | tf_op jit(solution)/shard_map/ppermute | solution.py:47
  62.1 6.0 %collective-permute-start.24 = (bf16[192,768]{1,0:T(8,128)(2,1)S(1)}, bf16[192,768]{1,0:T(8,128)(2,1)S(1)}, u32[]{:S(2)}, u32[]{:S(2)}) collective-permute-start(bf16[192,768]{1,0:T(8,128)(2,1)S(1)} %collective-permute-done.22.refs_3_), channel_id=1, source_target_pairs={{0,32},{1,33},{2,34},{3,35},{4,36},{5,37},{6,38},{7,39},{8,232},{9... | collective-permute-start | bytes 884744 | tf_op jit(solution)/shard_map/ppermute | solution.py:47
  65.3 6.3 %collective-permute-start.25 = (bf16[192,768]{1,0:T(8,128)(2,1)S(1)}, bf16[192,768]{1,0:T(8,128)(2,1)S(1)}, u32[]{:S(2)}, u32[]{:S(2)}) collective-permute-start(bf16[192,768]{1,0:T(8,128)(2,1)S(1)} %collective-permute-done.23.refs_4_), channel_id=1, source_target_pairs={{0,32},{1,33},{2,34},{3,35},{4,36},{5,37},{6,38},{7,39},{8,232},{9... | collective-permute-start | bytes 884744 | tf_op jit(solution)/shard_map/ppermute | solution.py:47
  68.2 7.4 %collective-permute-start.26 = (bf16[192,768]{1,0:T(8,128)(2,1)S(1)}, bf16[192,768]{1,0:T(8,128)(2,1)S(1)}, u32[]{:S(2)}, u32[]{:S(2)}) collective-permute-start(bf16[192,768]{1,0:T(8,128)(2,1)S(1)} %collective-permute-done.24.refs_5_), channel_id=1, source_target_pairs={{0,32},{1,33},{2,34},{3,35},{4,36},{5,37},{6,38},{7,39},{8,232},{9... | collective-permute-start | bytes 884744 | tf_op jit(solution)/shard_map/ppermute | solution.py:47
  71.6 8.9 %collective-permute-start.27 = (bf16[192,768]{1,0:T(8,128)(2,1)S(1)}, bf16[192,768]{1,0:T(8,128)(2,1)S(1)}, u32[]{:S(2)}, u32[]{:S(2)}) collective-permute-start(bf16[192,768]{1,0:T(8,128)(2,1)S(1)} %collective-permute-done.25.refs_6_), channel_id=1, source_target_pairs={{0,32},{1,33},{2,34},{3,35},{4,36},{5,37},{6,38},{7,39},{8,232},{9... | collective-permute-start | bytes 884744 | tf_op jit(solution)/shard_map/ppermute | solution.py:47
  74.4 13.7 %collective-permute-start.29 = (bf16[384,768]{1,0:T(8,128)(2,1)S(1)}, bf16[384,768]{1,0:T(8,128)(2,1)S(1)}, u32[]{:S(2)}, u32[]{:S(2)}) collective-permute-start(bf16[384,768]{1,0:T(8,128)(2,1)S(1)} %pad_maximum_fusion.3), channel_id=1, source_target_pairs={{0,8},{1,9},{2,10},{3,11},{4,12},{5,13},{6,14},{7,15},{8,0},{9,1},... | collective-permute-start | bytes 1769480 | tf_op jit(solution)/shard_map/ppermute | solution.py:47
  75.5 9.3 %collective-permute-start.28 = (bf16[192,768]{1,0:T(8,128)(2,1)S(1)}, bf16[192,768]{1,0:T(8,128)(2,1)S(1)}, u32[]{:S(2)}, u32[]{:S(2)}) collective-permute-start(bf16[192,768]{1,0:T(8,128)(2,1)S(1)} %collective-permute-done.26.refs_7_), channel_id=1, source_target_pairs={{0,32},{1,33},{2,34},{3,35},{4,36},{5,37},{6,38},{7,39},{8,232},{9... | collective-permute-start | bytes 884744 | tf_op jit(solution)/shard_map/ppermute | solution.py:47
  78.5 9.6 %collective-permute-start.30 = (bf16[384,768]{1,0:T(8,128)(2,1)S(1)}, bf16[384,768]{1,0:T(8,128)(2,1)S(1)}, u32[]{:S(2)}, u32[]{:S(2)}) collective-permute-start(bf16[384,768]{1,0:T(8,128)(2,1)S(1)} %pad_maximum_fusion.4), channel_id=1, source_target_pairs={{0,8},{1,9},{2,10},{3,11},{4,12},{5,13},{6,14},{7,15},{8,0},{9,1},... | collective-permute-start | bytes 1769480 | tf_op jit(solution)/shard_map/ppermute | solution.py:47
  80.6 8.7 %collective-permute-start.31 = (bf16[384,768]{1,0:T(8,128)(2,1)S(1)}, bf16[384,768]{1,0:T(8,128)(2,1)S(1)}, u32[]{:S(2)}, u32[]{:S(2)}) collective-permute-start(bf16[384,768]{1,0:T(8,128)(2,1)S(1)} %pad_maximum_fusion.5), channel_id=1, source_target_pairs={{0,8},{1,9},{2,10},{3,11},{4,12},{5,13},{6,14},{7,15},{8,0},{9,1},... | collective-permute-start | bytes 1769480 | tf_op jit(solution)/shard_map/ppermute | solution.py:47
  84.8 4.5 %collective-permute-start.32 = (bf16[192,768]{1,0:T(8,128)(2,1)S(1)}, bf16[192,768]{1,0:T(8,128)(2,1)S(1)}, u32[]{:S(2)}, u32[]{:S(2)}) collective-permute-start(bf16[192,768]{1,0:T(8,128)(2,1)S(1)} %collective-permute-done.28.a4), channel_id=1, source_target_pairs={{0,8},{1,9},{2,10},{3,11},{4,12},{5,13},{6,14},{7,15},{8,0},{9,1},... | collective-permute-start | bytes 884744 | tf_op jit(solution)/shard_map/ppermute | solution.py:47
  90.1 8.3 %collective-permute-start.33 = (bf16[192,768]{1,0:T(8,128)(2,1)S(1)}, bf16[192,768]{1,0:T(8,128)(2,1)S(1)}, u32[]{:S(2)}, u32[]{:S(2)}) collective-permute-start(bf16[192,768]{1,0:T(8,128)(2,1)S(1)} %shard_map.44), channel_id=1, source_target_pairs={{0,16},{1,17},{2,18},{3,19},{4,20},{5,21},{6,22},{7,23},{8,24},{9,... | collective-permute-start | bytes 884744 | tf_op jit(solution)/shard_map/ppermute | solution.py:47
